TPU v7x, 32 devices: a whole 2x2x4 slice. The times are simulated.
32 devices in a mesh: row: 4 (over y, x), col: 8 (over z, core).
Axes of the slice: x: 2, y: 2, z: 4, core: 2. Of those that a mesh axis runs over, the one named last changes fastest.
Arguments:
- observed: float32 [4, 32768], P(None, ('row', 'col')), may hold values from -50 to 50
- tile_values: bfloat16 [128, 16, 256, 256], P('row', 'col'), may hold values from -3.203125 to 3.203125
- tile_cols: int32 [128, 16], P('row', 'col'), may hold values from 0 to 511
Outputs:
- solution: float32 [4, 1048576], P(None, ('col', 'row'))
- residual_ratio: float32 [4], replicated
All inputs are finite; a program needn't handle non-finite values.
Results may differ from a plain program's by a relative error of at most 0.0021.
Values may be sent and summed in bfloat16 or wider, within the bound.
No kernel may reach another device: no remote copies, remote signals or barrier semaphores. Data moves between devices by JAX's collectives and lax.ppermute only.
A program may use at most 128 MiB of HBM per device.

v0:
```python
import jax
import jax.numpy as jnp
from jax import lax
from jax.sharding import PartitionSpec as P

ITERS = 2
N = 1048576


epsilon_sq = 1e-06


def local(observed, tile_values, tile_cols):
    right_sides = observed.shape[0]
    row_tiles = tile_values.shape[0]
    per_block = tile_values.shape[1]
    tile_size = tile_values.shape[2]
    col_tiles = N // (tile_size * lax.axis_size("col"))
    panel_len = col_tiles * tile_size
    share_len = panel_len // lax.axis_size("row")
    flat_cols = tile_cols.reshape(-1)

    def adjoint_map(left_bf):
        gathered = lax.all_gather(left_bf, "col", axis=1, tiled=True).reshape(
            right_sides, row_tiles, tile_size
        )
        tile_terms = jnp.einsum(
            "rktj,nrt->nrkj", tile_values, gathered, preferred_element_type=jnp.float32
        )
        tile_terms = tile_terms.reshape(right_sides, row_tiles * per_block, tile_size)
        placed = (
            jnp.zeros((right_sides, col_tiles, tile_size), jnp.float32)
            .at[:, flat_cols]
            .add(tile_terms)
        )
        placed = placed.reshape(right_sides, panel_len)
        summed = lax.psum_scatter(placed, "row", scatter_dimension=1, tiled=True)
        return summed

    def lanczos_pair(left_raw, right_vec):
        beta_sq = lax.psum(jnp.sum(left_raw * left_raw, axis=1), ("row", "col"))
        beta_norm = jnp.sqrt(beta_sq + epsilon_sq)
        product = adjoint_map(left_raw.astype(jnp.bfloat16))
        right_raw = product / beta_norm[:, None] - beta_norm[:, None] * right_vec
        alpha_sq = lax.psum(jnp.sum(right_raw * right_raw, axis=1), ("row", "col"))
        alpha_norm = jnp.sqrt(alpha_sq + epsilon_sq)
        return (beta_norm, alpha_norm, right_raw)

    blank_right = jnp.zeros((right_sides, share_len), jnp.float32)
    beta_norm, alpha_norm, right_raw = lanczos_pair(observed, blank_right)
    first_beta = beta_norm
    left_vec = observed / beta_norm[:, None]
    right_vec = right_raw / alpha_norm[:, None]
    right_bf = right_raw.astype(jnp.bfloat16)
    phibar = beta_norm
    rhobar = alpha_norm
    direction = right_vec
    solution = jnp.zeros_like(right_vec)
    for iteration in range(ITERS):
        whole_panel = lax.all_gather(right_bf, "row", axis=1, tiled=True)
        picked = jnp.take(whole_panel.reshape(right_sides, col_tiles, tile_size), tile_cols, axis=1)
        partial_rows = jnp.einsum(
            "rktj,nrkj->nrt", tile_values, picked, preferred_element_type=jnp.float32
        )
        left_raw = (
            lax.psum_scatter(
                partial_rows.reshape(right_sides, row_tiles * tile_size),
                "col",
                scatter_dimension=1,
                tiled=True,
            )
            / alpha_norm[:, None]
            - alpha_norm[:, None] * left_vec
        )
        beta_norm, alpha_norm, right_raw = lanczos_pair(left_raw, right_vec)
        left_vec = left_raw / beta_norm[:, None]
        right_vec = right_raw / alpha_norm[:, None]
        right_bf = right_raw.astype(jnp.bfloat16)
        rho_val = jnp.sqrt(rhobar * rhobar + beta_norm * beta_norm)
        cosine = rhobar / rho_val
        sine_val = beta_norm / rho_val
        theta_val = sine_val * alpha_norm
        rhobar = -cosine * alpha_norm
        phi_val = cosine * phibar
        phibar = sine_val * phibar
        solution = solution + (phi_val / rho_val)[:, None] * direction
        direction = right_vec - (theta_val / rho_val)[:, None] * direction
    return (solution, phibar / first_beta)


def solution(mesh):
    in_specs = (P(None, ("row", "col")), P("row", "col", None, None), P("row", "col"))
    out_specs = (P(None, ("col", "row")), P())
    return jax.shard_map(local, mesh=mesh, in_specs=in_specs, out_specs=out_specs, check_vma=False)
```

profile of v0, /device:TPU:0, one launch (start us, length us, event | category | flops | bytes accessed | tf_op | source)
XLA Modules:
  0.0 426.7 jit_solution(2282321328647885098)
XLA Ops:
  7.2 0.0 all-reduce.5.cloned.1.call-start
  7.2 0.9 fusion.22
  8.1 0.8 copy.17
  8.9 0.1 reshape.77
  9.0 15.7 %all_gather.12 = bf16[4,8192]{1,0:T(4,128)(2,1)S(1)} all-gather(bf16[4,1024]{1,0:T(4,128)(2,1)S(1)} %get-tuple-element.13), channel_id=1, replica_groups=mesh['row'=4,'col'=8] {'col'}, dimensions={1}, use_global_device_ids=true | all-gather | bytes 73728 | tf_op jit(solution)/shard_map/all_gather | solution.py:24
  24.7 4.6 %fusion.23 = f32[32,4,2,256]{3,1,2,0:T(4,128)S(1)} fusion(bf16[4,32,256,1]{2,0,3,1:T(4,128)(2,1)S(1)} %bitcast.73, bf16[32,2,256,256]{3,2,1,0:T(8,128)(2,1)} %param.6), kind=kOutput, calls=%fused_computation.52 | convolution fusion | flops 33554432 | bytes 8716288 | tf_op jit(solution)/shard_map/rktj,nrt->nrkj/dot_general | solution.py:27
  29.2 0.0 copy-start.4
  29.2 0.0 copy-start.3
  29.2 0.3 broadcast.38.clone
  29.5 2.8 scatter_fusion
  32.4 0.0 copy-start.1
  32.4 1.3 copy-done.1
  33.7 0.0 all-reduce.5.cloned.1.call-update
  33.7 0.0 all-gather.3.cloned.1.call-start
  33.7 40.4 %psum.35 = f32[4]{0:T(128)S(1)} all-reduce(f32[4]{0:T(128)S(1)} %get-tuple-element.14), channel_id=1, replica_groups=mesh['row'=4,'col'=8] {'row','col'}, use_global_device_ids=true, to_apply=%region_3.0 | all-reduce | flops 4 | bytes 32 | tf_op jit(solution)/shard_map/psum | solution.py:41
  74.2 0.0 copy-done.4
  74.2 0.6 dynamic-slice
  75.4 29.6 %all-reduce.5.cloned.1.call-done = f32[4,131072]{1,0:T(4,128)} async-done(((f32[4,131072]{1,0:T(4,128)}), f32[4,131072]{1,0:T(4,128)}) %all-reduce.5.cloned.1.call-update) | async-done | bytes 2097168
  105.0 1.5 multiply_reduce_fusion.1
  106.5 0.8 convert_element_type.13
  107.3 0.0 all-gather.3.cloned.1.call-update
  107.3 0.0 reduce-scatter.9.cloned.1.call-start
  107.3 0.0 copy-done.3
  107.4 0.1 copy.19
  107.4 0.1 reshape.124
  107.6 0.1 copy.18
  107.7 26.5 %all-gather.3.cloned.1.call-done = bf16[4,131072]{1,0:T(4,128)(2,1)} async-done(((bf16[4,32768]{1,0:T(4,128)(2,1)}), bf16[4,131072]{1,0:T(4,128)(2,1)}) %all-gather.3.cloned.1.call-update) | async-done | bytes 1048592 | tf_op jit(solution)/shard_map/all_gather | solution.py:60
  134.2 1.9 gather_fusion
  136.1 5.7 %fusion.3 = f32[32,4,256,1]{2,1,3,0:T(4,128)S(1)} fusion(bf16[32,2,256,256]{3,2,1,0:T(8,128)(2,1)} %param.6, bf16[32,2,4,256]{3,2,1,0:T(4,128)(2,1)S(1)} %bitcast.70, pred[32,2]{1,0:T(8,128)(4,1)S(1)} %copy.18), kind=kOutput, calls=%fused_computation.14 | convolution fusion | flops 33619968 | bytes 8650816 | tf_op jit(solution)/shard_map/rktj,nrkj->nrt/dot_general | solution.py:62
  141.8 0.0 copy-start.2
  141.8 2.6 copy.28
  144.4 0.0 reduce-scatter.9.cloned.1.call-update
  144.4 0.0 all-reduce.7.cloned.1.call-start
  144.5 41.1 %psum.36 = f32[4]{0:T(128)S(1)} all-reduce(f32[4]{0:T(128)S(1)} %get-tuple-element.11), channel_id=1, replica_groups=mesh['row'=4,'col'=8] {'row','col'}, use_global_device_ids=true, to_apply=%region_5.0 | all-reduce | flops 4 | bytes 32 | tf_op jit(solution)/shard_map/psum | solution.py:45
  185.6 10.0 %reduce-scatter.9.cloned.1.call-done = f32[1024,4]{1,0:T(8,128)} async-done(((f32[8192,4]{1,0:T(8,128)}), f32[1024,4]{1,0:T(8,128)}) %reduce-scatter.9.cloned.1.call-update) | async-done | bytes 16400
  195.6 1.2 copy.29
  196.9 0.0 copy-done.2
  196.9 0.2 multiply_reduce_fusion.2
  197.1 14.0 %all_gather.14 = bf16[4,8192]{1,0:T(4,128)(2,1)S(1)} all-gather(bf16[4,1024]{1,0:T(4,128)(2,1)S(1)} %convert_element_type.14), channel_id=1, replica_groups=mesh['row'=4,'col'=8] {'col'}, dimensions={1}, use_global_device_ids=true | all-gather | bytes 73728 | tf_op jit(solution)/shard_map/all_gather | solution.py:24
  211.1 4.6 %fusion.24 = f32[32,4,2,256]{3,1,2,0:T(4,128)S(1)} fusion(bf16[4,32,256,1]{2,0,3,1:T(4,128)(2,1)S(1)} %bitcast.74, bf16[32,2,256,256]{3,2,1,0:T(8,128)(2,1)} %param.6), kind=kOutput, calls=%fused_computation.53 | convolution fusion | flops 33554432 | bytes 8716288 | tf_op jit(solution)/shard_map/rktj,nrt->nrkj/dot_general | solution.py:27
  215.6 0.3 broadcast.38
  215.9 2.8 scatter_fusion.1
  218.8 0.0 copy-start
  218.8 1.3 copy-done
  220.0 0.0 all-reduce.7.cloned.1.call-update
  220.1 0.0 all-gather.5.cloned.1.call-start
  220.1 38.7 %psum.37 = f32[4]{0:T(128)S(1)} all-reduce(f32[4]{0:T(128)S(1)} %get-tuple-element.9), channel_id=1, replica_groups=mesh['row'=4,'col'=8] {'row','col'}, use_global_device_ids=true, to_apply=%region_8.10 | all-reduce | flops 4 | bytes 32 | tf_op jit(solution)/shard_map/psum | solution.py:41
  258.8 29.7 %all-reduce.7.cloned.1.call-done = f32[4,131072]{1,0:T(4,128)} async-done(((f32[4,131072]{1,0:T(4,128)}), f32[4,131072]{1,0:T(4,128)}) %all-reduce.7.cloned.1.call-update) | async-done | bytes 2097168
  288.5 2.0 fusion.20
  290.5 0.0 all-gather.5.cloned.1.call-update
  290.5 0.2 reduce-scatter.11.cloned.1.call-start
  290.7 26.7 %all-gather.5.cloned.1.call-done = bf16[4,131072]{1,0:T(4,128)(2,1)} async-done(((bf16[4,32768]{1,0:T(4,128)(2,1)}), bf16[4,131072]{1,0:T(4,128)(2,1)}) %all-gather.5.cloned.1.call-update) | async-done | bytes 1048592 | tf_op jit(solution)/shard_map/all_gather | solution.py:60
  317.4 1.9 gather_fusion.1
  319.3 5.7 %fusion.1 = f32[32,4,256,1]{2,1,3,0:T(4,128)S(1)} fusion(bf16[32,2,256,256]{3,2,1,0:T(8,128)(2,1)} %param.6, bf16[32,2,4,256]{3,2,1,0:T(4,128)(2,1)S(1)} %bitcast.69, pred[32,2]{1,0:T(8,128)(4,1)S(1)} %copy.18), kind=kOutput, calls=%fused_computation.12 | convolution fusion | flops 33619968 | bytes 8650816 | tf_op jit(solution)/shard_map/rktj,nrkj->nrt/dot_general | solution.py:62
  325.0 2.6 copy.32
  327.6 0.0 reduce-scatter.11.cloned.1.call-update
  327.6 0.4 multiply_reduce_fusion
  328.0 41.1 %psum.38 = f32[4]{0:T(128)S(1)} all-reduce(f32[4]{0:T(128)S(1)} %multiply_reduce_fusion), channel_id=1, replica_groups=mesh['row'=4,'col'=8] {'row','col'}, use_global_device_ids=true, to_apply=%region_12.14 | all-reduce | flops 4 | bytes 32 | tf_op jit(solution)/shard_map/psum | solution.py:45
  369.2 9.7 %reduce-scatter.11.cloned.1.call-done = f32[1024,4]{1,0:T(8,128)} async-done(((f32[8192,4]{1,0:T(8,128)}), f32[1024,4]{1,0:T(8,128)}) %reduce-scatter.11.cloned.1.call-update) | async-done | bytes 16400
  378.8 1.2 copy.33
  380.1 0.2 fusion.12
  380.3 37.8 %psum.39 = f32[4]{0:T(128)S(1)} all-reduce(f32[4]{0:T(128)S(1)} %fusion.12), channel_id=1, replica_groups=mesh['row'=4,'col'=8] {'row','col'}, use_global_device_ids=true, to_apply=%region_15.17 | all-reduce | flops 4 | bytes 32 | tf_op jit(solution)/shard_map/psum | solution.py:41
  418.1 0.6 multiply_divide_fusion
  418.7 1.1 multiply_add_fusion
  (10 shorter events, 0.1 us)
Async XLA Ops:
  7.2 97.8 %all-reduce.5.cloned.1.call-start = ((), (), s32[]{:S(2)}) async-start(), calls=%async_computation.6 | async-start | bytes 4194304
  29.2 44.9 %copy-start.4 = (u32[32]{0:T(128)S(1)}, u32[32]{0:T(128)}, u32[]{:S(2)}) copy-start(u32[32]{0:T(128)} %constant.24) | copy-start | bytes 388
  29.2 78.1 %copy-start.3 = (s32[32,2]{0,1:T(2,128)S(1)}, s32[32,2]{0,1:T(2,128)}, u32[]{:S(2)}) copy-start(s32[32,2]{0,1:T(2,128)} %param.7) | copy-start | bytes 772
  32.4 1.3 copy-start.1
  33.7 100.5 %all-gather.3.cloned.1.call-start = ((), (), s32[]{:S(2)}) async-start(), calls=%async_computation.2 | async-start | bytes 1310720 | tf_op jit(solution)/shard_map/all_gather | solution.py:60
  107.3 88.3 %reduce-scatter.9.cloned.1.call-start = ((), (), s32[]{:S(2)}) async-start(), calls=%async_computation.4 | async-start | bytes 4718592
  141.8 55.1 %copy-start.2 = (f32[4,1024]{1,0:T(4,128)S(1)}, f32[4,1024]{1,0:T(4,128)}, u32[]{:S(2)}) copy-start(f32[4,1024]{1,0:T(4,128)} %param.5) | copy-start | bytes 49156
  144.4 144.0 %all-reduce.7.cloned.1.call-start = ((), (), s32[]{:S(2)}) async-start(), calls=%async_computation.7 | async-start | bytes 4194304
  218.8 1.3 copy-start
  220.1 97.3 %all-gather.5.cloned.1.call-start = ((), (), s32[]{:S(2)}) async-start(), calls=%async_computation.3 | async-start | bytes 1310720 | tf_op jit(solution)/shard_map/all_gather | solution.py:60
  290.5 88.3 %reduce-scatter.11.cloned.1.call-start = ((), (), s32[]{:S(2)}) async-start(), calls=%async_computation.5 | async-start | bytes 4718592
Sparse Core Ops, SparseCore 0:
  33.8 71.1 all-reduce.4
  107.5 26.6 all-gather.2
  144.6 51.0 reduce-scatter.8
  220.2 68.2 all-reduce.6
  290.7 26.6 all-gather.4
  327.8 51.0 reduce-scatter.10
where the time goes:
time: 428 us; the launch traced here: 427 us
  blocking collectives  229 us (54%)
  waiting for transfers between devices  132 us (31%)
  matrix products  20.5 us (5%)
  local copies, waits for them, and re-layouts  16.4 us (4%)
  between operations  14.9 us (3%)
  other arithmetic  13.5 us (3%)
    psum x3, blocking collectives, lanczos_pair(): beta_sq = lax.psum(jnp.sum(left_raw * left_raw, axis=1), ('row', 'col'))  117 us
    psum x2, blocking collectives, lanczos_pair(): alpha_sq = lax.psum(jnp.sum(right_raw * right_raw, axis=1), ('row', 'col'))  82.2 us
    unnamed x10, waiting for transfers between devices  79.1 us
    all_gather x2, waiting for transfers between devices, local(): whole_panel = lax.all_gather(right_bf, 'row', axis=1, tiled=True)  53.2 us
    all_gather x2, blocking collectives, adjoint_map(): lax.all_gather(left_bf, 'col', axis=1, tiled=True)  29.6 us
    unnamed x16, local copies, waits for them, and re-layouts  11.6 us
    dot_general x2, matrix products, local(): jnp.einsum('rktj,nrkj->nrt', tile_values, picked, preferred_element_type=...  11.3 us
    dot_general x2, matrix products, adjoint_map(): jnp.einsum('rktj,nrt->nrkj', tile_values, gathered, preferred_element_typ...  9.14 us
  transfers between devices with their start and end apart: 6, of which 6 were waited for; matrix products, arithmetic and copies ran while one was open for 0% of the time, Pallas kernels for 0%

commit v1 on v0

v1 whole, which is shorter than its diff:
```python
import functools

import jax
import jax.numpy as jnp
from jax import lax
from jax.experimental import pallas as pl
from jax.experimental.pallas import tpu as pltpu
from jax.sharding import PartitionSpec as P

ITERS = 2
N = 1048576
epsilon_sq = 1e-06
LANES = 128
VMEM = pl.BlockSpec(memory_space=pltpu.VMEM)
SMEM = pl.BlockSpec(memory_space=pltpu.SMEM)
ANY = pl.BlockSpec(memory_space=pl.ANY)
PARAMS = pltpu.CompilerParams(vmem_limit_bytes=40 * 1024 * 1024)


def tree_sum(parts):
    while len(parts) > 1:
        parts = [parts[i] + parts[i + 1] for i in range(0, len(parts), 2)]
    return parts[0]


def lane_total(acc):
    rows = jnp.broadcast_to(jnp.sum(acc, axis=1, keepdims=True), acc.shape)
    return rows + pltpu.roll(rows, 4, 0)


def norm_of(acc):
    return jnp.sqrt(lane_total(acc) + epsilon_sq)


def low_half():
    return lax.broadcasted_iota(jnp.int32, (8, LANES), 0) < 4


def wide_to_block(wide, upper):
    first, second = wide[:, :LANES], wide[:, LANES:]
    if upper:
        return jnp.where(low_half(), pltpu.roll(first, 4, 0), second)
    return jnp.where(low_half(), first, pltpu.roll(second, 4, 0))


def write_payload(out_ref, blocks, acc):
    rows = out_ref.shape[0]
    first, second = [], []
    low = low_half()
    for q in range(0, len(blocks), 2):
        first.append(jnp.where(low, blocks[q], pltpu.roll(blocks[q + 1], 4, 0)))
        second.append(jnp.where(low, pltpu.roll(blocks[q], 4, 0), blocks[q + 1]))
    while len(first) * 8 < rows:
        first.append(jnp.zeros((8, LANES), jnp.float32))
        second.append(jnp.zeros((8, LANES), jnp.float32))
    out_ref[:, :LANES] = jnp.concatenate(first, axis=0).astype(jnp.bfloat16)
    out_ref[:, LANES : 2 * LANES] = jnp.concatenate(second, axis=0).astype(jnp.bfloat16)
    upper = acc.astype(jnp.bfloat16).astype(jnp.float32)
    pieces = [upper, acc - upper] + [jnp.zeros((8, LANES), jnp.float32)] * (rows // 8 - 2)
    out_ref[:, 2 * LANES :] = jnp.concatenate(pieces, axis=0).astype(jnp.bfloat16)


def read_squares(ref):
    both = ref[:, 2 * LANES :].astype(jnp.float32)
    return both[:8] + both[8:16]


def prepare_kernel(obs_ref, blocks_ref, payload_ref):
    obs = obs_ref[...]
    blocks = []
    for q in range(obs.shape[1] // (2 * LANES)):
        at = q * 2 * LANES
        blocks.append(jnp.concatenate([obs[:, at : at + LANES], obs[:, at + LANES : at + 2 * LANES]], axis=0))
    for q, block in enumerate(blocks):
        blocks_ref[q] = block
    write_payload(payload_ref, blocks, tree_sum([b * b for b in blocks]))


def fetch_tiles(tiles_ref, held, sems, me, shares):
    per_share = tiles_ref.shape[0] // shares
    copies = []
    for d in range(shares):
        start = jnp.bitwise_xor(me, d) * per_share
        copies.append(pltpu.make_async_copy(tiles_ref.at[pl.ds(start, per_share)], held.at[d], sems.at[d]))
        copies[-1].start()
    return copies


def adjoint_kernel(shares, pos_ref, tiles_ref, *refs):
    payloads = refs[:shares]
    out_ref, held, sems = refs[shares:]
    me = pos_ref[1]
    per_share, per_block = held.shape[1], held.shape[2]
    copies = fetch_tiles(tiles_ref, held, sems, me, shares)
    total = held.shape[0] * per_share * per_block
    out_ref[total] = tree_sum([read_squares(p) for p in payloads])
    for d in range(shares):
        copies[d].wait()
        rays = payloads[d][:, : 2 * LANES]
        base = jnp.bitwise_xor(me, d) * (per_share * per_block)
        for q in range(per_share):
            for k in range(per_block):
                wide = jnp.dot(rays, held[d, q, k], preferred_element_type=jnp.float32)
                at = 8 * (q // 2)
                out_ref[base + q * per_block + k] = wide_to_block(wide[at : at + 8], q % 2 == 1)


def voxel_kernel(shares, rows, first, pos_ref, cols_ref, tiles_ref, *refs):
    refs = list(refs)
    terms = [refs.pop(0) for _ in range(rows)]
    if not first:
        right_ref, alpha_ref = refs.pop(0), refs.pop(0)
    outs = [refs.pop(0) for _ in range(shares)]
    beta_ref, raw_ref, term_buf, held, term_sems, tile_sems = refs
    my_row, me = pos_ref[0], pos_ref[1]
    per_share, per_block = held.shape[1], held.shape[2]
    per_row = shares * per_share * per_block
    pitch = per_row + 1
    term_copies = []
    for d in range(rows):
        slot = jnp.bitwise_xor(my_row, d)
        term_copies.append(pltpu.make_async_copy(terms[d], term_buf.at[slot], term_sems.at[d]))
        term_copies[-1].start()
    copies = fetch_tiles(tiles_ref, held, tile_sems, me, shares)
    col_tiles = raw_ref.shape[0]
    chunk = 16
    zeros = jnp.zeros((chunk, 8, LANES), jnp.float32)

    @pl.loop(0, col_tiles // chunk)
    def _(step):
        raw_ref[pl.ds(step * chunk, chunk)] = zeros

    for copy in term_copies:
        copy.wait()
    beta = norm_of(tree_sum([term_buf[s, per_row] for s in range(rows)]))
    beta_ref[...] = beta
    unroll = 8
    for s in range(rows):
        col_base = jnp.bitwise_xor(my_row, s) * per_row

        @pl.loop(0, per_row // unroll)
        def _(step):
            for u in range(unroll):
                t = step * unroll + u
                col = cols_ref[col_base + t]
                raw_ref[col] = raw_ref[col] + term_buf[s, t]

    beta_inv = 1.0 / beta
    if not first:
        right_scale = beta / alpha_ref[...]

    def scale(step, acc):
        at = pl.ds(step * chunk, chunk)
        raw = raw_ref[at] * beta_inv
        if not first:
            raw = raw - right_ref[at] * right_scale
        raw_ref[at] = raw
        return acc + jnp.sum(raw * raw, axis=0)

    acc = lax.fori_loop(0, col_tiles // chunk, scale, jnp.zeros((8, LANES), jnp.float32))
    for d in range(shares):
        copies[d].wait()
        base = jnp.bitwise_xor(me, d) * (per_share * per_block)
        for q in range(per_share):
            wide = None
            for k in range(per_block):
                block = raw_ref[cols_ref[base + q * per_block + k]]
                lhs = jnp.concatenate([block, pltpu.roll(block, 4, 0)], axis=1).astype(jnp.bfloat16)
                part = lax.dot_general(
                    lhs, held[d, q, k], (((1,), (1,)), ((), ())), preferred_element_type=jnp.float32
                )
                wide = part if wide is None else wide + part
            outs[d][q] = wide_to_block(wide, False)
        outs[d][per_share] = acc


def ray_kernel(shares, *refs):
    parts = refs[:shares]
    left_ref, beta_ref, raw_ref, alpha_ref, payload_ref, acc_ref = refs[shares:]
    per_share = raw_ref.shape[0]
    alpha = norm_of(tree_sum([p[per_share] for p in parts]))
    alpha_ref[...] = alpha
    alpha_inv = 1.0 / alpha
    left_scale = alpha / beta_ref[...]
    blocks = []
    for q in range(per_share):
        total = tree_sum([p[q] for p in parts])
        blocks.append(total * alpha_inv - left_ref[q] * left_scale)
        raw_ref[q] = blocks[-1]
    acc = tree_sum([b * b for b in blocks])
    acc_ref[...] = acc
    write_payload(payload_ref, blocks, acc)


def final_kernel(rows, iters, pos_ref, *refs):
    refs = list(refs)
    last = [refs.pop(0) for _ in range(rows)]
    betas = [refs.pop(0) for _ in range(iters)]
    alphas = [refs.pop(0) for _ in range(iters)]
    raws = [refs.pop(0) for _ in range(iters)]
    out_ref, ratio_ref, held, sems = refs
    share = held.shape[1]
    start = pos_ref[0] * share
    copies = []
    for i in range(iters):
        copies.append(pltpu.make_async_copy(raws[i].at[pl.ds(start, share)], held.at[i], sems.at[i]))
        copies[-1].start()
    beta = [b[...] for b in betas] + [norm_of(tree_sum([p[...] for p in last]))]
    alpha = [a[...] for a in alphas]
    phibar, rhobar = beta[0], alpha[0]
    direction = [1.0 / alpha[0]] + [jnp.zeros_like(phibar)] * (iters - 1)
    weights = [jnp.zeros_like(phibar)] * iters
    for i in range(iters):
        rho = jnp.sqrt(rhobar * rhobar + beta[i + 1] * beta[i + 1])
        cosine, sine = rhobar / rho, beta[i + 1] / rho
        phi = cosine * phibar
        phibar = sine * phibar
        weights = [w + (phi / rho) * d for w, d in zip(weights, direction)]
        if i + 1 < iters:
            theta = sine * alpha[i + 1]
            rhobar = -cosine * alpha[i + 1]
            direction = [-(theta / rho) * d for d in direction]
            direction[i + 1] = direction[i + 1] + 1.0 / alpha[i + 1]
    ratio_ref[...] = phibar / beta[0]
    for copy in copies:
        copy.wait()
    unroll = 4

    @pl.loop(0, share // unroll)
    def _(step):
        for u in range(unroll):
            c = step * unroll + u
            block = held[0, c] * weights[0]
            for i in range(1, iters):
                block = block + held[i, c] * weights[i]
            at = pl.multiple_of(c * 2 * LANES, 2 * LANES)
            out_ref[:, pl.ds(at, LANES)] = block[:4]
            out_ref[:, pl.ds(at + LANES, LANES)] = block[4:]


def exchange(value, axis):
    size = lax.axis_size(axis)
    got = [value]
    for d in range(1, size):
        got.append(lax.ppermute(value, axis, [(i, i ^ d) for i in range(size)]))
    return got


def exchange_parts(values, axis):
    size = lax.axis_size(axis)
    got = [values[0]]
    for d in range(1, size):
        got.append(lax.ppermute(values[d], axis, [(i, i ^ d) for i in range(size)]))
    return got


def f32(*shape):
    return jax.ShapeDtypeStruct(shape, jnp.float32)


def local(observed, tile_values, tile_cols):
    row_tiles, per_block, tile_size = tile_values.shape[:3]
    rows, shares = lax.axis_size("row"), lax.axis_size("col")
    col_tiles = N // (tile_size * shares)
    per_share = row_tiles // shares
    terms = row_tiles * per_block
    payload = jax.ShapeDtypeStruct((max(16, 4 * per_share), 3 * LANES), jnp.bfloat16)
    pos = jnp.stack([lax.axis_index("row"), lax.axis_index("col")]).astype(jnp.int32)
    cols = jnp.concatenate(exchange(tile_cols.reshape(-1), "row"))
    held = pltpu.VMEM((shares, per_share, per_block, tile_size, tile_size), jnp.bfloat16)

    def adjoint(payloads):
        return pl.pallas_call(
            functools.partial(adjoint_kernel, shares),
            out_shape=f32(terms + 1, 8, LANES),
            in_specs=[SMEM, ANY] + [VMEM] * shares,
            out_specs=VMEM,
            scratch_shapes=[held, pltpu.SemaphoreType.DMA((shares,))],
            compiler_params=PARAMS,
            name="adjoint",
        )(pos, tile_values, *payloads)

    def voxel(term_list, previous):
        first = previous is None
        extra = [] if first else list(previous)
        outs = pl.pallas_call(
            functools.partial(voxel_kernel, shares, rows, first),
            out_shape=[f32(per_share + 1, 8, LANES)] * shares + [f32(8, LANES), f32(col_tiles, 8, LANES)],
            in_specs=[SMEM, SMEM, ANY] + [ANY] * rows + [VMEM] * len(extra),
            out_specs=[VMEM] * (shares + 2),
            scratch_shapes=[
                pltpu.VMEM((rows, terms + 1, 8, LANES), jnp.float32),
                held,
                pltpu.SemaphoreType.DMA((rows,)),
                pltpu.SemaphoreType.DMA((shares,)),
            ],
            compiler_params=PARAMS,
            name="voxel",
        )(pos, cols, tile_values, *term_list, *extra)
        return outs[:shares], outs[shares], outs[shares + 1]

    def ray(parts, left_raw, beta):
        return pl.pallas_call(
            functools.partial(ray_kernel, shares),
            out_shape=[f32(per_share, 8, LANES), f32(8, LANES), payload, f32(8, LANES)],
            in_specs=[VMEM] * (shares + 2),
            out_specs=[VMEM] * 4,
            compiler_params=PARAMS,
            name="ray",
        )(*parts, left_raw, beta)

    left_raw, message = pl.pallas_call(
        prepare_kernel,
        out_shape=[f32(per_share, 8, LANES), payload],
        in_specs=[VMEM],
        out_specs=[VMEM, VMEM],
        compiler_params=PARAMS,
        name="prepare",
    )(observed)
    betas, alphas, raws = [], [], []
    previous = None
    for iteration in range(ITERS + 1):
        summed = exchange(adjoint(exchange(message, "col")), "row")
        parts, beta, right_raw = voxel(summed, previous)
        if iteration == ITERS:
            break
        left_raw, alpha, message, squares = ray(exchange_parts(parts, "col"), left_raw, beta)
        betas.append(beta)
        alphas.append(alpha)
        raws.append(right_raw)
        previous = (right_raw, alpha)
    last = exchange(tree_sum(exchange(squares, "col")), "row")
    share = col_tiles // rows
    result, ratio = pl.pallas_call(
        functools.partial(final_kernel, rows, ITERS),
        out_shape=[f32(4, share * tile_size), f32(8, LANES)],
        in_specs=[SMEM] + [VMEM] * (rows + 2 * ITERS) + [ANY] * ITERS,
        out_specs=[VMEM, VMEM],
        scratch_shapes=[pltpu.VMEM((ITERS, share, 8, LANES), jnp.float32), pltpu.SemaphoreType.DMA((ITERS,))],
        compiler_params=PARAMS,
        name="final",
    )(pos, *last, *betas, *alphas, *raws)
    return result, ratio[:4, 0]


def solution(mesh):
    in_specs = (P(None, ("row", "col")), P("row", "col", None, None), P("row", "col"))
    out_specs = (P(None, ("col", "row")), P())
    return jax.shard_map(local, mesh=mesh, in_specs=in_specs, out_specs=out_specs, check_vma=False)
```

time: 428 us -> 130 us (0.30)
  blocking collectives: 229 us -> 0 us
  waiting for transfers between devices: 132 us -> 37.4 us
  starting transfers between devices: 0.43 us -> 57.1 us
  Pallas kernels: 0 us -> 22.6 us
  matrix products: 20.5 us -> 0 us
  between operations: 14.9 us -> 0.76 us
  other arithmetic: 13.5 us -> 0.16 us
  local copies, waits for them, and re-layouts: 16.4 us -> 11.6 us
    psum x5 -> x0, blocking collectives: 199 us -> none  [the longest x3 117 us: lanczos_pair(): beta_sq = lax.psum(jnp.sum(left_raw * left_raw, axis=1), ('row', 'col'))]
    unnamed x10 -> x0, waiting for transfers between devices: 79.1 us -> none
    ppermute x0 -> x47, starting transfers between devices: none -> 57.1 us  [the longest x33 40.9 us: exchange(): got.append(lax.ppermute(value, axis, [(i, i ^ d) for i in range(size)]))]
    all_gather x2 -> x0, waiting for transfers between devices: 53.2 us -> none  [local(): whole_panel = lax.all_gather(right_bf, 'row', axis=1, tiled=True)]
    ppermute x0 -> x47, waiting for transfers between devices: none -> 37.4 us  [the longest x33 30.2 us: exchange(): got.append(lax.ppermute(value, axis, [(i, i ^ d) for i in range(size)]))]
    all_gather x2 -> x0, blocking collectives: 29.6 us -> none  [adjoint_map(): lax.all_gather(left_bf, 'col', axis=1, tiled=True)]
    pallas_call x0 -> x8, Pallas kernels: none -> 22.6 us  [the longest x2 12.7 us: voxel(): pl.pallas_call(functools.partial(voxel_kernel, shares, rows, first), out_...]
    dot_general x4 -> x0, matrix products: 20.5 us -> none  [the longest x2 11.3 us: local(): jnp.einsum('rktj,nrkj->nrt', tile_values, picked, preferred_element_type=...]
  transfers between devices with their start and end apart: 6 -> 47, of which waited for: 6 -> 24; matrix products, arithmetic and copies ran while one was open for 0% -> 0% of each run, Pallas kernels for 0% -> 0%
where the time goes in v1:
time: 130 us
  starting transfers between devices  57.1 us (44%)
  waiting for transfers between devices  37.4 us (29%)
  Pallas kernels  22.6 us (17%)
  local copies, waits for them, and re-layouts  11.6 us (9%)
    ppermute x33, starting transfers between devices, exchange(): got.append(lax.ppermute(value, axis, [(i, i ^ d) for i in range(size)]))  40.9 us
    ppermute x33, waiting for transfers between devices, exchange(): got.append(lax.ppermute(value, axis, [(i, i ^ d) for i in range(size)]))  30.2 us
    ppermute x14, starting transfers between devices, exchange_parts(): got.append(lax.ppermute(values[d], axis, [(i, i ^ d) for i in range(size)]))  16.3 us
    pallas_call x2, Pallas kernels, voxel(): pl.pallas_call(functools.partial(voxel_kernel, shares, rows, first), out_...  12.7 us
    unnamed x19, local copies, waits for them, and re-layouts  10.9 us
    ppermute x14, waiting for transfers between devices, exchange_parts(): got.append(lax.ppermute(values[d], axis, [(i, i ^ d) for i in range(size)]))  7.19 us
    pallas_call x2, Pallas kernels, adjoint(): pl.pallas_call(functools.partial(adjoint_kernel, shares), out_shape=f32(t...  6.46 us
  transfers between devices with their start and end apart: 47, of which 24 were waited for; matrix products, arithmetic and copies ran while one was open for 0% of the time, Pallas kernels for 0%

profile of v1, /device:TPU:0, one launch (start us, length us, event | category | flops | bytes accessed | tf_op | source)
XLA Modules:
  0.0 129.6 jit_solution(4271618985460463785)
XLA Ops:
  0.6 0.7 copy-done.7
  1.4 4.6 %collective-permute-start.9 = (bf16[16,384]{1,0:T(8,128)(2,1)S(1)}, bf16[16,384]{1,0:T(8,128)(2,1)S(1)}, u32[]{:S(2)}, u32[]{:S(2)}) collective-permute-start(bf16[16,384]{1,0:T(8,128)(2,1)S(1)} %get-tuple-element.31.refs_0_), channel_id=1, source_target_pairs={{0,7},{1,6},{2,5},{3,4},{4,3},{5,2},{6,1},{7,0},{8,15},{9,14},{10,... | collective-permute-start | bytes 36872 | tf_op jit(solution)/shard_map/ppermute | solution.py:245
  5.9 0.6 collective-permute-start.8
  7.0 2.2 %collective-permute-start.6 = (bf16[16,384]{1,0:T(8,128)(2,1)S(1)}, bf16[16,384]{1,0:T(8,128)(2,1)S(1)}, u32[]{:S(2)}, u32[]{:S(2)}) collective-permute-start(bf16[16,384]{1,0:T(8,128)(2,1)S(1)} %get-tuple-element.31.refs_0_), channel_id=1, source_target_pairs={{0,4},{1,5},{2,6},{3,7},{4,0},{5,1},{6,2},{7,3},{8,12},{9,13},{10,... | collective-permute-start | bytes 36872 | tf_op jit(solution)/shard_map/ppermute | solution.py:245
  9.1 1.0 collective-permute-start.5
  10.1 0.9 collective-permute-start.4
  11.7 0.6 collective-permute-done.5.refs_3_
  12.2 1.6 %collective-permute-done.4.refs_2_ = bf16[16,384]{1,0:T(8,128)(2,1)S(1)} collective-permute-done((bf16[16,384]{1,0:T(8,128)(2,1)S(1)}, bf16[16,384]{1,0:T(8,128)(2,1)S(1)}, u32[]{:S(2)}, u32[]{:S(2)}) %collective-permute-start.4) | collective-permute-done | bytes 12320 | tf_op jit(solution)/shard_map/ppermute | solution.py:245
  13.8 3.4 %copy-done = bf16[32,2,256,256]{3,2,1,0:T(8,128)(2,1)S(1)} copy-done((bf16[32,2,256,256]{3,2,1,0:T(8,128)(2,1)S(1)}, bf16[32,2,256,256]{3,2,1,0:T(8,128)(2,1)}, u32[]{:S(2)}) %copy-start) | copy-done | bytes 8388632
  17.2 3.2 %adjoint.2.refs_0_ = f32[65,8,128]{2,1,0:T(8,128)S(1)} custom-call(s32[2]{0:T(128)S(1)} %pad_add_fusion.1.pos_ref, bf16[32,2,256,256]{3,2,1,0:T(8,128)(2,1)S(1)} %copy-done, bf16[16,384]{1,0:T(8,128)(2,1)S(1)} %get-tuple-element.31.refs_0_, bf16[16,384]{1,0:T(8,128)(2,1)S(1)} %collective-permute-done.3.refs_1_, ...), custom_call_target="tpu_custom_call" | custom-call | tf_op jit(solution)/shard_map/adjoint/pallas_call | solution.py:273
  20.4 2.5 %collective-permute-start.12 = (f32[65,8,128]{2,1,0:T(8,128)S(1)}, f32[65,8,128]{2,1,0:T(8,128)S(1)}, u32[]{:S(2)}, u32[]{:S(2)}) collective-permute-start(f32[65,8,128]{2,1,0:T(8,128)S(1)} %adjoint.2.refs_0_), channel_id=1, source_target_pairs={{0,24},{8,16},{16,8},{24,0},{1,25},{9,17},{17,9},{25,1},{2,26},{10... | collective-permute-start | bytes 798728 | tf_op jit(solution)/shard_map/ppermute | solution.py:245
  24.2 2.5 %collective-permute-start.2 = (s32[64]{0:T(128)S(1)}, s32[64]{0:T(128)S(1)}, u32[]{:S(2)}, u32[]{:S(2)}) collective-permute-start(s32[64]{0:T(128)S(1)} %reshape.7), channel_id=1, source_target_pairs={{0,24},{8,16},{16,8},{24,0},{1,25},{9,17},{17,9},{25,1},{2,26},{10... | collective-permute-start | bytes 776 | tf_op jit(solution)/shard_map/ppermute | solution.py:245
  27.2 7.4 %collective-permute-done.2 = s32[64]{0:T(128)S(1)} collective-permute-done((s32[64]{0:T(128)S(1)}, s32[64]{0:T(128)S(1)}, u32[]{:S(2)}, u32[]{:S(2)}) %collective-permute-start.2) | collective-permute-done | bytes 288 | tf_op jit(solution)/shard_map/ppermute | solution.py:245
  34.6 1.5 %collective-permute-start = (s32[64]{0:T(128)S(1)}, s32[64]{0:T(128)S(1)}, u32[]{:S(2)}, u32[]{:S(2)}) collective-permute-start(s32[64]{0:T(128)S(1)} %reshape.7), channel_id=1, source_target_pairs={{0,8},{8,0},{16,24},{24,16},{1,9},{9,1},{17,25},{25,17},{2,10},{10... | collective-permute-start | bytes 776 | tf_op jit(solution)/shard_map/ppermute | solution.py:245
  36.1 2.0 %collective-permute-done = s32[64]{0:T(128)S(1)} collective-permute-done((s32[64]{0:T(128)S(1)}, s32[64]{0:T(128)S(1)}, u32[]{:S(2)}, u32[]{:S(2)}) %collective-permute-start) | collective-permute-done | bytes 288 | tf_op jit(solution)/shard_map/ppermute | solution.py:245
  38.3 0.7 copy-done.3
  39.0 0.7 copy-done.5
  39.7 3.4 %copy-done.1 = bf16[32,2,256,256]{3,2,1,0:T(8,128)(2,1)S(1)} copy-done((bf16[32,2,256,256]{3,2,1,0:T(8,128)(2,1)S(1)}, bf16[32,2,256,256]{3,2,1,0:T(8,128)(2,1)}, u32[]{:S(2)}) %copy-start.1) | copy-done | bytes 8388632
  43.1 0.9 copy-done.4
  44.0 0.9 copy-done.6
  45.0 6.3 %voxel.2 = (f32[5,8,128]{2,1,0:T(8,128)S(1)}, f32[5,8,128]{2,1,0:T(8,128)S(1)}, f32[5,8,128]{2,1,0:T(8,128)S(1)}, f32[5,8,128]{2,1,0:T(8,128)S(1)}, f32[5,8,128]...) custom-call(s32[2]{0:T(128)S(1)} %pad_add_fusion.1.pos_ref, ...), custom_call_target="tpu_custom_call" | custom-call | tf_op jit(solution)/shard_map/voxel/pallas_call | solution.py:286
  51.3 0.9 collective-permute-start.14
  52.2 0.9 collective-permute-start.15
  53.2 2.9 %collective-permute-start.16 = (f32[5,8,128]{2,1,0:T(8,128)S(1)}, f32[5,8,128]{2,1,0:T(8,128)S(1)}, u32[]{:S(2)}, u32[]{:S(2)}) collective-permute-start(f32[5,8,128]{2,1,0:T(8,128)S(1)} %get-tuple-element.36), channel_id=1, source_target_pairs={{0,4},{1,5},{2,6},{3,7},{4,0},{5,1},{6,2},{7,3},{8,12},{9,13},{10,... | collective-permute-start | bytes 61448 | tf_op jit(solution)/shard_map/ppermute | solution.py:253
  56.1 2.7 %collective-permute-start.18 = (f32[5,8,128]{2,1,0:T(8,128)S(1)}, f32[5,8,128]{2,1,0:T(8,128)S(1)}, u32[]{:S(2)}, u32[]{:S(2)}) collective-permute-start(f32[5,8,128]{2,1,0:T(8,128)S(1)} %get-tuple-element.38), channel_id=1, source_target_pairs={{0,6},{1,7},{2,4},{3,5},{4,2},{5,3},{6,0},{7,1},{8,14},{9,15},{10,... | collective-permute-start | bytes 61448 | tf_op jit(solution)/shard_map/ppermute | solution.py:253
  58.8 0.6 collective-permute-start.19
  59.4 0.8 collective-permute-done.17.refs_5_
  60.2 1.5 %collective-permute-done.18.refs_6_ = f32[5,8,128]{2,1,0:T(8,128)S(1)} collective-permute-done((f32[5,8,128]{2,1,0:T(8,128)S(1)}, f32[5,8,128]{2,1,0:T(8,128)S(1)}, u32[]{:S(2)}, u32[]{:S(2)}) %collective-permute-start.18) | collective-permute-done | bytes 20512 | tf_op jit(solution)/shard_map/ppermute | solution.py:253
  61.7 2.1 %collective-permute-done.19.refs_7_ = f32[5,8,128]{2,1,0:T(8,128)S(1)} collective-permute-done((f32[5,8,128]{2,1,0:T(8,128)S(1)}, f32[5,8,128]{2,1,0:T(8,128)S(1)}, u32[]{:S(2)}, u32[]{:S(2)}) %collective-permute-start.19) | collective-permute-done | bytes 20512 | tf_op jit(solution)/shard_map/ppermute | solution.py:253
  63.8 0.7 ray.2
  64.5 1.0 collective-permute-start.26
  65.5 2.6 %collective-permute-start.25 = (bf16[16,384]{1,0:T(8,128)(2,1)S(1)}, bf16[16,384]{1,0:T(8,128)(2,1)S(1)}, u32[]{:S(2)}, u32[]{:S(2)}) collective-permute-start(bf16[16,384]{1,0:T(8,128)(2,1)S(1)} %get-tuple-element.42.refs_0_), channel_id=1, source_target_pairs={{0,6},{1,7},{2,4},{3,5},{4,2},{5,3},{6,0},{7,1},{8,14},{9,15},{10,... | collective-permute-start | bytes 36872 | tf_op jit(solution)/shard_map/ppermute | solution.py:245
  68.1 2.6 %collective-permute-start.23 = (bf16[16,384]{1,0:T(8,128)(2,1)S(1)}, bf16[16,384]{1,0:T(8,128)(2,1)S(1)}, u32[]{:S(2)}, u32[]{:S(2)}) collective-permute-start(bf16[16,384]{1,0:T(8,128)(2,1)S(1)} %get-tuple-element.42.refs_0_), channel_id=1, source_target_pairs={{0,4},{1,5},{2,6},{3,7},{4,0},{5,1},{6,2},{7,3},{8,12},{9,13},{10,... | collective-permute-start | bytes 36872 | tf_op jit(solution)/shard_map/ppermute | solution.py:245
  70.7 1.8 %collective-permute-start.21 = (bf16[16,384]{1,0:T(8,128)(2,1)S(1)}, bf16[16,384]{1,0:T(8,128)(2,1)S(1)}, u32[]{:S(2)}, u32[]{:S(2)}) collective-permute-start(bf16[16,384]{1,0:T(8,128)(2,1)S(1)} %get-tuple-element.42.refs_0_), channel_id=1, source_target_pairs={{0,2},{1,3},{2,0},{3,1},{4,6},{5,7},{6,4},{7,5},{8,10},{9,11},{10,... | collective-permute-start | bytes 36872 | tf_op jit(solution)/shard_map/ppermute | solution.py:245
  72.8 1.1 collective-permute-done.22.refs_3_
  73.8 0.6 collective-permute-done.21.refs_2_
  74.4 3.2 %adjoint.3.refs_0_ = f32[65,8,128]{2,1,0:T(8,128)S(1)} custom-call(s32[2]{0:T(128)S(1)} %pad_add_fusion.1.pos_ref, bf16[32,2,256,256]{3,2,1,0:T(8,128)(2,1)S(1)} %copy-done.2, bf16[16,384]{1,0:T(8,128)(2,1)S(1)} %get-tuple-element.42.refs_0_, bf16[16,384]{1,0:T(8,128)(2,1)S(1)} %collective-permute-done.20.refs_1_, ...), custom_call_target="tpu_custom_call" | custom-call | tf_op jit(solution)/shard_map/adjoint/pallas_call | solution.py:273
  77.7 2.5 %collective-permute-start.29 = (f32[65,8,128]{2,1,0:T(8,128)S(1)}, f32[65,8,128]{2,1,0:T(8,128)S(1)}, u32[]{:S(2)}, u32[]{:S(2)}) collective-permute-start(f32[65,8,128]{2,1,0:T(8,128)S(1)} %adjoint.3.refs_0_), channel_id=1, source_target_pairs={{0,24},{8,16},{16,8},{24,0},{1,25},{9,17},{17,9},{25,1},{2,26},{10... | collective-permute-start | bytes 798728 | tf_op jit(solution)/shard_map/ppermute | solution.py:245
  80.7 0.5 collective-permute-start.27
  81.2 6.8 %collective-permute-done.29.refs_3_ = f32[65,8,128]{2,1,0:T(8,128)S(1)} collective-permute-done((f32[65,8,128]{2,1,0:T(8,128)S(1)}, f32[65,8,128]{2,1,0:T(8,128)S(1)}, u32[]{:S(2)}, u32[]{:S(2)}) %collective-permute-start.29) | collective-permute-done | bytes 266272 | tf_op jit(solution)/shard_map/ppermute | solution.py:245
  88.0 4.2 %collective-permute-done.28.refs_2_ = f32[65,8,128]{2,1,0:T(8,128)S(1)} collective-permute-done((f32[65,8,128]{2,1,0:T(8,128)S(1)}, f32[65,8,128]{2,1,0:T(8,128)S(1)}, u32[]{:S(2)}, u32[]{:S(2)}) %collective-permute-start.28) | collective-permute-done | bytes 266272 | tf_op jit(solution)/shard_map/ppermute | solution.py:245
  92.3 6.4 %voxel.3 = (f32[5,8,128]{2,1,0:T(8,128)S(1)}, f32[5,8,128]{2,1,0:T(8,128)S(1)}, f32[5,8,128]{2,1,0:T(8,128)S(1)}, f32[5,8,128]{2,1,0:T(8,128)S(1)}, f32[5,8,128]...) custom-call(s32[2]{0:T(128)S(1)} %pad_add_fusion.1.pos_ref, ...), custom_call_target="tpu_custom_call" | custom-call | tf_op jit(solution)/shard_map/voxel/pallas_call | solution.py:286
  98.8 1.4 %collective-permute-start.31 = (f32[5,8,128]{2,1,0:T(8,128)S(1)}, f32[5,8,128]{2,1,0:T(8,128)S(1)}, u32[]{:S(2)}, u32[]{:S(2)}) collective-permute-start(f32[5,8,128]{2,1,0:T(8,128)S(1)} %get-tuple-element.47), channel_id=1, source_target_pairs={{0,2},{1,3},{2,0},{3,1},{4,6},{5,7},{6,4},{7,5},{8,10},{9,11},{10,... | collective-permute-start | bytes 61448 | tf_op jit(solution)/shard_map/ppermute | solution.py:253
  100.7 1.4 %collective-permute-start.33 = (f32[5,8,128]{2,1,0:T(8,128)S(1)}, f32[5,8,128]{2,1,0:T(8,128)S(1)}, u32[]{:S(2)}, u32[]{:S(2)}) collective-permute-start(f32[5,8,128]{2,1,0:T(8,128)S(1)} %get-tuple-element.49), channel_id=1, source_target_pairs={{0,4},{1,5},{2,6},{3,7},{4,0},{5,1},{6,2},{7,3},{8,12},{9,13},{10,... | collective-permute-start | bytes 61448 | tf_op jit(solution)/shard_map/ppermute | solution.py:253
  102.1 1.2 collective-permute-start.34
  103.3 1.3 %collective-permute-start.35 = (f32[5,8,128]{2,1,0:T(8,128)S(1)}, f32[5,8,128]{2,1,0:T(8,128)S(1)}, u32[]{:S(2)}, u32[]{:S(2)}) collective-permute-start(f32[5,8,128]{2,1,0:T(8,128)S(1)} %get-tuple-element.51), channel_id=1, source_target_pairs={{0,6},{1,7},{2,4},{3,5},{4,2},{5,3},{6,0},{7,1},{8,14},{9,15},{10,... | collective-permute-start | bytes 61448 | tf_op jit(solution)/shard_map/ppermute | solution.py:253
  104.7 2.2 %collective-permute-start.36 = (f32[5,8,128]{2,1,0:T(8,128)S(1)}, f32[5,8,128]{2,1,0:T(8,128)S(1)}, u32[]{:S(2)}, u32[]{:S(2)}) collective-permute-start(f32[5,8,128]{2,1,0:T(8,128)S(1)} %get-tuple-element.52), channel_id=1, source_target_pairs={{0,7},{1,6},{2,5},{3,4},{4,3},{5,2},{6,1},{7,0},{8,15},{9,14},{10,... | collective-permute-start | bytes 61448 | tf_op jit(solution)/shard_map/ppermute | solution.py:253
  107.0 1.9 %collective-permute-done.35.refs_6_ = f32[5,8,128]{2,1,0:T(8,128)S(1)} collective-permute-done((f32[5,8,128]{2,1,0:T(8,128)S(1)}, f32[5,8,128]{2,1,0:T(8,128)S(1)}, u32[]{:S(2)}, u32[]{:S(2)}) %collective-permute-start.35) | collective-permute-done | bytes 20512 | tf_op jit(solution)/shard_map/ppermute | solution.py:253
  108.9 0.8 collective-permute-done.36.refs_7_
  109.7 0.7 ray.3
  110.4 2.2 %collective-permute-start.43 = (f32[8,128]{1,0:T(8,128)S(1)}, f32[8,128]{1,0:T(8,128)S(1)}, u32[]{:S(2)}, u32[]{:S(2)}) collective-permute-start(f32[8,128]{1,0:T(8,128)S(1)} %get-tuple-element.55), channel_id=1, source_target_pairs={{0,7},{1,6},{2,5},{3,4},{4,3},{5,2},{6,1},{7,0},{8,15},{9,14},{10,... | collective-permute-start | bytes 12296 | tf_op jit(solution)/shard_map/ppermute | solution.py:245
  112.6 1.3 %collective-permute-start.42 = (f32[8,128]{1,0:T(8,128)S(1)}, f32[8,128]{1,0:T(8,128)S(1)}, u32[]{:S(2)}, u32[]{:S(2)}) collective-permute-start(f32[8,128]{1,0:T(8,128)S(1)} %get-tuple-element.55), channel_id=1, source_target_pairs={{0,6},{1,7},{2,4},{3,5},{4,2},{5,3},{6,0},{7,1},{8,14},{9,15},{10,... | collective-permute-start | bytes 12296 | tf_op jit(solution)/shard_map/ppermute | solution.py:245
  114.0 2.6 %collective-permute-start.40 = (f32[8,128]{1,0:T(8,128)S(1)}, f32[8,128]{1,0:T(8,128)S(1)}, u32[]{:S(2)}, u32[]{:S(2)}) collective-permute-start(f32[8,128]{1,0:T(8,128)S(1)} %get-tuple-element.55), channel_id=1, source_target_pairs={{0,4},{1,5},{2,6},{3,7},{4,0},{5,1},{6,2},{7,3},{8,12},{9,13},{10,... | collective-permute-start | bytes 12296 | tf_op jit(solution)/shard_map/ppermute | solution.py:245
  116.7 1.6 %collective-permute-start.38 = (f32[8,128]{1,0:T(8,128)S(1)}, f32[8,128]{1,0:T(8,128)S(1)}, u32[]{:S(2)}, u32[]{:S(2)}) collective-permute-start(f32[8,128]{1,0:T(8,128)S(1)} %get-tuple-element.55), channel_id=1, source_target_pairs={{0,2},{1,3},{2,0},{3,1},{4,6},{5,7},{6,4},{7,5},{8,10},{9,11},{10,... | collective-permute-start | bytes 12296 | tf_op jit(solution)/shard_map/ppermute | solution.py:245
  118.5 1.1 collective-permute-done.39
  119.6 0.7 collective-permute-done.38
  120.4 1.7 %collective-permute-start.46 = (f32[8,128]{1,0:T(8,128)S(1)}, f32[8,128]{1,0:T(8,128)S(1)}, u32[]{:S(2)}, u32[]{:S(2)}) collective-permute-start(f32[8,128]{1,0:T(8,128)S(1)} %add_add_fusion.refs_0_), channel_id=1, source_target_pairs={{0,24},{8,16},{16,8},{24,0},{1,25},{9,17},{17,9},{25,1},{2,26},{10... | collective-permute-start | bytes 12296 | tf_op jit(solution)/shard_map/ppermute | solution.py:245
  122.1 1.3 %collective-permute-start.45 = (f32[8,128]{1,0:T(8,128)S(1)}, f32[8,128]{1,0:T(8,128)S(1)}, u32[]{:S(2)}, u32[]{:S(2)}) collective-permute-start(f32[8,128]{1,0:T(8,128)S(1)} %add_add_fusion.refs_0_), channel_id=1, source_target_pairs={{0,16},{8,24},{16,0},{24,8},{1,17},{9,25},{17,1},{25,9},{2,18},{10... | collective-permute-start | bytes 12296 | tf_op jit(solution)/shard_map/ppermute | solution.py:245
  123.4 0.5 collective-permute-start.44
  123.9 1.0 collective-permute-done.46.refs_3_
  124.9 0.8 collective-permute-done.45.refs_2_
  125.7 1.3 %collective-permute-done.44.refs_1_ = f32[8,128]{1,0:T(8,128)S(1)} collective-permute-done((f32[8,128]{1,0:T(8,128)S(1)}, f32[8,128]{1,0:T(8,128)S(1)}, u32[]{:S(2)}, u32[]{:S(2)}) %collective-permute-start.44) | collective-permute-done | bytes 4128 | tf_op jit(solution)/shard_map/ppermute | solution.py:245
  127.0 2.0 %final.1 = (f32[4,32768]{1,0:T(4,128)}, f32[8,128]{1,0:T(8,128)S(1)}) custom-call(s32[2]{0:T(128)S(1)} %pad_add_fusion.1.pos_ref, f32[8,128]{1,0:T(8,128)S(1)} %add_add_fusion.refs_0_, f32[8,128]{1,0:T(8,128)S(1)} %collective-permute-done.44.refs_1_, f32[8,128]{1,0:T(8,128)S(1)} %collective-permute-done.45.refs_2_, ...), custom_call_target="tpu_custom_call" | custom-call | tf_op jit(solution)/shard_map/final/pallas_call | solution.py:334
  129.0 0.6 slice_reduce_fusion
  (62 shorter events, 4.8 us)
Async XLA Ops:
  0.6 0.7 copy-start.7
  1.4 8.7 %collective-permute-start.9 = (bf16[16,384]{1,0:T(8,128)(2,1)S(1)}, bf16[16,384]{1,0:T(8,128)(2,1)S(1)}, u32[]{:S(2)}, u32[]{:S(2)}) collective-permute-start(bf16[16,384]{1,0:T(8,128)(2,1)S(1)} %get-tuple-element.31.refs_0_), channel_id=1, source_target_pairs={{0,7},{1,6},{2,5},{3,4},{4,3},{5,2},{6,1},{7,0},{8,15},{9,14},{10,... | collective-permute-start | bytes 36872 | tf_op jit(solution)/shard_map/ppermute | solution.py:245
  5.9 5.5 %collective-permute-start.8 = (bf16[16,384]{1,0:T(8,128)(2,1)S(1)}, bf16[16,384]{1,0:T(8,128)(2,1)S(1)}, u32[]{:S(2)}, u32[]{:S(2)}) collective-permute-start(bf16[16,384]{1,0:T(8,128)(2,1)S(1)} %get-tuple-element.31.refs_0_), channel_id=1, source_target_pairs={{0,6},{1,7},{2,4},{3,5},{4,2},{5,3},{6,0},{7,1},{8,14},{9,15},{10,... | collective-permute-start | bytes 36872 | tf_op jit(solution)/shard_map/ppermute | solution.py:245
  6.6 4.9 %collective-permute-start.7 = (bf16[16,384]{1,0:T(8,128)(2,1)S(1)}, bf16[16,384]{1,0:T(8,128)(2,1)S(1)}, u32[]{:S(2)}, u32[]{:S(2)}) collective-permute-start(bf16[16,384]{1,0:T(8,128)(2,1)S(1)} %get-tuple-element.31.refs_0_), channel_id=1, source_target_pairs={{0,5},{1,4},{2,7},{3,6},{4,1},{5,0},{6,3},{7,2},{8,13},{9,12},{10,... | collective-permute-start | bytes 36872 | tf_op jit(solution)/shard_map/ppermute | solution.py:245
  7.0 4.7 %collective-permute-start.6 = (bf16[16,384]{1,0:T(8,128)(2,1)S(1)}, bf16[16,384]{1,0:T(8,128)(2,1)S(1)}, u32[]{:S(2)}, u32[]{:S(2)}) collective-permute-start(bf16[16,384]{1,0:T(8,128)(2,1)S(1)} %get-tuple-element.31.refs_0_), channel_id=1, source_target_pairs={{0,4},{1,5},{2,6},{3,7},{4,0},{5,1},{6,2},{7,3},{8,12},{9,13},{10,... | collective-permute-start | bytes 36872 | tf_op jit(solution)/shard_map/ppermute | solution.py:245
  9.1 3.1 %collective-permute-start.5 = (bf16[16,384]{1,0:T(8,128)(2,1)S(1)}, bf16[16,384]{1,0:T(8,128)(2,1)S(1)}, u32[]{:S(2)}, u32[]{:S(2)}) collective-permute-start(bf16[16,384]{1,0:T(8,128)(2,1)S(1)} %get-tuple-element.31.refs_0_), channel_id=1, source_target_pairs={{0,3},{1,2},{2,1},{3,0},{4,7},{5,6},{6,5},{7,4},{8,11},{9,10},{10,... | collective-permute-start | bytes 36872 | tf_op jit(solution)/shard_map/ppermute | solution.py:245
  10.1 3.7 %collective-permute-start.4 = (bf16[16,384]{1,0:T(8,128)(2,1)S(1)}, bf16[16,384]{1,0:T(8,128)(2,1)S(1)}, u32[]{:S(2)}, u32[]{:S(2)}) collective-permute-start(bf16[16,384]{1,0:T(8,128)(2,1)S(1)} %get-tuple-element.31.refs_0_), channel_id=1, source_target_pairs={{0,2},{1,3},{2,0},{3,1},{4,6},{5,7},{6,4},{7,5},{8,10},{9,11},{10,... | collective-permute-start | bytes 36872 | tf_op jit(solution)/shard_map/ppermute | solution.py:245
  11.4 2.4 %collective-permute-start.3 = (bf16[16,384]{1,0:T(8,128)(2,1)S(1)}, bf16[16,384]{1,0:T(8,128)(2,1)S(1)}, u32[]{:S(2)}, u32[]{:S(2)}) collective-permute-start(bf16[16,384]{1,0:T(8,128)(2,1)S(1)} %get-tuple-element.31.refs_0_), channel_id=1, source_target_pairs={{0,1},{1,0},{2,3},{3,2},{4,5},{5,4},{6,7},{7,6},{8,9},{9,8},{10,11... | collective-permute-start | bytes 36872 | tf_op jit(solution)/shard_map/ppermute | solution.py:245
  11.4 12.6 %copy-start.8 = (s32[32,2]{0,1:T(2,128)S(1)}, s32[32,2]{0,1:T(2,128)}, u32[]{:S(2)}) copy-start(s32[32,2]{0,1:T(2,128)} %param.5) | copy-start | bytes 772
  13.8 3.4 %copy-start = (bf16[32,2,256,256]{3,2,1,0:T(8,128)(2,1)S(1)}, bf16[32,2,256,256]{3,2,1,0:T(8,128)(2,1)}, u32[]{:S(2)}) copy-start(bf16[32,2,256,256]{3,2,1,0:T(8,128)(2,1)} %tiles_ref.7) | copy-start | bytes 25165828
  20.4 17.8 %collective-permute-start.12 = (f32[65,8,128]{2,1,0:T(8,128)S(1)}, f32[65,8,128]{2,1,0:T(8,128)S(1)}, u32[]{:S(2)}, u32[]{:S(2)}) collective-permute-start(f32[65,8,128]{2,1,0:T(8,128)S(1)} %adjoint.2.refs_0_), channel_id=1, source_target_pairs={{0,24},{8,16},{16,8},{24,0},{1,25},{9,17},{17,9},{25,1},{2,26},{10... | collective-permute-start | bytes 798728 | tf_op jit(solution)/shard_map/ppermute | solution.py:245
  22.9 15.3 %collective-permute-start.11 = (f32[65,8,128]{2,1,0:T(8,128)S(1)}, f32[65,8,128]{2,1,0:T(8,128)S(1)}, u32[]{:S(2)}, u32[]{:S(2)}) collective-permute-start(f32[65,8,128]{2,1,0:T(8,128)S(1)} %adjoint.2.refs_0_), channel_id=1, source_target_pairs={{0,16},{8,24},{16,0},{24,8},{1,17},{9,25},{17,1},{25,9},{2,18},{10... | collective-permute-start | bytes 798728 | tf_op jit(solution)/shard_map/ppermute | solution.py:245
  23.4 15.5 %collective-permute-start.10 = (f32[65,8,128]{2,1,0:T(8,128)S(1)}, f32[65,8,128]{2,1,0:T(8,128)S(1)}, u32[]{:S(2)}, u32[]{:S(2)}) collective-permute-start(f32[65,8,128]{2,1,0:T(8,128)S(1)} %adjoint.2.refs_0_), channel_id=1, source_target_pairs={{0,8},{8,0},{16,24},{24,16},{1,9},{9,1},{17,25},{25,17},{2,10},{10... | collective-permute-start | bytes 798728 | tf_op jit(solution)/shard_map/ppermute | solution.py:245
  24.2 10.5 %collective-permute-start.2 = (s32[64]{0:T(128)S(1)}, s32[64]{0:T(128)S(1)}, u32[]{:S(2)}, u32[]{:S(2)}) collective-permute-start(s32[64]{0:T(128)S(1)} %reshape.7), channel_id=1, source_target_pairs={{0,24},{8,16},{16,8},{24,0},{1,25},{9,17},{17,9},{25,1},{2,26},{10... | collective-permute-start | bytes 776 | tf_op jit(solution)/shard_map/ppermute | solution.py:245
  26.7 9.4 %collective-permute-start.1 = (s32[64]{0:T(128)S(1)}, s32[64]{0:T(128)S(1)}, u32[]{:S(2)}, u32[]{:S(2)}) collective-permute-start(s32[64]{0:T(128)S(1)} %reshape.7), channel_id=1, source_target_pairs={{0,16},{8,24},{16,0},{24,8},{1,17},{9,25},{17,1},{25,9},{2,18},{10... | collective-permute-start | bytes 776 | tf_op jit(solution)/shard_map/ppermute | solution.py:245
  34.6 3.5 %collective-permute-start = (s32[64]{0:T(128)S(1)}, s32[64]{0:T(128)S(1)}, u32[]{:S(2)}, u32[]{:S(2)}) collective-permute-start(s32[64]{0:T(128)S(1)} %reshape.7), channel_id=1, source_target_pairs={{0,8},{8,0},{16,24},{24,16},{1,9},{9,1},{17,25},{25,17},{2,10},{10... | collective-permute-start | bytes 776 | tf_op jit(solution)/shard_map/ppermute | solution.py:245
  38.3 0.7 copy-start.3
  39.0 0.7 copy-start.5
  39.7 3.4 %copy-start.1 = (bf16[32,2,256,256]{3,2,1,0:T(8,128)(2,1)S(1)}, bf16[32,2,256,256]{3,2,1,0:T(8,128)(2,1)}, u32[]{:S(2)}) copy-start(bf16[32,2,256,256]{3,2,1,0:T(8,128)(2,1)} %tiles_ref.7) | copy-start | bytes 25165828
  43.1 1.0 copy-start.4
  44.0 1.0 copy-start.6
  45.0 29.5 %copy-start.2 = (bf16[32,2,256,256]{3,2,1,0:T(8,128)(2,1)S(1)}, bf16[32,2,256,256]{3,2,1,0:T(8,128)(2,1)}, u32[]{:S(2)}) copy-start(bf16[32,2,256,256]{3,2,1,0:T(8,128)(2,1)} %tiles_ref.7) | copy-start | bytes 25165828
  51.2 4.9 %collective-permute-start.13 = (f32[5,8,128]{2,1,0:T(8,128)S(1)}, f32[5,8,128]{2,1,0:T(8,128)S(1)}, u32[]{:S(2)}, u32[]{:S(2)}) collective-permute-start(f32[5,8,128]{2,1,0:T(8,128)S(1)} %get-tuple-element.33), channel_id=1, source_target_pairs={{0,1},{1,0},{2,3},{3,2},{4,5},{5,4},{6,7},{7,6},{8,9},{9,8},{10,11... | collective-permute-start | bytes 61448 | tf_op jit(solution)/shard_map/ppermute | solution.py:253
  51.3 7.5 %collective-permute-start.14 = (f32[5,8,128]{2,1,0:T(8,128)S(1)}, f32[5,8,128]{2,1,0:T(8,128)S(1)}, u32[]{:S(2)}, u32[]{:S(2)}) collective-permute-start(f32[5,8,128]{2,1,0:T(8,128)S(1)} %get-tuple-element.34), channel_id=1, source_target_pairs={{0,2},{1,3},{2,0},{3,1},{4,6},{5,7},{6,4},{7,5},{8,10},{9,11},{10,... | collective-permute-start | bytes 61448 | tf_op jit(solution)/shard_map/ppermute | solution.py:253
  52.2 7.2 %collective-permute-start.15 = (f32[5,8,128]{2,1,0:T(8,128)S(1)}, f32[5,8,128]{2,1,0:T(8,128)S(1)}, u32[]{:S(2)}, u32[]{:S(2)}) collective-permute-start(f32[5,8,128]{2,1,0:T(8,128)S(1)} %get-tuple-element.35), channel_id=1, source_target_pairs={{0,3},{1,2},{2,1},{3,0},{4,7},{5,6},{6,5},{7,4},{8,11},{9,10},{10,... | collective-permute-start | bytes 61448 | tf_op jit(solution)/shard_map/ppermute | solution.py:253
  53.2 6.2 %collective-permute-start.16 = (f32[5,8,128]{2,1,0:T(8,128)S(1)}, f32[5,8,128]{2,1,0:T(8,128)S(1)}, u32[]{:S(2)}, u32[]{:S(2)}) collective-permute-start(f32[5,8,128]{2,1,0:T(8,128)S(1)} %get-tuple-element.36), channel_id=1, source_target_pairs={{0,4},{1,5},{2,6},{3,7},{4,0},{5,1},{6,2},{7,3},{8,12},{9,13},{10,... | collective-permute-start | bytes 61448 | tf_op jit(solution)/shard_map/ppermute | solution.py:253
  56.1 4.1 %collective-permute-start.17 = (f32[5,8,128]{2,1,0:T(8,128)S(1)}, f32[5,8,128]{2,1,0:T(8,128)S(1)}, u32[]{:S(2)}, u32[]{:S(2)}) collective-permute-start(f32[5,8,128]{2,1,0:T(8,128)S(1)} %get-tuple-element.37), channel_id=1, source_target_pairs={{0,5},{1,4},{2,7},{3,6},{4,1},{5,0},{6,3},{7,2},{8,13},{9,12},{10,... | collective-permute-start | bytes 61448 | tf_op jit(solution)/shard_map/ppermute | solution.py:253
  56.1 5.6 %collective-permute-start.18 = (f32[5,8,128]{2,1,0:T(8,128)S(1)}, f32[5,8,128]{2,1,0:T(8,128)S(1)}, u32[]{:S(2)}, u32[]{:S(2)}) collective-permute-start(f32[5,8,128]{2,1,0:T(8,128)S(1)} %get-tuple-element.38), channel_id=1, source_target_pairs={{0,6},{1,7},{2,4},{3,5},{4,2},{5,3},{6,0},{7,1},{8,14},{9,15},{10,... | collective-permute-start | bytes 61448 | tf_op jit(solution)/shard_map/ppermute | solution.py:253
  58.8 5.0 %collective-permute-start.19 = (f32[5,8,128]{2,1,0:T(8,128)S(1)}, f32[5,8,128]{2,1,0:T(8,128)S(1)}, u32[]{:S(2)}, u32[]{:S(2)}) collective-permute-start(f32[5,8,128]{2,1,0:T(8,128)S(1)} %get-tuple-element.39), channel_id=1, source_target_pairs={{0,7},{1,6},{2,5},{3,4},{4,3},{5,2},{6,1},{7,0},{8,15},{9,14},{10,... | collective-permute-start | bytes 61448 | tf_op jit(solution)/shard_map/ppermute | solution.py:253
  64.5 6.2 %collective-permute-start.26 = (bf16[16,384]{1,0:T(8,128)(2,1)S(1)}, bf16[16,384]{1,0:T(8,128)(2,1)S(1)}, u32[]{:S(2)}, u32[]{:S(2)}) collective-permute-start(bf16[16,384]{1,0:T(8,128)(2,1)S(1)} %get-tuple-element.42.refs_0_), channel_id=1, source_target_pairs={{0,7},{1,6},{2,5},{3,4},{4,3},{5,2},{6,1},{7,0},{8,15},{9,14},{10,... | collective-permute-start | bytes 36872 | tf_op jit(solution)/shard_map/ppermute | solution.py:245
  65.5 7.0 %collective-permute-start.25 = (bf16[16,384]{1,0:T(8,128)(2,1)S(1)}, bf16[16,384]{1,0:T(8,128)(2,1)S(1)}, u32[]{:S(2)}, u32[]{:S(2)}) collective-permute-start(bf16[16,384]{1,0:T(8,128)(2,1)S(1)} %get-tuple-element.42.refs_0_), channel_id=1, source_target_pairs={{0,6},{1,7},{2,4},{3,5},{4,2},{5,3},{6,0},{7,1},{8,14},{9,15},{10,... | collective-permute-start | bytes 36872 | tf_op jit(solution)/shard_map/ppermute | solution.py:245
  68.1 4.5 %collective-permute-start.24 = (bf16[16,384]{1,0:T(8,128)(2,1)S(1)}, bf16[16,384]{1,0:T(8,128)(2,1)S(1)}, u32[]{:S(2)}, u32[]{:S(2)}) collective-permute-start(bf16[16,384]{1,0:T(8,128)(2,1)S(1)} %get-tuple-element.42.refs_0_), channel_id=1, source_target_pairs={{0,5},{1,4},{2,7},{3,6},{4,1},{5,0},{6,3},{7,2},{8,13},{9,12},{10,... | collective-permute-start | bytes 36872 | tf_op jit(solution)/shard_map/ppermute | solution.py:245
  68.1 4.6 %collective-permute-start.23 = (bf16[16,384]{1,0:T(8,128)(2,1)S(1)}, bf16[16,384]{1,0:T(8,128)(2,1)S(1)}, u32[]{:S(2)}, u32[]{:S(2)}) collective-permute-start(bf16[16,384]{1,0:T(8,128)(2,1)S(1)} %get-tuple-element.42.refs_0_), channel_id=1, source_target_pairs={{0,4},{1,5},{2,6},{3,7},{4,0},{5,1},{6,2},{7,3},{8,12},{9,13},{10,... | collective-permute-start | bytes 36872 | tf_op jit(solution)/shard_map/ppermute | solution.py:245
  70.7 3.1 %collective-permute-start.22 = (bf16[16,384]{1,0:T(8,128)(2,1)S(1)}, bf16[16,384]{1,0:T(8,128)(2,1)S(1)}, u32[]{:S(2)}, u32[]{:S(2)}) collective-permute-start(bf16[16,384]{1,0:T(8,128)(2,1)S(1)} %get-tuple-element.42.refs_0_), channel_id=1, source_target_pairs={{0,3},{1,2},{2,1},{3,0},{4,7},{5,6},{6,5},{7,4},{8,11},{9,10},{10,... | collective-permute-start | bytes 36872 | tf_op jit(solution)/shard_map/ppermute | solution.py:245
  70.7 3.7 %collective-permute-start.21 = (bf16[16,384]{1,0:T(8,128)(2,1)S(1)}, bf16[16,384]{1,0:T(8,128)(2,1)S(1)}, u32[]{:S(2)}, u32[]{:S(2)}) collective-permute-start(bf16[16,384]{1,0:T(8,128)(2,1)S(1)} %get-tuple-element.42.refs_0_), channel_id=1, source_target_pairs={{0,2},{1,3},{2,0},{3,1},{4,6},{5,7},{6,4},{7,5},{8,10},{9,11},{10,... | collective-permute-start | bytes 36872 | tf_op jit(solution)/shard_map/ppermute | solution.py:245
  72.5 1.9 %collective-permute-start.20 = (bf16[16,384]{1,0:T(8,128)(2,1)S(1)}, bf16[16,384]{1,0:T(8,128)(2,1)S(1)}, u32[]{:S(2)}, u32[]{:S(2)}) collective-permute-start(bf16[16,384]{1,0:T(8,128)(2,1)S(1)} %get-tuple-element.42.refs_0_), channel_id=1, source_target_pairs={{0,1},{1,0},{2,3},{3,2},{4,5},{5,4},{6,7},{7,6},{8,9},{9,8},{10,11... | collective-permute-start | bytes 36872 | tf_op jit(solution)/shard_map/ppermute | solution.py:245
  77.7 10.3 %collective-permute-start.29 = (f32[65,8,128]{2,1,0:T(8,128)S(1)}, f32[65,8,128]{2,1,0:T(8,128)S(1)}, u32[]{:S(2)}, u32[]{:S(2)}) collective-permute-start(f32[65,8,128]{2,1,0:T(8,128)S(1)} %adjoint.3.refs_0_), channel_id=1, source_target_pairs={{0,24},{8,16},{16,8},{24,0},{1,25},{9,17},{17,9},{25,1},{2,26},{10... | collective-permute-start | bytes 798728 | tf_op jit(solution)/shard_map/ppermute | solution.py:245
  80.2 12.0 %collective-permute-start.28 = (f32[65,8,128]{2,1,0:T(8,128)S(1)}, f32[65,8,128]{2,1,0:T(8,128)S(1)}, u32[]{:S(2)}, u32[]{:S(2)}) collective-permute-start(f32[65,8,128]{2,1,0:T(8,128)S(1)} %adjoint.3.refs_0_), channel_id=1, source_target_pairs={{0,16},{8,24},{16,0},{24,8},{1,17},{9,25},{17,1},{25,9},{2,18},{10... | collective-permute-start | bytes 798728 | tf_op jit(solution)/shard_map/ppermute | solution.py:245
  80.7 11.6 %collective-permute-start.27 = (f32[65,8,128]{2,1,0:T(8,128)S(1)}, f32[65,8,128]{2,1,0:T(8,128)S(1)}, u32[]{:S(2)}, u32[]{:S(2)}) collective-permute-start(f32[65,8,128]{2,1,0:T(8,128)S(1)} %adjoint.3.refs_0_), channel_id=1, source_target_pairs={{0,8},{8,0},{16,24},{24,16},{1,9},{9,1},{17,25},{25,17},{2,10},{10... | collective-permute-start | bytes 798728 | tf_op jit(solution)/shard_map/ppermute | solution.py:245
  98.8 4.5 %collective-permute-start.30 = (f32[5,8,128]{2,1,0:T(8,128)S(1)}, f32[5,8,128]{2,1,0:T(8,128)S(1)}, u32[]{:S(2)}, u32[]{:S(2)}) collective-permute-start(f32[5,8,128]{2,1,0:T(8,128)S(1)} %get-tuple-element.46), channel_id=1, source_target_pairs={{0,1},{1,0},{2,3},{3,2},{4,5},{5,4},{6,7},{7,6},{8,9},{9,8},{10,11... | collective-permute-start | bytes 61448 | tf_op jit(solution)/shard_map/ppermute | solution.py:253
  98.8 5.8 %collective-permute-start.31 = (f32[5,8,128]{2,1,0:T(8,128)S(1)}, f32[5,8,128]{2,1,0:T(8,128)S(1)}, u32[]{:S(2)}, u32[]{:S(2)}) collective-permute-start(f32[5,8,128]{2,1,0:T(8,128)S(1)} %get-tuple-element.47), channel_id=1, source_target_pairs={{0,2},{1,3},{2,0},{3,1},{4,6},{5,7},{6,4},{7,5},{8,10},{9,11},{10,... | collective-permute-start | bytes 61448 | tf_op jit(solution)/shard_map/ppermute | solution.py:253
  100.3 6.6 %collective-permute-start.32 = (f32[5,8,128]{2,1,0:T(8,128)S(1)}, f32[5,8,128]{2,1,0:T(8,128)S(1)}, u32[]{:S(2)}, u32[]{:S(2)}) collective-permute-start(f32[5,8,128]{2,1,0:T(8,128)S(1)} %get-tuple-element.48), channel_id=1, source_target_pairs={{0,3},{1,2},{2,1},{3,0},{4,7},{5,6},{6,5},{7,4},{8,11},{9,10},{10,... | collective-permute-start | bytes 61448 | tf_op jit(solution)/shard_map/ppermute | solution.py:253
  100.7 6.2 %collective-permute-start.33 = (f32[5,8,128]{2,1,0:T(8,128)S(1)}, f32[5,8,128]{2,1,0:T(8,128)S(1)}, u32[]{:S(2)}, u32[]{:S(2)}) collective-permute-start(f32[5,8,128]{2,1,0:T(8,128)S(1)} %get-tuple-element.49), channel_id=1, source_target_pairs={{0,4},{1,5},{2,6},{3,7},{4,0},{5,1},{6,2},{7,3},{8,12},{9,13},{10,... | collective-permute-start | bytes 61448 | tf_op jit(solution)/shard_map/ppermute | solution.py:253
  102.1 4.9 %collective-permute-start.34 = (f32[5,8,128]{2,1,0:T(8,128)S(1)}, f32[5,8,128]{2,1,0:T(8,128)S(1)}, u32[]{:S(2)}, u32[]{:S(2)}) collective-permute-start(f32[5,8,128]{2,1,0:T(8,128)S(1)} %get-tuple-element.50), channel_id=1, source_target_pairs={{0,5},{1,4},{2,7},{3,6},{4,1},{5,0},{6,3},{7,2},{8,13},{9,12},{10,... | collective-permute-start | bytes 61448 | tf_op jit(solution)/shard_map/ppermute | solution.py:253
  103.3 5.6 %collective-permute-start.35 = (f32[5,8,128]{2,1,0:T(8,128)S(1)}, f32[5,8,128]{2,1,0:T(8,128)S(1)}, u32[]{:S(2)}, u32[]{:S(2)}) collective-permute-start(f32[5,8,128]{2,1,0:T(8,128)S(1)} %get-tuple-element.51), channel_id=1, source_target_pairs={{0,6},{1,7},{2,4},{3,5},{4,2},{5,3},{6,0},{7,1},{8,14},{9,15},{10,... | collective-permute-start | bytes 61448 | tf_op jit(solution)/shard_map/ppermute | solution.py:253
  104.7 5.0 %collective-permute-start.36 = (f32[5,8,128]{2,1,0:T(8,128)S(1)}, f32[5,8,128]{2,1,0:T(8,128)S(1)}, u32[]{:S(2)}, u32[]{:S(2)}) collective-permute-start(f32[5,8,128]{2,1,0:T(8,128)S(1)} %get-tuple-element.52), channel_id=1, source_target_pairs={{0,7},{1,6},{2,5},{3,4},{4,3},{5,2},{6,1},{7,0},{8,15},{9,14},{10,... | collective-permute-start | bytes 61448 | tf_op jit(solution)/shard_map/ppermute | solution.py:253
  110.4 6.4 %collective-permute-start.43 = (f32[8,128]{1,0:T(8,128)S(1)}, f32[8,128]{1,0:T(8,128)S(1)}, u32[]{:S(2)}, u32[]{:S(2)}) collective-permute-start(f32[8,128]{1,0:T(8,128)S(1)} %get-tuple-element.55), channel_id=1, source_target_pairs={{0,7},{1,6},{2,5},{3,4},{4,3},{5,2},{6,1},{7,0},{8,15},{9,14},{10,... | collective-permute-start | bytes 12296 | tf_op jit(solution)/shard_map/ppermute | solution.py:245
  112.6 5.7 %collective-permute-start.42 = (f32[8,128]{1,0:T(8,128)S(1)}, f32[8,128]{1,0:T(8,128)S(1)}, u32[]{:S(2)}, u32[]{:S(2)}) collective-permute-start(f32[8,128]{1,0:T(8,128)S(1)} %get-tuple-element.55), channel_id=1, source_target_pairs={{0,6},{1,7},{2,4},{3,5},{4,2},{5,3},{6,0},{7,1},{8,14},{9,15},{10,... | collective-permute-start | bytes 12296 | tf_op jit(solution)/shard_map/ppermute | solution.py:245
  114.0 4.5 %collective-permute-start.41 = (f32[8,128]{1,0:T(8,128)S(1)}, f32[8,128]{1,0:T(8,128)S(1)}, u32[]{:S(2)}, u32[]{:S(2)}) collective-permute-start(f32[8,128]{1,0:T(8,128)S(1)} %get-tuple-element.55), channel_id=1, source_target_pairs={{0,5},{1,4},{2,7},{3,6},{4,1},{5,0},{6,3},{7,2},{8,13},{9,12},{10,... | collective-permute-start | bytes 12296 | tf_op jit(solution)/shard_map/ppermute | solution.py:245
  114.0 4.5 %collective-permute-start.40 = (f32[8,128]{1,0:T(8,128)S(1)}, f32[8,128]{1,0:T(8,128)S(1)}, u32[]{:S(2)}, u32[]{:S(2)}) collective-permute-start(f32[8,128]{1,0:T(8,128)S(1)} %get-tuple-element.55), channel_id=1, source_target_pairs={{0,4},{1,5},{2,6},{3,7},{4,0},{5,1},{6,2},{7,3},{8,12},{9,13},{10,... | collective-permute-start | bytes 12296 | tf_op jit(solution)/shard_map/ppermute | solution.py:245
  116.6 3.0 %collective-permute-start.39 = (f32[8,128]{1,0:T(8,128)S(1)}, f32[8,128]{1,0:T(8,128)S(1)}, u32[]{:S(2)}, u32[]{:S(2)}) collective-permute-start(f32[8,128]{1,0:T(8,128)S(1)} %get-tuple-element.55), channel_id=1, source_target_pairs={{0,3},{1,2},{2,1},{3,0},{4,7},{5,6},{6,5},{7,4},{8,11},{9,10},{10,... | collective-permute-start | bytes 12296 | tf_op jit(solution)/shard_map/ppermute | solution.py:245
  116.7 3.6 %collective-permute-start.38 = (f32[8,128]{1,0:T(8,128)S(1)}, f32[8,128]{1,0:T(8,128)S(1)}, u32[]{:S(2)}, u32[]{:S(2)}) collective-permute-start(f32[8,128]{1,0:T(8,128)S(1)} %get-tuple-element.55), channel_id=1, source_target_pairs={{0,2},{1,3},{2,0},{3,1},{4,6},{5,7},{6,4},{7,5},{8,10},{9,11},{10,... | collective-permute-start | bytes 12296 | tf_op jit(solution)/shard_map/ppermute | solution.py:245
  118.4 2.0 %collective-permute-start.37 = (f32[8,128]{1,0:T(8,128)S(1)}, f32[8,128]{1,0:T(8,128)S(1)}, u32[]{:S(2)}, u32[]{:S(2)}) collective-permute-start(f32[8,128]{1,0:T(8,128)S(1)} %get-tuple-element.55), channel_id=1, source_target_pairs={{0,1},{1,0},{2,3},{3,2},{4,5},{5,4},{6,7},{7,6},{8,9},{9,8},{10,11... | collective-permute-start | bytes 12296 | tf_op jit(solution)/shard_map/ppermute | solution.py:245
  120.4 4.6 %collective-permute-start.46 = (f32[8,128]{1,0:T(8,128)S(1)}, f32[8,128]{1,0:T(8,128)S(1)}, u32[]{:S(2)}, u32[]{:S(2)}) collective-permute-start(f32[8,128]{1,0:T(8,128)S(1)} %add_add_fusion.refs_0_), channel_id=1, source_target_pairs={{0,24},{8,16},{16,8},{24,0},{1,25},{9,17},{17,9},{25,1},{2,26},{10... | collective-permute-start | bytes 12296 | tf_op jit(solution)/shard_map/ppermute | solution.py:245
  122.1 3.6 %collective-permute-start.45 = (f32[8,128]{1,0:T(8,128)S(1)}, f32[8,128]{1,0:T(8,128)S(1)}, u32[]{:S(2)}, u32[]{:S(2)}) collective-permute-start(f32[8,128]{1,0:T(8,128)S(1)} %add_add_fusion.refs_0_), channel_id=1, source_target_pairs={{0,16},{8,24},{16,0},{24,8},{1,17},{9,25},{17,1},{25,9},{2,18},{10... | collective-permute-start | bytes 12296 | tf_op jit(solution)/shard_map/ppermute | solution.py:245
  123.4 3.6 %collective-permute-start.44 = (f32[8,128]{1,0:T(8,128)S(1)}, f32[8,128]{1,0:T(8,128)S(1)}, u32[]{:S(2)}, u32[]{:S(2)}) collective-permute-start(f32[8,128]{1,0:T(8,128)S(1)} %add_add_fusion.refs_0_), channel_id=1, source_target_pairs={{0,8},{8,0},{16,24},{24,16},{1,9},{9,1},{17,25},{25,17},{2,10},{10... | collective-permute-start | bytes 12296 | tf_op jit(solution)/shard_map/ppermute | solution.py:245

commit v2 on v1

v2 whole, which is shorter than its diff:
```python
import functools

import jax
import jax.numpy as jnp
from jax import lax
from jax.experimental import pallas as pl
from jax.experimental.pallas import tpu as pltpu
from jax.sharding import PartitionSpec as P

ITERS = 2
N = 1048576
epsilon_sq = 1e-06
LANES = 128
VMEM = pl.BlockSpec(memory_space=pltpu.VMEM)
SMEM = pl.BlockSpec(memory_space=pltpu.SMEM)
ANY = pl.BlockSpec(memory_space=pl.ANY)
PARAMS = pltpu.CompilerParams(vmem_limit_bytes=32 * 1024 * 1024)


def tree_sum(parts):
    while len(parts) > 1:
        parts = [parts[i] + parts[i + 1] for i in range(0, len(parts), 2)]
    return parts[0]


def lane_total(acc):
    rows = jnp.broadcast_to(jnp.sum(acc, axis=1, keepdims=True), acc.shape)
    return rows + pltpu.roll(rows, 4, 0)


def norm_of(acc):
    return jnp.sqrt(lane_total(acc) + epsilon_sq)


def low_half():
    return lax.broadcasted_iota(jnp.int32, (8, LANES), 0) < 4


def wide_to_block(wide, upper):
    first, second = wide[:, :LANES], wide[:, LANES:]
    if upper:
        return jnp.where(low_half(), pltpu.roll(first, 4, 0), second)
    return jnp.where(low_half(), first, pltpu.roll(second, 4, 0))


def write_payload(out_ref, blocks, acc):
    rows = out_ref.shape[0]
    first, second = [], []
    low = low_half()
    for q in range(0, len(blocks), 2):
        first.append(jnp.where(low, blocks[q], pltpu.roll(blocks[q + 1], 4, 0)))
        second.append(jnp.where(low, pltpu.roll(blocks[q], 4, 0), blocks[q + 1]))
    while len(first) * 8 < rows:
        first.append(jnp.zeros((8, LANES), jnp.float32))
        second.append(jnp.zeros((8, LANES), jnp.float32))
    out_ref[:, :LANES] = jnp.concatenate(first, axis=0).astype(jnp.bfloat16)
    out_ref[:, LANES : 2 * LANES] = jnp.concatenate(second, axis=0).astype(jnp.bfloat16)
    upper = acc.astype(jnp.bfloat16).astype(jnp.float32)
    pieces = [upper, acc - upper] + [jnp.zeros((8, LANES), jnp.float32)] * (rows // 8 - 2)
    out_ref[:, 2 * LANES :] = jnp.concatenate(pieces, axis=0).astype(jnp.bfloat16)


def read_squares(ref):
    both = ref[:, 2 * LANES :].astype(jnp.float32)
    return both[:8] + both[8:16]


def prepare_kernel(obs_ref, blocks_ref, payload_ref):
    obs = obs_ref[...]
    blocks = []
    for q in range(obs.shape[1] // (2 * LANES)):
        at = q * 2 * LANES
        blocks.append(jnp.concatenate([obs[:, at : at + LANES], obs[:, at + LANES : at + 2 * LANES]], axis=0))
    for q, block in enumerate(blocks):
        blocks_ref[q] = block
    squares = tree_sum([b * b for b in blocks])
    for c in range(payload_ref.shape[0]):
        write_payload(payload_ref.at[c], blocks, squares)


def adjoint_kernel(cols_ref, tiles_ref, payload_ref, out_ref):
    row_tiles, per_block = tiles_ref.shape[:2]
    shares, copies = payload_ref.shape[0], out_ref.shape[0]
    per_share = row_tiles // shares
    total = row_tiles * per_block
    squares = tree_sum([read_squares(payload_ref.at[c]) for c in range(shares)])
    cols = cols_ref[...]
    for r in range(copies):
        out_ref[r, total] = squares
        out_ref[r, total + 1] = cols
    for c in range(shares):
        rays = payload_ref[c, :, : 2 * LANES]
        for q in range(per_share):
            for k in range(per_block):
                wide = jnp.dot(rays, tiles_ref[c * per_share + q, k], preferred_element_type=jnp.float32)
                at = 8 * (q // 2)
                block = wide_to_block(wide[at : at + 8], q % 2 == 1)
                for r in range(copies):
                    out_ref[r, (c * per_share + q) * per_block + k] = block


def voxel_kernel(first, own_cols_ref, tiles_ref, term_ref, *refs):
    if not first:
        right_ref, alpha_ref = refs[:2]
        refs = refs[2:]
    out_ref, beta_ref, raw_ref, cols_ref, sem = refs
    row_tiles, per_block = tiles_ref.shape[:2]
    shares, rows = out_ref.shape[0], term_ref.shape[0]
    per_share = row_tiles // shares
    per_row = row_tiles * per_block
    copy = pltpu.make_async_copy(term_ref.at[:, per_row + 1], cols_ref, sem)
    copy.start()
    col_tiles = raw_ref.shape[0]
    chunk = 16
    zeros = jnp.zeros((chunk, 8, LANES), jnp.float32)

    @pl.loop(0, col_tiles // chunk)
    def _(step):
        raw_ref[pl.ds(step * chunk, chunk)] = zeros

    beta = norm_of(tree_sum([term_ref[s, per_row] for s in range(rows)]))
    beta_ref[...] = beta
    unroll = 8
    copy.wait()
    for s in range(rows):

        @pl.loop(0, per_row // unroll)
        def _(step):
            for u in range(unroll):
                t = step * unroll + u
                col = cols_ref[s, 0, t].astype(jnp.int32)
                raw_ref[col] = raw_ref[col] + term_ref[s, t]

    beta_inv = 1.0 / beta
    if not first:
        right_scale = beta / alpha_ref[...]

    def scale(step, acc):
        at = pl.ds(step * chunk, chunk)
        raw = raw_ref[at] * beta_inv
        if not first:
            raw = raw - right_ref[at] * right_scale
        raw_ref[at] = raw
        return acc + jnp.sum(raw * raw, axis=0)

    acc = lax.fori_loop(0, col_tiles // chunk, scale, jnp.zeros((8, LANES), jnp.float32))
    for c in range(shares):
        for q in range(per_share):
            i = c * per_share + q
            wide = None
            for k in range(per_block):
                block = raw_ref[own_cols_ref[i * per_block + k]]
                lhs = jnp.concatenate([block, pltpu.roll(block, 4, 0)], axis=1).astype(jnp.bfloat16)
                part = lax.dot_general(
                    lhs, tiles_ref[i, k], (((1,), (1,)), ((), ())), preferred_element_type=jnp.float32
                )
                wide = part if wide is None else wide + part
            out_ref[c, q] = wide_to_block(wide, False)
        out_ref[c, per_share] = acc


def ray_kernel(part_ref, left_ref, beta_ref, raw_ref, alpha_ref, payload_ref, acc_ref):
    shares, per_share = part_ref.shape[0], raw_ref.shape[0]
    alpha = norm_of(tree_sum([part_ref[c, per_share] for c in range(shares)]))
    alpha_ref[...] = alpha
    alpha_inv = 1.0 / alpha
    left_scale = alpha / beta_ref[...]
    blocks = []
    for q in range(per_share):
        total = tree_sum([part_ref[c, q] for c in range(shares)])
        blocks.append(total * alpha_inv - left_ref[q] * left_scale)
        raw_ref[q] = blocks[-1]
    acc = tree_sum([b * b for b in blocks])
    for c in range(shares):
        acc_ref[c] = acc
        write_payload(payload_ref.at[c], blocks, acc)


def final_kernel(iters, pos_ref, last_ref, *refs):
    refs = list(refs)
    betas = [refs.pop(0) for _ in range(iters)]
    alphas = [refs.pop(0) for _ in range(iters)]
    raws = [refs.pop(0) for _ in range(iters)]
    out_ref, ratio_ref, held, sems = refs
    share = held.shape[1]
    start = pos_ref[0] * share
    copies = []
    for i in range(iters):
        copies.append(pltpu.make_async_copy(raws[i].at[pl.ds(start, share)], held.at[i], sems.at[i]))
        copies[-1].start()
    beta = [b[...] for b in betas] + [norm_of(tree_sum([last_ref[r] for r in range(last_ref.shape[0])]))]
    alpha = [a[...] for a in alphas]
    phibar, rhobar = beta[0], alpha[0]
    direction = [1.0 / alpha[0]] + [jnp.zeros_like(phibar)] * (iters - 1)
    weights = [jnp.zeros_like(phibar)] * iters
    for i in range(iters):
        rho = jnp.sqrt(rhobar * rhobar + beta[i + 1] * beta[i + 1])
        cosine, sine = rhobar / rho, beta[i + 1] / rho
        phi = cosine * phibar
        phibar = sine * phibar
        weights = [w + (phi / rho) * d for w, d in zip(weights, direction)]
        if i + 1 < iters:
            theta = sine * alpha[i + 1]
            rhobar = -cosine * alpha[i + 1]
            direction = [-(theta / rho) * d for d in direction]
            direction[i + 1] = direction[i + 1] + 1.0 / alpha[i + 1]
    ratio_ref[...] = phibar / beta[0]
    for copy in copies:
        copy.wait()
    unroll = 4

    @pl.loop(0, share // unroll)
    def _(step):
        for u in range(unroll):
            c = step * unroll + u
            block = held[0, c] * weights[0]
            for i in range(1, iters):
                block = block + held[i, c] * weights[i]
            at = pl.multiple_of(c * 2 * LANES, 2 * LANES)
            out_ref[:, pl.ds(at, LANES)] = block[:4]
            out_ref[:, pl.ds(at + LANES, LANES)] = block[4:]


def f32(*shape):
    return jax.ShapeDtypeStruct(shape, jnp.float32)


def swap(values, axis):
    return lax.all_to_all(values, axis, 0, 0)


def local(observed, tile_values, tile_cols):
    row_tiles, per_block, tile_size = tile_values.shape[:3]
    rows, shares = lax.axis_size("row"), lax.axis_size("col")
    col_tiles = N // (tile_size * shares)
    per_share = row_tiles // shares
    terms = row_tiles * per_block
    payload = jax.ShapeDtypeStruct((shares, max(16, 4 * per_share), 3 * LANES), jnp.bfloat16)
    pos = lax.axis_index("row").astype(jnp.int32).reshape(1)
    own_cols = tile_cols.reshape(-1)
    float_cols = jnp.zeros((8, LANES), jnp.float32).at[0, :terms].set(own_cols.astype(jnp.float32))

    def adjoint(payloads):
        return pl.pallas_call(
            adjoint_kernel,
            out_shape=f32(rows, terms + 2, 8, LANES),
            in_specs=[VMEM] * 3,
            out_specs=VMEM,
            compiler_params=PARAMS,
            name="adjoint",
        )(float_cols, tile_values, payloads)

    def voxel(term_array, previous):
        first = previous is None
        extra = [] if first else list(previous)
        return pl.pallas_call(
            functools.partial(voxel_kernel, first),
            out_shape=[f32(shares, per_share + 1, 8, LANES), f32(8, LANES), f32(col_tiles, 8, LANES)],
            in_specs=[SMEM] + [VMEM] * (2 + len(extra)),
            out_specs=[VMEM] * 3,
            scratch_shapes=[pltpu.SMEM((rows, 8, LANES), jnp.float32), pltpu.SemaphoreType.DMA],
            compiler_params=PARAMS,
            name="voxel",
        )(own_cols, tile_values, term_array, *extra)

    def ray(parts, left_raw, beta):
        return pl.pallas_call(
            ray_kernel,
            out_shape=[f32(per_share, 8, LANES), f32(8, LANES), payload, f32(shares, 8, LANES)],
            in_specs=[VMEM] * 3,
            out_specs=[VMEM] * 4,
            compiler_params=PARAMS,
            name="ray",
        )(parts, left_raw, beta)

    left_raw, message = pl.pallas_call(
        prepare_kernel,
        out_shape=[f32(per_share, 8, LANES), payload],
        in_specs=[VMEM],
        out_specs=[VMEM, VMEM],
        compiler_params=PARAMS,
        name="prepare",
    )(observed)
    betas, alphas, raws = [], [], []
    previous = None
    for iteration in range(ITERS + 1):
        parts, beta, right_raw = voxel(swap(adjoint(swap(message, "col")), "row"), previous)
        if iteration == ITERS:
            break
        left_raw, alpha, message, squares = ray(swap(parts, "col"), left_raw, beta)
        betas.append(beta)
        alphas.append(alpha)
        raws.append(right_raw)
        previous = (right_raw, alpha)
    shared = swap(squares, "col")
    shared = tree_sum([shared[c] for c in range(shares)])
    last = swap(jnp.broadcast_to(shared[None], (rows, 8, LANES)), "row")
    share = col_tiles // rows
    result, ratio = pl.pallas_call(
        functools.partial(final_kernel, ITERS),
        out_shape=[f32(4, share * tile_size), f32(8, LANES)],
        in_specs=[SMEM] + [VMEM] * (1 + 2 * ITERS) + [ANY] * ITERS,
        out_specs=[VMEM, VMEM],
        scratch_shapes=[pltpu.VMEM((ITERS, share, 8, LANES), jnp.float32), pltpu.SemaphoreType.DMA((ITERS,))],
        compiler_params=PARAMS,
        name="final",
    )(pos, last, *betas, *alphas, *raws)
    return result, ratio[:4, 0]


def solution(mesh):
    in_specs = (P(None, ("row", "col")), P("row", "col", None, None), P("row", "col"))
    out_specs = (P(None, ("col", "row")), P())
    return jax.shard_map(local, mesh=mesh, in_specs=in_specs, out_specs=out_specs, check_vma=False)
```

time: 130 us -> 124 us (0.954)
  blocking collectives: 0 us -> 54 us
  starting transfers between devices: 57.1 us -> 13.4 us
  waiting for transfers between devices: 37.4 us -> 23.8 us
  Pallas kernels: 22.6 us -> 18.2 us
    ppermute x47 -> x0, starting transfers between devices: 57.1 us -> none  [the longest x33 40.9 us: exchange(): got.append(lax.ppermute(value, axis, [(i, i ^ d) for i in range(size)]))]
    all_to_all x0 -> x5, blocking collectives: none -> 54 us  [swap(): return lax.all_to_all(values, axis, 0, 0)]
    ppermute x47 -> x0, waiting for transfers between devices: 37.4 us -> none  [the longest x33 30.2 us: exchange(): got.append(lax.ppermute(value, axis, [(i, i ^ d) for i in range(size)]))]
    all_to_all x0 -> x3, waiting for transfers between devices: none -> 23.8 us  [swap(): return lax.all_to_all(values, axis, 0, 0)]
    all_to_all x0 -> x3, starting transfers between devices: none -> 13.4 us  [swap(): return lax.all_to_all(values, axis, 0, 0)]
    pallas_call x7, Pallas kernels: 22.6 us -> 17.6 us  [the longest x2 11.3 us: voxel(): pl.pallas_call(functools.partial(voxel_kernel, first), out_shape=[f32(sha...]
    unnamed x19 -> x15, local copies, waits for them, and re-layouts: 10.9 us -> 10.5 us
  transfers between devices with their start and end apart: 47 -> 3, of which waited for: 24 -> 3; matrix products, arithmetic and copies ran while one was open for 0% -> 1% of each run, Pallas kernels for 0% -> 0%
where the time goes in v2:
time: 124 us; the launch traced here: 123 us
  blocking collectives  54 us (44%)
  waiting for transfers between devices  23.8 us (19%)
  Pallas kernels  18.2 us (15%)
  starting transfers between devices  13.4 us (11%)
  local copies, waits for them, and re-layouts  12 us (10%)
    all_to_all x5, blocking collectives, swap(): return lax.all_to_all(values, axis, 0, 0)  54 us
    all_to_all x3, waiting for transfers between devices, swap(): return lax.all_to_all(values, axis, 0, 0)  23.8 us
    all_to_all x3, starting transfers between devices, swap(): return lax.all_to_all(values, axis, 0, 0)  13.4 us
    pallas_call x2, Pallas kernels, voxel(): pl.pallas_call(functools.partial(voxel_kernel, first), out_shape=[f32(sha...  11.3 us
    unnamed x15, local copies, waits for them, and re-layouts  10.5 us
    pallas_call x2, Pallas kernels, adjoint(): pl.pallas_call(adjoint_kernel, out_shape=f32(rows, terms + 2, 8, LANES),...  3.38 us
  transfers between devices with their start and end apart: 3, of which 3 were waited for; matrix products, arithmetic and copies ran while one was open for 1% of the time, Pallas kernels for 0%

profile of v2, /device:TPU:0, one launch (start us, length us, event | category | flops | bytes accessed | tf_op | source)
XLA Modules:
  0.0 122.9 jit_solution(3746058362295820868)
XLA Ops:
  0.6 0.0 copy-start.5
  0.6 0.7 copy-done.5
  1.3 0.7 prepare.1
  2.0 6.3 %all-to-all-start = ((bf16[8,16,384]{2,1,0:T(8,128)(2,1)}), bf16[8,16,384]{2,1,0:T(8,128)(2,1)S(1)}, u32[]{:S(2)}, u32[]{:S(2)}) async-start(bf16[8,16,384]{2,1,0:T(8,128)(2,1)} %get-tuple-element.29), calls=%async_computation | async-start | bytes 196608 | tf_op jit(solution)/shard_map/all_to_all | solution.py:229
  8.3 0.7 convert_element_type.11
  9.0 0.1 copy.8
  9.1 0.1 convert_element_type.12
  9.2 5.5 %all-to-all-done.payload_ref = bf16[8,16,384]{2,1,0:T(8,128)(2,1)S(1)} async-done(((bf16[8,16,384]{2,1,0:T(8,128)(2,1)}), bf16[8,16,384]{2,1,0:T(8,128)(2,1)S(1)}, u32[]{:S(2)}, u32[]{:S(2)}) %all-to-all-start) | async-done | bytes 98336 | tf_op jit(solution)/shard_map/all_to_all | solution.py:229
  14.7 0.0 copy-start
  14.7 3.4 %copy-done = bf16[32,2,256,256]{3,2,1,0:T(8,128)(2,1)S(1)} copy-done((bf16[32,2,256,256]{3,2,1,0:T(8,128)(2,1)S(1)}, bf16[32,2,256,256]{3,2,1,0:T(8,128)(2,1)}, u32[]{:S(2)}) %copy-start) | copy-done | bytes 8388632
  18.1 2.2 %adjoint.2 = f32[4,66,8,128]{3,2,1,0:T(8,128)} custom-call(f32[8,128]{1,0:T(8,128)S(1)} %scatter.4.cols_ref, bf16[32,2,256,256]{3,2,1,0:T(8,128)(2,1)S(1)} %copy-done, bf16[8,16,384]{2,1,0:T(8,128)(2,1)S(1)} %all-to-all-done.payload_ref), custom_call_target="tpu_custom_call" | custom-call | tf_op jit(solution)/shard_map/adjoint/pallas_call | solution.py:244
  20.3 0.0 copy-start.6
  20.3 3.8 %all-to-all-start.1 = ((f32[4,66,8,128]{3,2,1,0:T(8,128)}), f32[4,66,8,128]{3,2,1,0:T(8,128)S(1)}, u32[]{:S(2)}, u32[]{:S(2)}) async-start(f32[4,66,8,128]{3,2,1,0:T(8,128)} %adjoint.2), calls=%async_computation.1 | async-start | bytes 2162688 | tf_op jit(solution)/shard_map/all_to_all | solution.py:229
  24.1 0.0 copy-done.6
  24.1 0.1 copy.7
  24.2 0.1 reshape.47.own_cols_ref
  24.3 13.6 %all-to-all-done.1.term_ref = f32[4,66,8,128]{3,2,1,0:T(8,128)S(1)} async-done(((f32[4,66,8,128]{3,2,1,0:T(8,128)}), f32[4,66,8,128]{3,2,1,0:T(8,128)S(1)}, u32[]{:S(2)}, u32[]{:S(2)}) %all-to-all-start.1) | async-done | bytes 1081376 | tf_op jit(solution)/shard_map/all_to_all | solution.py:229
  37.9 0.0 copy-start.1
  37.9 3.4 %copy-done.1 = bf16[32,2,256,256]{3,2,1,0:T(8,128)(2,1)S(1)} copy-done((bf16[32,2,256,256]{3,2,1,0:T(8,128)(2,1)S(1)}, bf16[32,2,256,256]{3,2,1,0:T(8,128)(2,1)}, u32[]{:S(2)}) %copy-start.1) | copy-done | bytes 8388632
  41.3 0.0 copy-start.2
  41.3 5.6 %voxel.2 = (f32[8,5,8,128]{3,2,1,0:T(8,128)S(1)}, f32[8,128]{1,0:T(8,128)S(1)}, f32[512,8,128]{2,1,0:T(8,128)S(1)}) custom-call(s32[64]{0:T(128)S(1)} %reshape.47.own_cols_ref, bf16[32,2,256,256]{3,2,1,0:T(8,128)(2,1)S(1)} %copy-done.1, f32[4,66,8,128]{3,2,1,0:T(8,128)S(1)} %all-to-all-done.1.term_ref), custom_call_target="tpu_custom_call" | custom-call | tf_op jit(solution)/shard_map/voxel/pallas_call | solution.py:256
  47.0 9.6 %all_to_all.42.part_ref = f32[8,5,8,128]{3,2,1,0:T(8,128)S(1)} all-to-all(f32[8,5,8,128]{3,2,1,0:T(8,128)S(1)} %get-tuple-element.30), channel_id=1, replica_groups=mesh['row'=4,'col'=8] {'col'}, dimensions={0} | all-to-all | bytes 327680 | tf_op jit(solution)/shard_map/all_to_all | solution.py:229
  56.6 0.7 ray.2
  57.3 9.1 %all_to_all.43.payload_ref = bf16[8,16,384]{2,1,0:T(8,128)(2,1)S(1)} all-to-all(bf16[8,16,384]{2,1,0:T(8,128)(2,1)S(1)} %get-tuple-element.33), channel_id=1, replica_groups=mesh['row'=4,'col'=8] {'col'}, dimensions={0} | all-to-all | bytes 196608 | tf_op jit(solution)/shard_map/all_to_all | solution.py:229
  66.4 0.0 copy-done.2
  66.4 1.2 adjoint.3
  67.6 17.2 %all_to_all.44.term_ref = f32[4,66,8,128]{3,2,1,0:T(8,128)S(1)} all-to-all(f32[4,66,8,128]{3,2,1,0:T(8,128)S(1)} %adjoint.3), channel_id=1, replica_groups=mesh['row'=4,'col'=8] {'row'}, dimensions={0} | all-to-all | bytes 2162688 | tf_op jit(solution)/shard_map/all_to_all | solution.py:229
  84.8 5.7 %voxel.3 = (f32[8,5,8,128]{3,2,1,0:T(8,128)S(1)}, f32[8,128]{1,0:T(8,128)S(1)}, f32[512,8,128]{2,1,0:T(8,128)S(1)}) custom-call(s32[64]{0:T(128)S(1)} %reshape.47.own_cols_ref, bf16[32,2,256,256]{3,2,1,0:T(8,128)(2,1)S(1)} %copy-done.2, f32[4,66,8,128]{3,2,1,0:T(8,128)S(1)} %all_to_all.44.term_ref, f32[512,8,128]{2,1,0:T(8,128)S(1)} %get-tuple-element.34.refs_0_.refs_4_, ...), custom_call_target="tpu_custom_call" | custom-call | tf_op jit(solution)/shard_map/voxel/pallas_call | solution.py:256
  90.5 0.0 copy-start.3
  90.5 1.3 %copy-done.3 = f32[512,8,128]{2,1,0:T(8,128)} copy-done((f32[512,8,128]{2,1,0:T(8,128)}, f32[512,8,128]{2,1,0:T(8,128)S(1)}, u32[]{:S(2)}) %copy-start.3) | copy-done | bytes 2097176
  91.8 9.6 %all_to_all.45.part_ref = f32[8,5,8,128]{3,2,1,0:T(8,128)S(1)} all-to-all(f32[8,5,8,128]{3,2,1,0:T(8,128)S(1)} %get-tuple-element.36), channel_id=1, replica_groups=mesh['row'=4,'col'=8] {'col'}, dimensions={0} | all-to-all | bytes 327680 | tf_op jit(solution)/shard_map/all_to_all | solution.py:229
  101.4 0.8 ray.3
  102.2 8.5 %all_to_all.46 = f32[8,8,128]{2,1,0:T(8,128)S(1)} all-to-all(f32[8,8,128]{2,1,0:T(8,128)S(1)} %get-tuple-element.39), channel_id=1, replica_groups=mesh['row'=4,'col'=8] {'col'}, dimensions={0} | all-to-all | bytes 65536 | tf_op jit(solution)/shard_map/all_to_all | solution.py:229
  110.6 0.6 broadcast_in_dim.10
  111.2 3.3 %all-to-all-start.7 = ((f32[4,8,128]{2,1,0:T(8,128)}), f32[4,8,128]{2,1,0:T(8,128)S(1)}, u32[]{:S(2)}, u32[]{:S(2)}) async-start(f32[4,8,128]{2,1,0:T(8,128)} %broadcast_in_dim.10), calls=%async_computation.7 | async-start | bytes 32768 | tf_op jit(solution)/shard_map/all_to_all | solution.py:229
  114.5 4.7 %all-to-all-done.7.last_ref = f32[4,8,128]{2,1,0:T(8,128)S(1)} async-done(((f32[4,8,128]{2,1,0:T(8,128)}), f32[4,8,128]{2,1,0:T(8,128)S(1)}, u32[]{:S(2)}, u32[]{:S(2)}) %all-to-all-start.7) | async-done | bytes 16416 | tf_op jit(solution)/shard_map/all_to_all | solution.py:229
  119.2 0.0 copy-start.4
  119.2 1.6 %copy-done.4 = f32[512,8,128]{2,1,0:T(8,128)S(1)} copy-done((f32[512,8,128]{2,1,0:T(8,128)S(1)}, f32[512,8,128]{2,1,0:T(8,128)}, u32[]{:S(2)}) %copy-start.4) | copy-done | bytes 2097176
  120.8 1.5 %final.1 = (f32[4,32768]{1,0:T(4,128)}, f32[8,128]{1,0:T(8,128)S(1)}) custom-call(s32[1]{0:T(128)} %bitcast.pos_ref, f32[4,8,128]{2,1,0:T(8,128)S(1)} %all-to-all-done.7.last_ref, f32[8,128]{1,0:T(8,128)S(1)} %get-tuple-element.32.beta_ref.refs_0_, f32[8,128]{1,0:T(8,128)S(1)} %get-tuple-element.38.beta_ref.refs_1_, ...), custom_call_target="tpu_custom_call" | custom-call | tf_op jit(solution)/shard_map/final/pallas_call | solution.py:299
  122.2 0.6 slice_reduce_fusion
  (2 shorter events, 0.0 us)
Async XLA Ops:
  0.6 0.7 copy-start.5
  2.0 12.7 %all-to-all-start = ((bf16[8,16,384]{2,1,0:T(8,128)(2,1)}), bf16[8,16,384]{2,1,0:T(8,128)(2,1)S(1)}, u32[]{:S(2)}, u32[]{:S(2)}) async-start(bf16[8,16,384]{2,1,0:T(8,128)(2,1)} %get-tuple-element.29), calls=%async_computation | async-start | bytes 196608 | tf_op jit(solution)/shard_map/all_to_all | solution.py:229
  14.7 3.4 %copy-start = (bf16[32,2,256,256]{3,2,1,0:T(8,128)(2,1)S(1)}, bf16[32,2,256,256]{3,2,1,0:T(8,128)(2,1)}, u32[]{:S(2)}) copy-start(bf16[32,2,256,256]{3,2,1,0:T(8,128)(2,1)} %tiles_ref.7) | copy-start | bytes 25165828
  20.3 3.9 %copy-start.6 = (s32[32,2]{0,1:T(2,128)S(1)}, s32[32,2]{0,1:T(2,128)}, u32[]{:S(2)}) copy-start(s32[32,2]{0,1:T(2,128)} %param.7) | copy-start | bytes 772
  20.3 17.7 %all-to-all-start.1 = ((f32[4,66,8,128]{3,2,1,0:T(8,128)}), f32[4,66,8,128]{3,2,1,0:T(8,128)S(1)}, u32[]{:S(2)}, u32[]{:S(2)}) async-start(f32[4,66,8,128]{3,2,1,0:T(8,128)} %adjoint.2), calls=%async_computation.1 | async-start | bytes 2162688 | tf_op jit(solution)/shard_map/all_to_all | solution.py:229
  37.9 3.4 %copy-start.1 = (bf16[32,2,256,256]{3,2,1,0:T(8,128)(2,1)S(1)}, bf16[32,2,256,256]{3,2,1,0:T(8,128)(2,1)}, u32[]{:S(2)}) copy-start(bf16[32,2,256,256]{3,2,1,0:T(8,128)(2,1)} %tiles_ref.7) | copy-start | bytes 25165828
  41.3 25.0 %copy-start.2 = (bf16[32,2,256,256]{3,2,1,0:T(8,128)(2,1)S(1)}, bf16[32,2,256,256]{3,2,1,0:T(8,128)(2,1)}, u32[]{:S(2)}) copy-start(bf16[32,2,256,256]{3,2,1,0:T(8,128)(2,1)} %tiles_ref.7) | copy-start | bytes 25165828
  90.5 1.3 %copy-start.3 = (f32[512,8,128]{2,1,0:T(8,128)}, f32[512,8,128]{2,1,0:T(8,128)S(1)}, u32[]{:S(2)}) copy-start(f32[512,8,128]{2,1,0:T(8,128)S(1)} %get-tuple-element.41.refs_5_) | copy-start | bytes 6291460
  111.2 7.9 %all-to-all-start.7 = ((f32[4,8,128]{2,1,0:T(8,128)}), f32[4,8,128]{2,1,0:T(8,128)S(1)}, u32[]{:S(2)}, u32[]{:S(2)}) async-start(f32[4,8,128]{2,1,0:T(8,128)} %broadcast_in_dim.10), calls=%async_computation.7 | async-start | bytes 32768 | tf_op jit(solution)/shard_map/all_to_all | solution.py:229
  119.2 1.6 %copy-start.4 = (f32[512,8,128]{2,1,0:T(8,128)S(1)}, f32[512,8,128]{2,1,0:T(8,128)}, u32[]{:S(2)}) copy-start(f32[512,8,128]{2,1,0:T(8,128)} %copy-done.3) | copy-start | bytes 6291460

commit v3 on v2

--- a/solution.py
+++ b/solution.py
@@ -13,7 +13,7 @@
 LANES = 128
 VMEM = pl.BlockSpec(memory_space=pltpu.VMEM)
 SMEM = pl.BlockSpec(memory_space=pltpu.SMEM)
-ANY = pl.BlockSpec(memory_space=pl.ANY)
+HBM = pl.BlockSpec(memory_space=pltpu.HBM)
 PARAMS = pltpu.CompilerParams(vmem_limit_bytes=32 * 1024 * 1024)
 
 
@@ -78,38 +78,61 @@
         write_payload(payload_ref.at[c], blocks, squares)
 
 
-def adjoint_kernel(cols_ref, tiles_ref, payload_ref, out_ref):
+def split_store(value, upper_ref, lower_ref, i):
+    upper = value.astype(jnp.bfloat16)
+    upper_ref[i] = upper
+    lower_ref[i] = (value - upper.astype(jnp.float32)).astype(jnp.bfloat16)
+
+
+def adjoint_kernel(load, cols_ref, tiles_ref, payload_ref, upper_ref, lower_ref, *refs):
     row_tiles, per_block = tiles_ref.shape[:2]
-    shares, copies = payload_ref.shape[0], out_ref.shape[0]
+    shares = payload_ref.shape[0]
     per_share = row_tiles // shares
-    total = row_tiles * per_block
+    copies = []
+    held_ref = tiles_ref
+    if load:
+        held_ref, sems = refs
+        for c in range(shares):
+            part = pl.ds(c * per_share, per_share)
+            copies.append(pltpu.make_async_copy(tiles_ref.at[part], held_ref.at[part], sems.at[c]))
+            copies[-1].start()
     squares = tree_sum([read_squares(payload_ref.at[c]) for c in range(shares)])
-    cols = cols_ref[...]
-    for r in range(copies):
-        out_ref[r, total] = squares
-        out_ref[r, total + 1] = cols
+    rounded = squares.astype(jnp.bfloat16).astype(jnp.float32)
+    upper_ref[row_tiles] = jnp.concatenate([rounded, squares - rounded], axis=0).astype(jnp.bfloat16)
+    upper_ref[row_tiles + 1] = cols_ref[...].astype(jnp.bfloat16)
     for c in range(shares):
+        if load:
+            copies[c].wait()
         rays = payload_ref[c, :, : 2 * LANES]
         for q in range(per_share):
+            i = c * per_share + q
+            at = 8 * (q // 2)
+            blocks = []
             for k in range(per_block):
-                wide = jnp.dot(rays, tiles_ref[c * per_share + q, k], preferred_element_type=jnp.float32)
-                at = 8 * (q // 2)
-                block = wide_to_block(wide[at : at + 8], q % 2 == 1)
-                for r in range(copies):
-                    out_ref[r, (c * per_share + q) * per_block + k] = block
-
-
-def voxel_kernel(first, own_cols_ref, tiles_ref, term_ref, *refs):
+                wide = jnp.dot(rays, held_ref[i, k], preferred_element_type=jnp.float32)
+                blocks.append(wide_to_block(wide[at : at + 8], q % 2 == 1))
+            split_store(jnp.concatenate(blocks, axis=0), upper_ref, lower_ref, i)
+
+
+def voxel_kernel(first, rows, pos_ref, own_cols_ref, tiles_ref, *refs):
+    terms, refs = refs[:rows], refs[rows:]
     if not first:
         right_ref, alpha_ref = refs[:2]
         refs = refs[2:]
-    out_ref, beta_ref, raw_ref, cols_ref, sem = refs
+    out_ref, beta_ref, raw_ref, share_ref, cols_ref, term_buf, cols_buf, cols_scalar, sem = refs
     row_tiles, per_block = tiles_ref.shape[:2]
-    shares, rows = out_ref.shape[0], term_ref.shape[0]
+    shares = out_ref.shape[0]
     per_share = row_tiles // shares
-    per_row = row_tiles * per_block
-    copy = pltpu.make_async_copy(term_ref.at[:, per_row + 1], cols_ref, sem)
+    for d in range(rows):
+        slot = jnp.bitwise_xor(pos_ref[0], d)
+        pieces = terms[d][row_tiles + 1].astype(jnp.float32)
+        cols_buf[slot] = (pieces[:8] * 16.0 + pieces[8:]).astype(jnp.int32)
+    copy = pltpu.make_async_copy(cols_buf, cols_scalar, sem)
     copy.start()
+    cols_ref[...] = cols_buf[...]
+    for d in range(rows):
+        slot = jnp.bitwise_xor(pos_ref[0], d)
+        term_buf[slot] = terms[d][:row_tiles]
     col_tiles = raw_ref.shape[0]
     chunk = 16
     zeros = jnp.zeros((chunk, 8, LANES), jnp.float32)
@@ -118,18 +141,24 @@
     def _(step):
         raw_ref[pl.ds(step * chunk, chunk)] = zeros
 
-    beta = norm_of(tree_sum([term_ref[s, per_row] for s in range(rows)]))
+    squares = []
+    for d in range(rows):
+        pieces = terms[d][row_tiles].astype(jnp.float32)
+        squares.append(pieces[:8] + pieces[8:])
+    beta = norm_of(tree_sum(squares))
     beta_ref[...] = beta
-    unroll = 8
+    unroll = 4
     copy.wait()
     for s in range(rows):
 
-        @pl.loop(0, per_row // unroll)
+        @pl.loop(0, row_tiles // unroll)
         def _(step):
             for u in range(unroll):
-                t = step * unroll + u
-                col = cols_ref[s, 0, t].astype(jnp.int32)
-                raw_ref[col] = raw_ref[col] + term_ref[s, t]
+                i = step * unroll + u
+                pair = term_buf[s, i].astype(jnp.float32)
+                for k in range(per_block):
+                    col = cols_scalar[s, 0, i * per_block + k]
+                    raw_ref[col] = raw_ref[col] + pair[8 * k : 8 * k + 8]
 
     beta_inv = 1.0 / beta
     if not first:
@@ -157,6 +186,30 @@
                 wide = part if wide is None else wide + part
             out_ref[c, q] = wide_to_block(wide, False)
         out_ref[c, per_share] = acc
+    share = share_ref.shape[0]
+    share_ref[...] = raw_ref[pl.ds(pos_ref[0] * share, share)]
+
+
+def lower_kernel(pos_ref, cols_ref, *refs):
+    terms, out_ref = refs[:-1], refs[-1]
+    row_tiles = terms[0].shape[0]
+    per_block = terms[0].shape[1] // 8
+    share = out_ref.shape[0] - 1
+    start = pos_ref[0] * share
+    out_ref[...] = jnp.zeros(out_ref.shape, jnp.float32)
+    unroll = 4
+    for d, term in enumerate(terms):
+        source = jnp.bitwise_xor(pos_ref[0], d)
+
+        @pl.loop(0, row_tiles // unroll)
+        def _(step):
+            for u in range(unroll):
+                i = step * unroll + u
+                pair = term[i].astype(jnp.float32)
+                for k in range(per_block):
+                    col = cols_ref[source, 0, i * per_block + k] - start
+                    col = jnp.where((col >= 0) & (col < share), col, share)
+                    out_ref[col] = out_ref[col] + pair[8 * k : 8 * k + 8]
 
 
 def ray_kernel(part_ref, left_ref, beta_ref, raw_ref, alpha_ref, payload_ref, acc_ref):
@@ -171,23 +224,19 @@
         blocks.append(total * alpha_inv - left_ref[q] * left_scale)
         raw_ref[q] = blocks[-1]
     acc = tree_sum([b * b for b in blocks])
+    for c in range(acc_ref.shape[0]):
+        acc_ref[c] = acc
     for c in range(shares):
-        acc_ref[c] = acc
         write_payload(payload_ref.at[c], blocks, acc)
 
 
-def final_kernel(iters, pos_ref, last_ref, *refs):
+def final_kernel(iters, last_ref, *refs):
     refs = list(refs)
     betas = [refs.pop(0) for _ in range(iters)]
     alphas = [refs.pop(0) for _ in range(iters)]
     raws = [refs.pop(0) for _ in range(iters)]
-    out_ref, ratio_ref, held, sems = refs
-    share = held.shape[1]
-    start = pos_ref[0] * share
-    copies = []
-    for i in range(iters):
-        copies.append(pltpu.make_async_copy(raws[i].at[pl.ds(start, share)], held.at[i], sems.at[i]))
-        copies[-1].start()
+    lowers = [refs.pop(0) for _ in range(iters)]
+    out_ref, ratio_ref = refs
     beta = [b[...] for b in betas] + [norm_of(tree_sum([last_ref[r] for r in range(last_ref.shape[0])]))]
     alpha = [a[...] for a in alphas]
     phibar, rhobar = beta[0], alpha[0]
@@ -204,18 +253,25 @@
             rhobar = -cosine * alpha[i + 1]
             direction = [-(theta / rho) * d for d in direction]
             direction[i + 1] = direction[i + 1] + 1.0 / alpha[i + 1]
-    ratio_ref[...] = phibar / beta[0]
-    for copy in copies:
-        copy.wait()
+    ratio = phibar / beta[0]
+    for n in range(4):
+        ratio_ref[n] = jnp.max(ratio[n : n + 1])
+    lower_weights = []
+    carried = jnp.zeros_like(phibar)
+    for i in reversed(range(iters)):
+        carried = weights[i] - carried
+        lower_weights.insert(0, carried / beta[i])
+        if i > 0:
+            carried = carried * (beta[i] / alpha[i - 1])
     unroll = 4
 
-    @pl.loop(0, share // unroll)
+    @pl.loop(0, raws[0].shape[0] // unroll)
     def _(step):
         for u in range(unroll):
             c = step * unroll + u
-            block = held[0, c] * weights[0]
-            for i in range(1, iters):
-                block = block + held[i, c] * weights[i]
+            parts = [r[c] * w for r, w in zip(raws, weights)]
+            parts += [r[c] * w for r, w in zip(lowers, lower_weights)]
+            block = tree_sum(parts) if len(parts) % 2 == 0 else sum(parts)
             at = pl.multiple_of(c * 2 * LANES, 2 * LANES)
             out_ref[:, pl.ds(at, LANES)] = block[:4]
             out_ref[:, pl.ds(at + LANES, LANES)] = block[4:]
@@ -223,6 +279,14 @@
 
 def f32(*shape):
     return jax.ShapeDtypeStruct(shape, jnp.float32)
+
+
+def exchange(value, axis):
+    size = lax.axis_size(axis)
+    got = [value]
+    for d in range(1, size):
+        got.append(lax.ppermute(value, axis, [(i, i ^ d) for i in range(size)]))
+    return got
 
 
 def swap(values, axis):
@@ -237,36 +301,64 @@
     terms = row_tiles * per_block
     payload = jax.ShapeDtypeStruct((shares, max(16, 4 * per_share), 3 * LANES), jnp.bfloat16)
     pos = lax.axis_index("row").astype(jnp.int32).reshape(1)
+    share = col_tiles // rows
     own_cols = tile_cols.reshape(-1)
-    float_cols = jnp.zeros((8, LANES), jnp.float32).at[0, :terms].set(own_cols.astype(jnp.float32))
-
-    def adjoint(payloads):
+    float_cols = jnp.zeros((16, LANES), jnp.float32)
+    float_cols = float_cols.at[0, :terms].set((own_cols // 16).astype(jnp.float32))
+    float_cols = float_cols.at[8, :terms].set((own_cols % 16).astype(jnp.float32))
+    upper_shape = jax.ShapeDtypeStruct((row_tiles + 2, 16, LANES), jnp.bfloat16)
+    lower_shape = jax.ShapeDtypeStruct((row_tiles, 16, LANES), jnp.bfloat16)
+
+    def adjoint(tiles, payloads, load):
+        held = jax.ShapeDtypeStruct(tile_values.shape, tile_values.dtype)
         return pl.pallas_call(
-            adjoint_kernel,
-            out_shape=f32(rows, terms + 2, 8, LANES),
-            in_specs=[VMEM] * 3,
-            out_specs=VMEM,
+            functools.partial(adjoint_kernel, load),
+            out_shape=[upper_shape, lower_shape] + [held] * load,
+            in_specs=[VMEM, HBM if load else VMEM, VMEM],
+            out_specs=[VMEM] * (2 + load),
+            scratch_shapes=[pltpu.SemaphoreType.DMA((shares,))] * load,
             compiler_params=PARAMS,
             name="adjoint",
-        )(float_cols, tile_values, payloads)
-
-    def voxel(term_array, previous):
+        )(float_cols, tiles, payloads)
+
+    def voxel(tiles, term_list, previous):
         first = previous is None
         extra = [] if first else list(previous)
         return pl.pallas_call(
-            functools.partial(voxel_kernel, first),
-            out_shape=[f32(shares, per_share + 1, 8, LANES), f32(8, LANES), f32(col_tiles, 8, LANES)],
-            in_specs=[SMEM] + [VMEM] * (2 + len(extra)),
-            out_specs=[VMEM] * 3,
-            scratch_shapes=[pltpu.SMEM((rows, 8, LANES), jnp.float32), pltpu.SemaphoreType.DMA],
+            functools.partial(voxel_kernel, first, rows),
+            out_shape=[
+                f32(shares, per_share + 1, 8, LANES),
+                f32(8, LANES),
+                f32(col_tiles, 8, LANES),
+                f32(share, 8, LANES),
+                jax.ShapeDtypeStruct((rows, 8, LANES), jnp.int32),
+            ],
+            in_specs=[SMEM, SMEM] + [VMEM] * (1 + rows + len(extra)),
+            out_specs=[VMEM] * 5,
+            scratch_shapes=[
+                pltpu.VMEM((rows, row_tiles, 16, LANES), jnp.bfloat16),
+                pltpu.VMEM((rows, 8, LANES), jnp.int32),
+                pltpu.SMEM((rows, 8, LANES), jnp.int32),
+                pltpu.SemaphoreType.DMA,
+            ],
             compiler_params=PARAMS,
             name="voxel",
-        )(own_cols, tile_values, term_array, *extra)
+        )(pos, own_cols, tiles, *term_list, *extra)
+
+    def lower(cols, term_list):
+        return pl.pallas_call(
+            lower_kernel,
+            out_shape=f32(share + 1, 8, LANES),
+            in_specs=[SMEM, SMEM] + [VMEM] * rows,
+            out_specs=VMEM,
+            compiler_params=PARAMS,
+            name="lower",
+        )(pos, cols, *term_list)
 
     def ray(parts, left_raw, beta):
         return pl.pallas_call(
             ray_kernel,
-            out_shape=[f32(per_share, 8, LANES), f32(8, LANES), payload, f32(shares, 8, LANES)],
+            out_shape=[f32(per_share, 8, LANES), f32(8, LANES), payload, f32(rows * shares, 8, LANES)],
             in_specs=[VMEM] * 3,
             out_specs=[VMEM] * 4,
             compiler_params=PARAMS,
@@ -281,31 +373,30 @@
         compiler_params=PARAMS,
         name="prepare",
     )(observed)
-    betas, alphas, raws = [], [], []
+    upper_terms, lower_terms, tiles = adjoint(pltpu.with_memory_space_constraint(tile_values, pltpu.HBM), swap(message, "col"), True)
+    betas, alphas, raws, lowers = [], [], [], []
     previous = None
     for iteration in range(ITERS + 1):
-        parts, beta, right_raw = voxel(swap(adjoint(swap(message, "col")), "row"), previous)
+        if iteration > 0:
+            upper_terms, lower_terms = adjoint(tiles, swap(message, "col"), False)
+        parts, beta, right_raw, right_share, cols = voxel(tiles, exchange(upper_terms, "row"), previous)
         if iteration == ITERS:
             break
+        lowers.append(lower(cols, exchange(lower_terms, "row")))
         left_raw, alpha, message, squares = ray(swap(parts, "col"), left_raw, beta)
         betas.append(beta)
         alphas.append(alpha)
-        raws.append(right_raw)
+        raws.append(right_share)
         previous = (right_raw, alpha)
-    shared = swap(squares, "col")
-    shared = tree_sum([shared[c] for c in range(shares)])
-    last = swap(jnp.broadcast_to(shared[None], (rows, 8, LANES)), "row")
-    share = col_tiles // rows
     result, ratio = pl.pallas_call(
         functools.partial(final_kernel, ITERS),
-        out_shape=[f32(4, share * tile_size), f32(8, LANES)],
-        in_specs=[SMEM] + [VMEM] * (1 + 2 * ITERS) + [ANY] * ITERS,
-        out_specs=[VMEM, VMEM],
-        scratch_shapes=[pltpu.VMEM((ITERS, share, 8, LANES), jnp.float32), pltpu.SemaphoreType.DMA((ITERS,))],
+        out_shape=[f32(4, share * tile_size), f32(4)],
+        in_specs=[VMEM] * (1 + 4 * ITERS),
+        out_specs=[VMEM, SMEM],
         compiler_params=PARAMS,
         name="final",
-    )(pos, last, *betas, *alphas, *raws)
-    return result, ratio[:4, 0]
+    )(swap(squares, ("row", "col")), *betas, *alphas, *raws, *lowers)
+    return result, ratio
 
 
 def solution(mesh):

time: 124 us -> 111 us (0.90)
  blocking collectives: 54 us -> 18.7 us
  starting transfers between devices: 13.4 us -> 27.6 us
  Pallas kernels: 18.2 us -> 25.3 us
  waiting for transfers between devices: 23.8 us -> 29.6 us
  local copies, waits for them, and re-layouts: 12 us -> 8.53 us
    all_to_all x5 -> x2, blocking collectives: 54 us -> 18.7 us  [swap(): return lax.all_to_all(values, axis, 0, 0)]
    ppermute x0 -> x12, waiting for transfers between devices: none -> 18.2 us  [exchange(): got.append(lax.ppermute(value, axis, [(i, i ^ d) for i in range(size)]))]
    ppermute x0 -> x12, starting transfers between devices: none -> 14.8 us  [exchange(): got.append(lax.ppermute(value, axis, [(i, i ^ d) for i in range(size)]))]
    all_to_all x3, waiting for transfers between devices: 23.8 us -> 11.4 us  [swap(): return lax.all_to_all(values, axis, 0, 0)]
    pallas_call x4 -> x6, Pallas kernels: 14.7 us -> 21.5 us  [the longest x2 12.2 us: voxel(): pl.pallas_call(functools.partial(voxel_kernel, first, rows), out_shape=[f...]
    unnamed x15 -> x9, local copies, waits for them, and re-layouts: 10.5 us -> 8.13 us
  transfers between devices with their start and end apart: 3 -> 15, of which waited for: 3 -> 8; matrix products, arithmetic and copies ran while one was open for 1% -> 1% of each run, Pallas kernels for 0% -> 5%
where the time goes in v3:
time: 111 us; the launch traced here: 110 us
  waiting for transfers between devices  29.6 us (27%)
  starting transfers between devices  27.6 us (25%)
  Pallas kernels  25.3 us (23%)
  blocking collectives  18.7 us (17%)
  local copies, waits for them, and re-layouts  8.53 us (8%)
    all_to_all x2, blocking collectives, swap(): return lax.all_to_all(values, axis, 0, 0)  18.7 us
    ppermute x12, waiting for transfers between devices, exchange(): got.append(lax.ppermute(value, axis, [(i, i ^ d) for i in range(size)]))  18.2 us
    ppermute x12, starting transfers between devices, exchange(): got.append(lax.ppermute(value, axis, [(i, i ^ d) for i in range(size)]))  14.8 us
    all_to_all x3, starting transfers between devices, swap(): return lax.all_to_all(values, axis, 0, 0)  12.8 us
    pallas_call x2, Pallas kernels, voxel(): pl.pallas_call(functools.partial(voxel_kernel, first, rows), out_shape=[f...  12.2 us
    all_to_all x3, waiting for transfers between devices, swap(): return lax.all_to_all(values, axis, 0, 0)  11.4 us
    unnamed x9, local copies, waits for them, and re-layouts  8.13 us
    pallas_call x2, Pallas kernels, adjoint(): pl.pallas_call(functools.partial(adjoint_kernel, load), out_shape=[upper_...  4.91 us
  transfers between devices with their start and end apart: 15, of which 8 were waited for; matrix products, arithmetic and copies ran while one was open for 1% of the time, Pallas kernels for 5%

profile of v3, /device:TPU:0, one launch (start us, length us, event | category | flops | bytes accessed | tf_op | source)
XLA Modules:
  0.0 110.5 jit_solution(17333429579791270567)
XLA Ops:
  0.6 0.0 copy-start.3
  0.6 0.7 copy-done.3
  1.3 0.7 prepare.1
  2.0 6.3 %all-to-all-start = ((bf16[8,16,384]{2,1,0:T(8,128)(2,1)}), bf16[8,16,384]{2,1,0:T(8,128)(2,1)S(1)}, u32[]{:S(2)}, u32[]{:S(2)}) async-start(bf16[8,16,384]{2,1,0:T(8,128)(2,1)} %get-tuple-element.47), calls=%async_computation | async-start | bytes 196608 | tf_op jit(solution)/shard_map/all_to_all | solution.py:293
  8.3 0.8 copy.7
  9.1 0.1 reshape.135
  9.2 0.2 scatter.9.cols_ref
  9.4 5.2 %all-to-all-done.payload_ref = bf16[8,16,384]{2,1,0:T(8,128)(2,1)S(1)} async-done(((bf16[8,16,384]{2,1,0:T(8,128)(2,1)}), bf16[8,16,384]{2,1,0:T(8,128)(2,1)S(1)}, u32[]{:S(2)}, u32[]{:S(2)}) %all-to-all-start) | async-done | bytes 98336 | tf_op jit(solution)/shard_map/all_to_all | solution.py:293
  14.7 3.7 %adjoint.2 = (bf16[34,16,128]{2,1,0:T(8,128)(2,1)S(1)}, bf16[32,16,128]{2,1,0:T(8,128)(2,1)S(1)}, bf16[32,2,256,256]{3,2,1,0:T(8,128)(2,1)S(1)}) custom-call(f32[16,128]{1,0:T(8,128)S(1)} %scatter.9.cols_ref, bf16[32,2,256,256]{3,2,1,0:T(8,128)(2,1)} %tiles_ref.1, bf16[8,16,384]{2,1,0:T(8,128)(2,1)S(1)} %all-to-all-done.payload_ref), custom_call_target="tpu_custom_call" | custom-call | tf_op jit(solution)/shard_map/adjoint/pallas_call | solution.py:314
  18.4 0.0 copy-start
  18.4 3.3 %copy-done = bf16[32,2,256,256]{3,2,1,0:T(8,128)(2,1)} copy-done((bf16[32,2,256,256]{3,2,1,0:T(8,128)(2,1)}, bf16[32,2,256,256]{3,2,1,0:T(8,128)(2,1)S(1)}, u32[]{:S(2)}) %copy-start) | copy-done | bytes 8388632
  21.7 1.5 %collective-permute-start = (bf16[34,16,128]{2,1,0:T(8,128)(2,1)S(1)}, bf16[34,16,128]{2,1,0:T(8,128)(2,1)S(1)}, u32[]{:S(2)}, u32[]{:S(2)}) collective-permute-start(bf16[34,16,128]{2,1,0:T(8,128)(2,1)S(1)} %get-tuple-element.49.refs_0_), channel_id=1, source_target_pairs={{0,8},{8,0},{16,24},{24,16},{1,9},{9,1},{17,25},{25,17},{2,10},{10... | collective-permute-start | bytes 417800 | tf_op jit(solution)/shard_map/ppermute | solution.py:288
  23.2 1.5 %collective-permute-start.1 = (bf16[34,16,128]{2,1,0:T(8,128)(2,1)S(1)}, bf16[34,16,128]{2,1,0:T(8,128)(2,1)S(1)}, u32[]{:S(2)}, u32[]{:S(2)}) collective-permute-start(bf16[34,16,128]{2,1,0:T(8,128)(2,1)S(1)} %get-tuple-element.49.refs_0_), channel_id=1, source_target_pairs={{0,16},{8,24},{16,0},{24,8},{1,17},{9,25},{17,1},{25,9},{2,18},{10... | collective-permute-start | bytes 417800 | tf_op jit(solution)/shard_map/ppermute | solution.py:288
  24.7 0.5 collective-permute-start.2
  25.2 0.1 reshape.134.own_cols_ref
  25.3 2.2 %collective-permute-done.refs_1_ = bf16[34,16,128]{2,1,0:T(8,128)(2,1)S(1)} collective-permute-done((bf16[34,16,128]{2,1,0:T(8,128)(2,1)S(1)}, bf16[34,16,128]{2,1,0:T(8,128)(2,1)S(1)}, u32[]{:S(2)}, u32[]{:S(2)}) %collective-permute-start) | collective-permute-done | bytes 139296 | tf_op jit(solution)/shard_map/ppermute | solution.py:288
  27.5 3.7 %collective-permute-done.1.refs_2_ = bf16[34,16,128]{2,1,0:T(8,128)(2,1)S(1)} collective-permute-done((bf16[34,16,128]{2,1,0:T(8,128)(2,1)S(1)}, bf16[34,16,128]{2,1,0:T(8,128)(2,1)S(1)}, u32[]{:S(2)}, u32[]{:S(2)}) %collective-permute-start.1) | collective-permute-done | bytes 139296 | tf_op jit(solution)/shard_map/ppermute | solution.py:288
  31.2 0.0 collective-permute-done.2.refs_3_
  31.2 0.0 copy-start.1
  31.2 3.4 %copy-done.1 = bf16[32,2,256,256]{3,2,1,0:T(8,128)(2,1)S(1)} copy-done((bf16[32,2,256,256]{3,2,1,0:T(8,128)(2,1)S(1)}, bf16[32,2,256,256]{3,2,1,0:T(8,128)(2,1)}, u32[]{:S(2)}) %copy-start.1) | copy-done | bytes 8388632
  34.6 0.0 copy-start.2
  34.6 5.5 %voxel.2 = (f32[8,5,8,128]{3,2,1,0:T(8,128)S(1)}, f32[8,128]{1,0:T(8,128)S(1)}, f32[512,8,128]{2,1,0:T(8,128)S(1)}, f32[128,8,128]{2,1,0:T(8,128)S(1)}, s32[4,8,128]{2,1,0:T(8,128)S(1)}) custom-call(s32[1]{0:T(128)} %bitcast.pos_ref, s32[64]{0:T(128)S(1)} %reshape.134.own_cols_ref, bf16[32,2,256,256]{3,2,1,0:T(8,128)(2,1)S(1)} %copy-done.1, ...), custom_call_target="tpu_custom_call" | custom-call | tf_op jit(solution)/shard_map/voxel/pallas_call | solution.py:327
  40.1 9.6 %all_to_all.26.part_ref = f32[8,5,8,128]{3,2,1,0:T(8,128)S(1)} all-to-all(f32[8,5,8,128]{3,2,1,0:T(8,128)S(1)} %get-tuple-element.50), channel_id=1, replica_groups=mesh['row'=4,'col'=8] {'col'}, dimensions={0} | all-to-all | bytes 327680 | tf_op jit(solution)/shard_map/all_to_all | solution.py:293
  49.7 0.8 ray.2
  50.5 9.1 %all_to_all.27.payload_ref = bf16[8,16,384]{2,1,0:T(8,128)(2,1)S(1)} all-to-all(bf16[8,16,384]{2,1,0:T(8,128)(2,1)S(1)} %get-tuple-element.53), channel_id=1, replica_groups=mesh['row'=4,'col'=8] {'col'}, dimensions={0} | all-to-all | bytes 196608 | tf_op jit(solution)/shard_map/all_to_all | solution.py:293
  59.6 0.0 copy-done.2
  59.6 1.2 %adjoint.3 = (bf16[34,16,128]{2,1,0:T(8,128)(2,1)S(1)}, bf16[32,16,128]{2,1,0:T(8,128)(2,1)S(1)}) custom-call(f32[16,128]{1,0:T(8,128)S(1)} %scatter.9.cols_ref, bf16[32,2,256,256]{3,2,1,0:T(8,128)(2,1)S(1)} %copy-done.2, bf16[8,16,384]{2,1,0:T(8,128)(2,1)S(1)} %all_to_all.27.payload_ref), custom_call_target="tpu_custom_call" | custom-call | tf_op jit(solution)/shard_map/adjoint/pallas_call | solution.py:314
  60.7 1.2 %collective-permute-start.3 = (bf16[34,16,128]{2,1,0:T(8,128)(2,1)S(1)}, bf16[34,16,128]{2,1,0:T(8,128)(2,1)S(1)}, u32[]{:S(2)}, u32[]{:S(2)}) collective-permute-start(bf16[34,16,128]{2,1,0:T(8,128)(2,1)S(1)} %get-tuple-element.54.refs_0_), channel_id=1, source_target_pairs={{0,8},{8,0},{16,24},{24,16},{1,9},{9,1},{17,25},{25,17},{2,10},{10... | collective-permute-start | bytes 417800 | tf_op jit(solution)/shard_map/ppermute | solution.py:288
  61.9 0.8 collective-permute-start.4
  62.7 1.6 %collective-permute-start.5 = (bf16[34,16,128]{2,1,0:T(8,128)(2,1)S(1)}, bf16[34,16,128]{2,1,0:T(8,128)(2,1)S(1)}, u32[]{:S(2)}, u32[]{:S(2)}) collective-permute-start(bf16[34,16,128]{2,1,0:T(8,128)(2,1)S(1)} %get-tuple-element.54.refs_0_), channel_id=1, source_target_pairs={{0,24},{8,16},{16,8},{24,0},{1,25},{9,17},{17,9},{25,1},{2,26},{10... | collective-permute-start | bytes 417800 | tf_op jit(solution)/shard_map/ppermute | solution.py:288
  64.3 2.7 %collective-permute-done.3.refs_1_ = bf16[34,16,128]{2,1,0:T(8,128)(2,1)S(1)} collective-permute-done((bf16[34,16,128]{2,1,0:T(8,128)(2,1)S(1)}, bf16[34,16,128]{2,1,0:T(8,128)(2,1)S(1)}, u32[]{:S(2)}, u32[]{:S(2)}) %collective-permute-start.3) | collective-permute-done | bytes 139296 | tf_op jit(solution)/shard_map/ppermute | solution.py:288
  67.0 2.9 %collective-permute-done.4.refs_2_ = bf16[34,16,128]{2,1,0:T(8,128)(2,1)S(1)} collective-permute-done((bf16[34,16,128]{2,1,0:T(8,128)(2,1)S(1)}, bf16[34,16,128]{2,1,0:T(8,128)(2,1)S(1)}, u32[]{:S(2)}, u32[]{:S(2)}) %collective-permute-start.4) | collective-permute-done | bytes 139296 | tf_op jit(solution)/shard_map/ppermute | solution.py:288
  70.0 0.0 collective-permute-done.5.refs_3_
  70.0 6.7 %voxel.3 = (f32[8,5,8,128]{3,2,1,0:T(8,128)}, f32[8,128]{1,0:T(8,128)S(1)}, f32[512,8,128]{2,1,0:T(8,128)}, f32[128,8,128]{2,1,0:T(8,128)S(1)}, s32[4,8,128]{2,1,0:T(8,128)S(1)}) custom-call(s32[1]{0:T(128)} %bitcast.pos_ref, s32[64]{0:T(128)S(1)} %reshape.134.own_cols_ref, bf16[32,2,256,256]{3,2,1,0:T(8,128)(2,1)S(1)} %copy-done.2, ...), custom_call_target="tpu_custom_call" | custom-call | tf_op jit(solution)/shard_map/voxel/pallas_call | solution.py:327
  76.7 3.4 %all-to-all-start.3 = ((f32[8,5,8,128]{3,2,1,0:T(8,128)}), f32[8,5,8,128]{3,2,1,0:T(8,128)S(1)}, u32[]{:S(2)}, u32[]{:S(2)}) async-start(f32[8,5,8,128]{3,2,1,0:T(8,128)} %get-tuple-element.57), calls=%async_computation.3 | async-start | bytes 327680 | tf_op jit(solution)/shard_map/all_to_all | solution.py:293
  80.1 1.0 collective-permute-start.6
  81.1 6.2 %all-to-all-done.3.part_ref = f32[8,5,8,128]{3,2,1,0:T(8,128)S(1)} async-done(((f32[8,5,8,128]{3,2,1,0:T(8,128)}), f32[8,5,8,128]{3,2,1,0:T(8,128)S(1)}, u32[]{:S(2)}, u32[]{:S(2)}) %all-to-all-start.3) | async-done | bytes 163872 | tf_op jit(solution)/shard_map/all_to_all | solution.py:293
  87.3 0.8 ray.3
  88.1 3.1 %all-to-all-start.4 = ((f32[32,8,128]{2,1,0:T(8,128)}), f32[32,8,128]{2,1,0:T(8,128)S(1)}, u32[]{:S(2)}, u32[]{:S(2)}) async-start(f32[32,8,128]{2,1,0:T(8,128)} %get-tuple-element.60), calls=%async_computation.4 | async-start | bytes 262144 | tf_op jit(solution)/shard_map/all_to_all | solution.py:293
  91.1 1.8 %collective-permute-start.7 = (bf16[32,16,128]{2,1,0:T(8,128)(2,1)S(1)}, bf16[32,16,128]{2,1,0:T(8,128)(2,1)S(1)}, u32[]{:S(2)}, u32[]{:S(2)}) collective-permute-start(bf16[32,16,128]{2,1,0:T(8,128)(2,1)S(1)} %get-tuple-element.65.refs_0_), channel_id=1, source_target_pairs={{0,16},{8,24},{16,0},{24,8},{1,17},{9,25},{17,1},{25,9},{2,18},{10... | collective-permute-start | bytes 393224 | tf_op jit(solution)/shard_map/ppermute | solution.py:288
  93.0 1.5 %collective-permute-start.8 = (bf16[32,16,128]{2,1,0:T(8,128)(2,1)S(1)}, bf16[32,16,128]{2,1,0:T(8,128)(2,1)S(1)}, u32[]{:S(2)}, u32[]{:S(2)}) collective-permute-start(bf16[32,16,128]{2,1,0:T(8,128)(2,1)S(1)} %get-tuple-element.65.refs_0_), channel_id=1, source_target_pairs={{0,24},{8,16},{16,8},{24,0},{1,25},{9,17},{17,9},{25,1},{2,26},{10... | collective-permute-start | bytes 393224 | tf_op jit(solution)/shard_map/ppermute | solution.py:288
  94.4 1.5 %collective-permute-start.10 = (bf16[32,16,128]{2,1,0:T(8,128)(2,1)S(1)}, bf16[32,16,128]{2,1,0:T(8,128)(2,1)S(1)}, u32[]{:S(2)}, u32[]{:S(2)}) collective-permute-start(bf16[32,16,128]{2,1,0:T(8,128)(2,1)S(1)} %get-tuple-element.67.refs_0_), channel_id=1, source_target_pairs={{0,16},{8,24},{16,0},{24,8},{1,17},{9,25},{17,1},{25,9},{2,18},{10... | collective-permute-start | bytes 393224 | tf_op jit(solution)/shard_map/ppermute | solution.py:288
  95.9 0.3 collective-permute-start.11
  96.2 0.0 collective-permute-done.6.refs_1_
  96.2 1.8 %collective-permute-start.9 = (bf16[32,16,128]{2,1,0:T(8,128)(2,1)S(1)}, bf16[32,16,128]{2,1,0:T(8,128)(2,1)S(1)}, u32[]{:S(2)}, u32[]{:S(2)}) collective-permute-start(bf16[32,16,128]{2,1,0:T(8,128)(2,1)S(1)} %get-tuple-element.67.refs_0_), channel_id=1, source_target_pairs={{0,8},{8,0},{16,24},{24,16},{1,9},{9,1},{17,25},{25,17},{2,10},{10... | collective-permute-start | bytes 393224 | tf_op jit(solution)/shard_map/ppermute | solution.py:288
  97.9 6.4 %collective-permute-done.7.refs_2_ = bf16[32,16,128]{2,1,0:T(8,128)(2,1)S(1)} collective-permute-done((bf16[32,16,128]{2,1,0:T(8,128)(2,1)S(1)}, bf16[32,16,128]{2,1,0:T(8,128)(2,1)S(1)}, u32[]{:S(2)}, u32[]{:S(2)}) %collective-permute-start.7) | collective-permute-done | bytes 131104 | tf_op jit(solution)/shard_map/ppermute | solution.py:288
  104.4 0.0 collective-permute-done.8.refs_3_
  104.4 2.2 %lower.2.refs_6_ = f32[129,8,128]{2,1,0:T(8,128)S(1)} custom-call(s32[1]{0:T(128)} %bitcast.pos_ref, s32[4,8,128]{2,1,0:T(8,128)S(1)} %get-tuple-element.64.cols_ref, bf16[32,16,128]{2,1,0:T(8,128)(2,1)S(1)} %get-tuple-element.65.refs_0_, bf16[32,16,128]{2,1,0:T(8,128)(2,1)S(1)} %collective-permute-done.6.refs_1_, ...), custom_call_target="tpu_custom_call" | custom-call | tf_op jit(solution)/shard_map/lower/pallas_call | solution.py:349
  106.6 0.1 collective-permute-done.10.refs_2_
  106.7 0.0 collective-permute-done.11.refs_3_
  106.7 0.0 collective-permute-done.9.refs_1_
  106.7 2.2 %lower.3.refs_7_ = f32[129,8,128]{2,1,0:T(8,128)S(1)} custom-call(s32[1]{0:T(128)} %bitcast.pos_ref, s32[4,8,128]{2,1,0:T(8,128)S(1)} %get-tuple-element.66.cols_ref, bf16[32,16,128]{2,1,0:T(8,128)(2,1)S(1)} %get-tuple-element.67.refs_0_, bf16[32,16,128]{2,1,0:T(8,128)(2,1)S(1)} %collective-permute-done.9.refs_1_, ...), custom_call_target="tpu_custom_call" | custom-call | tf_op jit(solution)/shard_map/lower/pallas_call | solution.py:349
  108.9 0.0 all-to-all-done.4.last_ref
  108.9 1.5 %final.1 = (f32[4,32768]{1,0:T(4,128)}, f32[4]{0:T(128)}) custom-call(f32[32,8,128]{2,1,0:T(8,128)S(1)} %all-to-all-done.4.last_ref, f32[8,128]{1,0:T(8,128)S(1)} %get-tuple-element.52.beta_ref.refs_0_, f32[8,128]{1,0:T(8,128)S(1)} %get-tuple-element.59.beta_ref.refs_1_, f32[8,128]{1,0:T(8,128)S(1)} %get-tuple-element.56.refs_5_.refs_2_, ...), custom_call_target="tpu_custom_call" | custom-call | tf_op jit(solution)/shard_map/final/pallas_call | solution.py:391
  (2 shorter events, 0.0 us)
Async XLA Ops:
  0.6 0.7 copy-start.3
  2.0 12.7 %all-to-all-start = ((bf16[8,16,384]{2,1,0:T(8,128)(2,1)}), bf16[8,16,384]{2,1,0:T(8,128)(2,1)S(1)}, u32[]{:S(2)}, u32[]{:S(2)}) async-start(bf16[8,16,384]{2,1,0:T(8,128)(2,1)} %get-tuple-element.47), calls=%async_computation | async-start | bytes 196608 | tf_op jit(solution)/shard_map/all_to_all | solution.py:293
  18.4 3.3 %copy-start = (bf16[32,2,256,256]{3,2,1,0:T(8,128)(2,1)}, bf16[32,2,256,256]{3,2,1,0:T(8,128)(2,1)S(1)}, u32[]{:S(2)}) copy-start(bf16[32,2,256,256]{3,2,1,0:T(8,128)(2,1)S(1)} %get-tuple-element.48.tiles_ref) | copy-start | bytes 25165828
  21.7 5.8 %collective-permute-start = (bf16[34,16,128]{2,1,0:T(8,128)(2,1)S(1)}, bf16[34,16,128]{2,1,0:T(8,128)(2,1)S(1)}, u32[]{:S(2)}, u32[]{:S(2)}) collective-permute-start(bf16[34,16,128]{2,1,0:T(8,128)(2,1)S(1)} %get-tuple-element.49.refs_0_), channel_id=1, source_target_pairs={{0,8},{8,0},{16,24},{24,16},{1,9},{9,1},{17,25},{25,17},{2,10},{10... | collective-permute-start | bytes 417800 | tf_op jit(solution)/shard_map/ppermute | solution.py:288
  23.2 8.0 %collective-permute-start.1 = (bf16[34,16,128]{2,1,0:T(8,128)(2,1)S(1)}, bf16[34,16,128]{2,1,0:T(8,128)(2,1)S(1)}, u32[]{:S(2)}, u32[]{:S(2)}) collective-permute-start(bf16[34,16,128]{2,1,0:T(8,128)(2,1)S(1)} %get-tuple-element.49.refs_0_), channel_id=1, source_target_pairs={{0,16},{8,24},{16,0},{24,8},{1,17},{9,25},{17,1},{25,9},{2,18},{10... | collective-permute-start | bytes 417800 | tf_op jit(solution)/shard_map/ppermute | solution.py:288
  24.7 6.5 %collective-permute-start.2 = (bf16[34,16,128]{2,1,0:T(8,128)(2,1)S(1)}, bf16[34,16,128]{2,1,0:T(8,128)(2,1)S(1)}, u32[]{:S(2)}, u32[]{:S(2)}) collective-permute-start(bf16[34,16,128]{2,1,0:T(8,128)(2,1)S(1)} %get-tuple-element.49.refs_0_), channel_id=1, source_target_pairs={{0,24},{8,16},{16,8},{24,0},{1,25},{9,17},{17,9},{25,1},{2,26},{10... | collective-permute-start | bytes 417800 | tf_op jit(solution)/shard_map/ppermute | solution.py:288
  31.2 3.4 %copy-start.1 = (bf16[32,2,256,256]{3,2,1,0:T(8,128)(2,1)S(1)}, bf16[32,2,256,256]{3,2,1,0:T(8,128)(2,1)}, u32[]{:S(2)}) copy-start(bf16[32,2,256,256]{3,2,1,0:T(8,128)(2,1)} %copy-done) | copy-start | bytes 25165828
  34.6 24.9 %copy-start.2 = (bf16[32,2,256,256]{3,2,1,0:T(8,128)(2,1)S(1)}, bf16[32,2,256,256]{3,2,1,0:T(8,128)(2,1)}, u32[]{:S(2)}) copy-start(bf16[32,2,256,256]{3,2,1,0:T(8,128)(2,1)} %copy-done) | copy-start | bytes 25165828
  60.7 6.3 %collective-permute-start.3 = (bf16[34,16,128]{2,1,0:T(8,128)(2,1)S(1)}, bf16[34,16,128]{2,1,0:T(8,128)(2,1)S(1)}, u32[]{:S(2)}, u32[]{:S(2)}) collective-permute-start(bf16[34,16,128]{2,1,0:T(8,128)(2,1)S(1)} %get-tuple-element.54.refs_0_), channel_id=1, source_target_pairs={{0,8},{8,0},{16,24},{24,16},{1,9},{9,1},{17,25},{25,17},{2,10},{10... | collective-permute-start | bytes 417800 | tf_op jit(solution)/shard_map/ppermute | solution.py:288
  61.9 8.0 %collective-permute-start.4 = (bf16[34,16,128]{2,1,0:T(8,128)(2,1)S(1)}, bf16[34,16,128]{2,1,0:T(8,128)(2,1)S(1)}, u32[]{:S(2)}, u32[]{:S(2)}) collective-permute-start(bf16[34,16,128]{2,1,0:T(8,128)(2,1)S(1)} %get-tuple-element.54.refs_0_), channel_id=1, source_target_pairs={{0,16},{8,24},{16,0},{24,8},{1,17},{9,25},{17,1},{25,9},{2,18},{10... | collective-permute-start | bytes 417800 | tf_op jit(solution)/shard_map/ppermute | solution.py:288
  62.7 7.2 %collective-permute-start.5 = (bf16[34,16,128]{2,1,0:T(8,128)(2,1)S(1)}, bf16[34,16,128]{2,1,0:T(8,128)(2,1)S(1)}, u32[]{:S(2)}, u32[]{:S(2)}) collective-permute-start(bf16[34,16,128]{2,1,0:T(8,128)(2,1)S(1)} %get-tuple-element.54.refs_0_), channel_id=1, source_target_pairs={{0,24},{8,16},{16,8},{24,0},{1,25},{9,17},{17,9},{25,1},{2,26},{10... | collective-permute-start | bytes 417800 | tf_op jit(solution)/shard_map/ppermute | solution.py:288
  76.7 10.6 %all-to-all-start.3 = ((f32[8,5,8,128]{3,2,1,0:T(8,128)}), f32[8,5,8,128]{3,2,1,0:T(8,128)S(1)}, u32[]{:S(2)}, u32[]{:S(2)}) async-start(f32[8,5,8,128]{3,2,1,0:T(8,128)} %get-tuple-element.57), calls=%async_computation.3 | async-start | bytes 327680 | tf_op jit(solution)/shard_map/all_to_all | solution.py:293
  80.1 16.1 %collective-permute-start.6 = (bf16[32,16,128]{2,1,0:T(8,128)(2,1)S(1)}, bf16[32,16,128]{2,1,0:T(8,128)(2,1)S(1)}, u32[]{:S(2)}, u32[]{:S(2)}) collective-permute-start(bf16[32,16,128]{2,1,0:T(8,128)(2,1)S(1)} %get-tuple-element.65.refs_0_), channel_id=1, source_target_pairs={{0,8},{8,0},{16,24},{24,16},{1,9},{9,1},{17,25},{25,17},{2,10},{10... | collective-permute-start | bytes 393224 | tf_op jit(solution)/shard_map/ppermute | solution.py:288
  88.1 20.9 %all-to-all-start.4 = ((f32[32,8,128]{2,1,0:T(8,128)}), f32[32,8,128]{2,1,0:T(8,128)S(1)}, u32[]{:S(2)}, u32[]{:S(2)}) async-start(f32[32,8,128]{2,1,0:T(8,128)} %get-tuple-element.60), calls=%async_computation.4 | async-start | bytes 262144 | tf_op jit(solution)/shard_map/all_to_all | solution.py:293
  91.1 13.2 %collective-permute-start.7 = (bf16[32,16,128]{2,1,0:T(8,128)(2,1)S(1)}, bf16[32,16,128]{2,1,0:T(8,128)(2,1)S(1)}, u32[]{:S(2)}, u32[]{:S(2)}) collective-permute-start(bf16[32,16,128]{2,1,0:T(8,128)(2,1)S(1)} %get-tuple-element.65.refs_0_), channel_id=1, source_target_pairs={{0,16},{8,24},{16,0},{24,8},{1,17},{9,25},{17,1},{25,9},{2,18},{10... | collective-permute-start | bytes 393224 | tf_op jit(solution)/shard_map/ppermute | solution.py:288
  93.0 11.4 %collective-permute-start.8 = (bf16[32,16,128]{2,1,0:T(8,128)(2,1)S(1)}, bf16[32,16,128]{2,1,0:T(8,128)(2,1)S(1)}, u32[]{:S(2)}, u32[]{:S(2)}) collective-permute-start(bf16[32,16,128]{2,1,0:T(8,128)(2,1)S(1)} %get-tuple-element.65.refs_0_), channel_id=1, source_target_pairs={{0,24},{8,16},{16,8},{24,0},{1,25},{9,17},{17,9},{25,1},{2,26},{10... | collective-permute-start | bytes 393224 | tf_op jit(solution)/shard_map/ppermute | solution.py:288
  94.4 12.3 %collective-permute-start.10 = (bf16[32,16,128]{2,1,0:T(8,128)(2,1)S(1)}, bf16[32,16,128]{2,1,0:T(8,128)(2,1)S(1)}, u32[]{:S(2)}, u32[]{:S(2)}) collective-permute-start(bf16[32,16,128]{2,1,0:T(8,128)(2,1)S(1)} %get-tuple-element.67.refs_0_), channel_id=1, source_target_pairs={{0,16},{8,24},{16,0},{24,8},{1,17},{9,25},{17,1},{25,9},{2,18},{10... | collective-permute-start | bytes 393224 | tf_op jit(solution)/shard_map/ppermute | solution.py:288
  95.9 10.8 %collective-permute-start.11 = (bf16[32,16,128]{2,1,0:T(8,128)(2,1)S(1)}, bf16[32,16,128]{2,1,0:T(8,128)(2,1)S(1)}, u32[]{:S(2)}, u32[]{:S(2)}) collective-permute-start(bf16[32,16,128]{2,1,0:T(8,128)(2,1)S(1)} %get-tuple-element.67.refs_0_), channel_id=1, source_target_pairs={{0,24},{8,16},{16,8},{24,0},{1,25},{9,17},{17,9},{25,1},{2,26},{10... | collective-permute-start | bytes 393224 | tf_op jit(solution)/shard_map/ppermute | solution.py:288
  96.2 10.5 %collective-permute-start.9 = (bf16[32,16,128]{2,1,0:T(8,128)(2,1)S(1)}, bf16[32,16,128]{2,1,0:T(8,128)(2,1)S(1)}, u32[]{:S(2)}, u32[]{:S(2)}) collective-permute-start(bf16[32,16,128]{2,1,0:T(8,128)(2,1)S(1)} %get-tuple-element.67.refs_0_), channel_id=1, source_target_pairs={{0,8},{8,0},{16,24},{24,16},{1,9},{9,1},{17,25},{25,17},{2,10},{10... | collective-permute-start | bytes 393224 | tf_op jit(solution)/shard_map/ppermute | solution.py:288

commit v4 on v3

v4 whole, which is shorter than its diff:
```python
import functools

import jax
import jax.numpy as jnp
from jax import lax
from jax.experimental import pallas as pl
from jax.experimental.pallas import tpu as pltpu
from jax.sharding import PartitionSpec as P

ITERS = 2
N = 1048576
epsilon_sq = 1e-06
LANES = 128
RHS = 4
VMEM = pl.BlockSpec(memory_space=pltpu.VMEM)
SMEM = pl.BlockSpec(memory_space=pltpu.SMEM)
HBM = pl.BlockSpec(memory_space=pltpu.HBM)
ANY = pl.BlockSpec(memory_space=pl.ANY)
PARAMS = pltpu.CompilerParams(vmem_limit_bytes=32 * 1024 * 1024)


def tree_sum(parts):
    while len(parts) > 1:
        paired = [parts[i] + parts[i + 1] for i in range(0, len(parts) - 1, 2)]
        parts = paired + parts[2 * len(paired) :]
    return parts[0]


def norm_of(acc):
    rows = jnp.broadcast_to(jnp.sum(acc, axis=1, keepdims=True), acc.shape)
    return jnp.sqrt(rows + pltpu.roll(rows, 4, 0) + epsilon_sq)


def low_half(width):
    return lax.broadcasted_iota(jnp.int32, (8, width), 0) < 4


def in_two(acc):
    upper = acc.astype(jnp.bfloat16).astype(jnp.float32)
    return upper, acc - upper


def write_payload(out_ref, blocks, acc):
    rows = out_ref.shape[0]
    blank = [jnp.zeros((8, LANES), jnp.float32)] * (rows // 8)
    for h in range(2):
        half = (blocks[h::2] + blank)[: rows // 8]
        out_ref[:, h * LANES : (h + 1) * LANES] = jnp.concatenate(half, axis=0).astype(jnp.bfloat16)
    pieces = (list(in_two(acc)) + blank)[: rows // 8]
    out_ref[:, 2 * LANES :] = jnp.concatenate(pieces, axis=0).astype(jnp.bfloat16)


def read_squares(ref):
    both = ref[:, 2 * LANES :].astype(jnp.float32)
    return both[:8] + both[8:16]


def prepare_kernel(obs_ref, blocks_ref, payload_ref):
    obs = obs_ref[...]
    blocks = []
    for b in range(blocks_ref.shape[0]):
        at = (b // 2) * 4 * LANES + (b % 2) * LANES
        blocks.append(jnp.concatenate([obs[:, at : at + LANES], obs[:, at + 2 * LANES : at + 3 * LANES]], axis=0))
    for b, block in enumerate(blocks):
        blocks_ref[b] = block
    squares = tree_sum([b * b for b in blocks])
    for c in range(payload_ref.shape[0]):
        write_payload(payload_ref.at[c], blocks, squares)


def match_kernel(pos_ref, *refs):
    keys_list, (equal_ref, weight_ref, pick_ref, held) = refs[:-4], refs[-4:]
    rows = len(keys_list)
    per_row = keys_list[0].shape[1]
    for d, keys in enumerate(keys_list):
        held[jnp.bitwise_xor(pos_ref[0], d)] = jnp.broadcast_to(keys[...], (8, per_row))

    @pl.loop(0, rows)
    def _(s):
        down = jnp.broadcast_to(held[s][:1], (LANES, per_row)).T
        at = pl.ds(pl.multiple_of(s * per_row, per_row), per_row)
        count = jnp.zeros((per_row, LANES), jnp.float32)
        for other in range(rows):
            for h in range(per_row // LANES):
                across = held[other, :1, h * LANES : (h + 1) * LANES]
                same = jnp.where(down == across, 1.0, 0.0)
                count = count + same
                lane = other * per_row + h * LANES
                equal_ref[at, lane : lane + LANES] = same.astype(jnp.bfloat16)
        weight_ref[at, :] = jnp.broadcast_to(1.0 / jnp.sum(count, axis=1, keepdims=True), (per_row, LANES))

    wanted = pick_ref.shape[0]
    step_rows = 128
    start = pos_ref[0] * wanted

    @pl.loop(0, wanted // step_rows)
    def _(step):
        down = lax.broadcasted_iota(jnp.int32, (step_rows, LANES), 0) + (start + step * step_rows)
        down = down.astype(jnp.float32)
        at = pl.ds(pl.multiple_of(step * step_rows, step_rows), step_rows)
        for other in range(rows):
            for h in range(per_row // LANES):
                across = held[other, :1, h * LANES : (h + 1) * LANES]
                lane = other * per_row + h * LANES
                pick_ref[at, lane : lane + LANES] = jnp.where(down == across, 1.0, 0.0).astype(jnp.bfloat16)


def fetch(tiles_ref, held_ref, sems, shares):
    per_share = tiles_ref.shape[0] // shares
    copies = []
    for c in range(shares):
        part = pl.ds(c * per_share, per_share)
        copies.append(pltpu.make_async_copy(tiles_ref.at[part], held_ref.at[part], sems.at[c]))
        copies[-1].start()
    return copies


def adjoint_kernel(load, unread, tiles_ref, payload_ref, *refs):
    refs = refs[unread:]
    row_tiles, per_block = tiles_ref.shape[:2]
    shares = payload_ref.shape[0]
    per_share = row_tiles // shares
    copies = None
    if load:
        upper_ref, lower_ref, tiles_held, sems = refs
        copies = fetch(tiles_ref, tiles_held, sems, shares)
        tiles_ref = tiles_held
    else:
        (upper_ref,) = refs
    squares = tree_sum([read_squares(payload_ref.at[c]) for c in range(shares)])
    pieces = jnp.concatenate(in_two(squares), axis=1)
    terms = row_tiles * per_block * RHS
    upper_ref[terms:] = jnp.concatenate([pieces, jnp.zeros_like(pieces)], axis=0).astype(jnp.bfloat16)
    low = low_half(2 * LANES)
    for c in range(shares):
        if load:
            copies[c].wait()
        rays = payload_ref[c, :, : 2 * LANES]
        for g in range(per_share // 2):
            i = c * per_share + 2 * g
            wide = [
                jnp.dot(rays, tiles_ref[i + e, k], preferred_element_type=jnp.float32)[8 * g : 8 * g + 8]
                for e in range(2)
                for k in range(2)
            ]
            value = jnp.concatenate(
                [
                    jnp.where(low, wide[0], pltpu.roll(wide[1], 4, 0)),
                    jnp.where(low, pltpu.roll(wide[2], 4, 0), wide[3]),
                ],
                axis=0,
            )
            upper = value.astype(jnp.bfloat16)
            upper_ref[8 * i : 8 * i + 16] = upper
            if load:
                lower_ref[8 * i : 8 * i + 16] = (value - upper.astype(jnp.float32)).astype(jnp.bfloat16)


def voxel_kernel(first, rows, pos_ref, tiles_ref, equal_ref, weight_ref, *refs):
    terms, refs = refs[:rows], refs[rows:]
    if not first:
        right_ref, alpha_ref = refs[:2]
        refs = refs[2:]
    out_ref, beta_ref, raw_ref, all_ref = refs[:4]
    row_tiles, per_block = tiles_ref.shape[:2]
    shares = out_ref.shape[0]
    per_share = row_tiles // shares
    copies = None
    if first:
        tiles_held, sems = refs[4:]
        copies = fetch(tiles_ref, tiles_held, sems, shares)
        tiles_ref = tiles_held
    per_row = row_tiles * per_block * RHS
    squares = []
    for d in range(rows):
        slot = jnp.bitwise_xor(pos_ref[0], d)
        all_ref[pl.ds(pl.multiple_of(slot * per_row, per_row), per_row), :] = terms[d][:per_row]
        pieces = terms[d][per_row:].astype(jnp.float32)[:8]
        squares.append(pieces[:, :LANES] + pieces[:, LANES:])
    beta = norm_of(tree_sum(squares))
    beta_ref[...] = beta
    wide_scale = jnp.concatenate([1.0 / beta] * 2, axis=1)
    if not first:
        wide_right = jnp.concatenate([beta / alpha_ref[...]] * 2, axis=1)
    acc = jnp.zeros((8, LANES), jnp.float32)
    for s in range(rows):
        summed = jnp.dot(
            equal_ref[s * per_row : (s + 1) * per_row, :], all_ref[...], preferred_element_type=jnp.float32
        )
        for m in range(per_row // 8):
            at = s * per_row + 8 * m
            raw = summed[8 * m : 8 * m + 8] * wide_scale
            if not first:
                raw = raw - right_ref[at : at + 8] * wide_right
            raw_ref[at : at + 8] = raw
            square = raw * raw
            acc = acc + (square[:, :LANES] + square[:, LANES:]) * weight_ref[at : at + 8]
    low = low_half(2 * LANES)
    own = pos_ref[0] * per_row
    for c in range(shares):
        if first:
            copies[c].wait()
        for g in range(per_share // 2):
            i = c * per_share + 2 * g
            lhs = raw_ref[pl.ds(pl.multiple_of(own + 8 * i, 16), 16), :].astype(jnp.bfloat16)
            wide = [
                lax.dot_general(
                    lhs, tiles_ref[i + e, k], (((1,), (1,)), ((), ())), preferred_element_type=jnp.float32
                )[8 * e : 8 * e + 8]
                for e in range(2)
                for k in range(2)
            ]
            value = jnp.where(low, wide[0], wide[3]) + pltpu.roll(jnp.where(low, wide[2], wide[1]), 4, 0)
            out_ref[c, 2 * g] = value[:, :LANES]
            out_ref[c, 2 * g + 1] = value[:, LANES:]
        out_ref[c, per_share] = acc


def share_kernel(pos_ref, pick_ref, all_ref, *refs):
    lower_terms, out_ref = refs[:-1], refs[-1]
    if lower_terms:
        lower_terms, out_ref, held = lower_terms[:-1], refs[-2], refs[-1]
        per_row = lower_terms[0].shape[0]
        for d, term in enumerate(lower_terms):
            slot = jnp.bitwise_xor(pos_ref[0], d)
            held[pl.ds(pl.multiple_of(slot * per_row, per_row), per_row), :] = term[...]
    step = 128
    for at in range(0, out_ref.shape[0], step):
        pick = pick_ref[at : at + step, :]
        total = jnp.dot(pick, all_ref[...], preferred_element_type=jnp.float32)
        if lower_terms:
            total = total + jnp.dot(pick, held[...], preferred_element_type=jnp.float32)
        out_ref[at : at + step, :] = total


def ray_kernel(part_ref, left_ref, beta_ref, raw_ref, alpha_ref, payload_ref, acc_ref):
    shares, count = part_ref.shape[0], raw_ref.shape[0]
    alpha = norm_of(tree_sum([part_ref[c, count] for c in range(shares)]))
    alpha_ref[...] = alpha
    alpha_inv = 1.0 / alpha
    left_scale = alpha / beta_ref[...]
    blocks = []
    for b in range(count):
        total = tree_sum([part_ref[c, b] for c in range(shares)])
        blocks.append(total * alpha_inv - left_ref[b] * left_scale)
        raw_ref[b] = blocks[-1]
    acc = tree_sum([b * b for b in blocks])
    for c in range(acc_ref.shape[0]):
        acc_ref[c] = acc
    for c in range(shares):
        write_payload(payload_ref.at[c], blocks, acc)


def final_kernel(iters, last_ref, *refs):
    refs = list(refs)
    betas = [refs.pop(0) for _ in range(iters)]
    alphas = [refs.pop(0) for _ in range(iters)]
    products = [refs.pop(0) for _ in range(iters)]
    out_ref, ratio_ref = refs
    beta = [b[...] for b in betas] + [norm_of(tree_sum([last_ref[r] for r in range(last_ref.shape[0])]))]
    alpha = [a[...] for a in alphas]
    phibar, rhobar = beta[0], alpha[0]
    direction = [1.0 / alpha[0]] + [jnp.zeros_like(phibar)] * (iters - 1)
    weights = [jnp.zeros_like(phibar)] * iters
    for i in range(iters):
        rho = jnp.sqrt(rhobar * rhobar + beta[i + 1] * beta[i + 1])
        cosine, sine = rhobar / rho, beta[i + 1] / rho
        phi = cosine * phibar
        phibar = sine * phibar
        weights = [w + (phi / rho) * d for w, d in zip(weights, direction)]
        if i + 1 < iters:
            theta = sine * alpha[i + 1]
            rhobar = -cosine * alpha[i + 1]
            direction = [-(theta / rho) * d for d in direction]
            direction[i + 1] = direction[i + 1] + 1.0 / alpha[i + 1]
    ratio = phibar / beta[0]
    for n in range(RHS):
        ratio_ref[n] = jnp.max(ratio[n : n + 1])
    scales = []
    carried = jnp.zeros_like(phibar)
    for i in reversed(range(iters)):
        carried = weights[i] - carried
        scales.insert(0, jnp.concatenate([carried / beta[i]] * 2, axis=1))
        if i > 0:
            carried = carried * (beta[i] / alpha[i - 1])
    unroll = 4

    @pl.loop(0, products[0].shape[0] // (8 * unroll))
    def _(step):
        for u in range(unroll):
            m = step * unroll + u
            at = pl.ds(pl.multiple_of(m * 8, 8), 8)
            both = tree_sum([p[at, :] * s for p, s in zip(products, scales)])
            lane = pl.multiple_of(m * 4 * LANES, 4 * LANES)
            out_ref[:, pl.ds(lane, 2 * LANES)] = both[:4]
            out_ref[:, pl.ds(lane + 2 * LANES, 2 * LANES)] = both[4:]


def f32(*shape):
    return jax.ShapeDtypeStruct(shape, jnp.float32)


def bf16(*shape):
    return jax.ShapeDtypeStruct(shape, jnp.bfloat16)


def exchange(value, axis):
    size = lax.axis_size(axis)
    got = [value]
    for d in range(1, size):
        got.append(lax.ppermute(value, axis, [(i, i ^ d) for i in range(size)]))
    return got


def swap(values, axis):
    return lax.all_to_all(values, axis, 0, 0)


def local(observed, tile_values, tile_cols):
    row_tiles, per_block, tile_size = tile_values.shape[:3]
    rows, shares = lax.axis_size("row"), lax.axis_size("col")
    col_tiles = N // (tile_size * shares)
    per_share = row_tiles // shares
    per_row = row_tiles * per_block * RHS
    share_rows = col_tiles // rows * RHS
    payload = bf16(shares, max(16, 4 * per_share), 3 * LANES)
    pos = lax.axis_index("row").astype(jnp.int32).reshape(1)
    tiles_far = pltpu.with_memory_space_constraint(tile_values, pltpu.HBM)
    held = pltpu.VMEM(tile_values.shape, tile_values.dtype)
    tile_sems = pltpu.SemaphoreType.DMA((shares,))
    keys = tile_cols.reshape(-1, 1) * RHS + jnp.arange(RHS, dtype=jnp.int32)[None]
    keys = keys.astype(jnp.float32).reshape(1, per_row)
    all_keys = exchange(keys, "row")
    equal, weight, pick = pl.pallas_call(
        match_kernel,
        out_shape=[bf16(rows * per_row, rows * per_row), f32(rows * per_row, LANES), bf16(share_rows, rows * per_row)],
        in_specs=[SMEM] + [VMEM] * rows,
        out_specs=[VMEM] * 3,
        scratch_shapes=[pltpu.VMEM((rows, 8, per_row), jnp.float32)],
        compiler_params=PARAMS,
        name="match",
    )(pos, *all_keys)

    def adjoint(payloads, load, after):
        upper, lower = bf16(per_row + 16, tile_size), bf16(per_row, tile_size)
        return pl.pallas_call(
            functools.partial(adjoint_kernel, load, len(after)),
            out_shape=[upper] + [lower] * load,
            in_specs=[HBM if load else VMEM, VMEM] + [ANY] * len(after),
            out_specs=[VMEM] * (1 + load),
            scratch_shapes=[held, tile_sems] * load,
            compiler_params=PARAMS,
            name="adjoint",
        )(tiles_far if load else tile_values, payloads, *after)

    def voxel(term_list, previous):
        first = previous is None
        extra = [] if first else list(previous)
        return pl.pallas_call(
            functools.partial(voxel_kernel, first, rows),
            out_shape=[
                f32(shares, per_share + 1, 8, LANES),
                f32(8, LANES),
                f32(rows * per_row, tile_size),
                bf16(rows * per_row, tile_size),
            ],
            in_specs=[SMEM, HBM if first else VMEM] + [VMEM] * (2 + rows + len(extra)),
            out_specs=[VMEM] * 4,
            scratch_shapes=[held, tile_sems] * first,
            compiler_params=PARAMS,
            name="voxel",
        )(pos, tiles_far if first else tile_values, equal, weight, *term_list, *extra)

    def share(all_terms, lower_terms):
        return pl.pallas_call(
            share_kernel,
            out_shape=f32(share_rows, tile_size),
            in_specs=[SMEM] + [VMEM] * (2 + len(lower_terms)),
            out_specs=VMEM,
            scratch_shapes=[pltpu.VMEM((rows * per_row, tile_size), jnp.bfloat16)] * (len(lower_terms) > 0),
            compiler_params=PARAMS,
            name="share",
        )(pos, pick, all_terms, *lower_terms)

    def ray(parts, left_raw, beta):
        return pl.pallas_call(
            ray_kernel,
            out_shape=[f32(per_share, 8, LANES), f32(8, LANES), payload, f32(rows * shares, 8, LANES)],
            in_specs=[VMEM] * 3,
            out_specs=[VMEM] * 4,
            compiler_params=PARAMS,
            name="ray",
        )(parts, left_raw, beta)

    left_raw, message = pl.pallas_call(
        prepare_kernel,
        out_shape=[f32(per_share, 8, LANES), payload],
        in_specs=[VMEM],
        out_specs=[VMEM, VMEM],
        compiler_params=PARAMS,
        name="prepare",
    )(observed)
    betas, alphas, products = [], [], []
    previous = None
    for iteration in range(ITERS + 1):
        gathered = swap(message, "col")
        upper_terms, *lower_terms = adjoint(gathered, iteration == 0, products[-1:] or all_keys[1:])
        parts, beta, right_raw, all_terms = voxel(exchange(upper_terms, "row"), previous)
        if iteration == ITERS:
            break
        products.append(share(all_terms, exchange(lower_terms[0], "row") if lower_terms else []))
        left_raw, alpha, message, squares = ray(swap(parts, "col"), left_raw, beta)
        betas.append(beta)
        alphas.append(alpha)
        previous = (right_raw, alpha)
    result, ratio = pl.pallas_call(
        functools.partial(final_kernel, ITERS),
        out_shape=[f32(RHS, col_tiles // rows * tile_size), f32(RHS)],
        in_specs=[VMEM] * (1 + 3 * ITERS),
        out_specs=[VMEM, SMEM],
        compiler_params=PARAMS,
        name="final",
    )(swap(squares, ("row", "col")), *betas, *alphas, *products)
    return result, ratio


def solution(mesh):
    in_specs = (P(None, ("row", "col")), P("row", "col", None, None), P("row", "col"))
    out_specs = (P(None, ("col", "row")), P())
    return jax.shard_map(local, mesh=mesh, in_specs=in_specs, out_specs=out_specs, check_vma=False)
```

time: 111 us -> 115 us (1.036)
  local copies, waits for them, and re-layouts: 8.53 us -> 20.1 us
  waiting for transfers between devices: 29.6 us -> 22.8 us
  Pallas kernels: 25.3 us -> 19.3 us
  blocking collectives: 18.7 us -> 23.5 us
    unnamed x9 -> x40, local copies, waits for them, and re-layouts: 8.13 us -> 19.8 us
    all_to_all x3, waiting for transfers between devices: 11.4 us -> 5.45 us  [swap(): return lax.all_to_all(values, axis, 0, 0)]
    all_to_all x2, blocking collectives: 18.7 us -> 23.5 us  [swap(): return lax.all_to_all(values, axis, 0, 0)]
    pallas_call x2, Pallas kernels: 12.2 us -> 8.18 us  [voxel(): pl.pallas_call(functools.partial(voxel_kernel, first, rows), out_shape=[f...]
    pallas_call x5 -> x6, Pallas kernels: 10.9 us -> 8.89 us  [the longest x2 4.9 us: adjoint(): pl.pallas_call(functools.partial(adjoint_kernel, load, len(after)), out_s...]
  transfers between devices with their start and end apart: 15 -> 15, of which waited for: 8 -> 10; matrix products, arithmetic and copies ran while one was open for 1% -> 1% of each run, Pallas kernels for 5% -> 2%
where the time goes in v4:
time: 115 us; the launch traced here: 114 us
  starting transfers between devices  27.1 us (24%)
  blocking collectives  23.5 us (20%)
  waiting for transfers between devices  22.8 us (20%)
  local copies, waits for them, and re-layouts  20.1 us (17%)
  Pallas kernels  19.3 us (17%)
    all_to_all x2, blocking collectives, swap(): return lax.all_to_all(values, axis, 0, 0)  23.5 us
    unnamed x40, local copies, waits for them, and re-layouts  19.8 us
    ppermute x12, waiting for transfers between devices, exchange(): got.append(lax.ppermute(value, axis, [(i, i ^ d) for i in range(size)]))  17.3 us
    ppermute x12, starting transfers between devices, exchange(): got.append(lax.ppermute(value, axis, [(i, i ^ d) for i in range(size)]))  14.2 us
    all_to_all x3, starting transfers between devices, swap(): return lax.all_to_all(values, axis, 0, 0)  12.9 us
    pallas_call x2, Pallas kernels, voxel(): pl.pallas_call(functools.partial(voxel_kernel, first, rows), out_shape=[f...  8.18 us
    all_to_all x3, waiting for transfers between devices, swap(): return lax.all_to_all(values, axis, 0, 0)  5.45 us
    pallas_call x2, Pallas kernels, adjoint(): pl.pallas_call(functools.partial(adjoint_kernel, load, len(after)), out_s...  4.9 us
  transfers between devices with their start and end apart: 15, of which 10 were waited for; matrix products, arithmetic and copies ran while one was open for 1% of the time, Pallas kernels for 2%

profile of v4, /device:TPU:0, one launch (start us, length us, event | category | flops | bytes accessed | tf_op | source)
XLA Modules:
  0.0 114.4 jit_solution(13946670432680780277)
XLA Ops:
  0.6 0.7 copy-done.19
  1.3 0.7 prepare.1
  2.0 0.6 copy-done.17
  2.6 6.3 %all-to-all-start = ((bf16[8,16,384]{2,1,0:T(8,128)(2,1)}), bf16[8,16,384]{2,1,0:T(8,128)(2,1)S(1)}, u32[]{:S(2)}, u32[]{:S(2)}) async-start(bf16[8,16,384]{2,1,0:T(8,128)(2,1)} %get-tuple-element.23), calls=%async_computation | async-start | bytes 196608 | tf_op jit(solution)/shard_map/all_to_all | solution.py:316
  8.9 0.7 broadcast_multiply_fusion
  9.6 0.1 copy.6
  9.7 0.1 mul.16
  9.8 0.1 add_convert_fusion
  9.9 0.1 convert_element_type.14.refs_0_
  10.0 2.5 %collective-permute-start.2 = (f32[1,256]{1,0:T(1,128)S(1)}, f32[1,256]{1,0:T(1,128)S(1)}, u32[]{:S(2)}, u32[]{:S(2)}) collective-permute-start(f32[1,256]{1,0:T(1,128)S(1)} %convert_element_type.14.refs_0_), channel_id=1, source_target_pairs={{0,24},{8,16},{16,8},{24,0},{1,25},{9,17},{17,9},{25,1},{2,26},{10... | collective-permute-start | bytes 3080 | tf_op jit(solution)/shard_map/ppermute | solution.py:311
  12.5 0.5 collective-permute-start.1
  13.0 0.5 collective-permute-start
  13.6 1.0 collective-permute-done.2.refs_3_.refs_2_
  14.5 1.5 %collective-permute-done.1.refs_2_.refs_1_ = f32[1,256]{1,0:T(1,128)S(1)} collective-permute-done((f32[1,256]{1,0:T(1,128)S(1)}, f32[1,256]{1,0:T(1,128)S(1)}, u32[]{:S(2)}, u32[]{:S(2)}) %collective-permute-start.1) | collective-permute-done | bytes 1056 | tf_op jit(solution)/shard_map/ppermute | solution.py:311
  16.1 0.5 collective-permute-done.refs_1_.refs_0_
  16.6 0.0 all-to-all-done.payload_ref
  16.6 3.7 %adjoint.2 = (bf16[272,256]{1,0:T(8,128)(2,1)S(1)}, bf16[256,256]{1,0:T(8,128)(2,1)S(1)}) custom-call(bf16[32,2,256,256]{3,2,1,0:T(8,128)(2,1)} %tiles_ref.7, bf16[8,16,384]{2,1,0:T(8,128)(2,1)S(1)} %all-to-all-done.payload_ref, f32[1,256]{1,0:T(1,128)S(1)} %collective-permute-done.refs_1_.refs_0_, f32[1,256]{1,0:T(1,128)S(1)} %collective-permute-done.1.refs_2_.refs_1_, ...), custom_call_target="tpu_custom_call" | custom-call | tf_op jit(solution)/shard_map/adjoint/pallas_call | solution.py:346
  20.3 1.6 %collective-permute-start.5 = (bf16[272,256]{1,0:T(8,128)(2,1)S(1)}, bf16[272,256]{1,0:T(8,128)(2,1)S(1)}, u32[]{:S(2)}, u32[]{:S(2)}) collective-permute-start(bf16[272,256]{1,0:T(8,128)(2,1)S(1)} %get-tuple-element.24.refs_0_), channel_id=1, source_target_pairs={{0,24},{8,16},{16,8},{24,0},{1,25},{9,17},{17,9},{25,1},{2,26},{10... | collective-permute-start | bytes 417800 | tf_op jit(solution)/shard_map/ppermute | solution.py:311
  21.9 0.5 collective-permute-start.4
  22.4 1.5 %collective-permute-start.3 = (bf16[272,256]{1,0:T(8,128)(2,1)S(1)}, bf16[272,256]{1,0:T(8,128)(2,1)S(1)}, u32[]{:S(2)}, u32[]{:S(2)}) collective-permute-start(bf16[272,256]{1,0:T(8,128)(2,1)S(1)} %get-tuple-element.24.refs_0_), channel_id=1, source_target_pairs={{0,8},{8,0},{16,24},{24,16},{1,9},{9,1},{17,25},{25,17},{2,10},{10... | collective-permute-start | bytes 417800 | tf_op jit(solution)/shard_map/ppermute | solution.py:311
  23.9 1.4 %match.1 = (bf16[1024,1024]{1,0:T(8,128)(2,1)S(1)}, f32[1024,128]{1,0:T(8,128)S(1)}, bf16[512,1024]{1,0:T(8,128)(2,1)S(1)}) custom-call(s32[1]{0:T(128)} %bitcast.pos_ref, f32[1,256]{1,0:T(1,128)S(1)} %convert_element_type.14.refs_0_, f32[1,256]{1,0:T(1,128)S(1)} %collective-permute-done.refs_1_.refs_0_, ...), custom_call_target="tpu_custom_call" | custom-call | tf_op jit(solution)/shard_map/match/pallas_call | solution.py:334
  25.3 1.0 copy-done.2
  26.3 1.4 %collective-permute-done.5.refs_3_ = bf16[272,256]{1,0:T(8,128)(2,1)S(1)} collective-permute-done((bf16[272,256]{1,0:T(8,128)(2,1)S(1)}, bf16[272,256]{1,0:T(8,128)(2,1)S(1)}, u32[]{:S(2)}, u32[]{:S(2)}) %collective-permute-start.5) | collective-permute-done | bytes 139296 | tf_op jit(solution)/shard_map/ppermute | solution.py:311
  27.7 0.9 collective-permute-done.4.refs_2_
  28.7 0.6 copy-done.11
  29.3 0.0 collective-permute-done.3.refs_1_
  29.3 0.7 copy-done.13
  30.0 0.9 copy-done.12
  30.9 0.9 copy-done.14
  31.8 4.6 %voxel.2 = (f32[8,5,8,128]{3,2,1,0:T(8,128)S(1)}, f32[8,128]{1,0:T(8,128)S(1)}, f32[1024,256]{1,0:T(8,128)S(1)}, bf16[1024,256]{1,0:T(8,128)(2,1)S(1)}) custom-call(s32[1]{0:T(128)} %bitcast.pos_ref, bf16[32,2,256,256]{3,2,1,0:T(8,128)(2,1)} %tiles_ref.7, bf16[1024,1024]{1,0:T(8,128)(2,1)S(1)} %get-tuple-element.21.equal_ref, ...), custom_call_target="tpu_custom_call" | custom-call | tf_op jit(solution)/shard_map/voxel/pallas_call | solution.py:359
  36.4 1.0 copy-done.5
  37.4 11.7 %all_to_all.26.part_ref = f32[8,5,8,128]{3,2,1,0:T(8,128)S(1)} all-to-all(f32[8,5,8,128]{3,2,1,0:T(8,128)S(1)} %get-tuple-element.25), channel_id=1, replica_groups=mesh['row'=4,'col'=8] {'col'}, dimensions={0} | all-to-all | bytes 327680 | tf_op jit(solution)/shard_map/all_to_all | solution.py:316
  49.2 0.7 copy-done.18
  49.9 0.8 ray.2
  50.7 0.6 copy-done.15
  51.3 3.4 %all-to-all-start.2 = ((bf16[8,16,384]{2,1,0:T(8,128)(2,1)}), bf16[8,16,384]{2,1,0:T(8,128)(2,1)S(1)}, u32[]{:S(2)}, u32[]{:S(2)}) async-start(bf16[8,16,384]{2,1,0:T(8,128)(2,1)} %get-tuple-element.28), calls=%async_computation.2 | async-start | bytes 196608 | tf_op jit(solution)/shard_map/all_to_all | solution.py:316
  54.6 1.8 %collective-permute-start.8 = (bf16[256,256]{1,0:T(8,128)(2,1)S(1)}, bf16[256,256]{1,0:T(8,128)(2,1)S(1)}, u32[]{:S(2)}, u32[]{:S(2)}) collective-permute-start(bf16[256,256]{1,0:T(8,128)(2,1)S(1)} %get-tuple-element.31.refs_0_), channel_id=1, source_target_pairs={{0,24},{8,16},{16,8},{24,0},{1,25},{9,17},{17,9},{25,1},{2,26},{10... | collective-permute-start | bytes 393224 | tf_op jit(solution)/shard_map/ppermute | solution.py:311
  56.4 0.5 collective-permute-start.7
  57.0 1.2 %collective-permute-start.6 = (bf16[256,256]{1,0:T(8,128)(2,1)S(1)}, bf16[256,256]{1,0:T(8,128)(2,1)S(1)}, u32[]{:S(2)}, u32[]{:S(2)}) collective-permute-start(bf16[256,256]{1,0:T(8,128)(2,1)S(1)} %get-tuple-element.31.refs_0_), channel_id=1, source_target_pairs={{0,8},{8,0},{16,24},{24,16},{1,9},{9,1},{17,25},{25,17},{2,10},{10... | collective-permute-start | bytes 393224 | tf_op jit(solution)/shard_map/ppermute | solution.py:311
  58.2 3.7 %collective-permute-done.8.refs_3_ = bf16[256,256]{1,0:T(8,128)(2,1)S(1)} collective-permute-done((bf16[256,256]{1,0:T(8,128)(2,1)S(1)}, bf16[256,256]{1,0:T(8,128)(2,1)S(1)}, u32[]{:S(2)}, u32[]{:S(2)}) %collective-permute-start.8) | collective-permute-done | bytes 131104 | tf_op jit(solution)/shard_map/ppermute | solution.py:311
  61.9 2.2 %collective-permute-done.7.refs_2_ = bf16[256,256]{1,0:T(8,128)(2,1)S(1)} collective-permute-done((bf16[256,256]{1,0:T(8,128)(2,1)S(1)}, bf16[256,256]{1,0:T(8,128)(2,1)S(1)}, u32[]{:S(2)}, u32[]{:S(2)}) %collective-permute-start.7) | collective-permute-done | bytes 131104 | tf_op jit(solution)/shard_map/ppermute | solution.py:311
  64.1 0.0 collective-permute-done.6.refs_1_
  64.1 1.2 %copy-done.3 = bf16[512,1024]{1,0:T(8,128)(2,1)S(1)} copy-done((bf16[512,1024]{1,0:T(8,128)(2,1)S(1)}, bf16[512,1024]{1,0:T(8,128)(2,1)}, u32[]{:S(2)}) %copy-start.3) | copy-done | bytes 1048600
  65.4 1.0 copy-done.10
  66.4 0.8 share.2.refs_0_.refs_4_
  67.2 0.0 copy-start
  67.2 3.4 %copy-done = bf16[32,2,256,256]{3,2,1,0:T(8,128)(2,1)S(1)} copy-done((bf16[32,2,256,256]{3,2,1,0:T(8,128)(2,1)S(1)}, bf16[32,2,256,256]{3,2,1,0:T(8,128)(2,1)}, u32[]{:S(2)}) %copy-start) | copy-done | bytes 8388632
  70.6 1.2 %adjoint.3.refs_0_ = bf16[272,256]{1,0:T(8,128)(2,1)S(1)} custom-call(bf16[32,2,256,256]{3,2,1,0:T(8,128)(2,1)S(1)} %copy-done, bf16[8,16,384]{2,1,0:T(8,128)(2,1)S(1)} %all-to-all-done.2.payload_ref, f32[512,256]{1,0:T(8,128)S(1)} %share.2.refs_0_.refs_4_), custom_call_target="tpu_custom_call" | custom-call | tf_op jit(solution)/shard_map/adjoint/pallas_call | solution.py:346
  71.8 1.8 %collective-permute-start.11 = (bf16[272,256]{1,0:T(8,128)(2,1)S(1)}, bf16[272,256]{1,0:T(8,128)(2,1)S(1)}, u32[]{:S(2)}, u32[]{:S(2)}) collective-permute-start(bf16[272,256]{1,0:T(8,128)(2,1)S(1)} %adjoint.3.refs_0_), channel_id=1, source_target_pairs={{0,24},{8,16},{16,8},{24,0},{1,25},{9,17},{17,9},{25,1},{2,26},{10... | collective-permute-start | bytes 417800 | tf_op jit(solution)/shard_map/ppermute | solution.py:311
  73.6 0.6 collective-permute-start.10
  74.2 1.1 collective-permute-start.9
  75.3 3.9 %collective-permute-done.11.refs_3_ = bf16[272,256]{1,0:T(8,128)(2,1)S(1)} collective-permute-done((bf16[272,256]{1,0:T(8,128)(2,1)S(1)}, bf16[272,256]{1,0:T(8,128)(2,1)S(1)}, u32[]{:S(2)}, u32[]{:S(2)}) %collective-permute-start.11) | collective-permute-done | bytes 139296 | tf_op jit(solution)/shard_map/ppermute | solution.py:311
  79.3 2.1 %collective-permute-done.10.refs_2_ = bf16[272,256]{1,0:T(8,128)(2,1)S(1)} collective-permute-done((bf16[272,256]{1,0:T(8,128)(2,1)S(1)}, bf16[272,256]{1,0:T(8,128)(2,1)S(1)}, u32[]{:S(2)}, u32[]{:S(2)}) %collective-permute-start.10) | collective-permute-done | bytes 139296 | tf_op jit(solution)/shard_map/ppermute | solution.py:311
  81.3 3.4 %copy-done.1 = bf16[32,2,256,256]{3,2,1,0:T(8,128)(2,1)S(1)} copy-done((bf16[32,2,256,256]{3,2,1,0:T(8,128)(2,1)S(1)}, bf16[32,2,256,256]{3,2,1,0:T(8,128)(2,1)}, u32[]{:S(2)}) %copy-start.1) | copy-done | bytes 8388632
  84.7 3.5 %voxel.3 = (f32[8,5,8,128]{3,2,1,0:T(8,128)S(1)}, f32[8,128]{1,0:T(8,128)S(1)}, f32[1024,256]{1,0:T(8,128)}, bf16[1024,256]{1,0:T(8,128)(2,1)S(1)}) custom-call(s32[1]{0:T(128)} %bitcast.pos_ref, bf16[32,2,256,256]{3,2,1,0:T(8,128)(2,1)S(1)} %copy-done.1, bf16[1024,1024]{1,0:T(8,128)(2,1)S(1)} %get-tuple-element.21.equal_ref, ...), custom_call_target="tpu_custom_call" | custom-call | tf_op jit(solution)/shard_map/voxel/pallas_call | solution.py:359
  88.2 0.8 copy-done.7
  89.0 11.8 %all_to_all.27.part_ref = f32[8,5,8,128]{3,2,1,0:T(8,128)S(1)} all-to-all(f32[8,5,8,128]{3,2,1,0:T(8,128)S(1)} %get-tuple-element.34), channel_id=1, replica_groups=mesh['row'=4,'col'=8] {'col'}, dimensions={0} | all-to-all | bytes 327680 | tf_op jit(solution)/shard_map/all_to_all | solution.py:316
  100.8 0.8 ray.3
  101.6 3.2 %all-to-all-start.4 = ((f32[32,8,128]{2,1,0:T(8,128)}), f32[32,8,128]{2,1,0:T(8,128)S(1)}, u32[]{:S(2)}, u32[]{:S(2)}) async-start(f32[32,8,128]{2,1,0:T(8,128)} %get-tuple-element.37), calls=%async_computation.4 | async-start | bytes 262144 | tf_op jit(solution)/shard_map/all_to_all | solution.py:316
  104.9 1.2 %copy-done.4 = bf16[512,1024]{1,0:T(8,128)(2,1)S(1)} copy-done((bf16[512,1024]{1,0:T(8,128)(2,1)S(1)}, bf16[512,1024]{1,0:T(8,128)(2,1)}, u32[]{:S(2)}) %copy-start.4) | copy-done | bytes 1048600
  106.1 1.0 copy-done.8
  107.1 0.5 share.3.refs_5_
  107.6 5.4 %all-to-all-done.4.last_ref = f32[32,8,128]{2,1,0:T(8,128)S(1)} async-done(((f32[32,8,128]{2,1,0:T(8,128)}), f32[32,8,128]{2,1,0:T(8,128)S(1)}, u32[]{:S(2)}, u32[]{:S(2)}) %all-to-all-start.4) | async-done | bytes 131104 | tf_op jit(solution)/shard_map/all_to_all | solution.py:316
  113.0 1.3 %final.1 = (f32[4,32768]{1,0:T(4,128)}, f32[4]{0:T(128)}) custom-call(f32[32,8,128]{2,1,0:T(8,128)S(1)} %all-to-all-done.4.last_ref, f32[8,128]{1,0:T(8,128)S(1)} %copy-done.16, f32[8,128]{1,0:T(8,128)S(1)} %get-tuple-element.36.beta_ref.refs_1_, f32[8,128]{1,0:T(8,128)S(1)} %get-tuple-element.33.refs_5_.refs_2_, f32[8,128]{1,0:T(8,128)S(1)} %get-tuple-element.38.refs_3_, ...), custom_call_target="tpu_custom_call" | custom-call | tf_op jit(solution)/shard_map/final/pallas_call | solution.py:416
  (24 shorter events, 0.0 us)
Async XLA Ops:
  0.6 0.7 copy-start.19
  2.0 0.6 copy-start.17
  2.6 14.0 %all-to-all-start = ((bf16[8,16,384]{2,1,0:T(8,128)(2,1)}), bf16[8,16,384]{2,1,0:T(8,128)(2,1)S(1)}, u32[]{:S(2)}, u32[]{:S(2)}) async-start(bf16[8,16,384]{2,1,0:T(8,128)(2,1)} %get-tuple-element.23), calls=%async_computation | async-start | bytes 196608 | tf_op jit(solution)/shard_map/all_to_all | solution.py:316
  10.0 4.5 %collective-permute-start.2 = (f32[1,256]{1,0:T(1,128)S(1)}, f32[1,256]{1,0:T(1,128)S(1)}, u32[]{:S(2)}, u32[]{:S(2)}) collective-permute-start(f32[1,256]{1,0:T(1,128)S(1)} %convert_element_type.14.refs_0_), channel_id=1, source_target_pairs={{0,24},{8,16},{16,8},{24,0},{1,25},{9,17},{17,9},{25,1},{2,26},{10... | collective-permute-start | bytes 3080 | tf_op jit(solution)/shard_map/ppermute | solution.py:311
  12.5 3.6 %collective-permute-start.1 = (f32[1,256]{1,0:T(1,128)S(1)}, f32[1,256]{1,0:T(1,128)S(1)}, u32[]{:S(2)}, u32[]{:S(2)}) collective-permute-start(f32[1,256]{1,0:T(1,128)S(1)} %convert_element_type.14.refs_0_), channel_id=1, source_target_pairs={{0,16},{8,24},{16,0},{24,8},{1,17},{9,25},{17,1},{25,9},{2,18},{10... | collective-permute-start | bytes 3080 | tf_op jit(solution)/shard_map/ppermute | solution.py:311
  13.0 3.6 %collective-permute-start = (f32[1,256]{1,0:T(1,128)S(1)}, f32[1,256]{1,0:T(1,128)S(1)}, u32[]{:S(2)}, u32[]{:S(2)}) collective-permute-start(f32[1,256]{1,0:T(1,128)S(1)} %convert_element_type.14.refs_0_), channel_id=1, source_target_pairs={{0,8},{8,0},{16,24},{24,16},{1,9},{9,1},{17,25},{25,17},{2,10},{10... | collective-permute-start | bytes 3080 | tf_op jit(solution)/shard_map/ppermute | solution.py:311
  20.3 7.4 %collective-permute-start.5 = (bf16[272,256]{1,0:T(8,128)(2,1)S(1)}, bf16[272,256]{1,0:T(8,128)(2,1)S(1)}, u32[]{:S(2)}, u32[]{:S(2)}) collective-permute-start(bf16[272,256]{1,0:T(8,128)(2,1)S(1)} %get-tuple-element.24.refs_0_), channel_id=1, source_target_pairs={{0,24},{8,16},{16,8},{24,0},{1,25},{9,17},{17,9},{25,1},{2,26},{10... | collective-permute-start | bytes 417800 | tf_op jit(solution)/shard_map/ppermute | solution.py:311
  21.9 6.8 %collective-permute-start.4 = (bf16[272,256]{1,0:T(8,128)(2,1)S(1)}, bf16[272,256]{1,0:T(8,128)(2,1)S(1)}, u32[]{:S(2)}, u32[]{:S(2)}) collective-permute-start(bf16[272,256]{1,0:T(8,128)(2,1)S(1)} %get-tuple-element.24.refs_0_), channel_id=1, source_target_pairs={{0,16},{8,24},{16,0},{24,8},{1,17},{9,25},{17,1},{25,9},{2,18},{10... | collective-permute-start | bytes 417800 | tf_op jit(solution)/shard_map/ppermute | solution.py:311
  22.4 6.9 %collective-permute-start.3 = (bf16[272,256]{1,0:T(8,128)(2,1)S(1)}, bf16[272,256]{1,0:T(8,128)(2,1)S(1)}, u32[]{:S(2)}, u32[]{:S(2)}) collective-permute-start(bf16[272,256]{1,0:T(8,128)(2,1)S(1)} %get-tuple-element.24.refs_0_), channel_id=1, source_target_pairs={{0,8},{8,0},{16,24},{24,16},{1,9},{9,1},{17,25},{25,17},{2,10},{10... | collective-permute-start | bytes 417800 | tf_op jit(solution)/shard_map/ppermute | solution.py:311
  25.3 1.0 copy-start.2
  28.7 0.6 copy-start.11
  29.3 0.7 copy-start.13
  30.0 0.9 copy-start.12
  30.9 0.9 copy-start.14
  36.4 1.0 copy-start.5
  37.4 26.7 %copy-start.9 = (bf16[1024,256]{1,0:T(8,128)(2,1)}, bf16[1024,256]{1,0:T(8,128)(2,1)S(1)}, u32[]{:S(2)}) copy-start(bf16[1024,256]{1,0:T(8,128)(2,1)S(1)} %get-tuple-element.30.all_ref) | copy-start | bytes 1572868
  49.2 0.7 copy-start.18
  50.7 0.6 copy-start.15
  51.3 15.9 %all-to-all-start.2 = ((bf16[8,16,384]{2,1,0:T(8,128)(2,1)}), bf16[8,16,384]{2,1,0:T(8,128)(2,1)S(1)}, u32[]{:S(2)}, u32[]{:S(2)}) async-start(bf16[8,16,384]{2,1,0:T(8,128)(2,1)} %get-tuple-element.28), calls=%async_computation.2 | async-start | bytes 196608 | tf_op jit(solution)/shard_map/all_to_all | solution.py:316
  54.6 7.3 %collective-permute-start.8 = (bf16[256,256]{1,0:T(8,128)(2,1)S(1)}, bf16[256,256]{1,0:T(8,128)(2,1)S(1)}, u32[]{:S(2)}, u32[]{:S(2)}) collective-permute-start(bf16[256,256]{1,0:T(8,128)(2,1)S(1)} %get-tuple-element.31.refs_0_), channel_id=1, source_target_pairs={{0,24},{8,16},{16,8},{24,0},{1,25},{9,17},{17,9},{25,1},{2,26},{10... | collective-permute-start | bytes 393224 | tf_op jit(solution)/shard_map/ppermute | solution.py:311
  56.4 7.7 %collective-permute-start.7 = (bf16[256,256]{1,0:T(8,128)(2,1)S(1)}, bf16[256,256]{1,0:T(8,128)(2,1)S(1)}, u32[]{:S(2)}, u32[]{:S(2)}) collective-permute-start(bf16[256,256]{1,0:T(8,128)(2,1)S(1)} %get-tuple-element.31.refs_0_), channel_id=1, source_target_pairs={{0,16},{8,24},{16,0},{24,8},{1,17},{9,25},{17,1},{25,9},{2,18},{10... | collective-permute-start | bytes 393224 | tf_op jit(solution)/shard_map/ppermute | solution.py:311
  57.0 7.2 %collective-permute-start.6 = (bf16[256,256]{1,0:T(8,128)(2,1)S(1)}, bf16[256,256]{1,0:T(8,128)(2,1)S(1)}, u32[]{:S(2)}, u32[]{:S(2)}) collective-permute-start(bf16[256,256]{1,0:T(8,128)(2,1)S(1)} %get-tuple-element.31.refs_0_), channel_id=1, source_target_pairs={{0,8},{8,0},{16,24},{24,16},{1,9},{9,1},{17,25},{25,17},{2,10},{10... | collective-permute-start | bytes 393224 | tf_op jit(solution)/shard_map/ppermute | solution.py:311
  64.1 1.2 %copy-start.3 = (bf16[512,1024]{1,0:T(8,128)(2,1)S(1)}, bf16[512,1024]{1,0:T(8,128)(2,1)}, u32[]{:S(2)}) copy-start(bf16[512,1024]{1,0:T(8,128)(2,1)} %copy-done.2) | copy-start | bytes 3145732
  65.4 1.0 copy-start.10
  67.2 3.4 %copy-start = (bf16[32,2,256,256]{3,2,1,0:T(8,128)(2,1)S(1)}, bf16[32,2,256,256]{3,2,1,0:T(8,128)(2,1)}, u32[]{:S(2)}) copy-start(bf16[32,2,256,256]{3,2,1,0:T(8,128)(2,1)} %tiles_ref.7) | copy-start | bytes 25165828
  70.6 10.7 %copy-start.6 = (f32[1024,256]{1,0:T(8,128)S(1)}, f32[1024,256]{1,0:T(8,128)}, u32[]{:S(2)}) copy-start(f32[1024,256]{1,0:T(8,128)} %copy-done.5) | copy-start | bytes 3145732
  70.6 42.4 %copy-start.16 = (f32[8,128]{1,0:T(8,128)S(1)}, f32[8,128]{1,0:T(8,128)}, u32[]{:S(2)}) copy-start(f32[8,128]{1,0:T(8,128)} %copy-done.15) | copy-start | bytes 12292
  71.8 7.5 %collective-permute-start.11 = (bf16[272,256]{1,0:T(8,128)(2,1)S(1)}, bf16[272,256]{1,0:T(8,128)(2,1)S(1)}, u32[]{:S(2)}, u32[]{:S(2)}) collective-permute-start(bf16[272,256]{1,0:T(8,128)(2,1)S(1)} %adjoint.3.refs_0_), channel_id=1, source_target_pairs={{0,24},{8,16},{16,8},{24,0},{1,25},{9,17},{17,9},{25,1},{2,26},{10... | collective-permute-start | bytes 417800 | tf_op jit(solution)/shard_map/ppermute | solution.py:311
  73.6 7.7 %collective-permute-start.10 = (bf16[272,256]{1,0:T(8,128)(2,1)S(1)}, bf16[272,256]{1,0:T(8,128)(2,1)S(1)}, u32[]{:S(2)}, u32[]{:S(2)}) collective-permute-start(bf16[272,256]{1,0:T(8,128)(2,1)S(1)} %adjoint.3.refs_0_), channel_id=1, source_target_pairs={{0,16},{8,24},{16,0},{24,8},{1,17},{9,25},{17,1},{25,9},{2,18},{10... | collective-permute-start | bytes 417800 | tf_op jit(solution)/shard_map/ppermute | solution.py:311
  74.2 7.1 %collective-permute-start.9 = (bf16[272,256]{1,0:T(8,128)(2,1)S(1)}, bf16[272,256]{1,0:T(8,128)(2,1)S(1)}, u32[]{:S(2)}, u32[]{:S(2)}) collective-permute-start(bf16[272,256]{1,0:T(8,128)(2,1)S(1)} %adjoint.3.refs_0_), channel_id=1, source_target_pairs={{0,8},{8,0},{16,24},{24,16},{1,9},{9,1},{17,25},{25,17},{2,10},{10... | collective-permute-start | bytes 417800 | tf_op jit(solution)/shard_map/ppermute | solution.py:311
  81.3 3.4 %copy-start.1 = (bf16[32,2,256,256]{3,2,1,0:T(8,128)(2,1)S(1)}, bf16[32,2,256,256]{3,2,1,0:T(8,128)(2,1)}, u32[]{:S(2)}) copy-start(bf16[32,2,256,256]{3,2,1,0:T(8,128)(2,1)} %tiles_ref.7) | copy-start | bytes 25165828
  88.2 0.8 copy-start.7
  101.6 11.4 %all-to-all-start.4 = ((f32[32,8,128]{2,1,0:T(8,128)}), f32[32,8,128]{2,1,0:T(8,128)S(1)}, u32[]{:S(2)}, u32[]{:S(2)}) async-start(f32[32,8,128]{2,1,0:T(8,128)} %get-tuple-element.37), calls=%async_computation.4 | async-start | bytes 262144 | tf_op jit(solution)/shard_map/all_to_all | solution.py:316
  104.8 1.2 %copy-start.4 = (bf16[512,1024]{1,0:T(8,128)(2,1)S(1)}, bf16[512,1024]{1,0:T(8,128)(2,1)}, u32[]{:S(2)}) copy-start(bf16[512,1024]{1,0:T(8,128)(2,1)} %copy-done.2) | copy-start | bytes 3145732
  106.1 1.0 copy-start.8

commit v5 on v4

v5 whole, which is shorter than its diff:
```python
import functools

import jax
import jax.numpy as jnp
from jax import lax
from jax.experimental import pallas as pl
from jax.experimental.pallas import tpu as pltpu
from jax.sharding import PartitionSpec as P

ITERS = 2
N = 1048576
epsilon_sq = 1e-06
LANES = 128
RHS = 4
VMEM = pl.BlockSpec(memory_space=pltpu.VMEM)
SMEM = pl.BlockSpec(memory_space=pltpu.SMEM)
HBM = pl.BlockSpec(memory_space=pltpu.HBM)
ANY = pl.BlockSpec(memory_space=pl.ANY)
PARAMS = pltpu.CompilerParams(vmem_limit_bytes=32 * 1024 * 1024)


def tree_sum(parts):
    while len(parts) > 1:
        paired = [parts[i] + parts[i + 1] for i in range(0, len(parts) - 1, 2)]
        parts = paired + parts[2 * len(paired) :]
    return parts[0]


def norm_of(acc):
    rows = jnp.broadcast_to(jnp.sum(acc, axis=1, keepdims=True), acc.shape)
    return jnp.sqrt(rows + pltpu.roll(rows, 4, 0) + epsilon_sq)


def low_half(width):
    return lax.broadcasted_iota(jnp.int32, (8, width), 0) < 4


def in_two(acc):
    upper = acc.astype(jnp.bfloat16).astype(jnp.float32)
    return upper, acc - upper


def write_payload(out_ref, blocks, acc):
    rows = out_ref.shape[0]
    blank = [jnp.zeros((8, LANES), jnp.float32)] * (rows // 8)
    for h in range(2):
        half = (blocks[h::2] + blank)[: rows // 8]
        out_ref[:, h * LANES : (h + 1) * LANES] = jnp.concatenate(half, axis=0).astype(jnp.bfloat16)
    pieces = (list(in_two(acc)) + blank)[: rows // 8]
    out_ref[:, 2 * LANES :] = jnp.concatenate(pieces, axis=0).astype(jnp.bfloat16)


def read_squares(ref):
    both = ref[:, 2 * LANES :].astype(jnp.float32)
    return both[:8] + both[8:16]


def ray_blocks(obs_ref, count):
    obs = obs_ref[...]
    blocks = []
    for b in range(count):
        at = (b // 2) * 4 * LANES + (b % 2) * LANES
        blocks.append(jnp.concatenate([obs[:, at : at + LANES], obs[:, at + 2 * LANES : at + 3 * LANES]], axis=0))
    return blocks


def prepare_kernel(obs_ref, payload_ref):
    blocks = ray_blocks(obs_ref, obs_ref.shape[1] // (2 * LANES))
    squares = tree_sum([b * b for b in blocks])
    for c in range(payload_ref.shape[0]):
        write_payload(payload_ref.at[c], blocks, squares)


def key_row(cols_ref):
    per_block, row_tiles = cols_ref.shape
    width = per_block * row_tiles * RHS
    lane = lax.broadcasted_iota(jnp.int32, (8, width), 1)
    keys = jnp.zeros((8, width), jnp.int32)
    for i in range(row_tiles):
        for k in range(per_block):
            keys = jnp.where(lane // RHS == i * per_block + k, cols_ref[k, i], keys)
    return (keys * RHS + lane % RHS).astype(jnp.float32)


def fill_equal(keys_ref, equal_ref, weight_ref):
    rows, _, per_row = keys_ref.shape

    @pl.loop(0, rows)
    def _(s):
        down = jnp.broadcast_to(keys_ref[s][:1], (LANES, per_row)).T
        at = pl.ds(pl.multiple_of(s * per_row, per_row), per_row)
        count = jnp.zeros((per_row, LANES), jnp.float32)
        for other in range(rows):
            for h in range(per_row // LANES):
                across = keys_ref[other, :1, h * LANES : (h + 1) * LANES]
                same = jnp.where(down == across, 1.0, 0.0)
                count = count + same
                lane = other * per_row + h * LANES
                equal_ref[at, lane : lane + LANES] = same.astype(jnp.bfloat16)
        weight_ref[at, :] = jnp.broadcast_to(1.0 / jnp.sum(count, axis=1, keepdims=True), (per_row, LANES))


def fill_pick(keys_ref, pick_ref):
    rows, _, per_row = keys_ref.shape
    wanted = pick_ref.shape[0]
    step_rows = 128
    start = lax.axis_index("row") * wanted

    @pl.loop(0, wanted // step_rows)
    def _(step):
        down = lax.broadcasted_iota(jnp.int32, (step_rows, LANES), 0) + (start + step * step_rows)
        down = down.astype(jnp.float32)
        at = pl.ds(pl.multiple_of(step * step_rows, step_rows), step_rows)
        for other in range(rows):
            for h in range(per_row // LANES):
                across = keys_ref[other, :1, h * LANES : (h + 1) * LANES]
                lane = other * per_row + h * LANES
                pick_ref[at, lane : lane + LANES] = jnp.where(down == across, 1.0, 0.0).astype(jnp.bfloat16)


def adjoint_kernel(first, *refs):
    if first:
        cols_ref, tiles_ref, payload_ref, term_ref = refs
    else:
        tiles_ref, payload_ref, term_ref = refs
    row_tiles, per_block = tiles_ref.shape[:2]
    shares = payload_ref.shape[0]
    per_share = row_tiles // shares
    terms = row_tiles * per_block * RHS
    squares = tree_sum([read_squares(payload_ref.at[c]) for c in range(shares)])
    if first:
        term_ref[terms : terms + 8] = jnp.concatenate([squares, jnp.zeros_like(squares)], axis=1)
        term_ref[terms + 8 :] = key_row(cols_ref)
    else:
        pieces = jnp.concatenate(in_two(squares), axis=1)
        term_ref[terms:] = jnp.concatenate([pieces, jnp.zeros_like(pieces)], axis=0).astype(jnp.bfloat16)
    low = low_half(2 * LANES)
    for c in range(shares):
        rays = payload_ref[c, :, : 2 * LANES]
        for g in range(per_share // 2):
            i = c * per_share + 2 * g
            wide = [
                jnp.dot(rays, tiles_ref[i + e, k], preferred_element_type=jnp.float32)[8 * g : 8 * g + 8]
                for e in range(2)
                for k in range(2)
            ]
            value = jnp.concatenate(
                [
                    jnp.where(low, wide[0], pltpu.roll(wide[1], 4, 0)),
                    jnp.where(low, pltpu.roll(wide[2], 4, 0), wide[3]),
                ],
                axis=0,
            )
            term_ref[8 * i : 8 * i + 16] = value.astype(term_ref.dtype)


def voxel_kernel(first, rows, tiles_ref, *refs):
    terms, refs = refs[:rows], list(refs[rows:])
    if first:
        out_ref, beta_ref, raw_ref, all_ref, low_ref, equal_ref, weight_ref, keys_ref = refs
    else:
        equal_ref, weight_ref, right_ref, alpha_ref = refs[:4]
        out_ref, beta_ref, raw_ref, all_ref = refs[-4:]
    my_row = lax.axis_index("row")
    row_tiles, per_block = tiles_ref.shape[:2]
    shares = out_ref.shape[0]
    per_share = row_tiles // shares
    per_row = row_tiles * per_block * RHS
    squares = []
    for d in range(rows):
        slot = jnp.bitwise_xor(my_row, d)
        at = pl.ds(pl.multiple_of(slot * per_row, per_row), per_row)
        if first:
            value = terms[d][:per_row]
            upper = value.astype(jnp.bfloat16)
            all_ref[at, :] = upper
            low_ref[at, :] = (value - upper.astype(jnp.float32)).astype(jnp.bfloat16)
            squares.append(terms[d][per_row : per_row + 8, :LANES])
            keys_ref[slot] = terms[d][per_row + 8 :]
        else:
            all_ref[at, :] = terms[d][:per_row]
            pieces = terms[d][per_row:].astype(jnp.float32)[:8]
            squares.append(pieces[:, :LANES] + pieces[:, LANES:])
    if first:
        fill_equal(keys_ref, equal_ref, weight_ref)
    beta = norm_of(tree_sum(squares))
    beta_ref[...] = beta
    wide_scale = jnp.concatenate([1.0 / beta] * 2, axis=1)
    if not first:
        wide_right = jnp.concatenate([beta / alpha_ref[...]] * 2, axis=1)
    acc = jnp.zeros((8, LANES), jnp.float32)
    for s in range(rows):
        same = equal_ref[s * per_row : (s + 1) * per_row, :]
        summed = jnp.dot(same, all_ref[...], preferred_element_type=jnp.float32)
        if first:
            summed = summed + jnp.dot(same, low_ref[...], preferred_element_type=jnp.float32)
        for m in range(per_row // 8):
            at = s * per_row + 8 * m
            raw = summed[8 * m : 8 * m + 8] * wide_scale
            if not first:
                raw = raw - right_ref[at : at + 8] * wide_right
            raw_ref[at : at + 8] = raw
            square = raw * raw
            acc = acc + (square[:, :LANES] + square[:, LANES:]) * weight_ref[at : at + 8]
    low = low_half(2 * LANES)
    own = my_row * per_row
    for c in range(shares):
        for g in range(per_share // 2):
            i = c * per_share + 2 * g
            lhs = raw_ref[pl.ds(pl.multiple_of(own + 8 * i, 16), 16), :].astype(jnp.bfloat16)
            wide = [
                lax.dot_general(
                    lhs, tiles_ref[i + e, k], (((1,), (1,)), ((), ())), preferred_element_type=jnp.float32
                )[8 * e : 8 * e + 8]
                for e in range(2)
                for k in range(2)
            ]
            value = jnp.where(low, wide[0], wide[3]) + pltpu.roll(jnp.where(low, wide[2], wide[1]), 4, 0)
            out_ref[c, 2 * g] = value[:, :LANES]
            out_ref[c, 2 * g + 1] = value[:, LANES:]
        out_ref[c, per_share] = acc


def share_kernel(pieces, first, unread, *refs):
    refs = refs[unread:]
    if first:
        keys_ref, values, out_ref, pick_ref = refs[0], refs[1 : 1 + pieces], refs[-2], refs[-1]
        fill_pick(keys_ref, pick_ref)
    else:
        pick_ref, values, out_ref = refs[0], refs[1 : 1 + pieces], refs[-1]
    step = 128
    for at in range(0, out_ref.shape[0], step):
        pick = pick_ref[at : at + step, :]
        out_ref[at : at + step, :] = tree_sum(
            [jnp.dot(pick, v[...], preferred_element_type=jnp.float32) for v in values]
        )


def ray_kernel(first, part_ref, left_ref, beta_ref, raw_ref, alpha_ref, payload_ref, acc_ref):
    shares, count = part_ref.shape[0], raw_ref.shape[0]
    alpha = norm_of(tree_sum([part_ref[c, count] for c in range(shares)]))
    alpha_ref[...] = alpha
    alpha_inv = 1.0 / alpha
    left_scale = alpha / beta_ref[...]
    left = ray_blocks(left_ref, count) if first else [left_ref[b] for b in range(count)]
    blocks = []
    for b in range(count):
        total = tree_sum([part_ref[c, b] for c in range(shares)])
        blocks.append(total * alpha_inv - left[b] * left_scale)
        raw_ref[b] = blocks[-1]
    acc = tree_sum([b * b for b in blocks])
    for c in range(acc_ref.shape[0]):
        acc_ref[c] = acc
    for c in range(shares):
        write_payload(payload_ref.at[c], blocks, acc)


def final_kernel(iters, last_ref, *refs):
    refs = list(refs)
    betas = [refs.pop(0) for _ in range(iters)]
    alphas = [refs.pop(0) for _ in range(iters)]
    products = [refs.pop(0) for _ in range(iters)]
    out_ref, ratio_ref = refs
    beta = [b[...] for b in betas] + [norm_of(tree_sum([last_ref[r] for r in range(last_ref.shape[0])]))]
    alpha = [a[...] for a in alphas]
    phibar, rhobar = beta[0], alpha[0]
    direction = [1.0 / alpha[0]] + [jnp.zeros_like(phibar)] * (iters - 1)
    weights = [jnp.zeros_like(phibar)] * iters
    for i in range(iters):
        rho = jnp.sqrt(rhobar * rhobar + beta[i + 1] * beta[i + 1])
        cosine, sine = rhobar / rho, beta[i + 1] / rho
        phi = cosine * phibar
        phibar = sine * phibar
        weights = [w + (phi / rho) * d for w, d in zip(weights, direction)]
        if i + 1 < iters:
            theta = sine * alpha[i + 1]
            rhobar = -cosine * alpha[i + 1]
            direction = [-(theta / rho) * d for d in direction]
            direction[i + 1] = direction[i + 1] + 1.0 / alpha[i + 1]
    ratio = phibar / beta[0]
    for n in range(RHS):
        ratio_ref[n] = jnp.max(ratio[n : n + 1])
    scales = []
    carried = jnp.zeros_like(phibar)
    for i in reversed(range(iters)):
        carried = weights[i] - carried
        scales.insert(0, jnp.concatenate([carried / beta[i]] * 2, axis=1))
        if i > 0:
            carried = carried * (beta[i] / alpha[i - 1])
    unroll = 4

    @pl.loop(0, products[0].shape[0] // (8 * unroll))
    def _(step):
        for u in range(unroll):
            m = step * unroll + u
            at = pl.ds(pl.multiple_of(m * 8, 8), 8)
            both = tree_sum([p[at, :] * s for p, s in zip(products, scales)])
            lane = pl.multiple_of(m * 4 * LANES, 4 * LANES)
            out_ref[:, pl.ds(lane, 2 * LANES)] = both[:4]
            out_ref[:, pl.ds(lane + 2 * LANES, 2 * LANES)] = both[4:]


def f32(*shape):
    return jax.ShapeDtypeStruct(shape, jnp.float32)


def bf16(*shape):
    return jax.ShapeDtypeStruct(shape, jnp.bfloat16)


def exchange(value, axis):
    size = lax.axis_size(axis)
    got = [value]
    for d in range(1, size):
        got.append(lax.ppermute(value, axis, [(i, i ^ d) for i in range(size)]))
    return got


def swap(values, axis):
    return lax.all_to_all(values, axis, 0, 0)


def local(observed, tile_values, tile_cols):
    row_tiles, per_block, tile_size = tile_values.shape[:3]
    rows, shares = lax.axis_size("row"), lax.axis_size("col")
    col_tiles = N // (tile_size * shares)
    per_share = row_tiles // shares
    per_row = row_tiles * per_block * RHS
    share_rows = col_tiles // rows * RHS
    payload = bf16(shares, max(16, 4 * per_share), 3 * LANES)

    def call(kernel, name, out_shape, args, in_specs=None):
        return pl.pallas_call(
            kernel,
            out_shape=out_shape,
            in_specs=in_specs or [VMEM] * len(args),
            out_specs=jax.tree.map(lambda _: VMEM, out_shape),
            compiler_params=PARAMS,
            name=name,
        )(*args)

    def adjoint(payloads, first):
        terms = (f32 if first else bf16)(per_row + 16, tile_size)
        args = [tile_cols.T] * first + [tile_values, payloads]
        return call(
            functools.partial(adjoint_kernel, first), "adjoint", terms, args, [SMEM] * first + [VMEM] * 2
        )

    def voxel(term_list, previous):
        first = not previous
        out_shape = [
            f32(shares, per_share + 1, 8, LANES),
            f32(8, LANES),
            f32(rows * per_row, tile_size),
            bf16(rows * per_row, tile_size),
        ]
        if first:
            out_shape += [
                bf16(rows * per_row, tile_size),
                bf16(rows * per_row, rows * per_row),
                f32(rows * per_row, LANES),
                f32(rows, 8, per_row),
            ]
        args = [tile_values, *term_list, *previous]
        specs = [VMEM] * len(args)
        return call(functools.partial(voxel_kernel, first, rows), "voxel", out_shape, args, specs)

    def share(selector, values, after, first):
        out_shape = [f32(share_rows, tile_size)] + [bf16(share_rows, rows * per_row)] * first
        return call(
            functools.partial(share_kernel, len(values), first, len(after)),
            "share",
            out_shape,
            [*after, selector, *values],
            [ANY] * len(after) + [VMEM] * (1 + len(values)),
        )

    def ray(parts, left_raw, beta, first):
        out_shape = [f32(per_share, 8, LANES), f32(8, LANES), payload, f32(rows * shares, 8, LANES)]
        return call(functools.partial(ray_kernel, first), "ray", out_shape, [parts, left_raw, beta])

    message = call(prepare_kernel, "prepare", payload, [observed])
    left_raw = observed
    betas, alphas, products = [], [], []
    previous = []
    waiting = None
    for iteration in range(ITERS + 1):
        first = iteration == 0
        terms = adjoint(swap(message, "col"), first)
        if waiting:
            product, *pick = share(*waiting, [squares if iteration == ITERS else terms], not products)
            selector = pick[0] if pick else selector
            products.append(product)
        parts, beta, right_raw, upper_terms, *fixed = voxel(exchange(terms, "row"), previous)
        if first:
            lower_terms, equal, weight, selector = fixed
        if iteration == ITERS:
            break
        waiting = (selector, [upper_terms, lower_terms] if first else [upper_terms])
        left_raw, alpha, message, squares = ray(swap(parts, "col"), left_raw, beta, first)
        betas.append(beta)
        alphas.append(alpha)
        previous = [equal, weight, right_raw, alpha]
    result, ratio = pl.pallas_call(
        functools.partial(final_kernel, ITERS),
        out_shape=[f32(RHS, col_tiles // rows * tile_size), f32(RHS)],
        in_specs=[VMEM] * (1 + 3 * ITERS),
        out_specs=[VMEM, SMEM],
        compiler_params=PARAMS,
        name="final",
    )(swap(squares, ("row", "col")), *betas, *alphas, *products)
    return result, ratio


def solution(mesh):
    in_specs = (P(None, ("row", "col")), P("row", "col", None, None), P("row", "col"))
    out_specs = (P(None, ("col", "row")), P())
    return jax.shard_map(local, mesh=mesh, in_specs=in_specs, out_specs=out_specs, check_vma=False)
```

time: 115 us -> 96.4 us (0.84)
  blocking collectives: 23.5 us -> 40.8 us
  starting transfers between devices: 27.1 us -> 10.2 us
  local copies, waits for them, and re-layouts: 20.1 us -> 4.78 us
  Pallas kernels: 19.3 us -> 15.5 us
    all_to_all x2 -> x4, blocking collectives: 23.5 us -> 40.8 us  [swap(): return lax.all_to_all(values, axis, 0, 0)]
    unnamed x40 -> x10, local copies, waits for them, and re-layouts: 19.8 us -> 4.78 us
    all_to_all x3 -> x1, starting transfers between devices: 12.9 us -> 3.11 us  [swap(): return lax.all_to_all(values, axis, 0, 0)]
    ppermute x12 -> x6, starting transfers between devices: 14.2 us -> 7.11 us  [exchange(): got.append(lax.ppermute(value, axis, [(i, i ^ d) for i in range(size)]))]
    pallas_call x10 -> x9, Pallas kernels: 18 us -> 14.1 us  [call(): pl.pallas_call(kernel, out_shape=out_shape, in_specs=in_specs or [VMEM] *...]
    all_to_all x3 -> x1, waiting for transfers between devices: 5.45 us -> 6.64 us  [swap(): return lax.all_to_all(values, axis, 0, 0)]
    ppermute x12 -> x6, waiting for transfers between devices: 17.3 us -> 17.3 us  [exchange(): got.append(lax.ppermute(value, axis, [(i, i ^ d) for i in range(size)]))]
  transfers between devices with their start and end apart: 15 -> 7, of which waited for: 10 -> 6; matrix products, arithmetic and copies ran while one was open for 1% -> 0% of each run, Pallas kernels for 2% -> 2%
where the time goes in v5:
time: 96.4 us; the launch traced here: 95.9 us
  blocking collectives  40.8 us (42%)
  waiting for transfers between devices  23.9 us (25%)
  Pallas kernels  15.5 us (16%)
  starting transfers between devices  10.2 us (11%)
  local copies, waits for them, and re-layouts  4.78 us (5%)
    all_to_all x4, blocking collectives, swap(): return lax.all_to_all(values, axis, 0, 0)  40.8 us
    ppermute x6, waiting for transfers between devices, exchange(): got.append(lax.ppermute(value, axis, [(i, i ^ d) for i in range(size)]))  17.3 us
    pallas_call x9, Pallas kernels, call(): pl.pallas_call(kernel, out_shape=out_shape, in_specs=in_specs or [VMEM] *...  14.1 us
    ppermute x6, starting transfers between devices, exchange(): got.append(lax.ppermute(value, axis, [(i, i ^ d) for i in range(size)]))  7.11 us
    all_to_all x1, waiting for transfers between devices, swap(): return lax.all_to_all(values, axis, 0, 0)  6.64 us
    unnamed x10, local copies, waits for them, and re-layouts  4.78 us
    all_to_all x1, starting transfers between devices, swap(): return lax.all_to_all(values, axis, 0, 0)  3.11 us
  transfers between devices with their start and end apart: 7, of which 6 were waited for; matrix products, arithmetic and copies ran while one was open for 0% of the time, Pallas kernels for 2%

profile of v5, /device:TPU:0, one launch (start us, length us, event | category | flops | bytes accessed | tf_op | source)
XLA Modules:
  0.0 95.9 jit_solution(11655344282025260736)
XLA Ops:
  0.6 0.0 copy-start.2
  0.6 0.7 copy-done.2
  1.4 12.5 %all_to_all.26.refs_2_ = bf16[8,16,384]{2,1,0:T(8,128)(2,1)S(1)} all-to-all(bf16[8,16,384]{2,1,0:T(8,128)(2,1)S(1)} %prepare.1), channel_id=1, replica_groups=mesh['row'=4,'col'=8] {'col'}, dimensions={0} | all-to-all | bytes 196608 | tf_op jit(solution)/shard_map/all_to_all | solution.py:320
  13.8 0.0 copy-start
  13.8 3.4 %copy-done = bf16[32,2,256,256]{3,2,1,0:T(8,128)(2,1)S(1)} copy-done((bf16[32,2,256,256]{3,2,1,0:T(8,128)(2,1)S(1)}, bf16[32,2,256,256]{3,2,1,0:T(8,128)(2,1)}, u32[]{:S(2)}) %copy-start) | copy-done | bytes 8388632
  17.2 0.0 copy-start.4
  17.2 0.7 copy-done.4
  17.9 0.0 copy-start.1
  17.9 0.0 copy-start.3
  17.9 1.7 %adjoint.2.refs_0_ = f32[272,256]{1,0:T(8,128)S(1)} custom-call(s32[2,32]{1,0:T(2,128)S(1)} %bitcast.1, bf16[32,2,256,256]{3,2,1,0:T(8,128)(2,1)S(1)} %copy-done, bf16[8,16,384]{2,1,0:T(8,128)(2,1)S(1)} %all_to_all.26.refs_2_), custom_call_target="tpu_custom_call" | custom-call | tf_op jit(solution)/shard_map/adjoint/pallas_call | solution.py:333
  19.6 2.5 %collective-permute-start.2 = (f32[272,256]{1,0:T(8,128)S(1)}, f32[272,256]{1,0:T(8,128)S(1)}, u32[]{:S(2)}, u32[]{:S(2)}) collective-permute-start(f32[272,256]{1,0:T(8,128)S(1)} %adjoint.2.refs_0_), channel_id=1, source_target_pairs={{0,24},{8,16},{16,8},{24,0},{1,25},{9,17},{17,9},{25,1},{2,26},{10... | collective-permute-start | bytes 835592 | tf_op jit(solution)/shard_map/ppermute | solution.py:315
  22.1 0.5 collective-permute-start.1
  22.6 0.5 collective-permute-start
  23.2 7.0 %collective-permute-done.2.refs_3_ = f32[272,256]{1,0:T(8,128)S(1)} collective-permute-done((f32[272,256]{1,0:T(8,128)S(1)}, f32[272,256]{1,0:T(8,128)S(1)}, u32[]{:S(2)}, u32[]{:S(2)}) %collective-permute-start.2) | collective-permute-done | bytes 278560 | tf_op jit(solution)/shard_map/ppermute | solution.py:315
  30.2 4.6 %collective-permute-done.1.refs_2_ = f32[272,256]{1,0:T(8,128)S(1)} collective-permute-done((f32[272,256]{1,0:T(8,128)S(1)}, f32[272,256]{1,0:T(8,128)S(1)}, u32[]{:S(2)}, u32[]{:S(2)}) %collective-permute-start.1) | collective-permute-done | bytes 278560 | tf_op jit(solution)/shard_map/ppermute | solution.py:315
  34.8 0.1 collective-permute-done.refs_1_
  34.9 0.0 copy-done.1
  34.9 4.6 %voxel.2 = (f32[8,5,8,128]{3,2,1,0:T(8,128)S(1)}, f32[8,128]{1,0:T(8,128)S(1)}, f32[1024,256]{1,0:T(8,128)S(1)}, bf16[1024,256]{1,0:T(8,128)(2,1)S(1)}, bf16[102...) custom-call(bf16[32,2,256,256]{3,2,1,0:T(8,128)(2,1)S(1)} %copy-done, ...), custom_call_target="tpu_custom_call" | custom-call | tf_op jit(solution)/shard_map/voxel/pallas_call | solution.py:333
  39.5 9.7 %all_to_all.27.part_ref = f32[8,5,8,128]{3,2,1,0:T(8,128)S(1)} all-to-all(f32[8,5,8,128]{3,2,1,0:T(8,128)S(1)} %get-tuple-element.20), channel_id=1, replica_groups=mesh['row'=4,'col'=8] {'col'}, dimensions={0} | all-to-all | bytes 327680 | tf_op jit(solution)/shard_map/all_to_all | solution.py:320
  49.2 0.0 copy-done.3
  49.2 0.8 ray.2
  50.0 9.1 %all_to_all.28.refs_1_ = bf16[8,16,384]{2,1,0:T(8,128)(2,1)S(1)} all-to-all(bf16[8,16,384]{2,1,0:T(8,128)(2,1)S(1)} %get-tuple-element.22), channel_id=1, replica_groups=mesh['row'=4,'col'=8] {'col'}, dimensions={0} | all-to-all | bytes 196608 | tf_op jit(solution)/shard_map/all_to_all | solution.py:320
  59.0 1.2 %adjoint.3.refs_0_ = bf16[272,256]{1,0:T(8,128)(2,1)S(1)} custom-call(bf16[32,2,256,256]{3,2,1,0:T(8,128)(2,1)S(1)} %copy-done.1, bf16[8,16,384]{2,1,0:T(8,128)(2,1)S(1)} %all_to_all.28.refs_1_), custom_call_target="tpu_custom_call" | custom-call | tf_op jit(solution)/shard_map/adjoint/pallas_call | solution.py:333
  60.2 1.7 %collective-permute-start.5 = (bf16[272,256]{1,0:T(8,128)(2,1)S(1)}, bf16[272,256]{1,0:T(8,128)(2,1)S(1)}, u32[]{:S(2)}, u32[]{:S(2)}) collective-permute-start(bf16[272,256]{1,0:T(8,128)(2,1)S(1)} %adjoint.3.refs_0_), channel_id=1, source_target_pairs={{0,24},{8,16},{16,8},{24,0},{1,25},{9,17},{17,9},{25,1},{2,26},{10... | collective-permute-start | bytes 417800 | tf_op jit(solution)/shard_map/ppermute | solution.py:315
  61.9 1.3 %collective-permute-start.4 = (bf16[272,256]{1,0:T(8,128)(2,1)S(1)}, bf16[272,256]{1,0:T(8,128)(2,1)S(1)}, u32[]{:S(2)}, u32[]{:S(2)}) collective-permute-start(bf16[272,256]{1,0:T(8,128)(2,1)S(1)} %adjoint.3.refs_0_), channel_id=1, source_target_pairs={{0,16},{8,24},{16,0},{24,8},{1,17},{9,25},{17,1},{25,9},{2,18},{10... | collective-permute-start | bytes 417800 | tf_op jit(solution)/shard_map/ppermute | solution.py:315
  63.2 0.5 collective-permute-start.3
  63.8 4.0 %collective-permute-done.5.refs_3_ = bf16[272,256]{1,0:T(8,128)(2,1)S(1)} collective-permute-done((bf16[272,256]{1,0:T(8,128)(2,1)S(1)}, bf16[272,256]{1,0:T(8,128)(2,1)S(1)}, u32[]{:S(2)}, u32[]{:S(2)}) %collective-permute-start.5) | collective-permute-done | bytes 139296 | tf_op jit(solution)/shard_map/ppermute | solution.py:315
  67.7 1.7 %collective-permute-done.4.refs_2_ = bf16[272,256]{1,0:T(8,128)(2,1)S(1)} collective-permute-done((bf16[272,256]{1,0:T(8,128)(2,1)S(1)}, bf16[272,256]{1,0:T(8,128)(2,1)S(1)}, u32[]{:S(2)}, u32[]{:S(2)}) %collective-permute-start.4) | collective-permute-done | bytes 139296 | tf_op jit(solution)/shard_map/ppermute | solution.py:315
  69.4 0.0 collective-permute-done.3.refs_1_
  69.4 3.5 %voxel.3 = (f32[8,5,8,128]{3,2,1,0:T(8,128)S(1)}, f32[8,128]{1,0:T(8,128)S(1)}, f32[1024,256]{1,0:T(8,128)}, bf16[1024,256]{1,0:T(8,128)(2,1)S(1)}) custom-call(bf16[32,2,256,256]{3,2,1,0:T(8,128)(2,1)S(1)} %copy-done.1, bf16[272,256]{1,0:T(8,128)(2,1)S(1)} %adjoint.3.refs_0_, bf16[272,256]{1,0:T(8,128)(2,1)S(1)} %collective-permute-done.3.refs_1_, ...), custom_call_target="tpu_custom_call" | custom-call | tf_op jit(solution)/shard_map/voxel/pallas_call | solution.py:333
  72.9 9.6 %all_to_all.29.part_ref = f32[8,5,8,128]{3,2,1,0:T(8,128)S(1)} all-to-all(f32[8,5,8,128]{3,2,1,0:T(8,128)S(1)} %get-tuple-element.27), channel_id=1, replica_groups=mesh['row'=4,'col'=8] {'col'}, dimensions={0} | all-to-all | bytes 327680 | tf_op jit(solution)/shard_map/all_to_all | solution.py:320
  82.5 0.8 ray.3
  83.3 3.1 %all-to-all-start.4 = ((f32[32,8,128]{2,1,0:T(8,128)}), f32[32,8,128]{2,1,0:T(8,128)S(1)}, u32[]{:S(2)}, u32[]{:S(2)}) async-start(f32[32,8,128]{2,1,0:T(8,128)} %get-tuple-element.30.refs_0_), calls=%async_computation.4 | async-start | bytes 262144 | tf_op jit(solution)/shard_map/all_to_all | solution.py:320
  86.4 1.0 %share.2 = (f32[512,256]{1,0:T(8,128)S(1)}, bf16[512,1024]{1,0:T(8,128)(2,1)S(1)}) custom-call(bf16[272,256]{1,0:T(8,128)(2,1)S(1)} %adjoint.3.refs_0_, f32[4,8,256]{2,1,0:T(8,128)S(1)} %get-tuple-element.32.refs_1_, bf16[1024,256]{1,0:T(8,128)(2,1)S(1)} %get-tuple-element.33.refs_2_, bf16[1024,256]{1,0:T(8,128)(2,1)S(1)} %get-tuple-element.34.refs_3_), custom_call_target="tpu_custom_call" | custom-call | tf_op jit(solution)/shard_map/share/pallas_call | solution.py:333
  87.5 0.5 share.3.refs_5_
  88.0 6.6 %all-to-all-done.4.last_ref = f32[32,8,128]{2,1,0:T(8,128)S(1)} async-done(((f32[32,8,128]{2,1,0:T(8,128)}), f32[32,8,128]{2,1,0:T(8,128)S(1)}, u32[]{:S(2)}, u32[]{:S(2)}) %all-to-all-start.4) | async-done | bytes 131104 | tf_op jit(solution)/shard_map/all_to_all | solution.py:320
  94.6 1.3 %final.1 = (f32[4,32768]{1,0:T(4,128)}, f32[4]{0:T(128)}) custom-call(f32[32,8,128]{2,1,0:T(8,128)S(1)} %all-to-all-done.4.last_ref, f32[8,128]{1,0:T(8,128)S(1)} %get-tuple-element.21.beta_ref.refs_0_, f32[8,128]{1,0:T(8,128)S(1)} %get-tuple-element.29.beta_ref.refs_1_, f32[8,128]{1,0:T(8,128)S(1)} %get-tuple-element.26.refs_7_.refs_2_, ...), custom_call_target="tpu_custom_call" | custom-call | tf_op jit(solution)/shard_map/final/pallas_call | solution.py:404
  (1 shorter events, 0.0 us)
Async XLA Ops:
  0.6 0.7 copy-start.2
  13.8 3.4 %copy-start = (bf16[32,2,256,256]{3,2,1,0:T(8,128)(2,1)S(1)}, bf16[32,2,256,256]{3,2,1,0:T(8,128)(2,1)}, u32[]{:S(2)}) copy-start(bf16[32,2,256,256]{3,2,1,0:T(8,128)(2,1)} %tiles_ref.3) | copy-start | bytes 25165828
  17.2 0.7 copy-start.4
  17.9 17.0 %copy-start.1 = (bf16[32,2,256,256]{3,2,1,0:T(8,128)(2,1)S(1)}, bf16[32,2,256,256]{3,2,1,0:T(8,128)(2,1)}, u32[]{:S(2)}) copy-start(bf16[32,2,256,256]{3,2,1,0:T(8,128)(2,1)} %tiles_ref.3) | copy-start | bytes 25165828
  17.9 31.3 %copy-start.3 = (f32[4,1024]{1,0:T(4,128)S(1)}, f32[4,1024]{1,0:T(4,128)}, u32[]{:S(2)}) copy-start(f32[4,1024]{1,0:T(4,128)} %left_ref.1) | copy-start | bytes 49156
  19.6 10.6 %collective-permute-start.2 = (f32[272,256]{1,0:T(8,128)S(1)}, f32[272,256]{1,0:T(8,128)S(1)}, u32[]{:S(2)}, u32[]{:S(2)}) collective-permute-start(f32[272,256]{1,0:T(8,128)S(1)} %adjoint.2.refs_0_), channel_id=1, source_target_pairs={{0,24},{8,16},{16,8},{24,0},{1,25},{9,17},{17,9},{25,1},{2,26},{10... | collective-permute-start | bytes 835592 | tf_op jit(solution)/shard_map/ppermute | solution.py:315
  22.1 12.6 %collective-permute-start.1 = (f32[272,256]{1,0:T(8,128)S(1)}, f32[272,256]{1,0:T(8,128)S(1)}, u32[]{:S(2)}, u32[]{:S(2)}) collective-permute-start(f32[272,256]{1,0:T(8,128)S(1)} %adjoint.2.refs_0_), channel_id=1, source_target_pairs={{0,16},{8,24},{16,0},{24,8},{1,17},{9,25},{17,1},{25,9},{2,18},{10... | collective-permute-start | bytes 835592 | tf_op jit(solution)/shard_map/ppermute | solution.py:315
  22.6 12.2 %collective-permute-start = (f32[272,256]{1,0:T(8,128)S(1)}, f32[272,256]{1,0:T(8,128)S(1)}, u32[]{:S(2)}, u32[]{:S(2)}) collective-permute-start(f32[272,256]{1,0:T(8,128)S(1)} %adjoint.2.refs_0_), channel_id=1, source_target_pairs={{0,8},{8,0},{16,24},{24,16},{1,9},{9,1},{17,25},{25,17},{2,10},{10... | collective-permute-start | bytes 835592 | tf_op jit(solution)/shard_map/ppermute | solution.py:315
  60.2 7.5 %collective-permute-start.5 = (bf16[272,256]{1,0:T(8,128)(2,1)S(1)}, bf16[272,256]{1,0:T(8,128)(2,1)S(1)}, u32[]{:S(2)}, u32[]{:S(2)}) collective-permute-start(bf16[272,256]{1,0:T(8,128)(2,1)S(1)} %adjoint.3.refs_0_), channel_id=1, source_target_pairs={{0,24},{8,16},{16,8},{24,0},{1,25},{9,17},{17,9},{25,1},{2,26},{10... | collective-permute-start | bytes 417800 | tf_op jit(solution)/shard_map/ppermute | solution.py:315
  61.9 7.4 %collective-permute-start.4 = (bf16[272,256]{1,0:T(8,128)(2,1)S(1)}, bf16[272,256]{1,0:T(8,128)(2,1)S(1)}, u32[]{:S(2)}, u32[]{:S(2)}) collective-permute-start(bf16[272,256]{1,0:T(8,128)(2,1)S(1)} %adjoint.3.refs_0_), channel_id=1, source_target_pairs={{0,16},{8,24},{16,0},{24,8},{1,17},{9,25},{17,1},{25,9},{2,18},{10... | collective-permute-start | bytes 417800 | tf_op jit(solution)/shard_map/ppermute | solution.py:315
  63.2 6.1 %collective-permute-start.3 = (bf16[272,256]{1,0:T(8,128)(2,1)S(1)}, bf16[272,256]{1,0:T(8,128)(2,1)S(1)}, u32[]{:S(2)}, u32[]{:S(2)}) collective-permute-start(bf16[272,256]{1,0:T(8,128)(2,1)S(1)} %adjoint.3.refs_0_), channel_id=1, source_target_pairs={{0,8},{8,0},{16,24},{24,16},{1,9},{9,1},{17,25},{25,17},{2,10},{10... | collective-permute-start | bytes 417800 | tf_op jit(solution)/shard_map/ppermute | solution.py:315
  83.3 11.3 %all-to-all-start.4 = ((f32[32,8,128]{2,1,0:T(8,128)}), f32[32,8,128]{2,1,0:T(8,128)S(1)}, u32[]{:S(2)}, u32[]{:S(2)}) async-start(f32[32,8,128]{2,1,0:T(8,128)} %get-tuple-element.30.refs_0_), calls=%async_computation.4 | async-start | bytes 262144 | tf_op jit(solution)/shard_map/all_to_all | solution.py:320

commit v6 on v5

--- a/solution.py
+++ b/solution.py
@@ -66,9 +66,14 @@
 
 def prepare_kernel(obs_ref, payload_ref):
     blocks = ray_blocks(obs_ref, obs_ref.shape[1] // (2 * LANES))
-    squares = tree_sum([b * b for b in blocks])
-    for c in range(payload_ref.shape[0]):
-        write_payload(payload_ref.at[c], blocks, squares)
+    write_payload(payload_ref, blocks, tree_sum([b * b for b in blocks]))
+
+
+def load_kernel(unread_ref, cols_ref, tiles_ref, held_ref, keys_ref, sem):
+    copy = pltpu.make_async_copy(tiles_ref, held_ref, sem)
+    copy.start()
+    keys_ref[...] = key_row(cols_ref)
+    copy.wait()
 
 
 def key_row(cols_ref):
@@ -120,25 +125,29 @@
 
 def adjoint_kernel(first, *refs):
     if first:
-        cols_ref, tiles_ref, payload_ref, term_ref = refs
+        keys_ref, tiles_ref = refs[:2]
+        payloads, term_ref = refs[2:-1], refs[-1]
+        shares = len(payloads)
     else:
         tiles_ref, payload_ref, term_ref = refs
+        shares = payload_ref.shape[0]
+        payloads = [payload_ref.at[c] for c in range(shares)]
     row_tiles, per_block = tiles_ref.shape[:2]
-    shares = payload_ref.shape[0]
     per_share = row_tiles // shares
     terms = row_tiles * per_block * RHS
-    squares = tree_sum([read_squares(payload_ref.at[c]) for c in range(shares)])
+    squares = tree_sum([read_squares(p) for p in payloads])
     if first:
         term_ref[terms : terms + 8] = jnp.concatenate([squares, jnp.zeros_like(squares)], axis=1)
-        term_ref[terms + 8 :] = key_row(cols_ref)
+        term_ref[terms + 8 :] = keys_ref[...]
     else:
         pieces = jnp.concatenate(in_two(squares), axis=1)
         term_ref[terms:] = jnp.concatenate([pieces, jnp.zeros_like(pieces)], axis=0).astype(jnp.bfloat16)
     low = low_half(2 * LANES)
     for c in range(shares):
-        rays = payload_ref[c, :, : 2 * LANES]
+        rays = payloads[c][:, : 2 * LANES]
+        owner = jnp.bitwise_xor(lax.axis_index("col"), c) if first else c
         for g in range(per_share // 2):
-            i = c * per_share + 2 * g
+            i = owner * per_share + 2 * g
             wide = [
                 jnp.dot(rays, tiles_ref[i + e, k], preferred_element_type=jnp.float32)[8 * g : 8 * g + 8]
                 for e in range(2)
@@ -151,7 +160,8 @@
                 ],
                 axis=0,
             )
-            term_ref[8 * i : 8 * i + 16] = value.astype(term_ref.dtype)
+            at = pl.multiple_of(8 * i, 16) if first else 8 * i
+            term_ref[pl.ds(at, 16), :] = value.astype(term_ref.dtype)
 
 
 def voxel_kernel(first, rows, tiles_ref, *refs):
@@ -327,7 +337,8 @@
     per_share = row_tiles // shares
     per_row = row_tiles * per_block * RHS
     share_rows = col_tiles // rows * RHS
-    payload = bf16(shares, max(16, 4 * per_share), 3 * LANES)
+    payload = bf16(max(16, 4 * per_share), 3 * LANES)
+    payloads = bf16(shares, *payload.shape)
 
     def call(kernel, name, out_shape, args, in_specs=None):
         return pl.pallas_call(
@@ -341,10 +352,8 @@
 
     def adjoint(payloads, first):
         terms = (f32 if first else bf16)(per_row + 16, tile_size)
-        args = [tile_cols.T] * first + [tile_values, payloads]
-        return call(
-            functools.partial(adjoint_kernel, first), "adjoint", terms, args, [SMEM] * first + [VMEM] * 2
-        )
+        args = [keys, tiles, *payloads] if first else [tiles, payloads]
+        return call(functools.partial(adjoint_kernel, first), "adjoint", terms, args)
 
     def voxel(term_list, previous):
         first = not previous
@@ -361,9 +370,8 @@
                 f32(rows * per_row, LANES),
                 f32(rows, 8, per_row),
             ]
-        args = [tile_values, *term_list, *previous]
-        specs = [VMEM] * len(args)
-        return call(functools.partial(voxel_kernel, first, rows), "voxel", out_shape, args, specs)
+        args = [tiles, *term_list, *previous]
+        return call(functools.partial(voxel_kernel, first, rows), "voxel", out_shape, args)
 
     def share(selector, values, after, first):
         out_shape = [f32(share_rows, tile_size)] + [bf16(share_rows, rows * per_row)] * first
@@ -376,17 +384,26 @@
         )
 
     def ray(parts, left_raw, beta, first):
-        out_shape = [f32(per_share, 8, LANES), f32(8, LANES), payload, f32(rows * shares, 8, LANES)]
+        out_shape = [f32(per_share, 8, LANES), f32(8, LANES), payloads, f32(rows * shares, 8, LANES)]
         return call(functools.partial(ray_kernel, first), "ray", out_shape, [parts, left_raw, beta])
 
     message = call(prepare_kernel, "prepare", payload, [observed])
+    tiles, keys = pl.pallas_call(
+        load_kernel,
+        out_shape=[jax.ShapeDtypeStruct(tile_values.shape, tile_values.dtype), f32(8, per_row)],
+        in_specs=[ANY, SMEM, HBM],
+        out_specs=[VMEM, VMEM],
+        scratch_shapes=[pltpu.SemaphoreType.DMA],
+        compiler_params=PARAMS,
+        name="load",
+    )(message, tile_cols.T, pltpu.with_memory_space_constraint(tile_values, pltpu.HBM))
     left_raw = observed
     betas, alphas, products = [], [], []
     previous = []
     waiting = None
     for iteration in range(ITERS + 1):
         first = iteration == 0
-        terms = adjoint(swap(message, "col"), first)
+        terms = adjoint(exchange(message, "col") if first else swap(message, "col"), first)
         if waiting:
             product, *pick = share(*waiting, [squares if iteration == ITERS else terms], not products)
             selector = pick[0] if pick else selector

time: 96.4 us -> 96.3 us (level)
  blocking collectives: 40.8 us -> 29.8 us
  starting transfers between devices: 10.2 us -> 19.8 us
  Pallas kernels: 15.5 us -> 18.9 us
  local copies, waits for them, and re-layouts: 4.78 us -> 1.4 us
  waiting for transfers between devices: 23.9 us -> 25.3 us
    all_to_all x4 -> x3, blocking collectives: 40.8 us -> 29.8 us  [swap(): return lax.all_to_all(values, axis, 0, 0)]
    ppermute x6 -> x13, starting transfers between devices: 7.11 us -> 16.7 us  [exchange(): got.append(lax.ppermute(value, axis, [(i, i ^ d) for i in range(size)]))]
    pallas_call x0 -> x1, Pallas kernels: none -> 3.94 us  [local(): pl.pallas_call(load_kernel, out_shape=[jax.ShapeDtypeStruct(tile_values.s...]
    unnamed x10 -> x6, local copies, waits for them, and re-layouts: 4.78 us -> 1.4 us
    ppermute x6 -> x13, waiting for transfers between devices: 17.3 us -> 18.6 us  [exchange(): got.append(lax.ppermute(value, axis, [(i, i ^ d) for i in range(size)]))]
  transfers between devices with their start and end apart: 7 -> 14, of which waited for: 6 -> 7; matrix products, arithmetic and copies ran while one was open for 0% -> 0% of each run, Pallas kernels for 2% -> 6%
where the time goes in v6:
time: 96.3 us; the launch traced here: 95.9 us
  blocking collectives  29.8 us (31%)
  waiting for transfers between devices  25.3 us (26%)
  starting transfers between devices  19.8 us (21%)
  Pallas kernels  18.9 us (20%)
  local copies, waits for them, and re-layouts  1.4 us (1%)
    all_to_all x3, blocking collectives, swap(): return lax.all_to_all(values, axis, 0, 0)  29.8 us
    ppermute x13, waiting for transfers between devices, exchange(): got.append(lax.ppermute(value, axis, [(i, i ^ d) for i in range(size)]))  18.6 us
    ppermute x13, starting transfers between devices, exchange(): got.append(lax.ppermute(value, axis, [(i, i ^ d) for i in range(size)]))  16.7 us
    pallas_call x9, Pallas kernels, call(): pl.pallas_call(kernel, out_shape=out_shape, in_specs=in_specs or [VMEM] *...  13.6 us
    all_to_all x1, waiting for transfers between devices, swap(): return lax.all_to_all(values, axis, 0, 0)  6.64 us
    pallas_call x1, Pallas kernels, local(): pl.pallas_call(load_kernel, out_shape=[jax.ShapeDtypeStruct(tile_values.s...  3.94 us
    all_to_all x1, starting transfers between devices, swap(): return lax.all_to_all(values, axis, 0, 0)  3.11 us
  transfers between devices with their start and end apart: 14, of which 7 were waited for; matrix products, arithmetic and copies ran while one was open for 0% of the time, Pallas kernels for 6%

profile of v6, /device:TPU:0, one launch (start us, length us, event | category | flops | bytes accessed | tf_op | source)
XLA Modules:
  0.0 95.9 jit_solution(14220197230584990034)
XLA Ops:
  0.6 0.0 copy-start
  0.6 0.7 copy-done
  1.4 4.6 %collective-permute-start.6 = (bf16[16,384]{1,0:T(8,128)(2,1)S(1)}, bf16[16,384]{1,0:T(8,128)(2,1)S(1)}, u32[]{:S(2)}, u32[]{:S(2)}) collective-permute-start(bf16[16,384]{1,0:T(8,128)(2,1)S(1)} %prepare.1.unread_ref.refs_2_), channel_id=1, source_target_pairs={{0,7},{1,6},{2,5},{3,4},{4,3},{5,2},{6,1},{7,0},{8,15},{9,14},{10,... | collective-permute-start | bytes 36872 | tf_op jit(solution)/shard_map/ppermute | solution.py:325
  5.9 0.6 collective-permute-start.5
  6.6 0.4 collective-permute-start.4
  7.0 2.2 %collective-permute-start.3 = (bf16[16,384]{1,0:T(8,128)(2,1)S(1)}, bf16[16,384]{1,0:T(8,128)(2,1)S(1)}, u32[]{:S(2)}, u32[]{:S(2)}) collective-permute-start(bf16[16,384]{1,0:T(8,128)(2,1)S(1)} %prepare.1.unread_ref.refs_2_), channel_id=1, source_target_pairs={{0,4},{1,5},{2,6},{3,7},{4,0},{5,1},{6,2},{7,3},{8,12},{9,13},{10,... | collective-permute-start | bytes 36872 | tf_op jit(solution)/shard_map/ppermute | solution.py:325
  9.1 1.0 %collective-permute-start.2 = (bf16[16,384]{1,0:T(8,128)(2,1)S(1)}, bf16[16,384]{1,0:T(8,128)(2,1)S(1)}, u32[]{:S(2)}, u32[]{:S(2)}) collective-permute-start(bf16[16,384]{1,0:T(8,128)(2,1)S(1)} %prepare.1.unread_ref.refs_2_), channel_id=1, source_target_pairs={{0,3},{1,2},{2,1},{3,0},{4,7},{5,6},{6,5},{7,4},{8,11},{9,10},{10,... | collective-permute-start | bytes 36872 | tf_op jit(solution)/shard_map/ppermute | solution.py:325
  10.1 0.0 collective-permute-done.6.refs_9_
  10.1 0.9 collective-permute-start.1
  11.0 0.5 collective-permute-done.5.refs_8_
  11.4 0.0 collective-permute-start
  11.4 0.0 copy-start.2
  11.4 0.7 copy-done.2
  12.1 3.9 %load.1 = (bf16[32,2,256,256]{3,2,1,0:T(8,128)(2,1)S(1)}, f32[8,256]{1,0:T(8,128)S(1)}) custom-call(bf16[16,384]{1,0:T(8,128)(2,1)S(1)} %prepare.1.unread_ref.refs_2_, s32[2,32]{1,0:T(2,128)S(1)} %bitcast.1, bf16[32,2,256,256]{3,2,1,0:T(8,128)(2,1)} %tiles_ref.1), custom_call_target="tpu_custom_call" | custom-call | tf_op jit(solution)/shard_map/load/pallas_call | solution.py:391
  16.0 0.0 collective-permute-done.4.refs_7_
  16.0 0.0 collective-permute-done.3.refs_6_
  16.1 0.0 collective-permute-done.2.refs_5_
  16.1 0.0 collective-permute-done.1.refs_4_
  16.1 0.0 collective-permute-done.refs_3_
  16.1 0.0 copy-start.1
  16.1 1.2 %adjoint.2.refs_0_ = f32[272,256]{1,0:T(8,128)S(1)} custom-call(f32[8,256]{1,0:T(8,128)S(1)} %get-tuple-element.23.refs_0_, bf16[32,2,256,256]{3,2,1,0:T(8,128)(2,1)S(1)} %get-tuple-element.22.refs_1_.tiles_ref.refs_0_, bf16[16,384]{1,0:T(8,128)(2,1)S(1)} %prepare.1.unread_ref.refs_2_, bf16[16,384]{1,0:T(8,128)(2,1)S(1)} %collective-permute-done.refs_3_, ...), custom_call_target="tpu_custom_call" | custom-call | tf_op jit(solution)/shard_map/adjoint/pallas_call | solution.py:344
  17.3 2.5 %collective-permute-start.9 = (f32[272,256]{1,0:T(8,128)S(1)}, f32[272,256]{1,0:T(8,128)S(1)}, u32[]{:S(2)}, u32[]{:S(2)}) collective-permute-start(f32[272,256]{1,0:T(8,128)S(1)} %adjoint.2.refs_0_), channel_id=1, source_target_pairs={{0,24},{8,16},{16,8},{24,0},{1,25},{9,17},{17,9},{25,1},{2,26},{10... | collective-permute-start | bytes 835592 | tf_op jit(solution)/shard_map/ppermute | solution.py:325
  19.8 0.5 collective-permute-start.8
  20.3 0.5 collective-permute-start.7
  20.8 6.9 %collective-permute-done.9.refs_3_ = f32[272,256]{1,0:T(8,128)S(1)} collective-permute-done((f32[272,256]{1,0:T(8,128)S(1)}, f32[272,256]{1,0:T(8,128)S(1)}, u32[]{:S(2)}, u32[]{:S(2)}) %collective-permute-start.9) | collective-permute-done | bytes 278560 | tf_op jit(solution)/shard_map/ppermute | solution.py:325
  27.7 5.5 %collective-permute-done.8.refs_2_ = f32[272,256]{1,0:T(8,128)S(1)} collective-permute-done((f32[272,256]{1,0:T(8,128)S(1)}, f32[272,256]{1,0:T(8,128)S(1)}, u32[]{:S(2)}, u32[]{:S(2)}) %collective-permute-start.8) | collective-permute-done | bytes 278560 | tf_op jit(solution)/shard_map/ppermute | solution.py:325
  33.3 0.1 collective-permute-done.7.refs_1_
  33.4 4.6 %voxel.2 = (f32[8,5,8,128]{3,2,1,0:T(8,128)S(1)}, f32[8,128]{1,0:T(8,128)S(1)}, f32[1024,256]{1,0:T(8,128)S(1)}, bf16[1024,256]{1,0:T(8,128)(2,1)S(1)}, bf16[102...) custom-call(bf16[32,2,256,256]{3,2,1,0:T(8,128)(2,1)S(1)} %get-tuple, ...), custom_call_target="tpu_custom_call" | custom-call | tf_op jit(solution)/shard_map/voxel/pallas_call | solution.py:344
  38.0 11.1 %all_to_all.21.part_ref = f32[8,5,8,128]{3,2,1,0:T(8,128)S(1)} all-to-all(f32[8,5,8,128]{3,2,1,0:T(8,128)S(1)} %get-tuple-element.24), channel_id=1, replica_groups=mesh['row'=4,'col'=8] {'col'}, dimensions={0} | all-to-all | bytes 327680 | tf_op jit(solution)/shard_map/all_to_all | solution.py:330
  49.1 0.0 copy-done.1
  49.1 0.8 ray.2
  49.9 9.1 %all_to_all.22.refs_1_ = bf16[8,16,384]{2,1,0:T(8,128)(2,1)S(1)} all-to-all(bf16[8,16,384]{2,1,0:T(8,128)(2,1)S(1)} %get-tuple-element.26), channel_id=1, replica_groups=mesh['row'=4,'col'=8] {'col'}, dimensions={0} | all-to-all | bytes 196608 | tf_op jit(solution)/shard_map/all_to_all | solution.py:330
  59.0 1.2 %adjoint.3.refs_0_ = bf16[272,256]{1,0:T(8,128)(2,1)S(1)} custom-call(bf16[32,2,256,256]{3,2,1,0:T(8,128)(2,1)S(1)} %get-tuple-element.22.refs_1_.tiles_ref.refs_0_, bf16[8,16,384]{2,1,0:T(8,128)(2,1)S(1)} %all_to_all.22.refs_1_), custom_call_target="tpu_custom_call" | custom-call | tf_op jit(solution)/shard_map/adjoint/pallas_call | solution.py:344
  60.2 1.7 %collective-permute-start.12 = (bf16[272,256]{1,0:T(8,128)(2,1)S(1)}, bf16[272,256]{1,0:T(8,128)(2,1)S(1)}, u32[]{:S(2)}, u32[]{:S(2)}) collective-permute-start(bf16[272,256]{1,0:T(8,128)(2,1)S(1)} %adjoint.3.refs_0_), channel_id=1, source_target_pairs={{0,24},{8,16},{16,8},{24,0},{1,25},{9,17},{17,9},{25,1},{2,26},{10... | collective-permute-start | bytes 417800 | tf_op jit(solution)/shard_map/ppermute | solution.py:325
  61.9 1.3 %collective-permute-start.11 = (bf16[272,256]{1,0:T(8,128)(2,1)S(1)}, bf16[272,256]{1,0:T(8,128)(2,1)S(1)}, u32[]{:S(2)}, u32[]{:S(2)}) collective-permute-start(bf16[272,256]{1,0:T(8,128)(2,1)S(1)} %adjoint.3.refs_0_), channel_id=1, source_target_pairs={{0,16},{8,24},{16,0},{24,8},{1,17},{9,25},{17,1},{25,9},{2,18},{10... | collective-permute-start | bytes 417800 | tf_op jit(solution)/shard_map/ppermute | solution.py:325
  63.2 0.5 collective-permute-start.10
  63.7 4.0 %collective-permute-done.12.refs_3_ = bf16[272,256]{1,0:T(8,128)(2,1)S(1)} collective-permute-done((bf16[272,256]{1,0:T(8,128)(2,1)S(1)}, bf16[272,256]{1,0:T(8,128)(2,1)S(1)}, u32[]{:S(2)}, u32[]{:S(2)}) %collective-permute-start.12) | collective-permute-done | bytes 139296 | tf_op jit(solution)/shard_map/ppermute | solution.py:325
  67.7 1.7 %collective-permute-done.11.refs_2_ = bf16[272,256]{1,0:T(8,128)(2,1)S(1)} collective-permute-done((bf16[272,256]{1,0:T(8,128)(2,1)S(1)}, bf16[272,256]{1,0:T(8,128)(2,1)S(1)}, u32[]{:S(2)}, u32[]{:S(2)}) %collective-permute-start.11) | collective-permute-done | bytes 139296 | tf_op jit(solution)/shard_map/ppermute | solution.py:325
  69.3 0.0 collective-permute-done.10.refs_1_
  69.3 3.5 %voxel.3 = (f32[8,5,8,128]{3,2,1,0:T(8,128)S(1)}, f32[8,128]{1,0:T(8,128)S(1)}, f32[1024,256]{1,0:T(8,128)}, bf16[1024,256]{1,0:T(8,128)(2,1)S(1)}) custom-call(bf16[32,2,256,256]{3,2,1,0:T(8,128)(2,1)S(1)} %get-tuple-element.22.refs_1_.tiles_ref.refs_0_, bf16[272,256]{1,0:T(8,128)(2,1)S(1)} %adjoint.3.refs_0_, ...), custom_call_target="tpu_custom_call" | custom-call | tf_op jit(solution)/shard_map/voxel/pallas_call | solution.py:344
  72.9 9.6 %all_to_all.23.part_ref = f32[8,5,8,128]{3,2,1,0:T(8,128)S(1)} all-to-all(f32[8,5,8,128]{3,2,1,0:T(8,128)S(1)} %get-tuple-element.31), channel_id=1, replica_groups=mesh['row'=4,'col'=8] {'col'}, dimensions={0} | all-to-all | bytes 327680 | tf_op jit(solution)/shard_map/all_to_all | solution.py:330
  82.5 0.8 ray.3
  83.3 3.1 %all-to-all-start.3 = ((f32[32,8,128]{2,1,0:T(8,128)}), f32[32,8,128]{2,1,0:T(8,128)S(1)}, u32[]{:S(2)}, u32[]{:S(2)}) async-start(f32[32,8,128]{2,1,0:T(8,128)} %get-tuple-element.34.refs_0_), calls=%async_computation.3 | async-start | bytes 262144 | tf_op jit(solution)/shard_map/all_to_all | solution.py:330
  86.4 1.0 %share.2 = (f32[512,256]{1,0:T(8,128)S(1)}, bf16[512,1024]{1,0:T(8,128)(2,1)S(1)}) custom-call(bf16[272,256]{1,0:T(8,128)(2,1)S(1)} %adjoint.3.refs_0_, f32[4,8,256]{2,1,0:T(8,128)S(1)} %get-tuple-element.36.refs_1_, bf16[1024,256]{1,0:T(8,128)(2,1)S(1)} %get-tuple-element.37.refs_2_, bf16[1024,256]{1,0:T(8,128)(2,1)S(1)} %get-tuple-element.38.refs_3_), custom_call_target="tpu_custom_call" | custom-call | tf_op jit(solution)/shard_map/share/pallas_call | solution.py:344
  87.4 0.5 share.3.refs_5_
  87.9 6.6 %all-to-all-done.3.last_ref = f32[32,8,128]{2,1,0:T(8,128)S(1)} async-done(((f32[32,8,128]{2,1,0:T(8,128)}), f32[32,8,128]{2,1,0:T(8,128)S(1)}, u32[]{:S(2)}, u32[]{:S(2)}) %all-to-all-start.3) | async-done | bytes 131104 | tf_op jit(solution)/shard_map/all_to_all | solution.py:330
  94.6 1.3 %final.1 = (f32[4,32768]{1,0:T(4,128)}, f32[4]{0:T(128)}) custom-call(f32[32,8,128]{2,1,0:T(8,128)S(1)} %all-to-all-done.3.last_ref, f32[8,128]{1,0:T(8,128)S(1)} %get-tuple-element.25.beta_ref.refs_0_, f32[8,128]{1,0:T(8,128)S(1)} %get-tuple-element.33.beta_ref.refs_1_, f32[8,128]{1,0:T(8,128)S(1)} %get-tuple-element.30.refs_7_.refs_2_, ...), custom_call_target="tpu_custom_call" | custom-call | tf_op jit(solution)/shard_map/final/pallas_call | solution.py:421
  (1 shorter events, 0.0 us)
Async XLA Ops:
  0.6 0.7 copy-start
  1.4 8.7 %collective-permute-start.6 = (bf16[16,384]{1,0:T(8,128)(2,1)S(1)}, bf16[16,384]{1,0:T(8,128)(2,1)S(1)}, u32[]{:S(2)}, u32[]{:S(2)}) collective-permute-start(bf16[16,384]{1,0:T(8,128)(2,1)S(1)} %prepare.1.unread_ref.refs_2_), channel_id=1, source_target_pairs={{0,7},{1,6},{2,5},{3,4},{4,3},{5,2},{6,1},{7,0},{8,15},{9,14},{10,... | collective-permute-start | bytes 36872 | tf_op jit(solution)/shard_map/ppermute | solution.py:325
  5.9 5.5 %collective-permute-start.5 = (bf16[16,384]{1,0:T(8,128)(2,1)S(1)}, bf16[16,384]{1,0:T(8,128)(2,1)S(1)}, u32[]{:S(2)}, u32[]{:S(2)}) collective-permute-start(bf16[16,384]{1,0:T(8,128)(2,1)S(1)} %prepare.1.unread_ref.refs_2_), channel_id=1, source_target_pairs={{0,6},{1,7},{2,4},{3,5},{4,2},{5,3},{6,0},{7,1},{8,14},{9,15},{10,... | collective-permute-start | bytes 36872 | tf_op jit(solution)/shard_map/ppermute | solution.py:325
  6.6 9.5 %collective-permute-start.4 = (bf16[16,384]{1,0:T(8,128)(2,1)S(1)}, bf16[16,384]{1,0:T(8,128)(2,1)S(1)}, u32[]{:S(2)}, u32[]{:S(2)}) collective-permute-start(bf16[16,384]{1,0:T(8,128)(2,1)S(1)} %prepare.1.unread_ref.refs_2_), channel_id=1, source_target_pairs={{0,5},{1,4},{2,7},{3,6},{4,1},{5,0},{6,3},{7,2},{8,13},{9,12},{10,... | collective-permute-start | bytes 36872 | tf_op jit(solution)/shard_map/ppermute | solution.py:325
  7.0 9.1 %collective-permute-start.3 = (bf16[16,384]{1,0:T(8,128)(2,1)S(1)}, bf16[16,384]{1,0:T(8,128)(2,1)S(1)}, u32[]{:S(2)}, u32[]{:S(2)}) collective-permute-start(bf16[16,384]{1,0:T(8,128)(2,1)S(1)} %prepare.1.unread_ref.refs_2_), channel_id=1, source_target_pairs={{0,4},{1,5},{2,6},{3,7},{4,0},{5,1},{6,2},{7,3},{8,12},{9,13},{10,... | collective-permute-start | bytes 36872 | tf_op jit(solution)/shard_map/ppermute | solution.py:325
  9.1 6.9 %collective-permute-start.2 = (bf16[16,384]{1,0:T(8,128)(2,1)S(1)}, bf16[16,384]{1,0:T(8,128)(2,1)S(1)}, u32[]{:S(2)}, u32[]{:S(2)}) collective-permute-start(bf16[16,384]{1,0:T(8,128)(2,1)S(1)} %prepare.1.unread_ref.refs_2_), channel_id=1, source_target_pairs={{0,3},{1,2},{2,1},{3,0},{4,7},{5,6},{6,5},{7,4},{8,11},{9,10},{10,... | collective-permute-start | bytes 36872 | tf_op jit(solution)/shard_map/ppermute | solution.py:325
  10.1 6.0 %collective-permute-start.1 = (bf16[16,384]{1,0:T(8,128)(2,1)S(1)}, bf16[16,384]{1,0:T(8,128)(2,1)S(1)}, u32[]{:S(2)}, u32[]{:S(2)}) collective-permute-start(bf16[16,384]{1,0:T(8,128)(2,1)S(1)} %prepare.1.unread_ref.refs_2_), channel_id=1, source_target_pairs={{0,2},{1,3},{2,0},{3,1},{4,6},{5,7},{6,4},{7,5},{8,10},{9,11},{10,... | collective-permute-start | bytes 36872 | tf_op jit(solution)/shard_map/ppermute | solution.py:325
  11.4 4.7 %collective-permute-start = (bf16[16,384]{1,0:T(8,128)(2,1)S(1)}, bf16[16,384]{1,0:T(8,128)(2,1)S(1)}, u32[]{:S(2)}, u32[]{:S(2)}) collective-permute-start(bf16[16,384]{1,0:T(8,128)(2,1)S(1)} %prepare.1.unread_ref.refs_2_), channel_id=1, source_target_pairs={{0,1},{1,0},{2,3},{3,2},{4,5},{5,4},{6,7},{7,6},{8,9},{9,8},{10,11... | collective-permute-start | bytes 36872 | tf_op jit(solution)/shard_map/ppermute | solution.py:325
  11.4 0.7 copy-start.2
  16.1 33.0 %copy-start.1 = (f32[4,1024]{1,0:T(4,128)S(1)}, f32[4,1024]{1,0:T(4,128)}, u32[]{:S(2)}) copy-start(f32[4,1024]{1,0:T(4,128)} %left_ref.1) | copy-start | bytes 49156
  17.3 10.5 %collective-permute-start.9 = (f32[272,256]{1,0:T(8,128)S(1)}, f32[272,256]{1,0:T(8,128)S(1)}, u32[]{:S(2)}, u32[]{:S(2)}) collective-permute-start(f32[272,256]{1,0:T(8,128)S(1)} %adjoint.2.refs_0_), channel_id=1, source_target_pairs={{0,24},{8,16},{16,8},{24,0},{1,25},{9,17},{17,9},{25,1},{2,26},{10... | collective-permute-start | bytes 835592 | tf_op jit(solution)/shard_map/ppermute | solution.py:325
  19.8 13.5 %collective-permute-start.8 = (f32[272,256]{1,0:T(8,128)S(1)}, f32[272,256]{1,0:T(8,128)S(1)}, u32[]{:S(2)}, u32[]{:S(2)}) collective-permute-start(f32[272,256]{1,0:T(8,128)S(1)} %adjoint.2.refs_0_), channel_id=1, source_target_pairs={{0,16},{8,24},{16,0},{24,8},{1,17},{9,25},{17,1},{25,9},{2,18},{10... | collective-permute-start | bytes 835592 | tf_op jit(solution)/shard_map/ppermute | solution.py:325
  20.3 13.1 %collective-permute-start.7 = (f32[272,256]{1,0:T(8,128)S(1)}, f32[272,256]{1,0:T(8,128)S(1)}, u32[]{:S(2)}, u32[]{:S(2)}) collective-permute-start(f32[272,256]{1,0:T(8,128)S(1)} %adjoint.2.refs_0_), channel_id=1, source_target_pairs={{0,8},{8,0},{16,24},{24,16},{1,9},{9,1},{17,25},{25,17},{2,10},{10... | collective-permute-start | bytes 835592 | tf_op jit(solution)/shard_map/ppermute | solution.py:325
  60.2 7.5 %collective-permute-start.12 = (bf16[272,256]{1,0:T(8,128)(2,1)S(1)}, bf16[272,256]{1,0:T(8,128)(2,1)S(1)}, u32[]{:S(2)}, u32[]{:S(2)}) collective-permute-start(bf16[272,256]{1,0:T(8,128)(2,1)S(1)} %adjoint.3.refs_0_), channel_id=1, source_target_pairs={{0,24},{8,16},{16,8},{24,0},{1,25},{9,17},{17,9},{25,1},{2,26},{10... | collective-permute-start | bytes 417800 | tf_op jit(solution)/shard_map/ppermute | solution.py:325
  61.9 7.4 %collective-permute-start.11 = (bf16[272,256]{1,0:T(8,128)(2,1)S(1)}, bf16[272,256]{1,0:T(8,128)(2,1)S(1)}, u32[]{:S(2)}, u32[]{:S(2)}) collective-permute-start(bf16[272,256]{1,0:T(8,128)(2,1)S(1)} %adjoint.3.refs_0_), channel_id=1, source_target_pairs={{0,16},{8,24},{16,0},{24,8},{1,17},{9,25},{17,1},{25,9},{2,18},{10... | collective-permute-start | bytes 417800 | tf_op jit(solution)/shard_map/ppermute | solution.py:325
  63.2 6.1 %collective-permute-start.10 = (bf16[272,256]{1,0:T(8,128)(2,1)S(1)}, bf16[272,256]{1,0:T(8,128)(2,1)S(1)}, u32[]{:S(2)}, u32[]{:S(2)}) collective-permute-start(bf16[272,256]{1,0:T(8,128)(2,1)S(1)} %adjoint.3.refs_0_), channel_id=1, source_target_pairs={{0,8},{8,0},{16,24},{24,16},{1,9},{9,1},{17,25},{25,17},{2,10},{10... | collective-permute-start | bytes 417800 | tf_op jit(solution)/shard_map/ppermute | solution.py:325
  83.3 11.3 %all-to-all-start.3 = ((f32[32,8,128]{2,1,0:T(8,128)}), f32[32,8,128]{2,1,0:T(8,128)S(1)}, u32[]{:S(2)}, u32[]{:S(2)}) async-start(f32[32,8,128]{2,1,0:T(8,128)} %get-tuple-element.34.refs_0_), calls=%async_computation.3 | async-start | bytes 262144 | tf_op jit(solution)/shard_map/all_to_all | solution.py:330

commit v7 on v6

--- a/solution.py
+++ b/solution.py
@@ -64,16 +64,13 @@
     return blocks
 
 
-def prepare_kernel(obs_ref, payload_ref):
+def prepare_kernel(obs_ref, unread_ref, payload_ref):
     blocks = ray_blocks(obs_ref, obs_ref.shape[1] // (2 * LANES))
     write_payload(payload_ref, blocks, tree_sum([b * b for b in blocks]))
 
 
-def load_kernel(unread_ref, cols_ref, tiles_ref, held_ref, keys_ref, sem):
-    copy = pltpu.make_async_copy(tiles_ref, held_ref, sem)
-    copy.start()
+def keys_kernel(unread_ref, cols_ref, keys_ref):
     keys_ref[...] = key_row(cols_ref)
-    copy.wait()
 
 
 def key_row(cols_ref):
@@ -126,7 +123,7 @@
 def adjoint_kernel(first, *refs):
     if first:
         keys_ref, tiles_ref = refs[:2]
-        payloads, term_ref = refs[2:-1], refs[-1]
+        payloads, (term_ref, lower_ref) = refs[2:-2], refs[-2:]
         shares = len(payloads)
     else:
         tiles_ref, payload_ref, term_ref = refs
@@ -136,13 +133,14 @@
     per_share = row_tiles // shares
     terms = row_tiles * per_block * RHS
     squares = tree_sum([read_squares(p) for p in payloads])
+    low = low_half(2 * LANES)
+    pieces = jnp.concatenate(in_two(squares), axis=1)
+    extra = jnp.zeros_like(pieces)
     if first:
-        term_ref[terms : terms + 8] = jnp.concatenate([squares, jnp.zeros_like(squares)], axis=1)
-        term_ref[terms + 8 :] = keys_ref[...]
-    else:
-        pieces = jnp.concatenate(in_two(squares), axis=1)
-        term_ref[terms:] = jnp.concatenate([pieces, jnp.zeros_like(pieces)], axis=0).astype(jnp.bfloat16)
-    low = low_half(2 * LANES)
+        keys = keys_ref[...]
+        coarse = jnp.floor(keys * (1.0 / 64))
+        extra = jnp.where(low, coarse, keys - 64 * coarse)
+    term_ref[terms:] = jnp.concatenate([pieces, extra], axis=0).astype(jnp.bfloat16)
     for c in range(shares):
         rays = payloads[c][:, : 2 * LANES]
         owner = jnp.bitwise_xor(lax.axis_index("col"), c) if first else c
@@ -161,13 +159,16 @@
                 axis=0,
             )
             at = pl.multiple_of(8 * i, 16) if first else 8 * i
-            term_ref[pl.ds(at, 16), :] = value.astype(term_ref.dtype)
+            upper = value.astype(jnp.bfloat16)
+            term_ref[pl.ds(at, 16), :] = upper
+            if first:
+                lower_ref[pl.ds(at, 16), :] = (value - upper.astype(jnp.float32)).astype(jnp.bfloat16)
 
 
 def voxel_kernel(first, rows, tiles_ref, *refs):
     terms, refs = refs[:rows], list(refs[rows:])
     if first:
-        out_ref, beta_ref, raw_ref, all_ref, low_ref, equal_ref, weight_ref, keys_ref = refs
+        out_ref, beta_ref, raw_ref, all_ref, equal_ref, weight_ref, keys_ref = refs
     else:
         equal_ref, weight_ref, right_ref, alpha_ref = refs[:4]
         out_ref, beta_ref, raw_ref, all_ref = refs[-4:]
@@ -176,21 +177,17 @@
     shares = out_ref.shape[0]
     per_share = row_tiles // shares
     per_row = row_tiles * per_block * RHS
+    low = low_half(2 * LANES)
     squares = []
     for d in range(rows):
         slot = jnp.bitwise_xor(my_row, d)
         at = pl.ds(pl.multiple_of(slot * per_row, per_row), per_row)
+        all_ref[at, :] = terms[d][:per_row]
+        extra = terms[d][per_row:].astype(jnp.float32)
+        squares.append(extra[:8, :LANES] + extra[:8, LANES:])
         if first:
-            value = terms[d][:per_row]
-            upper = value.astype(jnp.bfloat16)
-            all_ref[at, :] = upper
-            low_ref[at, :] = (value - upper.astype(jnp.float32)).astype(jnp.bfloat16)
-            squares.append(terms[d][per_row : per_row + 8, :LANES])
-            keys_ref[slot] = terms[d][per_row + 8 :]
-        else:
-            all_ref[at, :] = terms[d][:per_row]
-            pieces = terms[d][per_row:].astype(jnp.float32)[:8]
-            squares.append(pieces[:, :LANES] + pieces[:, LANES:])
+            pieces = jnp.where(low, extra[8:] * 64, extra[8:])
+            keys_ref[slot] = pieces + pltpu.roll(pieces, 4, 0)
     if first:
         fill_equal(keys_ref, equal_ref, weight_ref)
     beta = norm_of(tree_sum(squares))
@@ -202,8 +199,6 @@
     for s in range(rows):
         same = equal_ref[s * per_row : (s + 1) * per_row, :]
         summed = jnp.dot(same, all_ref[...], preferred_element_type=jnp.float32)
-        if first:
-            summed = summed + jnp.dot(same, low_ref[...], preferred_element_type=jnp.float32)
         for m in range(per_row // 8):
             at = s * per_row + 8 * m
             raw = summed[8 * m : 8 * m + 8] * wide_scale
@@ -212,7 +207,6 @@
             raw_ref[at : at + 8] = raw
             square = raw * raw
             acc = acc + (square[:, :LANES] + square[:, LANES:]) * weight_ref[at : at + 8]
-    low = low_half(2 * LANES)
     own = my_row * per_row
     for c in range(shares):
         for g in range(per_share // 2):
@@ -231,13 +225,17 @@
         out_ref[c, per_share] = acc
 
 
-def share_kernel(pieces, first, unread, *refs):
-    refs = refs[unread:]
-    if first:
-        keys_ref, values, out_ref, pick_ref = refs[0], refs[1 : 1 + pieces], refs[-2], refs[-1]
-        fill_pick(keys_ref, pick_ref)
-    else:
-        pick_ref, values, out_ref = refs[0], refs[1 : 1 + pieces], refs[-1]
+def share_kernel(remainders, *refs):
+    pick_ref, all_ref = refs[1:3]
+    lower_terms, out_ref = refs[3 : 3 + remainders], refs[3 + remainders]
+    values = [all_ref]
+    if remainders:
+        held = refs[-1]
+        per_row = lower_terms[0].shape[0]
+        for d, term in enumerate(lower_terms):
+            slot = jnp.bitwise_xor(lax.axis_index("row"), d)
+            held[pl.ds(pl.multiple_of(slot * per_row, per_row), per_row), :] = term[...]
+        values.append(held)
     step = 128
     for at in range(0, out_ref.shape[0], step):
         pick = pick_ref[at : at + step, :]
@@ -246,7 +244,15 @@
         )
 
 
-def ray_kernel(first, part_ref, left_ref, beta_ref, raw_ref, alpha_ref, payload_ref, acc_ref):
+def pick_kernel(unread_ref, keys_ref, pick_ref):
+    fill_pick(keys_ref, pick_ref)
+
+
+def ray_kernel(first, part_ref, left_ref, beta_ref, *refs):
+    if not first:
+        refs[-1][...] = refs[0][...]
+        refs = refs[1:-1]
+    raw_ref, alpha_ref, payload_ref, acc_ref = refs
     shares, count = part_ref.shape[0], raw_ref.shape[0]
     alpha = norm_of(tree_sum([part_ref[c, count] for c in range(shares)]))
     alpha_ref[...] = alpha
@@ -340,20 +346,21 @@
     payload = bf16(max(16, 4 * per_share), 3 * LANES)
     payloads = bf16(shares, *payload.shape)
 
-    def call(kernel, name, out_shape, args, in_specs=None):
+    def call(kernel, name, out_shape, args, in_specs=None, scratch=()):
         return pl.pallas_call(
             kernel,
             out_shape=out_shape,
             in_specs=in_specs or [VMEM] * len(args),
             out_specs=jax.tree.map(lambda _: VMEM, out_shape),
+            scratch_shapes=list(scratch),
             compiler_params=PARAMS,
             name=name,
         )(*args)
 
     def adjoint(payloads, first):
-        terms = (f32 if first else bf16)(per_row + 16, tile_size)
-        args = [keys, tiles, *payloads] if first else [tiles, payloads]
-        return call(functools.partial(adjoint_kernel, first), "adjoint", terms, args)
+        out_shape = [bf16(per_row + 16, tile_size)] + [bf16(per_row, tile_size)] * first
+        args = [keys, tile_values, *payloads] if first else [tile_values, payloads]
+        return call(functools.partial(adjoint_kernel, first), "adjoint", out_shape, args)
 
     def voxel(term_list, previous):
         first = not previous
@@ -365,59 +372,53 @@
         ]
         if first:
             out_shape += [
-                bf16(rows * per_row, tile_size),
                 bf16(rows * per_row, rows * per_row),
                 f32(rows * per_row, LANES),
                 f32(rows, 8, per_row),
             ]
-        args = [tiles, *term_list, *previous]
+        args = [tile_values, *term_list, *previous]
         return call(functools.partial(voxel_kernel, first, rows), "voxel", out_shape, args)
 
-    def share(selector, values, after, first):
-        out_shape = [f32(share_rows, tile_size)] + [bf16(share_rows, rows * per_row)] * first
-        return call(
-            functools.partial(share_kernel, len(values), first, len(after)),
-            "share",
-            out_shape,
-            [*after, selector, *values],
-            [ANY] * len(after) + [VMEM] * (1 + len(values)),
-        )
-
-    def ray(parts, left_raw, beta, first):
+    def share(selector, all_terms, lower_terms):
+        scratch = [pltpu.VMEM((rows * per_row, tile_size), jnp.bfloat16)] * (len(lower_terms) > 0)
+        kernel = functools.partial(share_kernel, len(lower_terms))
+        args = [squares, selector, all_terms, *lower_terms]
+        specs = [ANY] + [VMEM] * (len(args) - 1)
+        return call(kernel, "share", f32(share_rows, tile_size), args, specs, scratch)
+
+    def ray(parts, left_raw, beta, passed):
         out_shape = [f32(per_share, 8, LANES), f32(8, LANES), payloads, f32(rows * shares, 8, LANES)]
-        return call(functools.partial(ray_kernel, first), "ray", out_shape, [parts, left_raw, beta])
-
-    message = call(prepare_kernel, "prepare", payload, [observed])
-    tiles, keys = pl.pallas_call(
-        load_kernel,
-        out_shape=[jax.ShapeDtypeStruct(tile_values.shape, tile_values.dtype), f32(8, per_row)],
-        in_specs=[ANY, SMEM, HBM],
-        out_specs=[VMEM, VMEM],
-        scratch_shapes=[pltpu.SemaphoreType.DMA],
-        compiler_params=PARAMS,
-        name="load",
-    )(message, tile_cols.T, pltpu.with_memory_space_constraint(tile_values, pltpu.HBM))
+        out_shape += [bf16(per_row, tile_size) for _ in passed]
+        return call(functools.partial(ray_kernel, not passed), "ray", out_shape, [parts, left_raw, beta, *passed])
+
+    far = pltpu.with_memory_space_constraint(tile_values, pltpu.HBM)
+    message = call(prepare_kernel, "prepare", payload, [observed, far], [VMEM, HBM])
+    keys = call(keys_kernel, "keys", f32(8, per_row), [message, tile_cols.T], [ANY, SMEM])
     left_raw = observed
-    betas, alphas, products = [], [], []
+    betas, alphas, combined = [], [], []
     previous = []
-    waiting = None
     for iteration in range(ITERS + 1):
         first = iteration == 0
-        terms = adjoint(exchange(message, "col") if first else swap(message, "col"), first)
-        if waiting:
-            product, *pick = share(*waiting, [squares if iteration == ITERS else terms], not products)
-            selector = pick[0] if pick else selector
-            products.append(product)
+        terms, *lower = adjoint(exchange(message, "col") if first else swap(message, "col"), first)
+        if iteration == 1:
+            selector = call(pick_kernel, "pick", bf16(share_rows, rows * per_row), [terms, all_keys], [ANY, VMEM])
         parts, beta, right_raw, upper_terms, *fixed = voxel(exchange(terms, "row"), previous)
-        if first:
-            lower_terms, equal, weight, selector = fixed
         if iteration == ITERS:
             break
-        waiting = (selector, [upper_terms, lower_terms] if first else [upper_terms])
-        left_raw, alpha, message, squares = ray(swap(parts, "col"), left_raw, beta, first)
+        if first:
+            equal, weight, all_keys = fixed
+            remainder = lower[0]
+        combined.append(upper_terms)
+        left_raw, alpha, message, squares, *passed = ray(
+            swap(parts, "col"), left_raw, beta, [] if first else [remainder]
+        )
+        if passed:
+            remainder = passed[0]
         betas.append(beta)
         alphas.append(alpha)
         previous = [equal, weight, right_raw, alpha]
+    remainders = exchange(remainder, "row")
+    products = [share(selector, c, [] if i else remainders) for i, c in enumerate(combined)]
     result, ratio = pl.pallas_call(
         functools.partial(final_kernel, ITERS),
         out_shape=[f32(RHS, col_tiles // rows * tile_size), f32(RHS)],

time: 96.3 us -> 89.8 us (0.933)
  waiting for transfers between devices: 25.3 us -> 19.4 us
  Pallas kernels: 18.9 us -> 14.9 us
  starting transfers between devices: 19.8 us -> 23.4 us
    all_to_all x1, waiting for transfers between devices: 6.64 us -> 0.01 us  [swap(): return lax.all_to_all(values, axis, 0, 0)]
    pallas_call x1 -> x0, Pallas kernels: 3.94 us -> none  [local(): pl.pallas_call(load_kernel, out_shape=[jax.ShapeDtypeStruct(tile_values.s...]
    ppermute x13 -> x16, starting transfers between devices: 16.7 us -> 20.2 us  [exchange(): got.append(lax.ppermute(value, axis, [(i, i ^ d) for i in range(size)]))]
    ppermute x13 -> x16, waiting for transfers between devices: 18.6 us -> 19.4 us  [exchange(): got.append(lax.ppermute(value, axis, [(i, i ^ d) for i in range(size)]))]
    pallas_call x9 -> x11, Pallas kernels: 13.6 us -> 13.5 us  [call(): pl.pallas_call(kernel, out_shape=out_shape, in_specs=in_specs or [VMEM] *...]
  transfers between devices with their start and end apart: 14 -> 17, of which waited for: 7 -> 10; matrix products, arithmetic and copies ran while one was open for 0% -> 0% of each run, Pallas kernels for 6% -> 2%
where the time goes in v7:
time: 89.8 us; the launch traced here: 89.4 us
  blocking collectives  30.1 us (34%)
  starting transfers between devices  23.4 us (26%)
  waiting for transfers between devices  19.4 us (22%)
  Pallas kernels  14.9 us (17%)
    all_to_all x3, blocking collectives, swap(): return lax.all_to_all(values, axis, 0, 0)  30.1 us
    ppermute x16, starting transfers between devices, exchange(): got.append(lax.ppermute(value, axis, [(i, i ^ d) for i in range(size)]))  20.2 us
    ppermute x16, waiting for transfers between devices, exchange(): got.append(lax.ppermute(value, axis, [(i, i ^ d) for i in range(size)]))  19.4 us
    pallas_call x11, Pallas kernels, call(): pl.pallas_call(kernel, out_shape=out_shape, in_specs=in_specs or [VMEM] *...  13.5 us
    all_to_all x1, starting transfers between devices, swap(): return lax.all_to_all(values, axis, 0, 0)  3.16 us
  transfers between devices with their start and end apart: 17, of which 10 were waited for; matrix products, arithmetic and copies ran while one was open for 0% of the time, Pallas kernels for 2%

profile of v7, /device:TPU:0, one launch (start us, length us, event | category | flops | bytes accessed | tf_op | source)
XLA Modules:
  0.0 89.4 jit_solution(6051462423671865009)
XLA Ops:
  0.6 0.0 copy-start
  0.6 0.0 copy-start.1
  0.6 0.9 copy-done.1
  1.5 0.0 copy-start.2
  1.5 4.6 %collective-permute-start.6 = (bf16[16,384]{1,0:T(8,128)(2,1)S(1)}, bf16[16,384]{1,0:T(8,128)(2,1)S(1)}, u32[]{:S(2)}, u32[]{:S(2)}) collective-permute-start(bf16[16,384]{1,0:T(8,128)(2,1)S(1)} %prepare.1.unread_ref.refs_2_), channel_id=1, source_target_pairs={{0,7},{1,6},{2,5},{3,4},{4,3},{5,2},{6,1},{7,0},{8,15},{9,14},{10,... | collective-permute-start | bytes 36872 | tf_op jit(solution)/shard_map/ppermute | solution.py:331
  6.1 0.6 collective-permute-start.5
  6.7 0.4 collective-permute-start.4
  7.1 2.2 %collective-permute-start.3 = (bf16[16,384]{1,0:T(8,128)(2,1)S(1)}, bf16[16,384]{1,0:T(8,128)(2,1)S(1)}, u32[]{:S(2)}, u32[]{:S(2)}) collective-permute-start(bf16[16,384]{1,0:T(8,128)(2,1)S(1)} %prepare.1.unread_ref.refs_2_), channel_id=1, source_target_pairs={{0,4},{1,5},{2,6},{3,7},{4,0},{5,1},{6,2},{7,3},{8,12},{9,13},{10,... | collective-permute-start | bytes 36872 | tf_op jit(solution)/shard_map/ppermute | solution.py:331
  9.3 1.0 %collective-permute-start.2 = (bf16[16,384]{1,0:T(8,128)(2,1)S(1)}, bf16[16,384]{1,0:T(8,128)(2,1)S(1)}, u32[]{:S(2)}, u32[]{:S(2)}) collective-permute-start(bf16[16,384]{1,0:T(8,128)(2,1)S(1)} %prepare.1.unread_ref.refs_2_), channel_id=1, source_target_pairs={{0,3},{1,2},{2,1},{3,0},{4,7},{5,6},{6,5},{7,4},{8,11},{9,10},{10,... | collective-permute-start | bytes 36872 | tf_op jit(solution)/shard_map/ppermute | solution.py:331
  10.3 0.0 collective-permute-done.6.refs_9_
  10.3 0.9 collective-permute-start.1
  11.1 0.5 collective-permute-done.5.refs_8_
  11.6 0.0 collective-permute-start
  11.6 0.0 copy-done.2
  11.6 0.6 keys.1.refs_0_
  12.2 0.0 collective-permute-done.4.refs_7_
  12.2 0.0 collective-permute-done.3.refs_6_
  12.2 0.2 collective-permute-done.2.refs_5_
  12.4 1.6 %collective-permute-done.1.refs_4_ = bf16[16,384]{1,0:T(8,128)(2,1)S(1)} collective-permute-done((bf16[16,384]{1,0:T(8,128)(2,1)S(1)}, bf16[16,384]{1,0:T(8,128)(2,1)S(1)}, u32[]{:S(2)}, u32[]{:S(2)}) %collective-permute-start.1) | collective-permute-done | bytes 12320 | tf_op jit(solution)/shard_map/ppermute | solution.py:331
  14.0 0.0 collective-permute-done.refs_3_
  14.0 0.0 copy-done
  14.0 1.2 %adjoint.2 = (bf16[272,256]{1,0:T(8,128)(2,1)S(1)}, bf16[256,256]{1,0:T(8,128)(2,1)S(1)}) custom-call(f32[8,256]{1,0:T(8,128)S(1)} %keys.1.refs_0_, bf16[32,2,256,256]{3,2,1,0:T(8,128)(2,1)S(1)} %copy-done, bf16[16,384]{1,0:T(8,128)(2,1)S(1)} %prepare.1.unread_ref.refs_2_, bf16[16,384]{1,0:T(8,128)(2,1)S(1)} %collective-permute-done.refs_3_, ...), custom_call_target="tpu_custom_call" | custom-call | tf_op jit(solution)/shard_map/adjoint/pallas_call | solution.py:350
  15.2 2.5 %collective-permute-start.9 = (bf16[272,256]{1,0:T(8,128)(2,1)S(1)}, bf16[272,256]{1,0:T(8,128)(2,1)S(1)}, u32[]{:S(2)}, u32[]{:S(2)}) collective-permute-start(bf16[272,256]{1,0:T(8,128)(2,1)S(1)} %get-tuple-element.20.refs_0_), channel_id=1, source_target_pairs={{0,24},{8,16},{16,8},{24,0},{1,25},{9,17},{17,9},{25,1},{2,26},{10... | collective-permute-start | bytes 417800 | tf_op jit(solution)/shard_map/ppermute | solution.py:331
  17.7 0.5 collective-permute-start.8
  18.2 0.5 collective-permute-start.7
  18.7 3.3 %collective-permute-done.9.refs_3_ = bf16[272,256]{1,0:T(8,128)(2,1)S(1)} collective-permute-done((bf16[272,256]{1,0:T(8,128)(2,1)S(1)}, bf16[272,256]{1,0:T(8,128)(2,1)S(1)}, u32[]{:S(2)}, u32[]{:S(2)}) %collective-permute-start.9) | collective-permute-done | bytes 139296 | tf_op jit(solution)/shard_map/ppermute | solution.py:331
  22.0 1.9 %collective-permute-done.8.refs_2_ = bf16[272,256]{1,0:T(8,128)(2,1)S(1)} collective-permute-done((bf16[272,256]{1,0:T(8,128)(2,1)S(1)}, bf16[272,256]{1,0:T(8,128)(2,1)S(1)}, u32[]{:S(2)}, u32[]{:S(2)}) %collective-permute-start.8) | collective-permute-done | bytes 139296 | tf_op jit(solution)/shard_map/ppermute | solution.py:331
  23.9 0.1 collective-permute-done.7.refs_1_
  24.0 4.0 %voxel.2 = (f32[8,5,8,128]{3,2,1,0:T(8,128)S(1)}, f32[8,128]{1,0:T(8,128)S(1)}, f32[1024,256]{1,0:T(8,128)S(1)}, bf16[1024,256]{1,0:T(8,128)(2,1)S(1)}, bf16[102...) custom-call(bf16[32,2,256,256]{3,2,1,0:T(8,128)(2,1)S(1)} %copy-done, ...), custom_call_target="tpu_custom_call" | custom-call | tf_op jit(solution)/shard_map/voxel/pallas_call | solution.py:350
  27.9 11.4 %all_to_all.21.part_ref = f32[8,5,8,128]{3,2,1,0:T(8,128)S(1)} all-to-all(f32[8,5,8,128]{3,2,1,0:T(8,128)S(1)} %get-tuple-element.21), channel_id=1, replica_groups=mesh['row'=4,'col'=8] {'col'}, dimensions={0} | all-to-all | bytes 327680 | tf_op jit(solution)/shard_map/all_to_all | solution.py:336
  39.3 0.8 ray.2
  40.1 9.1 %all_to_all.22.refs_1_ = bf16[8,16,384]{2,1,0:T(8,128)(2,1)S(1)} all-to-all(bf16[8,16,384]{2,1,0:T(8,128)(2,1)S(1)} %get-tuple-element.23), channel_id=1, replica_groups=mesh['row'=4,'col'=8] {'col'}, dimensions={0} | all-to-all | bytes 196608 | tf_op jit(solution)/shard_map/all_to_all | solution.py:336
  49.2 1.2 %adjoint.3.refs_0_.unread_ref = bf16[272,256]{1,0:T(8,128)(2,1)S(1)} custom-call(bf16[32,2,256,256]{3,2,1,0:T(8,128)(2,1)S(1)} %copy-done, bf16[8,16,384]{2,1,0:T(8,128)(2,1)S(1)} %all_to_all.22.refs_1_), custom_call_target="tpu_custom_call" | custom-call | tf_op jit(solution)/shard_map/adjoint/pallas_call | solution.py:350
  50.4 1.8 %collective-permute-start.12 = (bf16[272,256]{1,0:T(8,128)(2,1)S(1)}, bf16[272,256]{1,0:T(8,128)(2,1)S(1)}, u32[]{:S(2)}, u32[]{:S(2)}) collective-permute-start(bf16[272,256]{1,0:T(8,128)(2,1)S(1)} %adjoint.3.refs_0_.unread_ref), channel_id=1, source_target_pairs={{0,24},{8,16},{16,8},{24,0},{1,25},{9,17},{17,9},{25,1},{2,26},{10... | collective-permute-start | bytes 417800 | tf_op jit(solution)/shard_map/ppermute | solution.py:331
  52.1 1.3 %collective-permute-start.11 = (bf16[272,256]{1,0:T(8,128)(2,1)S(1)}, bf16[272,256]{1,0:T(8,128)(2,1)S(1)}, u32[]{:S(2)}, u32[]{:S(2)}) collective-permute-start(bf16[272,256]{1,0:T(8,128)(2,1)S(1)} %adjoint.3.refs_0_.unread_ref), channel_id=1, source_target_pairs={{0,16},{8,24},{16,0},{24,8},{1,17},{9,25},{17,1},{25,9},{2,18},{10... | collective-permute-start | bytes 417800 | tf_op jit(solution)/shard_map/ppermute | solution.py:331
  53.4 0.5 collective-permute-start.10
  53.9 3.9 %collective-permute-done.12.refs_3_ = bf16[272,256]{1,0:T(8,128)(2,1)S(1)} collective-permute-done((bf16[272,256]{1,0:T(8,128)(2,1)S(1)}, bf16[272,256]{1,0:T(8,128)(2,1)S(1)}, u32[]{:S(2)}, u32[]{:S(2)}) %collective-permute-start.12) | collective-permute-done | bytes 139296 | tf_op jit(solution)/shard_map/ppermute | solution.py:331
  57.8 1.7 %collective-permute-done.11.refs_2_ = bf16[272,256]{1,0:T(8,128)(2,1)S(1)} collective-permute-done((bf16[272,256]{1,0:T(8,128)(2,1)S(1)}, bf16[272,256]{1,0:T(8,128)(2,1)S(1)}, u32[]{:S(2)}, u32[]{:S(2)}) %collective-permute-start.11) | collective-permute-done | bytes 139296 | tf_op jit(solution)/shard_map/ppermute | solution.py:331
  59.5 0.0 collective-permute-done.10.refs_1_
  59.5 3.5 %voxel.3 = (f32[8,5,8,128]{3,2,1,0:T(8,128)S(1)}, f32[8,128]{1,0:T(8,128)S(1)}, f32[1024,256]{1,0:T(8,128)}, bf16[1024,256]{1,0:T(8,128)(2,1)S(1)}) custom-call(bf16[32,2,256,256]{3,2,1,0:T(8,128)(2,1)S(1)} %copy-done, bf16[272,256]{1,0:T(8,128)(2,1)S(1)} %adjoint.3.refs_0_.unread_ref, bf16[272,256]{1,0:T(8,128)(2,1)S(1)} %collective-permute-done.10.refs_1_, ...), custom_call_target="tpu_custom_call" | custom-call | tf_op jit(solution)/shard_map/voxel/pallas_call | solution.py:350
  63.1 9.6 %all_to_all.23.part_ref = f32[8,5,8,128]{3,2,1,0:T(8,128)S(1)} all-to-all(f32[8,5,8,128]{3,2,1,0:T(8,128)S(1)} %get-tuple-element.28), channel_id=1, replica_groups=mesh['row'=4,'col'=8] {'col'}, dimensions={0} | all-to-all | bytes 327680 | tf_op jit(solution)/shard_map/all_to_all | solution.py:336
  72.7 0.8 ray.3
  73.5 3.2 %all-to-all-start.3 = ((f32[32,8,128]{2,1,0:T(8,128)}), f32[32,8,128]{2,1,0:T(8,128)S(1)}, u32[]{:S(2)}, u32[]{:S(2)}) async-start(f32[32,8,128]{2,1,0:T(8,128)} %get-tuple-element.32.refs_0_), calls=%async_computation.3 | async-start | bytes 262144 | tf_op jit(solution)/shard_map/all_to_all | solution.py:336
  76.6 2.7 %collective-permute-start.15 = (bf16[256,256]{1,0:T(8,128)(2,1)S(1)}, bf16[256,256]{1,0:T(8,128)(2,1)S(1)}, u32[]{:S(2)}, u32[]{:S(2)}) collective-permute-start(bf16[256,256]{1,0:T(8,128)(2,1)S(1)} %get-tuple-element.36.refs_3_), channel_id=1, source_target_pairs={{0,24},{8,16},{16,8},{24,0},{1,25},{9,17},{17,9},{25,1},{2,26},{10... | collective-permute-start | bytes 393224 | tf_op jit(solution)/shard_map/ppermute | solution.py:331
  79.4 0.6 collective-permute-start.14
  79.9 0.3 collective-permute-start.13
  80.2 0.3 pick.1.refs_1_
  80.5 0.4 share.3.refs_5_
  81.0 4.0 %collective-permute-done.15.refs_6_ = bf16[256,256]{1,0:T(8,128)(2,1)S(1)} collective-permute-done((bf16[256,256]{1,0:T(8,128)(2,1)S(1)}, bf16[256,256]{1,0:T(8,128)(2,1)S(1)}, u32[]{:S(2)}, u32[]{:S(2)}) %collective-permute-start.15) | collective-permute-done | bytes 131104 | tf_op jit(solution)/shard_map/ppermute | solution.py:331
  85.0 2.3 %collective-permute-done.14.refs_5_ = bf16[256,256]{1,0:T(8,128)(2,1)S(1)} collective-permute-done((bf16[256,256]{1,0:T(8,128)(2,1)S(1)}, bf16[256,256]{1,0:T(8,128)(2,1)S(1)}, u32[]{:S(2)}, u32[]{:S(2)}) %collective-permute-start.14) | collective-permute-done | bytes 131104 | tf_op jit(solution)/shard_map/ppermute | solution.py:331
  87.3 0.0 collective-permute-done.13.refs_4_
  87.3 0.8 share.2.refs_4_
  88.1 0.0 all-to-all-done.3.last_ref
  88.1 1.3 %final.1 = (f32[4,32768]{1,0:T(4,128)}, f32[4]{0:T(128)}) custom-call(f32[32,8,128]{2,1,0:T(8,128)S(1)} %all-to-all-done.3.last_ref, f32[8,128]{1,0:T(8,128)S(1)} %get-tuple-element.22.beta_ref.refs_0_, f32[8,128]{1,0:T(8,128)S(1)} %get-tuple-element.30.beta_ref.refs_1_, f32[8,128]{1,0:T(8,128)S(1)} %get-tuple-element.27.refs_7_.refs_2_, ...), custom_call_target="tpu_custom_call" | custom-call | tf_op jit(solution)/shard_map/final/pallas_call | solution.py:422
  (1 shorter events, 0.0 us)
Async XLA Ops:
  0.6 13.3 %copy-start = (bf16[32,2,256,256]{3,2,1,0:T(8,128)(2,1)S(1)}, bf16[32,2,256,256]{3,2,1,0:T(8,128)(2,1)}, u32[]{:S(2)}) copy-start(bf16[32,2,256,256]{3,2,1,0:T(8,128)(2,1)} %tiles_ref.3) | copy-start | bytes 25165828
  0.6 0.9 copy-start.1
  1.5 10.1 %copy-start.2 = (s32[32,2]{0,1:T(2,128)S(1)}, s32[32,2]{0,1:T(2,128)}, u32[]{:S(2)}) copy-start(s32[32,2]{0,1:T(2,128)} %param.5) | copy-start | bytes 772
  1.5 8.7 %collective-permute-start.6 = (bf16[16,384]{1,0:T(8,128)(2,1)S(1)}, bf16[16,384]{1,0:T(8,128)(2,1)S(1)}, u32[]{:S(2)}, u32[]{:S(2)}) collective-permute-start(bf16[16,384]{1,0:T(8,128)(2,1)S(1)} %prepare.1.unread_ref.refs_2_), channel_id=1, source_target_pairs={{0,7},{1,6},{2,5},{3,4},{4,3},{5,2},{6,1},{7,0},{8,15},{9,14},{10,... | collective-permute-start | bytes 36872 | tf_op jit(solution)/shard_map/ppermute | solution.py:331
  6.1 5.5 %collective-permute-start.5 = (bf16[16,384]{1,0:T(8,128)(2,1)S(1)}, bf16[16,384]{1,0:T(8,128)(2,1)S(1)}, u32[]{:S(2)}, u32[]{:S(2)}) collective-permute-start(bf16[16,384]{1,0:T(8,128)(2,1)S(1)} %prepare.1.unread_ref.refs_2_), channel_id=1, source_target_pairs={{0,6},{1,7},{2,4},{3,5},{4,2},{5,3},{6,0},{7,1},{8,14},{9,15},{10,... | collective-permute-start | bytes 36872 | tf_op jit(solution)/shard_map/ppermute | solution.py:331
  6.7 5.5 %collective-permute-start.4 = (bf16[16,384]{1,0:T(8,128)(2,1)S(1)}, bf16[16,384]{1,0:T(8,128)(2,1)S(1)}, u32[]{:S(2)}, u32[]{:S(2)}) collective-permute-start(bf16[16,384]{1,0:T(8,128)(2,1)S(1)} %prepare.1.unread_ref.refs_2_), channel_id=1, source_target_pairs={{0,5},{1,4},{2,7},{3,6},{4,1},{5,0},{6,3},{7,2},{8,13},{9,12},{10,... | collective-permute-start | bytes 36872 | tf_op jit(solution)/shard_map/ppermute | solution.py:331
  7.1 5.1 %collective-permute-start.3 = (bf16[16,384]{1,0:T(8,128)(2,1)S(1)}, bf16[16,384]{1,0:T(8,128)(2,1)S(1)}, u32[]{:S(2)}, u32[]{:S(2)}) collective-permute-start(bf16[16,384]{1,0:T(8,128)(2,1)S(1)} %prepare.1.unread_ref.refs_2_), channel_id=1, source_target_pairs={{0,4},{1,5},{2,6},{3,7},{4,0},{5,1},{6,2},{7,3},{8,12},{9,13},{10,... | collective-permute-start | bytes 36872 | tf_op jit(solution)/shard_map/ppermute | solution.py:331
  9.3 3.1 %collective-permute-start.2 = (bf16[16,384]{1,0:T(8,128)(2,1)S(1)}, bf16[16,384]{1,0:T(8,128)(2,1)S(1)}, u32[]{:S(2)}, u32[]{:S(2)}) collective-permute-start(bf16[16,384]{1,0:T(8,128)(2,1)S(1)} %prepare.1.unread_ref.refs_2_), channel_id=1, source_target_pairs={{0,3},{1,2},{2,1},{3,0},{4,7},{5,6},{6,5},{7,4},{8,11},{9,10},{10,... | collective-permute-start | bytes 36872 | tf_op jit(solution)/shard_map/ppermute | solution.py:331
  10.3 3.7 %collective-permute-start.1 = (bf16[16,384]{1,0:T(8,128)(2,1)S(1)}, bf16[16,384]{1,0:T(8,128)(2,1)S(1)}, u32[]{:S(2)}, u32[]{:S(2)}) collective-permute-start(bf16[16,384]{1,0:T(8,128)(2,1)S(1)} %prepare.1.unread_ref.refs_2_), channel_id=1, source_target_pairs={{0,2},{1,3},{2,0},{3,1},{4,6},{5,7},{6,4},{7,5},{8,10},{9,11},{10,... | collective-permute-start | bytes 36872 | tf_op jit(solution)/shard_map/ppermute | solution.py:331
  11.6 2.4 %collective-permute-start = (bf16[16,384]{1,0:T(8,128)(2,1)S(1)}, bf16[16,384]{1,0:T(8,128)(2,1)S(1)}, u32[]{:S(2)}, u32[]{:S(2)}) collective-permute-start(bf16[16,384]{1,0:T(8,128)(2,1)S(1)} %prepare.1.unread_ref.refs_2_), channel_id=1, source_target_pairs={{0,1},{1,0},{2,3},{3,2},{4,5},{5,4},{6,7},{7,6},{8,9},{9,8},{10,11... | collective-permute-start | bytes 36872 | tf_op jit(solution)/shard_map/ppermute | solution.py:331
  15.2 6.9 %collective-permute-start.9 = (bf16[272,256]{1,0:T(8,128)(2,1)S(1)}, bf16[272,256]{1,0:T(8,128)(2,1)S(1)}, u32[]{:S(2)}, u32[]{:S(2)}) collective-permute-start(bf16[272,256]{1,0:T(8,128)(2,1)S(1)} %get-tuple-element.20.refs_0_), channel_id=1, source_target_pairs={{0,24},{8,16},{16,8},{24,0},{1,25},{9,17},{17,9},{25,1},{2,26},{10... | collective-permute-start | bytes 417800 | tf_op jit(solution)/shard_map/ppermute | solution.py:331
  17.7 6.2 %collective-permute-start.8 = (bf16[272,256]{1,0:T(8,128)(2,1)S(1)}, bf16[272,256]{1,0:T(8,128)(2,1)S(1)}, u32[]{:S(2)}, u32[]{:S(2)}) collective-permute-start(bf16[272,256]{1,0:T(8,128)(2,1)S(1)} %get-tuple-element.20.refs_0_), channel_id=1, source_target_pairs={{0,16},{8,24},{16,0},{24,8},{1,17},{9,25},{17,1},{25,9},{2,18},{10... | collective-permute-start | bytes 417800 | tf_op jit(solution)/shard_map/ppermute | solution.py:331
  18.2 5.8 %collective-permute-start.7 = (bf16[272,256]{1,0:T(8,128)(2,1)S(1)}, bf16[272,256]{1,0:T(8,128)(2,1)S(1)}, u32[]{:S(2)}, u32[]{:S(2)}) collective-permute-start(bf16[272,256]{1,0:T(8,128)(2,1)S(1)} %get-tuple-element.20.refs_0_), channel_id=1, source_target_pairs={{0,8},{8,0},{16,24},{24,16},{1,9},{9,1},{17,25},{25,17},{2,10},{10... | collective-permute-start | bytes 417800 | tf_op jit(solution)/shard_map/ppermute | solution.py:331
  50.4 7.5 %collective-permute-start.12 = (bf16[272,256]{1,0:T(8,128)(2,1)S(1)}, bf16[272,256]{1,0:T(8,128)(2,1)S(1)}, u32[]{:S(2)}, u32[]{:S(2)}) collective-permute-start(bf16[272,256]{1,0:T(8,128)(2,1)S(1)} %adjoint.3.refs_0_.unread_ref), channel_id=1, source_target_pairs={{0,24},{8,16},{16,8},{24,0},{1,25},{9,17},{17,9},{25,1},{2,26},{10... | collective-permute-start | bytes 417800 | tf_op jit(solution)/shard_map/ppermute | solution.py:331
  52.1 7.4 %collective-permute-start.11 = (bf16[272,256]{1,0:T(8,128)(2,1)S(1)}, bf16[272,256]{1,0:T(8,128)(2,1)S(1)}, u32[]{:S(2)}, u32[]{:S(2)}) collective-permute-start(bf16[272,256]{1,0:T(8,128)(2,1)S(1)} %adjoint.3.refs_0_.unread_ref), channel_id=1, source_target_pairs={{0,16},{8,24},{16,0},{24,8},{1,17},{9,25},{17,1},{25,9},{2,18},{10... | collective-permute-start | bytes 417800 | tf_op jit(solution)/shard_map/ppermute | solution.py:331
  53.4 6.1 %collective-permute-start.10 = (bf16[272,256]{1,0:T(8,128)(2,1)S(1)}, bf16[272,256]{1,0:T(8,128)(2,1)S(1)}, u32[]{:S(2)}, u32[]{:S(2)}) collective-permute-start(bf16[272,256]{1,0:T(8,128)(2,1)S(1)} %adjoint.3.refs_0_.unread_ref), channel_id=1, source_target_pairs={{0,8},{8,0},{16,24},{24,16},{1,9},{9,1},{17,25},{25,17},{2,10},{10... | collective-permute-start | bytes 417800 | tf_op jit(solution)/shard_map/ppermute | solution.py:331
  73.5 14.6 %all-to-all-start.3 = ((f32[32,8,128]{2,1,0:T(8,128)}), f32[32,8,128]{2,1,0:T(8,128)S(1)}, u32[]{:S(2)}, u32[]{:S(2)}) async-start(f32[32,8,128]{2,1,0:T(8,128)} %get-tuple-element.32.refs_0_), calls=%async_computation.3 | async-start | bytes 262144 | tf_op jit(solution)/shard_map/all_to_all | solution.py:336
  76.6 8.4 %collective-permute-start.15 = (bf16[256,256]{1,0:T(8,128)(2,1)S(1)}, bf16[256,256]{1,0:T(8,128)(2,1)S(1)}, u32[]{:S(2)}, u32[]{:S(2)}) collective-permute-start(bf16[256,256]{1,0:T(8,128)(2,1)S(1)} %get-tuple-element.36.refs_3_), channel_id=1, source_target_pairs={{0,24},{8,16},{16,8},{24,0},{1,25},{9,17},{17,9},{25,1},{2,26},{10... | collective-permute-start | bytes 393224 | tf_op jit(solution)/shard_map/ppermute | solution.py:331
  79.4 7.9 %collective-permute-start.14 = (bf16[256,256]{1,0:T(8,128)(2,1)S(1)}, bf16[256,256]{1,0:T(8,128)(2,1)S(1)}, u32[]{:S(2)}, u32[]{:S(2)}) collective-permute-start(bf16[256,256]{1,0:T(8,128)(2,1)S(1)} %get-tuple-element.36.refs_3_), channel_id=1, source_target_pairs={{0,16},{8,24},{16,0},{24,8},{1,17},{9,25},{17,1},{25,9},{2,18},{10... | collective-permute-start | bytes 393224 | tf_op jit(solution)/shard_map/ppermute | solution.py:331
  79.9 7.4 %collective-permute-start.13 = (bf16[256,256]{1,0:T(8,128)(2,1)S(1)}, bf16[256,256]{1,0:T(8,128)(2,1)S(1)}, u32[]{:S(2)}, u32[]{:S(2)}) collective-permute-start(bf16[256,256]{1,0:T(8,128)(2,1)S(1)} %get-tuple-element.36.refs_3_), channel_id=1, source_target_pairs={{0,8},{8,0},{16,24},{24,16},{1,9},{9,1},{17,25},{25,17},{2,10},{10... | collective-permute-start | bytes 393224 | tf_op jit(solution)/shard_map/ppermute | solution.py:331

commit v8 on v7

--- a/solution.py
+++ b/solution.py
@@ -40,18 +40,18 @@
     return upper, acc - upper
 
 
-def write_payload(out_ref, blocks, acc):
-    rows = out_ref.shape[0]
+def packed(blocks, rows):
     blank = [jnp.zeros((8, LANES), jnp.float32)] * (rows // 8)
-    for h in range(2):
-        half = (blocks[h::2] + blank)[: rows // 8]
-        out_ref[:, h * LANES : (h + 1) * LANES] = jnp.concatenate(half, axis=0).astype(jnp.bfloat16)
-    pieces = (list(in_two(acc)) + blank)[: rows // 8]
-    out_ref[:, 2 * LANES :] = jnp.concatenate(pieces, axis=0).astype(jnp.bfloat16)
-
-
-def read_squares(ref):
-    both = ref[:, 2 * LANES :].astype(jnp.float32)
+    halves = [jnp.concatenate((blocks[h::2] + blank)[: rows // 8], axis=0) for h in range(2)]
+    return jnp.concatenate(halves, axis=1).astype(jnp.bfloat16)
+
+
+def packed_squares(acc):
+    return jnp.concatenate(in_two(acc), axis=0).astype(jnp.bfloat16)
+
+
+def read_squares(both):
+    both = both.astype(jnp.float32)
     return both[:8] + both[8:16]
 
 
@@ -64,9 +64,17 @@
     return blocks
 
 
-def prepare_kernel(obs_ref, unread_ref, payload_ref):
-    blocks = ray_blocks(obs_ref, obs_ref.shape[1] // (2 * LANES))
-    write_payload(payload_ref, blocks, tree_sum([b * b for b in blocks]))
+def pack_kernel(flat, left_ref, unread_ref, payload_ref, blocks_ref):
+    count = blocks_ref.shape[0] - 1
+    blocks = ray_blocks(left_ref, count) if flat else [left_ref[b] for b in range(count)]
+    rows = payload_ref.shape[0]
+    payload_ref[:, : 2 * LANES] = packed(blocks, rows)
+    payload_ref[:, 2 * LANES :] = jnp.zeros((rows, LANES), jnp.bfloat16)
+    squares = packed_squares(tree_sum([b * b for b in blocks]))
+    payload_ref[:16, 2 * LANES :] = squares
+    for b, block in enumerate(blocks):
+        blocks_ref[b] = block
+    blocks_ref[count] = read_squares(squares)
 
 
 def keys_kernel(unread_ref, cols_ref, keys_ref):
@@ -120,19 +128,34 @@
                 pick_ref[at, lane : lane + LANES] = jnp.where(down == across, 1.0, 0.0).astype(jnp.bfloat16)
 
 
-def adjoint_kernel(first, *refs):
-    if first:
-        keys_ref, tiles_ref = refs[:2]
-        payloads, (term_ref, lower_ref) = refs[2:-2], refs[-2:]
-        shares = len(payloads)
-    else:
-        tiles_ref, payload_ref, term_ref = refs
-        shares = payload_ref.shape[0]
-        payloads = [payload_ref.at[c] for c in range(shares)]
+def adjoint_kernel(first, keys_ref, tiles_ref, *refs):
     row_tiles, per_block = tiles_ref.shape[:2]
+    shares = lax.axis_size("col")
+    me = lax.axis_index("col")
     per_share = row_tiles // shares
     terms = row_tiles * per_block * RHS
-    squares = tree_sum([read_squares(p) for p in payloads])
+    if first:
+        payloads, (term_ref, lower_ref) = refs[:shares], refs[shares:]
+        rows = payloads[1].shape[0]
+        squares, sources = [], []
+        for d in range(shares):
+            owner = jnp.bitwise_xor(me, d)
+            if d % 2:
+                squares.append(read_squares(payloads[d][:16, 2 * LANES :]))
+                sources.append((owner, payloads[d][:, : 2 * LANES]))
+            else:
+                squares.append(payloads[d][per_share])
+                sources.append((owner, packed([payloads[d][b] for b in range(per_share)], rows)))
+    else:
+        halves, (term_ref,) = refs[:2], refs[2:]
+        rows = (halves[0].shape[0] - 16) // (shares // 2)
+        squares = [read_squares(half[-16:, :LANES]) for half in halves]
+        sources = [
+            (2 * slot + jnp.bitwise_xor(me % 2, h), half[slot * rows : (slot + 1) * rows])
+            for h, half in enumerate(halves)
+            for slot in range(shares // 2)
+        ]
+    squares = tree_sum(squares)
     low = low_half(2 * LANES)
     pieces = jnp.concatenate(in_two(squares), axis=1)
     extra = jnp.zeros_like(pieces)
@@ -141,9 +164,7 @@
         coarse = jnp.floor(keys * (1.0 / 64))
         extra = jnp.where(low, coarse, keys - 64 * coarse)
     term_ref[terms:] = jnp.concatenate([pieces, extra], axis=0).astype(jnp.bfloat16)
-    for c in range(shares):
-        rays = payloads[c][:, : 2 * LANES]
-        owner = jnp.bitwise_xor(lax.axis_index("col"), c) if first else c
+    for owner, rays in sources:
         for g in range(per_share // 2):
             i = owner * per_share + 2 * g
             wide = [
@@ -158,7 +179,7 @@
                 ],
                 axis=0,
             )
-            at = pl.multiple_of(8 * i, 16) if first else 8 * i
+            at = pl.multiple_of(8 * i, 16)
             upper = value.astype(jnp.bfloat16)
             term_ref[pl.ds(at, 16), :] = upper
             if first:
@@ -168,13 +189,13 @@
 def voxel_kernel(first, rows, tiles_ref, *refs):
     terms, refs = refs[:rows], list(refs[rows:])
     if first:
-        out_ref, beta_ref, raw_ref, all_ref, equal_ref, weight_ref, keys_ref = refs
+        own_ref, other_ref, beta_ref, raw_ref, all_ref, equal_ref, weight_ref, keys_ref = refs
     else:
         equal_ref, weight_ref, right_ref, alpha_ref = refs[:4]
         out_ref, beta_ref, raw_ref, all_ref = refs[-4:]
     my_row = lax.axis_index("row")
     row_tiles, per_block = tiles_ref.shape[:2]
-    shares = out_ref.shape[0]
+    shares = lax.axis_size("col")
     per_share = row_tiles // shares
     per_row = row_tiles * per_block * RHS
     low = low_half(2 * LANES)
@@ -208,7 +229,14 @@
             square = raw * raw
             acc = acc + (square[:, :LANES] + square[:, LANES:]) * weight_ref[at : at + 8]
     own = my_row * per_row
-    for c in range(shares):
+    core = lax.axis_index("col") % 2
+    for e in range(shares):
+        if first:
+            half, slot = divmod(e, shares // 2)
+            c = 2 * slot + jnp.bitwise_xor(core, half)
+            ref, at = (own_ref, other_ref)[half], slot * per_share
+        else:
+            c, ref, at = e, out_ref.at[e], 0
         for g in range(per_share // 2):
             i = c * per_share + 2 * g
             lhs = raw_ref[pl.ds(pl.multiple_of(own + 8 * i, 16), 16), :].astype(jnp.bfloat16)
@@ -220,9 +248,42 @@
                 for k in range(2)
             ]
             value = jnp.where(low, wide[0], wide[3]) + pltpu.roll(jnp.where(low, wide[2], wide[1]), 4, 0)
-            out_ref[c, 2 * g] = value[:, :LANES]
-            out_ref[c, 2 * g + 1] = value[:, LANES:]
-        out_ref[c, per_share] = acc
+            ref[at + 2 * g] = value[:, :LANES]
+            ref[at + 2 * g + 1] = value[:, LANES:]
+        if not first:
+            ref[per_share] = acc
+    if first:
+        own_ref[own_ref.shape[0] - 1] = acc
+        other_ref[own_ref.shape[0] - 1] = acc
+
+
+def pair_kernel(own_ref, other_ref, out_ref):
+    out_ref[...] = own_ref[...] + other_ref[...]
+
+
+def half_ray_kernel(peers, *refs):
+    parts, lefts = refs[:peers], refs[peers : 2 * peers]
+    beta_ref, raw_ref, alpha_ref, half_ref = refs[2 * peers :]
+    per_share = raw_ref.shape[0]
+    rows = (half_ref.shape[0] - 16) // peers
+    alpha = norm_of(tree_sum([p[p.shape[0] - 1] for p in parts]))
+    alpha_ref[...] = alpha
+    alpha_inv = 1.0 / alpha
+    left_scale = alpha / beta_ref[...]
+    squares = []
+    for e in range(peers):
+        slot = jnp.bitwise_xor(lax.axis_index("col") // 2, e)
+        blocks = []
+        for b in range(per_share):
+            total = tree_sum([p[slot * per_share + b] for p in parts])
+            blocks.append(total * alpha_inv - lefts[e][b] * left_scale)
+            if e == 0:
+                raw_ref[b] = blocks[-1]
+        half_ref[pl.ds(pl.multiple_of(slot * rows, 16), rows), :] = packed(blocks, rows)
+        squares.append(tree_sum([b * b for b in blocks]))
+    pieces = packed_squares(tree_sum(squares))
+    half_ref[peers * rows :, :LANES] = pieces
+    half_ref[peers * rows :, LANES:] = jnp.zeros_like(pieces)
 
 
 def share_kernel(remainders, *refs):
@@ -248,27 +309,21 @@
     fill_pick(keys_ref, pick_ref)
 
 
-def ray_kernel(first, part_ref, left_ref, beta_ref, *refs):
-    if not first:
-        refs[-1][...] = refs[0][...]
-        refs = refs[1:-1]
-    raw_ref, alpha_ref, payload_ref, acc_ref = refs
+def ray_kernel(part_ref, left_ref, beta_ref, lower_ref, raw_ref, alpha_ref, acc_ref, passed_ref):
+    passed_ref[...] = lower_ref[...]
     shares, count = part_ref.shape[0], raw_ref.shape[0]
     alpha = norm_of(tree_sum([part_ref[c, count] for c in range(shares)]))
     alpha_ref[...] = alpha
     alpha_inv = 1.0 / alpha
     left_scale = alpha / beta_ref[...]
-    left = ray_blocks(left_ref, count) if first else [left_ref[b] for b in range(count)]
     blocks = []
     for b in range(count):
         total = tree_sum([part_ref[c, b] for c in range(shares)])
-        blocks.append(total * alpha_inv - left[b] * left_scale)
+        blocks.append(total * alpha_inv - left_ref[b] * left_scale)
         raw_ref[b] = blocks[-1]
     acc = tree_sum([b * b for b in blocks])
     for c in range(acc_ref.shape[0]):
         acc_ref[c] = acc
-    for c in range(shares):
-        write_payload(payload_ref.at[c], blocks, acc)
 
 
 def final_kernel(iters, last_ref, *refs):
@@ -324,12 +379,12 @@
     return jax.ShapeDtypeStruct(shape, jnp.bfloat16)
 
 
-def exchange(value, axis):
-    size = lax.axis_size(axis)
-    got = [value]
-    for d in range(1, size):
-        got.append(lax.ppermute(value, axis, [(i, i ^ d) for i in range(size)]))
-    return got
+def from_peer(value, axis, d):
+    return lax.ppermute(value, axis, [(i, i ^ d) for i in range(lax.axis_size(axis))])
+
+
+def exchange(value, axis, step=1):
+    return [value] + [from_peer(value, axis, d) for d in range(step, lax.axis_size(axis), step)]
 
 
 def swap(values, axis):
@@ -344,8 +399,8 @@
     per_row = row_tiles * per_block * RHS
     share_rows = col_tiles // rows * RHS
     payload = bf16(max(16, 4 * per_share), 3 * LANES)
-    payloads = bf16(shares, *payload.shape)
-
+    half_shares = shares // 2
+    half_parts = f32(half_shares * per_share + 1, 8, LANES)
     def call(kernel, name, out_shape, args, in_specs=None, scratch=()):
         return pl.pallas_call(
             kernel,
@@ -357,19 +412,29 @@
             name=name,
         )(*args)
 
+    def pack(left, unread):
+        flat = left.ndim == 2
+        message, blocks = call(
+            functools.partial(pack_kernel, flat),
+            "pack",
+            [payload, f32(per_share + 1, 8, LANES)],
+            [left, unread],
+            [VMEM, HBM],
+        )
+        gathered = [blocks]
+        for d in range(1, shares):
+            gathered.append(from_peer(message if d % 2 else blocks, "col", d))
+        return message, gathered
+
     def adjoint(payloads, first):
         out_shape = [bf16(per_row + 16, tile_size)] + [bf16(per_row, tile_size)] * first
-        args = [keys, tile_values, *payloads] if first else [tile_values, payloads]
+        args = [keys, tile_values, *payloads]
         return call(functools.partial(adjoint_kernel, first), "adjoint", out_shape, args)
 
     def voxel(term_list, previous):
         first = not previous
-        out_shape = [
-            f32(shares, per_share + 1, 8, LANES),
-            f32(8, LANES),
-            f32(rows * per_row, tile_size),
-            bf16(rows * per_row, tile_size),
-        ]
+        out_shape = [half_parts] * 2 if first else [f32(shares, per_share + 1, 8, LANES)]
+        out_shape += [f32(8, LANES), f32(rows * per_row, tile_size), bf16(rows * per_row, tile_size)]
         if first:
             out_shape += [
                 bf16(rows * per_row, rows * per_row),
@@ -379,6 +444,11 @@
         args = [tile_values, *term_list, *previous]
         return call(functools.partial(voxel_kernel, first, rows), "voxel", out_shape, args)
 
+    def half_ray(parts, lefts, beta):
+        out_shape = [f32(per_share, 8, LANES), f32(8, LANES), bf16(half_shares * payload.shape[0] + 16, 2 * LANES)]
+        kernel = functools.partial(half_ray_kernel, half_shares)
+        return call(kernel, "half_ray", out_shape, [*parts, *lefts, beta])
+
     def share(selector, all_terms, lower_terms):
         scratch = [pltpu.VMEM((rows * per_row, tile_size), jnp.bfloat16)] * (len(lower_terms) > 0)
         kernel = functools.partial(share_kernel, len(lower_terms))
@@ -387,38 +457,24 @@
         return call(kernel, "share", f32(share_rows, tile_size), args, specs, scratch)
 
     def ray(parts, left_raw, beta, passed):
-        out_shape = [f32(per_share, 8, LANES), f32(8, LANES), payloads, f32(rows * shares, 8, LANES)]
-        out_shape += [bf16(per_row, tile_size) for _ in passed]
-        return call(functools.partial(ray_kernel, not passed), "ray", out_shape, [parts, left_raw, beta, *passed])
+        out_shape = [f32(per_share, 8, LANES), f32(8, LANES), f32(rows * shares, 8, LANES), bf16(per_row, tile_size)]
+        return call(ray_kernel, "ray", out_shape, [parts, left_raw, beta, passed])
 
     far = pltpu.with_memory_space_constraint(tile_values, pltpu.HBM)
-    message = call(prepare_kernel, "prepare", payload, [observed, far], [VMEM, HBM])
+    message, gathered = pack(observed, far)
     keys = call(keys_kernel, "keys", f32(8, per_row), [message, tile_cols.T], [ANY, SMEM])
-    left_raw = observed
-    betas, alphas, combined = [], [], []
-    previous = []
-    for iteration in range(ITERS + 1):
-        first = iteration == 0
-        terms, *lower = adjoint(exchange(message, "col") if first else swap(message, "col"), first)
-        if iteration == 1:
-            selector = call(pick_kernel, "pick", bf16(share_rows, rows * per_row), [terms, all_keys], [ANY, VMEM])
-        parts, beta, right_raw, upper_terms, *fixed = voxel(exchange(terms, "row"), previous)
-        if iteration == ITERS:
-            break
-        if first:
-            equal, weight, all_keys = fixed
-            remainder = lower[0]
-        combined.append(upper_terms)
-        left_raw, alpha, message, squares, *passed = ray(
-            swap(parts, "col"), left_raw, beta, [] if first else [remainder]
-        )
-        if passed:
-            remainder = passed[0]
-        betas.append(beta)
-        alphas.append(alpha)
-        previous = [equal, weight, right_raw, alpha]
-    remainders = exchange(remainder, "row")
-    products = [share(selector, c, [] if i else remainders) for i, c in enumerate(combined)]
+    terms, remainder = adjoint(gathered, True)
+    own, other, beta0, right_raw0, combined0, equal, weight, all_keys = voxel(exchange(terms, "row"), [])
+    pair = call(pair_kernel, "pair", half_parts, [own, from_peer(other, "col", 1)])
+    left_raw, alpha0, half = half_ray(exchange(pair, "col", 2), gathered[::2], beta0)
+    (terms,) = adjoint([half, from_peer(half, "col", 1)], False)
+    selector = call(pick_kernel, "pick", bf16(share_rows, rows * per_row), [terms, all_keys], [ANY, VMEM])
+    parts, beta1, right_raw1, combined1 = voxel(exchange(terms, "row"), [equal, weight, right_raw0, alpha0])
+    left_raw, alpha1, squares, remainder = ray(swap(parts, "col"), left_raw, beta1, remainder)
+    terms, _ = adjoint(pack(left_raw, far)[1], True)
+    voxel(exchange(terms, "row"), [equal, weight, right_raw1, alpha1])
+    products = [share(selector, combined0, exchange(remainder, "row")), share(selector, combined1, [])]
+    betas, alphas = [beta0, beta1], [alpha0, alpha1]
     result, ratio = pl.pallas_call(
         functools.partial(final_kernel, ITERS),
         out_shape=[f32(RHS, col_tiles // rows * tile_size), f32(RHS)],

time: 89.8 us -> 82.5 us (0.919)
  blocking collectives: 30.1 us -> 10.6 us
  waiting for transfers between devices: 19.4 us -> 27.4 us
  starting transfers between devices: 23.4 us -> 28.3 us
    all_to_all x3 -> x1, blocking collectives: 30.1 us -> 10.6 us  [swap(): return lax.all_to_all(values, axis, 0, 0)]
    ppermute x16 -> x21, waiting for transfers between devices: 19.4 us -> 27.4 us  [from_peer(): lax.ppermute(value, axis, [(i, i ^ d) for i in range(lax.axis_size(axis))])]
    ppermute x16 -> x21, starting transfers between devices: 20.2 us -> 25.2 us  [from_peer(): lax.ppermute(value, axis, [(i, i ^ d) for i in range(lax.axis_size(axis))])]
    pallas_call x11 -> x12, Pallas kernels: 13.5 us -> 12.9 us  [call(): pl.pallas_call(kernel, out_shape=out_shape, in_specs=in_specs or [VMEM] *...]
  transfers between devices with their start and end apart: 17 -> 22, of which waited for: 10 -> 12; matrix products, arithmetic and copies ran while one was open for 0% -> 0% of each run, Pallas kernels for 2% -> 3%
where the time goes in v8:
time: 82.5 us; the launch traced here: 82.2 us
  starting transfers between devices  28.3 us (34%)
  waiting for transfers between devices  27.4 us (33%)
  Pallas kernels  14.2 us (17%)
  blocking collectives  10.6 us (13%)
  local copies, waits for them, and re-layouts  0.87 us (1%)
    ppermute x21, waiting for transfers between devices, from_peer(): lax.ppermute(value, axis, [(i, i ^ d) for i in range(lax.axis_size(axis))])  27.4 us
    ppermute x21, starting transfers between devices, from_peer(): lax.ppermute(value, axis, [(i, i ^ d) for i in range(lax.axis_size(axis))])  25.2 us
    pallas_call x12, Pallas kernels, call(): pl.pallas_call(kernel, out_shape=out_shape, in_specs=in_specs or [VMEM] *...  12.9 us
    all_to_all x1, blocking collectives, swap(): return lax.all_to_all(values, axis, 0, 0)  10.6 us
    all_to_all x1, starting transfers between devices, swap(): return lax.all_to_all(values, axis, 0, 0)  3.12 us
  transfers between devices with their start and end apart: 22, of which 12 were waited for; matrix products, arithmetic and copies ran while one was open for 0% of the time, Pallas kernels for 3%

profile of v8, /device:TPU:0, one launch (start us, length us, event | category | flops | bytes accessed | tf_op | source)
XLA Modules:
  0.0 82.2 jit_solution(12513139154468611766)
XLA Ops:
  0.6 0.0 copy-start
  0.6 0.0 copy-start.1
  0.6 0.9 %copy-done.1 = f32[4,1024]{1,0:T(4,128)S(1)} copy-done((f32[4,1024]{1,0:T(4,128)S(1)}, f32[4,1024]{1,0:T(4,128)}, u32[]{:S(2)}) %copy-start.1) | copy-done | bytes 16408
  1.5 0.0 copy-start.2
  1.5 4.6 %collective-permute-start.6 = (bf16[16,384]{1,0:T(8,128)(2,1)S(1)}, bf16[16,384]{1,0:T(8,128)(2,1)S(1)}, u32[]{:S(2)}, u32[]{:S(2)}) collective-permute-start(bf16[16,384]{1,0:T(8,128)(2,1)S(1)} %get-tuple-element.23.unread_ref), channel_id=1, source_target_pairs={{0,7},{1,6},{2,5},{3,4},{4,3},{5,2},{6,1},{7,0},{8,15},{9,14},{10,... | collective-permute-start | bytes 36872 | tf_op jit(solution)/shard_map/ppermute | solution.py:383
  6.1 0.0 collective-permute-start.4
  6.1 2.2 %collective-permute-start.5 = (f32[5,8,128]{2,1,0:T(8,128)S(1)}, f32[5,8,128]{2,1,0:T(8,128)S(1)}, u32[]{:S(2)}, u32[]{:S(2)}) collective-permute-start(f32[5,8,128]{2,1,0:T(8,128)S(1)} %get-tuple-element.24.refs_0_.refs_4_), channel_id=1, source_target_pairs={{0,6},{1,7},{2,4},{3,5},{4,2},{5,3},{6,0},{7,1},{8,14},{9,15},{10,... | collective-permute-start | bytes 61448 | tf_op jit(solution)/shard_map/ppermute | solution.py:383
  8.3 1.0 %collective-permute-start.3 = (f32[5,8,128]{2,1,0:T(8,128)S(1)}, f32[5,8,128]{2,1,0:T(8,128)S(1)}, u32[]{:S(2)}, u32[]{:S(2)}) collective-permute-start(f32[5,8,128]{2,1,0:T(8,128)S(1)} %get-tuple-element.24.refs_0_.refs_4_), channel_id=1, source_target_pairs={{0,4},{1,5},{2,6},{3,7},{4,0},{5,1},{6,2},{7,3},{8,12},{9,13},{10,... | collective-permute-start | bytes 61448 | tf_op jit(solution)/shard_map/ppermute | solution.py:383
  9.3 1.2 %collective-permute-start.1 = (f32[5,8,128]{2,1,0:T(8,128)S(1)}, f32[5,8,128]{2,1,0:T(8,128)S(1)}, u32[]{:S(2)}, u32[]{:S(2)}) collective-permute-start(f32[5,8,128]{2,1,0:T(8,128)S(1)} %get-tuple-element.24.refs_0_.refs_4_), channel_id=1, source_target_pairs={{0,2},{1,3},{2,0},{3,1},{4,6},{5,7},{6,4},{7,5},{8,10},{9,11},{10,... | collective-permute-start | bytes 61448 | tf_op jit(solution)/shard_map/ppermute | solution.py:383
  10.5 0.0 collective-permute-done.6.refs_7_
  10.5 0.0 collective-permute-start.2
  10.5 0.0 collective-permute-done.4.refs_5_
  10.5 1.0 %collective-permute-start = (bf16[16,384]{1,0:T(8,128)(2,1)S(1)}, bf16[16,384]{1,0:T(8,128)(2,1)S(1)}, u32[]{:S(2)}, u32[]{:S(2)}) collective-permute-start(bf16[16,384]{1,0:T(8,128)(2,1)S(1)} %get-tuple-element.23.unread_ref), channel_id=1, source_target_pairs={{0,1},{1,0},{2,3},{3,2},{4,5},{5,4},{6,7},{7,6},{8,9},{9,8},{10,11... | collective-permute-start | bytes 36872 | tf_op jit(solution)/shard_map/ppermute | solution.py:383
  11.4 0.0 copy-done.2
  11.4 0.6 keys.1.keys_ref
  12.0 1.6 %collective-permute-done.2.refs_3_ = bf16[16,384]{1,0:T(8,128)(2,1)S(1)} collective-permute-done((bf16[16,384]{1,0:T(8,128)(2,1)S(1)}, bf16[16,384]{1,0:T(8,128)(2,1)S(1)}, u32[]{:S(2)}, u32[]{:S(2)}) %collective-permute-start.2) | collective-permute-done | bytes 12320 | tf_op jit(solution)/shard_map/ppermute | solution.py:383
  13.7 0.0 collective-permute-done.refs_1_
  13.7 0.0 collective-permute-done.5.refs_6_.refs_7_
  13.7 0.0 collective-permute-done.3.refs_4_.refs_6_
  13.7 0.0 collective-permute-done.1.refs_2_.refs_5_
  13.7 0.0 copy-done
  13.7 1.2 %adjoint.2 = (bf16[272,256]{1,0:T(8,128)(2,1)S(1)}, bf16[256,256]{1,0:T(8,128)(2,1)S(1)}) custom-call(f32[8,256]{1,0:T(8,128)S(1)} %keys.1.keys_ref, bf16[32,2,256,256]{3,2,1,0:T(8,128)(2,1)S(1)} %copy-done, f32[5,8,128]{2,1,0:T(8,128)S(1)} %get-tuple-element.24.refs_0_.refs_4_, bf16[16,384]{1,0:T(8,128)(2,1)S(1)} %collective-permute-done.refs_1_, ...), custom_call_target="tpu_custom_call" | custom-call | tf_op jit(solution)/shard_map/adjoint/pallas_call | solution.py:405
  14.9 2.5 %collective-permute-start.9 = (bf16[272,256]{1,0:T(8,128)(2,1)S(1)}, bf16[272,256]{1,0:T(8,128)(2,1)S(1)}, u32[]{:S(2)}, u32[]{:S(2)}) collective-permute-start(bf16[272,256]{1,0:T(8,128)(2,1)S(1)} %get-tuple-element.25.refs_0_), channel_id=1, source_target_pairs={{0,24},{8,16},{16,8},{24,0},{1,25},{9,17},{17,9},{25,1},{2,26},{10... | collective-permute-start | bytes 417800 | tf_op jit(solution)/shard_map/ppermute | solution.py:383
  17.4 0.5 collective-permute-start.8
  17.9 0.5 collective-permute-start.7
  18.5 3.6 %collective-permute-done.9.refs_3_ = bf16[272,256]{1,0:T(8,128)(2,1)S(1)} collective-permute-done((bf16[272,256]{1,0:T(8,128)(2,1)S(1)}, bf16[272,256]{1,0:T(8,128)(2,1)S(1)}, u32[]{:S(2)}, u32[]{:S(2)}) %collective-permute-start.9) | collective-permute-done | bytes 139296 | tf_op jit(solution)/shard_map/ppermute | solution.py:383
  22.0 2.5 %collective-permute-done.8.refs_2_ = bf16[272,256]{1,0:T(8,128)(2,1)S(1)} collective-permute-done((bf16[272,256]{1,0:T(8,128)(2,1)S(1)}, bf16[272,256]{1,0:T(8,128)(2,1)S(1)}, u32[]{:S(2)}, u32[]{:S(2)}) %collective-permute-start.8) | collective-permute-done | bytes 139296 | tf_op jit(solution)/shard_map/ppermute | solution.py:383
  24.5 0.1 collective-permute-done.7.refs_1_
  24.6 4.0 %voxel.2 = (f32[17,8,128]{2,1,0:T(8,128)S(1)}, f32[17,8,128]{2,1,0:T(8,128)S(1)}, f32[8,128]{1,0:T(8,128)S(1)}, f32[1024,256]{1,0:T(8,128)S(1)}, bf16[1024,256]{...) custom-call(bf16[32,2,256,256]{3,2,1,0:T(8,128)(2,1)S(1)} %copy-done, ...), custom_call_target="tpu_custom_call" | custom-call | tf_op jit(solution)/shard_map/voxel/pallas_call | solution.py:405
  28.7 0.1 collective-permute-start.10
  28.7 1.3 %collective-permute-done.10.other_ref = f32[17,8,128]{2,1,0:T(8,128)S(1)} collective-permute-done((f32[17,8,128]{2,1,0:T(8,128)S(1)}, f32[17,8,128]{2,1,0:T(8,128)S(1)}, u32[]{:S(2)}, u32[]{:S(2)}) %collective-permute-start.10) | collective-permute-done | bytes 69664 | tf_op jit(solution)/shard_map/ppermute | solution.py:383
  30.0 2.4 %collective-permute-start.13 = (f32[17,8,128]{2,1,0:T(8,128)S(1)}, f32[17,8,128]{2,1,0:T(8,128)S(1)}, u32[]{:S(2)}, u32[]{:S(2)}) collective-permute-start(f32[17,8,128]{2,1,0:T(8,128)S(1)} %pair.1.refs_0_), channel_id=1, source_target_pairs={{0,6},{1,7},{2,4},{3,5},{4,2},{5,3},{6,0},{7,1},{8,14},{9,15},{10,... | collective-permute-start | bytes 208904 | tf_op jit(solution)/shard_map/ppermute | solution.py:383
  32.4 0.0 collective-permute-start.12
  32.4 2.1 %collective-permute-start.11 = (f32[17,8,128]{2,1,0:T(8,128)S(1)}, f32[17,8,128]{2,1,0:T(8,128)S(1)}, u32[]{:S(2)}, u32[]{:S(2)}) collective-permute-start(f32[17,8,128]{2,1,0:T(8,128)S(1)} %pair.1.refs_0_), channel_id=1, source_target_pairs={{0,2},{1,3},{2,0},{3,1},{4,6},{5,7},{6,4},{7,5},{8,10},{9,11},{10,... | collective-permute-start | bytes 208904 | tf_op jit(solution)/shard_map/ppermute | solution.py:383
  34.5 2.5 %collective-permute-done.13.refs_3_ = f32[17,8,128]{2,1,0:T(8,128)S(1)} collective-permute-done((f32[17,8,128]{2,1,0:T(8,128)S(1)}, f32[17,8,128]{2,1,0:T(8,128)S(1)}, u32[]{:S(2)}, u32[]{:S(2)}) %collective-permute-start.13) | collective-permute-done | bytes 69664 | tf_op jit(solution)/shard_map/ppermute | solution.py:383
  37.0 2.1 %collective-permute-done.12.refs_2_ = f32[17,8,128]{2,1,0:T(8,128)S(1)} collective-permute-done((f32[17,8,128]{2,1,0:T(8,128)S(1)}, f32[17,8,128]{2,1,0:T(8,128)S(1)}, u32[]{:S(2)}, u32[]{:S(2)}) %collective-permute-start.12) | collective-permute-done | bytes 69664 | tf_op jit(solution)/shard_map/ppermute | solution.py:383
  39.1 0.0 collective-permute-done.11.refs_1_
  39.1 0.1 half_ray.1
  39.2 0.1 collective-permute-start.14
  39.3 1.2 %collective-permute-done.14.refs_1_ = bf16[80,256]{1,0:T(8,128)(2,1)S(1)} collective-permute-done((bf16[80,256]{1,0:T(8,128)(2,1)S(1)}, bf16[80,256]{1,0:T(8,128)(2,1)S(1)}, u32[]{:S(2)}, u32[]{:S(2)}) %collective-permute-start.14) | collective-permute-done | bytes 40992 | tf_op jit(solution)/shard_map/ppermute | solution.py:383
  40.5 1.2 %adjoint.3.refs_0_.unread_ref = bf16[272,256]{1,0:T(8,128)(2,1)S(1)} custom-call(f32[8,256]{1,0:T(8,128)S(1)} %keys.1.keys_ref, bf16[32,2,256,256]{3,2,1,0:T(8,128)(2,1)S(1)} %copy-done, bf16[80,256]{1,0:T(8,128)(2,1)S(1)} %get-tuple-element.29.refs_0_, bf16[80,256]{1,0:T(8,128)(2,1)S(1)} %collective-permute-done.14.refs_1_), custom_call_target="tpu_custom_call" | custom-call | tf_op jit(solution)/shard_map/adjoint/pallas_call | solution.py:405
  41.7 1.7 %collective-permute-start.17 = (bf16[272,256]{1,0:T(8,128)(2,1)S(1)}, bf16[272,256]{1,0:T(8,128)(2,1)S(1)}, u32[]{:S(2)}, u32[]{:S(2)}) collective-permute-start(bf16[272,256]{1,0:T(8,128)(2,1)S(1)} %adjoint.3.refs_0_.unread_ref), channel_id=1, source_target_pairs={{0,24},{8,16},{16,8},{24,0},{1,25},{9,17},{17,9},{25,1},{2,26},{10... | collective-permute-start | bytes 417800 | tf_op jit(solution)/shard_map/ppermute | solution.py:383
  43.4 1.3 %collective-permute-start.16 = (bf16[272,256]{1,0:T(8,128)(2,1)S(1)}, bf16[272,256]{1,0:T(8,128)(2,1)S(1)}, u32[]{:S(2)}, u32[]{:S(2)}) collective-permute-start(bf16[272,256]{1,0:T(8,128)(2,1)S(1)} %adjoint.3.refs_0_.unread_ref), channel_id=1, source_target_pairs={{0,16},{8,24},{16,0},{24,8},{1,17},{9,25},{17,1},{25,9},{2,18},{10... | collective-permute-start | bytes 417800 | tf_op jit(solution)/shard_map/ppermute | solution.py:383
  44.7 0.5 collective-permute-start.15
  45.3 4.0 %collective-permute-done.17.refs_3_ = bf16[272,256]{1,0:T(8,128)(2,1)S(1)} collective-permute-done((bf16[272,256]{1,0:T(8,128)(2,1)S(1)}, bf16[272,256]{1,0:T(8,128)(2,1)S(1)}, u32[]{:S(2)}, u32[]{:S(2)}) %collective-permute-start.17) | collective-permute-done | bytes 139296 | tf_op jit(solution)/shard_map/ppermute | solution.py:383
  49.2 2.2 %collective-permute-done.16.refs_2_ = bf16[272,256]{1,0:T(8,128)(2,1)S(1)} collective-permute-done((bf16[272,256]{1,0:T(8,128)(2,1)S(1)}, bf16[272,256]{1,0:T(8,128)(2,1)S(1)}, u32[]{:S(2)}, u32[]{:S(2)}) %collective-permute-start.16) | collective-permute-done | bytes 139296 | tf_op jit(solution)/shard_map/ppermute | solution.py:383
  51.4 0.0 collective-permute-done.15.refs_1_
  51.4 3.5 %voxel.3 = (f32[8,5,8,128]{3,2,1,0:T(8,128)S(1)}, f32[8,128]{1,0:T(8,128)S(1)}, f32[1024,256]{1,0:T(8,128)}, bf16[1024,256]{1,0:T(8,128)(2,1)S(1)}) custom-call(bf16[32,2,256,256]{3,2,1,0:T(8,128)(2,1)S(1)} %copy-done, bf16[272,256]{1,0:T(8,128)(2,1)S(1)} %adjoint.3.refs_0_.unread_ref, bf16[272,256]{1,0:T(8,128)(2,1)S(1)} %collective-permute-done.15.refs_1_, ...), custom_call_target="tpu_custom_call" | custom-call | tf_op jit(solution)/shard_map/voxel/pallas_call | solution.py:405
  54.9 10.6 %all_to_all.10.part_ref = f32[8,5,8,128]{3,2,1,0:T(8,128)S(1)} all-to-all(f32[8,5,8,128]{3,2,1,0:T(8,128)S(1)} %get-tuple-element.34), channel_id=1, replica_groups=mesh['row'=4,'col'=8] {'col'}, dimensions={0} | all-to-all | bytes 327680 | tf_op jit(solution)/shard_map/all_to_all | solution.py:391
  65.5 0.8 ray.1
  66.3 3.1 %all-to-all-start.1 = ((f32[32,8,128]{2,1,0:T(8,128)}), f32[32,8,128]{2,1,0:T(8,128)S(1)}, u32[]{:S(2)}, u32[]{:S(2)}) async-start(f32[32,8,128]{2,1,0:T(8,128)} %get-tuple-element.38.refs_0_), calls=%async_computation.1 | async-start | bytes 262144 | tf_op jit(solution)/shard_map/all_to_all | solution.py:391
  69.4 2.7 %collective-permute-start.20 = (bf16[256,256]{1,0:T(8,128)(2,1)S(1)}, bf16[256,256]{1,0:T(8,128)(2,1)S(1)}, u32[]{:S(2)}, u32[]{:S(2)}) collective-permute-start(bf16[256,256]{1,0:T(8,128)(2,1)S(1)} %get-tuple-element.42.refs_3_), channel_id=1, source_target_pairs={{0,24},{8,16},{16,8},{24,0},{1,25},{9,17},{17,9},{25,1},{2,26},{10... | collective-permute-start | bytes 393224 | tf_op jit(solution)/shard_map/ppermute | solution.py:383
  72.2 0.6 collective-permute-start.19
  72.7 0.3 collective-permute-start.18
  73.0 0.3 pick.1.refs_1_
  73.3 0.4 share.3.refs_5_
  73.7 4.0 %collective-permute-done.20.refs_6_ = bf16[256,256]{1,0:T(8,128)(2,1)S(1)} collective-permute-done((bf16[256,256]{1,0:T(8,128)(2,1)S(1)}, bf16[256,256]{1,0:T(8,128)(2,1)S(1)}, u32[]{:S(2)}, u32[]{:S(2)}) %collective-permute-start.20) | collective-permute-done | bytes 131104 | tf_op jit(solution)/shard_map/ppermute | solution.py:383
  77.8 2.3 %collective-permute-done.19.refs_5_ = bf16[256,256]{1,0:T(8,128)(2,1)S(1)} collective-permute-done((bf16[256,256]{1,0:T(8,128)(2,1)S(1)}, bf16[256,256]{1,0:T(8,128)(2,1)S(1)}, u32[]{:S(2)}, u32[]{:S(2)}) %collective-permute-start.19) | collective-permute-done | bytes 131104 | tf_op jit(solution)/shard_map/ppermute | solution.py:383
  80.1 0.0 collective-permute-done.18.refs_4_
  80.1 0.8 share.2.refs_4_
  80.8 0.0 all-to-all-done.1.last_ref
  80.9 1.3 %final.1 = (f32[4,32768]{1,0:T(4,128)}, f32[4]{0:T(128)}) custom-call(f32[32,8,128]{2,1,0:T(8,128)S(1)} %all-to-all-done.1.last_ref, f32[8,128]{1,0:T(8,128)S(1)} %get-tuple-element.28.refs_8_.refs_0_, f32[8,128]{1,0:T(8,128)S(1)} %get-tuple-element.36.beta_ref.refs_1_, f32[8,128]{1,0:T(8,128)S(1)} %get-tuple-element.33.refs_7_.refs_2_, ...), custom_call_target="tpu_custom_call" | custom-call | tf_op jit(solution)/shard_map/final/pallas_call | solution.py:478
  (2 shorter events, 0.0 us)
Async XLA Ops:
  0.6 13.1 %copy-start = (bf16[32,2,256,256]{3,2,1,0:T(8,128)(2,1)S(1)}, bf16[32,2,256,256]{3,2,1,0:T(8,128)(2,1)}, u32[]{:S(2)}) copy-start(bf16[32,2,256,256]{3,2,1,0:T(8,128)(2,1)} %tiles_ref.7) | copy-start | bytes 25165828
  0.6 0.9 %copy-start.1 = (f32[4,1024]{1,0:T(4,128)S(1)}, f32[4,1024]{1,0:T(4,128)}, u32[]{:S(2)}) copy-start(f32[4,1024]{1,0:T(4,128)} %left_ref.1) | copy-start | bytes 49156
  1.5 9.9 %copy-start.2 = (s32[32,2]{0,1:T(2,128)S(1)}, s32[32,2]{0,1:T(2,128)}, u32[]{:S(2)}) copy-start(s32[32,2]{0,1:T(2,128)} %param.5) | copy-start | bytes 772
  1.5 8.9 %collective-permute-start.6 = (bf16[16,384]{1,0:T(8,128)(2,1)S(1)}, bf16[16,384]{1,0:T(8,128)(2,1)S(1)}, u32[]{:S(2)}, u32[]{:S(2)}) collective-permute-start(bf16[16,384]{1,0:T(8,128)(2,1)S(1)} %get-tuple-element.23.unread_ref), channel_id=1, source_target_pairs={{0,7},{1,6},{2,5},{3,4},{4,3},{5,2},{6,1},{7,0},{8,15},{9,14},{10,... | collective-permute-start | bytes 36872 | tf_op jit(solution)/shard_map/ppermute | solution.py:383
  6.1 4.4 %collective-permute-start.4 = (bf16[16,384]{1,0:T(8,128)(2,1)S(1)}, bf16[16,384]{1,0:T(8,128)(2,1)S(1)}, u32[]{:S(2)}, u32[]{:S(2)}) collective-permute-start(bf16[16,384]{1,0:T(8,128)(2,1)S(1)} %get-tuple-element.23.unread_ref), channel_id=1, source_target_pairs={{0,5},{1,4},{2,7},{3,6},{4,1},{5,0},{6,3},{7,2},{8,13},{9,12},{10,... | collective-permute-start | bytes 36872 | tf_op jit(solution)/shard_map/ppermute | solution.py:383
  6.1 7.6 %collective-permute-start.5 = (f32[5,8,128]{2,1,0:T(8,128)S(1)}, f32[5,8,128]{2,1,0:T(8,128)S(1)}, u32[]{:S(2)}, u32[]{:S(2)}) collective-permute-start(f32[5,8,128]{2,1,0:T(8,128)S(1)} %get-tuple-element.24.refs_0_.refs_4_), channel_id=1, source_target_pairs={{0,6},{1,7},{2,4},{3,5},{4,2},{5,3},{6,0},{7,1},{8,14},{9,15},{10,... | collective-permute-start | bytes 61448 | tf_op jit(solution)/shard_map/ppermute | solution.py:383
  8.3 5.4 %collective-permute-start.3 = (f32[5,8,128]{2,1,0:T(8,128)S(1)}, f32[5,8,128]{2,1,0:T(8,128)S(1)}, u32[]{:S(2)}, u32[]{:S(2)}) collective-permute-start(f32[5,8,128]{2,1,0:T(8,128)S(1)} %get-tuple-element.24.refs_0_.refs_4_), channel_id=1, source_target_pairs={{0,4},{1,5},{2,6},{3,7},{4,0},{5,1},{6,2},{7,3},{8,12},{9,13},{10,... | collective-permute-start | bytes 61448 | tf_op jit(solution)/shard_map/ppermute | solution.py:383
  9.3 4.4 %collective-permute-start.1 = (f32[5,8,128]{2,1,0:T(8,128)S(1)}, f32[5,8,128]{2,1,0:T(8,128)S(1)}, u32[]{:S(2)}, u32[]{:S(2)}) collective-permute-start(f32[5,8,128]{2,1,0:T(8,128)S(1)} %get-tuple-element.24.refs_0_.refs_4_), channel_id=1, source_target_pairs={{0,2},{1,3},{2,0},{3,1},{4,6},{5,7},{6,4},{7,5},{8,10},{9,11},{10,... | collective-permute-start | bytes 61448 | tf_op jit(solution)/shard_map/ppermute | solution.py:383
  10.5 3.2 %collective-permute-start.2 = (bf16[16,384]{1,0:T(8,128)(2,1)S(1)}, bf16[16,384]{1,0:T(8,128)(2,1)S(1)}, u32[]{:S(2)}, u32[]{:S(2)}) collective-permute-start(bf16[16,384]{1,0:T(8,128)(2,1)S(1)} %get-tuple-element.23.unread_ref), channel_id=1, source_target_pairs={{0,3},{1,2},{2,1},{3,0},{4,7},{5,6},{6,5},{7,4},{8,11},{9,10},{10,... | collective-permute-start | bytes 36872 | tf_op jit(solution)/shard_map/ppermute | solution.py:383
  10.5 3.2 %collective-permute-start = (bf16[16,384]{1,0:T(8,128)(2,1)S(1)}, bf16[16,384]{1,0:T(8,128)(2,1)S(1)}, u32[]{:S(2)}, u32[]{:S(2)}) collective-permute-start(bf16[16,384]{1,0:T(8,128)(2,1)S(1)} %get-tuple-element.23.unread_ref), channel_id=1, source_target_pairs={{0,1},{1,0},{2,3},{3,2},{4,5},{5,4},{6,7},{7,6},{8,9},{9,8},{10,11... | collective-permute-start | bytes 36872 | tf_op jit(solution)/shard_map/ppermute | solution.py:383
  14.9 7.1 %collective-permute-start.9 = (bf16[272,256]{1,0:T(8,128)(2,1)S(1)}, bf16[272,256]{1,0:T(8,128)(2,1)S(1)}, u32[]{:S(2)}, u32[]{:S(2)}) collective-permute-start(bf16[272,256]{1,0:T(8,128)(2,1)S(1)} %get-tuple-element.25.refs_0_), channel_id=1, source_target_pairs={{0,24},{8,16},{16,8},{24,0},{1,25},{9,17},{17,9},{25,1},{2,26},{10... | collective-permute-start | bytes 417800 | tf_op jit(solution)/shard_map/ppermute | solution.py:383
  17.4 7.1 %collective-permute-start.8 = (bf16[272,256]{1,0:T(8,128)(2,1)S(1)}, bf16[272,256]{1,0:T(8,128)(2,1)S(1)}, u32[]{:S(2)}, u32[]{:S(2)}) collective-permute-start(bf16[272,256]{1,0:T(8,128)(2,1)S(1)} %get-tuple-element.25.refs_0_), channel_id=1, source_target_pairs={{0,16},{8,24},{16,0},{24,8},{1,17},{9,25},{17,1},{25,9},{2,18},{10... | collective-permute-start | bytes 417800 | tf_op jit(solution)/shard_map/ppermute | solution.py:383
  17.9 6.7 %collective-permute-start.7 = (bf16[272,256]{1,0:T(8,128)(2,1)S(1)}, bf16[272,256]{1,0:T(8,128)(2,1)S(1)}, u32[]{:S(2)}, u32[]{:S(2)}) collective-permute-start(bf16[272,256]{1,0:T(8,128)(2,1)S(1)} %get-tuple-element.25.refs_0_), channel_id=1, source_target_pairs={{0,8},{8,0},{16,24},{24,16},{1,9},{9,1},{17,25},{25,17},{2,10},{10... | collective-permute-start | bytes 417800 | tf_op jit(solution)/shard_map/ppermute | solution.py:383
  28.7 1.3 %collective-permute-start.10 = (f32[17,8,128]{2,1,0:T(8,128)S(1)}, f32[17,8,128]{2,1,0:T(8,128)S(1)}, u32[]{:S(2)}, u32[]{:S(2)}) collective-permute-start(f32[17,8,128]{2,1,0:T(8,128)S(1)} %get-tuple-element.27), channel_id=1, source_target_pairs={{0,1},{1,0},{2,3},{3,2},{4,5},{5,4},{6,7},{7,6},{8,9},{9,8},{10,11... | collective-permute-start | bytes 208904 | tf_op jit(solution)/shard_map/ppermute | solution.py:383
  30.0 7.0 %collective-permute-start.13 = (f32[17,8,128]{2,1,0:T(8,128)S(1)}, f32[17,8,128]{2,1,0:T(8,128)S(1)}, u32[]{:S(2)}, u32[]{:S(2)}) collective-permute-start(f32[17,8,128]{2,1,0:T(8,128)S(1)} %pair.1.refs_0_), channel_id=1, source_target_pairs={{0,6},{1,7},{2,4},{3,5},{4,2},{5,3},{6,0},{7,1},{8,14},{9,15},{10,... | collective-permute-start | bytes 208904 | tf_op jit(solution)/shard_map/ppermute | solution.py:383
  32.4 6.7 %collective-permute-start.12 = (f32[17,8,128]{2,1,0:T(8,128)S(1)}, f32[17,8,128]{2,1,0:T(8,128)S(1)}, u32[]{:S(2)}, u32[]{:S(2)}) collective-permute-start(f32[17,8,128]{2,1,0:T(8,128)S(1)} %pair.1.refs_0_), channel_id=1, source_target_pairs={{0,4},{1,5},{2,6},{3,7},{4,0},{5,1},{6,2},{7,3},{8,12},{9,13},{10,... | collective-permute-start | bytes 208904 | tf_op jit(solution)/shard_map/ppermute | solution.py:383
  32.4 6.7 %collective-permute-start.11 = (f32[17,8,128]{2,1,0:T(8,128)S(1)}, f32[17,8,128]{2,1,0:T(8,128)S(1)}, u32[]{:S(2)}, u32[]{:S(2)}) collective-permute-start(f32[17,8,128]{2,1,0:T(8,128)S(1)} %pair.1.refs_0_), channel_id=1, source_target_pairs={{0,2},{1,3},{2,0},{3,1},{4,6},{5,7},{6,4},{7,5},{8,10},{9,11},{10,... | collective-permute-start | bytes 208904 | tf_op jit(solution)/shard_map/ppermute | solution.py:383
  39.2 1.3 %collective-permute-start.14 = (bf16[80,256]{1,0:T(8,128)(2,1)S(1)}, bf16[80,256]{1,0:T(8,128)(2,1)S(1)}, u32[]{:S(2)}, u32[]{:S(2)}) collective-permute-start(bf16[80,256]{1,0:T(8,128)(2,1)S(1)} %get-tuple-element.29.refs_0_), channel_id=1, source_target_pairs={{0,1},{1,0},{2,3},{3,2},{4,5},{5,4},{6,7},{7,6},{8,9},{9,8},{10,11... | collective-permute-start | bytes 122888 | tf_op jit(solution)/shard_map/ppermute | solution.py:383
  41.7 7.5 %collective-permute-start.17 = (bf16[272,256]{1,0:T(8,128)(2,1)S(1)}, bf16[272,256]{1,0:T(8,128)(2,1)S(1)}, u32[]{:S(2)}, u32[]{:S(2)}) collective-permute-start(bf16[272,256]{1,0:T(8,128)(2,1)S(1)} %adjoint.3.refs_0_.unread_ref), channel_id=1, source_target_pairs={{0,24},{8,16},{16,8},{24,0},{1,25},{9,17},{17,9},{25,1},{2,26},{10... | collective-permute-start | bytes 417800 | tf_op jit(solution)/shard_map/ppermute | solution.py:383
  43.4 8.0 %collective-permute-start.16 = (bf16[272,256]{1,0:T(8,128)(2,1)S(1)}, bf16[272,256]{1,0:T(8,128)(2,1)S(1)}, u32[]{:S(2)}, u32[]{:S(2)}) collective-permute-start(bf16[272,256]{1,0:T(8,128)(2,1)S(1)} %adjoint.3.refs_0_.unread_ref), channel_id=1, source_target_pairs={{0,16},{8,24},{16,0},{24,8},{1,17},{9,25},{17,1},{25,9},{2,18},{10... | collective-permute-start | bytes 417800 | tf_op jit(solution)/shard_map/ppermute | solution.py:383
  44.7 6.7 %collective-permute-start.15 = (bf16[272,256]{1,0:T(8,128)(2,1)S(1)}, bf16[272,256]{1,0:T(8,128)(2,1)S(1)}, u32[]{:S(2)}, u32[]{:S(2)}) collective-permute-start(bf16[272,256]{1,0:T(8,128)(2,1)S(1)} %adjoint.3.refs_0_.unread_ref), channel_id=1, source_target_pairs={{0,8},{8,0},{16,24},{24,16},{1,9},{9,1},{17,25},{25,17},{2,10},{10... | collective-permute-start | bytes 417800 | tf_op jit(solution)/shard_map/ppermute | solution.py:383
  66.3 14.6 %all-to-all-start.1 = ((f32[32,8,128]{2,1,0:T(8,128)}), f32[32,8,128]{2,1,0:T(8,128)S(1)}, u32[]{:S(2)}, u32[]{:S(2)}) async-start(f32[32,8,128]{2,1,0:T(8,128)} %get-tuple-element.38.refs_0_), calls=%async_computation.1 | async-start | bytes 262144 | tf_op jit(solution)/shard_map/all_to_all | solution.py:391
  69.4 8.4 %collective-permute-start.20 = (bf16[256,256]{1,0:T(8,128)(2,1)S(1)}, bf16[256,256]{1,0:T(8,128)(2,1)S(1)}, u32[]{:S(2)}, u32[]{:S(2)}) collective-permute-start(bf16[256,256]{1,0:T(8,128)(2,1)S(1)} %get-tuple-element.42.refs_3_), channel_id=1, source_target_pairs={{0,24},{8,16},{16,8},{24,0},{1,25},{9,17},{17,9},{25,1},{2,26},{10... | collective-permute-start | bytes 393224 | tf_op jit(solution)/shard_map/ppermute | solution.py:383
  72.2 7.9 %collective-permute-start.19 = (bf16[256,256]{1,0:T(8,128)(2,1)S(1)}, bf16[256,256]{1,0:T(8,128)(2,1)S(1)}, u32[]{:S(2)}, u32[]{:S(2)}) collective-permute-start(bf16[256,256]{1,0:T(8,128)(2,1)S(1)} %get-tuple-element.42.refs_3_), channel_id=1, source_target_pairs={{0,16},{8,24},{16,0},{24,8},{1,17},{9,25},{17,1},{25,9},{2,18},{10... | collective-permute-start | bytes 393224 | tf_op jit(solution)/shard_map/ppermute | solution.py:383
  72.7 7.4 %collective-permute-start.18 = (bf16[256,256]{1,0:T(8,128)(2,1)S(1)}, bf16[256,256]{1,0:T(8,128)(2,1)S(1)}, u32[]{:S(2)}, u32[]{:S(2)}) collective-permute-start(bf16[256,256]{1,0:T(8,128)(2,1)S(1)} %get-tuple-element.42.refs_3_), channel_id=1, source_target_pairs={{0,8},{8,0},{16,24},{24,16},{1,9},{9,1},{17,25},{25,17},{2,10},{10... | collective-permute-start | bytes 393224 | tf_op jit(solution)/shard_map/ppermute | solution.py:383

commit v9 on v8

--- a/solution.py
+++ b/solution.py
@@ -64,17 +64,19 @@
     return blocks
 
 
-def pack_kernel(flat, left_ref, unread_ref, payload_ref, blocks_ref):
+def pack_kernel(obs_ref, unread_ref, blocks_ref):
     count = blocks_ref.shape[0] - 1
-    blocks = ray_blocks(left_ref, count) if flat else [left_ref[b] for b in range(count)]
-    rows = payload_ref.shape[0]
-    payload_ref[:, : 2 * LANES] = packed(blocks, rows)
-    payload_ref[:, 2 * LANES :] = jnp.zeros((rows, LANES), jnp.bfloat16)
-    squares = packed_squares(tree_sum([b * b for b in blocks]))
-    payload_ref[:16, 2 * LANES :] = squares
+    blocks = ray_blocks(obs_ref, count)
     for b, block in enumerate(blocks):
         blocks_ref[b] = block
-    blocks_ref[count] = read_squares(squares)
+    blocks_ref[count] = tree_sum([b * b for b in blocks])
+
+
+def join_kernel(own_ref, other_ref, both_ref):
+    count = own_ref.shape[0] - 1
+    both_ref[:count] = own_ref[:count]
+    both_ref[count : 2 * count] = other_ref[:count]
+    both_ref[2 * count] = own_ref[count] + other_ref[count]
 
 
 def keys_kernel(unread_ref, cols_ref, keys_ref):
@@ -135,17 +137,14 @@
     per_share = row_tiles // shares
     terms = row_tiles * per_block * RHS
     if first:
-        payloads, (term_ref, lower_ref) = refs[:shares], refs[shares:]
-        rows = payloads[1].shape[0]
+        pairs, (term_ref, lower_ref) = refs[: shares // 2], refs[shares // 2 :]
         squares, sources = [], []
-        for d in range(shares):
-            owner = jnp.bitwise_xor(me, d)
-            if d % 2:
-                squares.append(read_squares(payloads[d][:16, 2 * LANES :]))
-                sources.append((owner, payloads[d][:, : 2 * LANES]))
-            else:
-                squares.append(payloads[d][per_share])
-                sources.append((owner, packed([payloads[d][b] for b in range(per_share)], rows)))
+        for e, pair in enumerate(pairs):
+            squares.append(pair[2 * per_share])
+            for h in range(2):
+                blocks = [pair[h * per_share + b] for b in range(per_share)]
+                owner = jnp.bitwise_xor(me, 2 * e + h)
+                sources.append((owner, packed(blocks, max(16, 4 * per_share))))
     else:
         halves, (term_ref,) = refs[:2], refs[2:]
         rows = (halves[0].shape[0] - 16) // (shares // 2)
@@ -192,7 +191,7 @@
         own_ref, other_ref, beta_ref, raw_ref, all_ref, equal_ref, weight_ref, keys_ref = refs
     else:
         equal_ref, weight_ref, right_ref, alpha_ref = refs[:4]
-        out_ref, beta_ref, raw_ref, all_ref = refs[-4:]
+        own_ref, other_ref, beta_ref, raw_ref, all_ref = refs[-5:]
     my_row = lax.axis_index("row")
     row_tiles, per_block = tiles_ref.shape[:2]
     shares = lax.axis_size("col")
@@ -230,13 +229,9 @@
             acc = acc + (square[:, :LANES] + square[:, LANES:]) * weight_ref[at : at + 8]
     own = my_row * per_row
     core = lax.axis_index("col") % 2
-    for e in range(shares):
-        if first:
-            half, slot = divmod(e, shares // 2)
-            c = 2 * slot + jnp.bitwise_xor(core, half)
-            ref, at = (own_ref, other_ref)[half], slot * per_share
-        else:
-            c, ref, at = e, out_ref.at[e], 0
+    for half, slot in [(h, s) for h in range(2) for s in range(shares // 2)]:
+        c = 2 * slot + jnp.bitwise_xor(core, half)
+        ref, at = (own_ref, other_ref)[half], slot * per_share
         for g in range(per_share // 2):
             i = c * per_share + 2 * g
             lhs = raw_ref[pl.ds(pl.multiple_of(own + 8 * i, 16), 16), :].astype(jnp.bfloat16)
@@ -250,21 +245,22 @@
             value = jnp.where(low, wide[0], wide[3]) + pltpu.roll(jnp.where(low, wide[2], wide[1]), 4, 0)
             ref[at + 2 * g] = value[:, :LANES]
             ref[at + 2 * g + 1] = value[:, LANES:]
-        if not first:
-            ref[per_share] = acc
-    if first:
-        own_ref[own_ref.shape[0] - 1] = acc
-        other_ref[own_ref.shape[0] - 1] = acc
-
-
-def pair_kernel(own_ref, other_ref, out_ref):
-    out_ref[...] = own_ref[...] + other_ref[...]
-
-
-def half_ray_kernel(peers, *refs):
-    parts, lefts = refs[:peers], refs[peers : 2 * peers]
-    beta_ref, raw_ref, alpha_ref, half_ref = refs[2 * peers :]
-    per_share = raw_ref.shape[0]
+    own_ref[own_ref.shape[0] - 1] = acc
+    other_ref[own_ref.shape[0] - 1] = acc
+
+
+def pair_kernel(*refs):
+    passed = (len(refs) - 3) // 2
+    refs[2 + passed][...] = refs[0][...] + refs[1][...]
+    for i in range(passed):
+        refs[3 + passed + i][...] = refs[2 + i][...]
+
+
+def half_ray_kernel(peers, first, unread, *refs):
+    refs = refs[unread:]
+    parts, refs = refs[:peers], refs[peers:]
+    lefts, (beta_ref, raw_ref, alpha_ref, half_ref, acc_ref) = refs[:-5], refs[-5:]
+    per_share = raw_ref.shape[0] // peers
     rows = (half_ref.shape[0] - 16) // peers
     alpha = norm_of(tree_sum([p[p.shape[0] - 1] for p in parts]))
     alpha_ref[...] = alpha
@@ -275,20 +271,22 @@
         slot = jnp.bitwise_xor(lax.axis_index("col") // 2, e)
         blocks = []
         for b in range(per_share):
-            total = tree_sum([p[slot * per_share + b] for p in parts])
-            blocks.append(total * alpha_inv - lefts[e][b] * left_scale)
-            if e == 0:
-                raw_ref[b] = blocks[-1]
+            at = slot * per_share + b
+            left = lefts[e][b] if first else lefts[0][at]
+            blocks.append(tree_sum([p[at] for p in parts]) * alpha_inv - left * left_scale)
+            raw_ref[at] = blocks[-1]
         half_ref[pl.ds(pl.multiple_of(slot * rows, 16), rows), :] = packed(blocks, rows)
         squares.append(tree_sum([b * b for b in blocks]))
-    pieces = packed_squares(tree_sum(squares))
+    acc = tree_sum(squares)
+    acc_ref[...] = acc
+    pieces = packed_squares(acc)
     half_ref[peers * rows :, :LANES] = pieces
     half_ref[peers * rows :, LANES:] = jnp.zeros_like(pieces)
 
 
 def share_kernel(remainders, *refs):
-    pick_ref, all_ref = refs[1:3]
-    lower_terms, out_ref = refs[3 : 3 + remainders], refs[3 + remainders]
+    pick_ref, all_ref = refs[:2]
+    lower_terms, out_ref = refs[2 : 2 + remainders], refs[2 + remainders]
     values = [all_ref]
     if remainders:
         held = refs[-1]
@@ -309,30 +307,14 @@
     fill_pick(keys_ref, pick_ref)
 
 
-def ray_kernel(part_ref, left_ref, beta_ref, lower_ref, raw_ref, alpha_ref, acc_ref, passed_ref):
-    passed_ref[...] = lower_ref[...]
-    shares, count = part_ref.shape[0], raw_ref.shape[0]
-    alpha = norm_of(tree_sum([part_ref[c, count] for c in range(shares)]))
-    alpha_ref[...] = alpha
-    alpha_inv = 1.0 / alpha
-    left_scale = alpha / beta_ref[...]
-    blocks = []
-    for b in range(count):
-        total = tree_sum([part_ref[c, b] for c in range(shares)])
-        blocks.append(total * alpha_inv - left_ref[b] * left_scale)
-        raw_ref[b] = blocks[-1]
-    acc = tree_sum([b * b for b in blocks])
-    for c in range(acc_ref.shape[0]):
-        acc_ref[c] = acc
-
-
-def final_kernel(iters, last_ref, *refs):
+def final_kernel(rows, iters, *refs):
     refs = list(refs)
+    last = [refs.pop(0) for _ in range(rows)]
     betas = [refs.pop(0) for _ in range(iters)]
     alphas = [refs.pop(0) for _ in range(iters)]
     products = [refs.pop(0) for _ in range(iters)]
     out_ref, ratio_ref = refs
-    beta = [b[...] for b in betas] + [norm_of(tree_sum([last_ref[r] for r in range(last_ref.shape[0])]))]
+    beta = [b[...] for b in betas] + [norm_of(tree_sum([p[...] for p in last]))]
     alpha = [a[...] for a in alphas]
     phibar, rhobar = beta[0], alpha[0]
     direction = [1.0 / alpha[0]] + [jnp.zeros_like(phibar)] * (iters - 1)
@@ -387,10 +369,6 @@
     return [value] + [from_peer(value, axis, d) for d in range(step, lax.axis_size(axis), step)]
 
 
-def swap(values, axis):
-    return lax.all_to_all(values, axis, 0, 0)
-
-
 def local(observed, tile_values, tile_cols):
     row_tiles, per_block, tile_size = tile_values.shape[:3]
     rows, shares = lax.axis_size("row"), lax.axis_size("col")
@@ -398,9 +376,9 @@
     per_share = row_tiles // shares
     per_row = row_tiles * per_block * RHS
     share_rows = col_tiles // rows * RHS
-    payload = bf16(max(16, 4 * per_share), 3 * LANES)
+    ray_rows = max(16, RHS * per_share)
     half_shares = shares // 2
-    half_parts = f32(half_shares * per_share + 1, 8, LANES)
+    half_blocks = half_shares * per_share
     def call(kernel, name, out_shape, args, in_specs=None, scratch=()):
         return pl.pallas_call(
             kernel,
@@ -412,20 +390,6 @@
             name=name,
         )(*args)
 
-    def pack(left, unread):
-        flat = left.ndim == 2
-        message, blocks = call(
-            functools.partial(pack_kernel, flat),
-            "pack",
-            [payload, f32(per_share + 1, 8, LANES)],
-            [left, unread],
-            [VMEM, HBM],
-        )
-        gathered = [blocks]
-        for d in range(1, shares):
-            gathered.append(from_peer(message if d % 2 else blocks, "col", d))
-        return message, gathered
-
     def adjoint(payloads, first):
         out_shape = [bf16(per_row + 16, tile_size)] + [bf16(per_row, tile_size)] * first
         args = [keys, tile_values, *payloads]
@@ -433,7 +397,7 @@
 
     def voxel(term_list, previous):
         first = not previous
-        out_shape = [half_parts] * 2 if first else [f32(shares, per_share + 1, 8, LANES)]
+        out_shape = [f32(half_blocks + 1, 8, LANES)] * 2
         out_shape += [f32(8, LANES), f32(rows * per_row, tile_size), bf16(rows * per_row, tile_size)]
         if first:
             out_shape += [
@@ -444,45 +408,62 @@
         args = [tile_values, *term_list, *previous]
         return call(functools.partial(voxel_kernel, first, rows), "voxel", out_shape, args)
 
-    def half_ray(parts, lefts, beta):
-        out_shape = [f32(per_share, 8, LANES), f32(8, LANES), bf16(half_shares * payload.shape[0] + 16, 2 * LANES)]
-        kernel = functools.partial(half_ray_kernel, half_shares)
-        return call(kernel, "half_ray", out_shape, [*parts, *lefts, beta])
+    def pair(own, other, passed):
+        args = [own, from_peer(other, "col", 1), *passed]
+        out_shape = [jax.ShapeDtypeStruct(x.shape, x.dtype) for x in [own, *passed]]
+        return call(pair_kernel, "pair", out_shape, args)
+
+    def half_ray(parts, lefts, beta, after):
+        out_shape = [
+            f32(half_blocks, 8, LANES),
+            f32(8, LANES),
+            bf16(half_shares * ray_rows + 16, 2 * LANES),
+            f32(8, LANES),
+        ]
+        kernel = functools.partial(half_ray_kernel, half_shares, len(lefts) > 1, len(after))
+        args = [*after, *parts, *lefts, beta]
+        specs = [ANY] * len(after) + [VMEM] * (len(args) - len(after))
+        return call(kernel, "half_ray", out_shape, args, specs)
 
     def share(selector, all_terms, lower_terms):
         scratch = [pltpu.VMEM((rows * per_row, tile_size), jnp.bfloat16)] * (len(lower_terms) > 0)
         kernel = functools.partial(share_kernel, len(lower_terms))
-        args = [squares, selector, all_terms, *lower_terms]
-        specs = [ANY] + [VMEM] * (len(args) - 1)
-        return call(kernel, "share", f32(share_rows, tile_size), args, specs, scratch)
-
-    def ray(parts, left_raw, beta, passed):
-        out_shape = [f32(per_share, 8, LANES), f32(8, LANES), f32(rows * shares, 8, LANES), bf16(per_row, tile_size)]
-        return call(ray_kernel, "ray", out_shape, [parts, left_raw, beta, passed])
+        args = [selector, all_terms, *lower_terms]
+        return call(kernel, "share", f32(share_rows, tile_size), args, None, scratch)
 
     far = pltpu.with_memory_space_constraint(tile_values, pltpu.HBM)
-    message, gathered = pack(observed, far)
-    keys = call(keys_kernel, "keys", f32(8, per_row), [message, tile_cols.T], [ANY, SMEM])
-    terms, remainder = adjoint(gathered, True)
-    own, other, beta0, right_raw0, combined0, equal, weight, all_keys = voxel(exchange(terms, "row"), [])
-    pair = call(pair_kernel, "pair", half_parts, [own, from_peer(other, "col", 1)])
-    left_raw, alpha0, half = half_ray(exchange(pair, "col", 2), gathered[::2], beta0)
-    (terms,) = adjoint([half, from_peer(half, "col", 1)], False)
-    selector = call(pick_kernel, "pick", bf16(share_rows, rows * per_row), [terms, all_keys], [ANY, VMEM])
-    parts, beta1, right_raw1, combined1 = voxel(exchange(terms, "row"), [equal, weight, right_raw0, alpha0])
-    left_raw, alpha1, squares, remainder = ray(swap(parts, "col"), left_raw, beta1, remainder)
-    terms, _ = adjoint(pack(left_raw, far)[1], True)
-    voxel(exchange(terms, "row"), [equal, weight, right_raw1, alpha1])
-    products = [share(selector, combined0, exchange(remainder, "row")), share(selector, combined1, [])]
-    betas, alphas = [beta0, beta1], [alpha0, alpha1]
+    blocks = call(pack_kernel, "pack", f32(per_share + 1, 8, LANES), [observed, far], [VMEM, HBM])
+    keys = call(keys_kernel, "keys", f32(8, per_row), [blocks, tile_cols.T], [ANY, SMEM])
+    both = call(join_kernel, "join", f32(2 * per_share + 1, 8, LANES), [blocks, from_peer(blocks, "col", 1)])
+    lefts = exchange(both, "col", 2)
+    terms, remainder = adjoint(lefts, True)
+    own, other, beta, right_raw, upper_terms, equal, weight, all_keys = voxel(exchange(terms, "row"), [])
+    betas, alphas, combined = [], [], []
+    for iteration in range(ITERS):
+        last = iteration == ITERS - 1
+        betas.append(beta)
+        combined.append(upper_terms)
+        summed, *passed = pair(own, other, [remainder] * last)
+        remainders = exchange(passed[0], "row") if last else []
+        left_raw, alpha, half, squares = half_ray(exchange(summed, "col", 2), lefts, beta, remainders)
+        alphas.append(alpha)
+        lefts = [left_raw]
+        (terms,) = adjoint([half, from_peer(half, "col", 1)], False)
+        if iteration == 0:
+            selector = call(pick_kernel, "pick", bf16(share_rows, rows * per_row), [terms, all_keys], [ANY, VMEM])
+        own, other, beta, right_raw, upper_terms = voxel(
+            exchange(terms, "row"), [equal, weight, right_raw, alpha]
+        )
+    products = [share(selector, c, [] if i else remainders) for i, c in enumerate(combined)]
+    (squares,) = call(pair_kernel, "pair", [f32(8, LANES)], [squares, from_peer(squares, "col", 1)])
     result, ratio = pl.pallas_call(
-        functools.partial(final_kernel, ITERS),
+        functools.partial(final_kernel, rows, ITERS),
         out_shape=[f32(RHS, col_tiles // rows * tile_size), f32(RHS)],
-        in_specs=[VMEM] * (1 + 3 * ITERS),
+        in_specs=[VMEM] * (rows + 3 * ITERS),
         out_specs=[VMEM, SMEM],
         compiler_params=PARAMS,
         name="final",
-    )(swap(squares, ("row", "col")), *betas, *alphas, *products)
+    )(*exchange(squares, "row"), *betas, *alphas, *products)
     return result, ratio
 
 

time: 82.5 us -> 75.7 us (0.918)
  blocking collectives: 10.6 us -> 0 us
  waiting for transfers between devices: 27.4 us -> 30.6 us
    all_to_all x1 -> x0, blocking collectives: 10.6 us -> none  [swap(): return lax.all_to_all(values, axis, 0, 0)]
    ppermute x21 -> x26, starting transfers between devices: 25.2 us -> 28.9 us  [from_peer(): lax.ppermute(value, axis, [(i, i ^ d) for i in range(lax.axis_size(axis))])]
    ppermute x21 -> x26, waiting for transfers between devices: 27.4 us -> 30.6 us  [from_peer(): lax.ppermute(value, axis, [(i, i ^ d) for i in range(lax.axis_size(axis))])]
    all_to_all x1 -> x0, starting transfers between devices: 3.12 us -> none  [swap(): return lax.all_to_all(values, axis, 0, 0)]
    pallas_call x12 -> x15, Pallas kernels: 12.9 us -> 13 us  [call(): pl.pallas_call(kernel, out_shape=out_shape, in_specs=in_specs or [VMEM] *...]
  transfers between devices with their start and end apart: 22 -> 26, of which waited for: 12 -> 19; matrix products, arithmetic and copies ran while one was open for 0% -> 0% of each run, Pallas kernels for 3% -> 3%
where the time goes in v9:
time: 75.7 us; the launch traced here: 75.5 us
  waiting for transfers between devices  30.6 us (40%)
  starting transfers between devices  28.9 us (38%)
  Pallas kernels  14.3 us (19%)
  local copies, waits for them, and re-layouts  0.87 us (1%)
  between operations  0.76 us (1%)
    ppermute x26, waiting for transfers between devices, from_peer(): lax.ppermute(value, axis, [(i, i ^ d) for i in range(lax.axis_size(axis))])  30.6 us
    ppermute x26, starting transfers between devices, from_peer(): lax.ppermute(value, axis, [(i, i ^ d) for i in range(lax.axis_size(axis))])  28.9 us
    pallas_call x15, Pallas kernels, call(): pl.pallas_call(kernel, out_shape=out_shape, in_specs=in_specs or [VMEM] *...  13 us
  transfers between devices with their start and end apart: 26, of which 19 were waited for; matrix products, arithmetic and copies ran while one was open for 0% of the time, Pallas kernels for 3%

profile of v9, /device:TPU:0, one launch (start us, length us, event | category | flops | bytes accessed | tf_op | source)
XLA Modules:
  0.0 75.5 jit_solution(3626963547566812467)
XLA Ops:
  0.6 0.9 %copy-done.1 = f32[4,1024]{1,0:T(4,128)S(1)} copy-done((f32[4,1024]{1,0:T(4,128)S(1)}, f32[4,1024]{1,0:T(4,128)}, u32[]{:S(2)}) %copy-start.1) | copy-done | bytes 16408
  1.5 0.5 collective-permute-start
  2.0 0.8 %collective-permute-done.other_ref = f32[5,8,128]{2,1,0:T(8,128)S(1)} collective-permute-done((f32[5,8,128]{2,1,0:T(8,128)S(1)}, f32[5,8,128]{2,1,0:T(8,128)S(1)}, u32[]{:S(2)}, u32[]{:S(2)}) %collective-permute-start) | collective-permute-done | bytes 20512 | tf_op jit(solution)/shard_map/ppermute | solution.py:365
  2.9 4.9 %collective-permute-start.3 = (f32[9,8,128]{2,1,0:T(8,128)S(1)}, f32[9,8,128]{2,1,0:T(8,128)S(1)}, u32[]{:S(2)}, u32[]{:S(2)}) collective-permute-start(f32[9,8,128]{2,1,0:T(8,128)S(1)} %join.1.refs_0_.refs_4_), channel_id=1, source_target_pairs={{0,6},{1,7},{2,4},{3,5},{4,2},{5,3},{6,0},{7,1},{8,14},{9,15},{10,... | collective-permute-start | bytes 110600 | tf_op jit(solution)/shard_map/ppermute | solution.py:365
  7.8 0.0 collective-permute-start.2
  7.8 0.6 collective-permute-start.1
  8.5 0.6 keys.1.keys_ref
  9.1 0.7 collective-permute-done.3.refs_3_.refs_7_
  9.8 2.9 %collective-permute-done.2.refs_2_.refs_6_ = f32[9,8,128]{2,1,0:T(8,128)S(1)} collective-permute-done((f32[9,8,128]{2,1,0:T(8,128)S(1)}, f32[9,8,128]{2,1,0:T(8,128)S(1)}, u32[]{:S(2)}, u32[]{:S(2)}) %collective-permute-start.2) | collective-permute-done | bytes 36896 | tf_op jit(solution)/shard_map/ppermute | solution.py:365
  12.7 0.0 collective-permute-done.1.refs_1_.refs_5_
  12.7 1.2 %adjoint.2 = (bf16[272,256]{1,0:T(8,128)(2,1)S(1)}, bf16[256,256]{1,0:T(8,128)(2,1)S(1)}) custom-call(f32[8,256]{1,0:T(8,128)S(1)} %keys.1.keys_ref, bf16[32,2,256,256]{3,2,1,0:T(8,128)(2,1)S(1)} %copy-done, f32[9,8,128]{2,1,0:T(8,128)S(1)} %join.1.refs_0_.refs_4_, f32[9,8,128]{2,1,0:T(8,128)S(1)} %collective-permute-done.1.refs_1_.refs_5_, ...), custom_call_target="tpu_custom_call" | custom-call | tf_op jit(solution)/shard_map/adjoint/pallas_call | solution.py:383
  13.9 2.5 %collective-permute-start.6 = (bf16[272,256]{1,0:T(8,128)(2,1)S(1)}, bf16[272,256]{1,0:T(8,128)(2,1)S(1)}, u32[]{:S(2)}, u32[]{:S(2)}) collective-permute-start(bf16[272,256]{1,0:T(8,128)(2,1)S(1)} %get-tuple-element.23.refs_0_), channel_id=1, source_target_pairs={{0,24},{8,16},{16,8},{24,0},{1,25},{9,17},{17,9},{25,1},{2,26},{10... | collective-permute-start | bytes 417800 | tf_op jit(solution)/shard_map/ppermute | solution.py:365
  16.4 0.5 collective-permute-start.5
  16.9 0.5 collective-permute-start.4
  17.4 3.4 %collective-permute-done.6.refs_3_ = bf16[272,256]{1,0:T(8,128)(2,1)S(1)} collective-permute-done((bf16[272,256]{1,0:T(8,128)(2,1)S(1)}, bf16[272,256]{1,0:T(8,128)(2,1)S(1)}, u32[]{:S(2)}, u32[]{:S(2)}) %collective-permute-start.6) | collective-permute-done | bytes 139296 | tf_op jit(solution)/shard_map/ppermute | solution.py:365
  20.8 1.7 %collective-permute-done.5.refs_2_ = bf16[272,256]{1,0:T(8,128)(2,1)S(1)} collective-permute-done((bf16[272,256]{1,0:T(8,128)(2,1)S(1)}, bf16[272,256]{1,0:T(8,128)(2,1)S(1)}, u32[]{:S(2)}, u32[]{:S(2)}) %collective-permute-start.5) | collective-permute-done | bytes 139296 | tf_op jit(solution)/shard_map/ppermute | solution.py:365
  22.6 0.1 collective-permute-done.4.refs_1_
  22.6 4.0 %voxel.2 = (f32[17,8,128]{2,1,0:T(8,128)S(1)}, f32[17,8,128]{2,1,0:T(8,128)S(1)}, f32[8,128]{1,0:T(8,128)S(1)}, f32[1024,256]{1,0:T(8,128)S(1)}, bf16[1024,256]{...) custom-call(bf16[32,2,256,256]{3,2,1,0:T(8,128)(2,1)S(1)} %copy-done, ...), custom_call_target="tpu_custom_call" | custom-call | tf_op jit(solution)/shard_map/voxel/pallas_call | solution.py:383
  26.6 0.1 collective-permute-start.7
  26.7 1.3 %collective-permute-done.7.refs_1_ = f32[17,8,128]{2,1,0:T(8,128)S(1)} collective-permute-done((f32[17,8,128]{2,1,0:T(8,128)S(1)}, f32[17,8,128]{2,1,0:T(8,128)S(1)}, u32[]{:S(2)}, u32[]{:S(2)}) %collective-permute-start.7) | collective-permute-done | bytes 69664 | tf_op jit(solution)/shard_map/ppermute | solution.py:365
  28.0 1.6 %collective-permute-start.10 = (f32[17,8,128]{2,1,0:T(8,128)S(1)}, f32[17,8,128]{2,1,0:T(8,128)S(1)}, u32[]{:S(2)}, u32[]{:S(2)}) collective-permute-start(f32[17,8,128]{2,1,0:T(8,128)S(1)} %pair.3.refs_0_), channel_id=1, source_target_pairs={{0,6},{1,7},{2,4},{3,5},{4,2},{5,3},{6,0},{7,1},{8,14},{9,15},{10,... | collective-permute-start | bytes 208904 | tf_op jit(solution)/shard_map/ppermute | solution.py:365
  29.6 0.4 collective-permute-start.9
  30.0 2.5 %collective-permute-start.8 = (f32[17,8,128]{2,1,0:T(8,128)S(1)}, f32[17,8,128]{2,1,0:T(8,128)S(1)}, u32[]{:S(2)}, u32[]{:S(2)}) collective-permute-start(f32[17,8,128]{2,1,0:T(8,128)S(1)} %pair.3.refs_0_), channel_id=1, source_target_pairs={{0,2},{1,3},{2,0},{3,1},{4,6},{5,7},{6,4},{7,5},{8,10},{9,11},{10,... | collective-permute-start | bytes 208904 | tf_op jit(solution)/shard_map/ppermute | solution.py:365
  32.4 2.5 %collective-permute-done.10.refs_3_ = f32[17,8,128]{2,1,0:T(8,128)S(1)} collective-permute-done((f32[17,8,128]{2,1,0:T(8,128)S(1)}, f32[17,8,128]{2,1,0:T(8,128)S(1)}, u32[]{:S(2)}, u32[]{:S(2)}) %collective-permute-start.10) | collective-permute-done | bytes 69664 | tf_op jit(solution)/shard_map/ppermute | solution.py:365
  34.9 2.1 %collective-permute-done.9.refs_2_ = f32[17,8,128]{2,1,0:T(8,128)S(1)} collective-permute-done((f32[17,8,128]{2,1,0:T(8,128)S(1)}, f32[17,8,128]{2,1,0:T(8,128)S(1)}, u32[]{:S(2)}, u32[]{:S(2)}) %collective-permute-start.9) | collective-permute-done | bytes 69664 | tf_op jit(solution)/shard_map/ppermute | solution.py:365
  37.1 0.0 collective-permute-done.8.refs_1_
  37.1 0.7 half_ray.2
  37.8 0.0 collective-permute-start.11
  37.8 1.2 %collective-permute-done.11.refs_1_ = bf16[80,256]{1,0:T(8,128)(2,1)S(1)} collective-permute-done((bf16[80,256]{1,0:T(8,128)(2,1)S(1)}, bf16[80,256]{1,0:T(8,128)(2,1)S(1)}, u32[]{:S(2)}, u32[]{:S(2)}) %collective-permute-start.11) | collective-permute-done | bytes 40992 | tf_op jit(solution)/shard_map/ppermute | solution.py:365
  39.0 1.2 %adjoint.3.refs_0_.unread_ref = bf16[272,256]{1,0:T(8,128)(2,1)S(1)} custom-call(f32[8,256]{1,0:T(8,128)S(1)} %keys.1.keys_ref, bf16[32,2,256,256]{3,2,1,0:T(8,128)(2,1)S(1)} %copy-done, bf16[80,256]{1,0:T(8,128)(2,1)S(1)} %get-tuple-element.27.refs_0_, bf16[80,256]{1,0:T(8,128)(2,1)S(1)} %collective-permute-done.11.refs_1_), custom_call_target="tpu_custom_call" | custom-call | tf_op jit(solution)/shard_map/adjoint/pallas_call | solution.py:383
  40.2 1.8 %collective-permute-start.14 = (bf16[272,256]{1,0:T(8,128)(2,1)S(1)}, bf16[272,256]{1,0:T(8,128)(2,1)S(1)}, u32[]{:S(2)}, u32[]{:S(2)}) collective-permute-start(bf16[272,256]{1,0:T(8,128)(2,1)S(1)} %adjoint.3.refs_0_.unread_ref), channel_id=1, source_target_pairs={{0,24},{8,16},{16,8},{24,0},{1,25},{9,17},{17,9},{25,1},{2,26},{10... | collective-permute-start | bytes 417800 | tf_op jit(solution)/shard_map/ppermute | solution.py:365
  42.0 1.3 %collective-permute-start.13 = (bf16[272,256]{1,0:T(8,128)(2,1)S(1)}, bf16[272,256]{1,0:T(8,128)(2,1)S(1)}, u32[]{:S(2)}, u32[]{:S(2)}) collective-permute-start(bf16[272,256]{1,0:T(8,128)(2,1)S(1)} %adjoint.3.refs_0_.unread_ref), channel_id=1, source_target_pairs={{0,16},{8,24},{16,0},{24,8},{1,17},{9,25},{17,1},{25,9},{2,18},{10... | collective-permute-start | bytes 417800 | tf_op jit(solution)/shard_map/ppermute | solution.py:365
  43.3 0.5 collective-permute-start.12
  43.8 3.9 %collective-permute-done.14.refs_3_ = bf16[272,256]{1,0:T(8,128)(2,1)S(1)} collective-permute-done((bf16[272,256]{1,0:T(8,128)(2,1)S(1)}, bf16[272,256]{1,0:T(8,128)(2,1)S(1)}, u32[]{:S(2)}, u32[]{:S(2)}) %collective-permute-start.14) | collective-permute-done | bytes 139296 | tf_op jit(solution)/shard_map/ppermute | solution.py:365
  47.7 2.2 %collective-permute-done.13.refs_2_ = bf16[272,256]{1,0:T(8,128)(2,1)S(1)} collective-permute-done((bf16[272,256]{1,0:T(8,128)(2,1)S(1)}, bf16[272,256]{1,0:T(8,128)(2,1)S(1)}, u32[]{:S(2)}, u32[]{:S(2)}) %collective-permute-start.13) | collective-permute-done | bytes 139296 | tf_op jit(solution)/shard_map/ppermute | solution.py:365
  49.9 0.0 collective-permute-done.12.refs_1_
  49.9 3.0 %voxel.3 = (f32[17,8,128]{2,1,0:T(8,128)S(1)}, f32[17,8,128]{2,1,0:T(8,128)S(1)}, f32[8,128]{1,0:T(8,128)S(1)}, f32[1024,256]{1,0:T(8,128)}, bf16[1024,256]{1,0:T(8,128)(2,1)S(1)}) custom-call(bf16[32,2,256,256]{3,2,1,0:T(8,128)(2,1)S(1)} %copy-done, bf16[272,256]{1,0:T(8,128)(2,1)S(1)} %adjoint.3.refs_0_.unread_ref, ...), custom_call_target="tpu_custom_call" | custom-call | tf_op jit(solution)/shard_map/voxel/pallas_call | solution.py:383
  52.9 0.1 collective-permute-start.15
  53.0 1.3 %collective-permute-done.15.refs_1_ = f32[17,8,128]{2,1,0:T(8,128)S(1)} collective-permute-done((f32[17,8,128]{2,1,0:T(8,128)S(1)}, f32[17,8,128]{2,1,0:T(8,128)S(1)}, u32[]{:S(2)}, u32[]{:S(2)}) %collective-permute-start.15) | collective-permute-done | bytes 69664 | tf_op jit(solution)/shard_map/ppermute | solution.py:365
  54.3 2.3 %collective-permute-start.21 = (f32[17,8,128]{2,1,0:T(8,128)S(1)}, f32[17,8,128]{2,1,0:T(8,128)S(1)}, u32[]{:S(2)}, u32[]{:S(2)}) collective-permute-start(f32[17,8,128]{2,1,0:T(8,128)S(1)} %get-tuple-element.36.refs_4_), channel_id=1, source_target_pairs={{0,6},{1,7},{2,4},{3,5},{4,2},{5,3},{6,0},{7,1},{8,14},{9,15},{10,... | collective-permute-start | bytes 208904 | tf_op jit(solution)/shard_map/ppermute | solution.py:365
  56.6 1.7 %collective-permute-start.18 = (bf16[256,256]{1,0:T(8,128)(2,1)S(1)}, bf16[256,256]{1,0:T(8,128)(2,1)S(1)}, u32[]{:S(2)}, u32[]{:S(2)}) collective-permute-start(bf16[256,256]{1,0:T(8,128)(2,1)S(1)} %get-tuple-element.35.refs_0_.refs_2_), channel_id=1, source_target_pairs={{0,24},{8,16},{16,8},{24,0},{1,25},{9,17},{17,9},{25,1},{2,26},{10... | collective-permute-start | bytes 393224 | tf_op jit(solution)/shard_map/ppermute | solution.py:365
  58.3 1.3 %collective-permute-start.17 = (bf16[256,256]{1,0:T(8,128)(2,1)S(1)}, bf16[256,256]{1,0:T(8,128)(2,1)S(1)}, u32[]{:S(2)}, u32[]{:S(2)}) collective-permute-start(bf16[256,256]{1,0:T(8,128)(2,1)S(1)} %get-tuple-element.35.refs_0_.refs_2_), channel_id=1, source_target_pairs={{0,16},{8,24},{16,0},{24,8},{1,17},{9,25},{17,1},{25,9},{2,18},{10... | collective-permute-start | bytes 393224 | tf_op jit(solution)/shard_map/ppermute | solution.py:365
  59.6 0.5 collective-permute-start.16
  60.1 0.0 collective-permute-start.20
  60.1 0.3 collective-permute-done.21.refs_7_
  60.5 1.8 %collective-permute-start.19 = (f32[17,8,128]{2,1,0:T(8,128)S(1)}, f32[17,8,128]{2,1,0:T(8,128)S(1)}, u32[]{:S(2)}, u32[]{:S(2)}) collective-permute-start(f32[17,8,128]{2,1,0:T(8,128)S(1)} %get-tuple-element.36.refs_4_), channel_id=1, source_target_pairs={{0,2},{1,3},{2,0},{3,1},{4,6},{5,7},{6,4},{7,5},{8,10},{9,11},{10,... | collective-permute-start | bytes 208904 | tf_op jit(solution)/shard_map/ppermute | solution.py:365
  62.3 3.2 %collective-permute-done.20.refs_6_ = f32[17,8,128]{2,1,0:T(8,128)S(1)} collective-permute-done((f32[17,8,128]{2,1,0:T(8,128)S(1)}, f32[17,8,128]{2,1,0:T(8,128)S(1)}, u32[]{:S(2)}, u32[]{:S(2)}) %collective-permute-start.20) | collective-permute-done | bytes 69664 | tf_op jit(solution)/shard_map/ppermute | solution.py:365
  65.4 0.1 collective-permute-done.19.refs_5_
  65.6 0.0 collective-permute-done.18.refs_3_.refs_5_
  65.6 0.0 collective-permute-done.17.refs_2_.refs_4_
  65.6 0.0 collective-permute-done.16.refs_1_.refs_3_
  65.6 0.7 half_ray.3
  66.4 0.0 collective-permute-start.22
  66.4 1.2 %collective-permute-done.22.refs_1_ = f32[8,128]{1,0:T(8,128)S(1)} collective-permute-done((f32[8,128]{1,0:T(8,128)S(1)}, f32[8,128]{1,0:T(8,128)S(1)}, u32[]{:S(2)}, u32[]{:S(2)}) %collective-permute-start.22) | collective-permute-done | bytes 4128 | tf_op jit(solution)/shard_map/ppermute | solution.py:365
  67.5 1.7 %collective-permute-start.25 = (f32[8,128]{1,0:T(8,128)S(1)}, f32[8,128]{1,0:T(8,128)S(1)}, u32[]{:S(2)}, u32[]{:S(2)}) collective-permute-start(f32[8,128]{1,0:T(8,128)S(1)} %pair.5.refs_0_), channel_id=1, source_target_pairs={{0,24},{8,16},{16,8},{24,0},{1,25},{9,17},{17,9},{25,1},{2,26},{10... | collective-permute-start | bytes 12296 | tf_op jit(solution)/shard_map/ppermute | solution.py:365
  69.2 1.3 %collective-permute-start.24 = (f32[8,128]{1,0:T(8,128)S(1)}, f32[8,128]{1,0:T(8,128)S(1)}, u32[]{:S(2)}, u32[]{:S(2)}) collective-permute-start(f32[8,128]{1,0:T(8,128)S(1)} %pair.5.refs_0_), channel_id=1, source_target_pairs={{0,16},{8,24},{16,0},{24,8},{1,17},{9,25},{17,1},{25,9},{2,18},{10... | collective-permute-start | bytes 12296 | tf_op jit(solution)/shard_map/ppermute | solution.py:365
  70.5 0.5 collective-permute-start.23
  71.0 0.3 pick.1.refs_0_
  71.3 0.5 share.3.refs_9_
  71.8 0.8 %share.2.refs_8_ = f32[512,256]{1,0:T(8,128)S(1)} custom-call(bf16[512,1024]{1,0:T(8,128)(2,1)S(1)} %pick.1.refs_0_, bf16[1024,256]{1,0:T(8,128)(2,1)S(1)} %get-tuple-element.42.refs_1_, bf16[256,256]{1,0:T(8,128)(2,1)S(1)} %get-tuple-element.35.refs_0_.refs_2_, bf16[256,256]{1,0:T(8,128)(2,1)S(1)} %collective-permute-done.16.refs_1_.refs_3_, ...), custom_call_target="tpu_custom_call" | custom-call | tf_op jit(solution)/shard_map/share/pallas_call | solution.py:383
  72.6 0.0 collective-permute-done.25.refs_3_
  72.6 0.2 collective-permute-done.24.refs_2_
  72.8 1.3 %collective-permute-done.23.refs_1_ = f32[8,128]{1,0:T(8,128)S(1)} collective-permute-done((f32[8,128]{1,0:T(8,128)S(1)}, f32[8,128]{1,0:T(8,128)S(1)}, u32[]{:S(2)}, u32[]{:S(2)}) %collective-permute-start.23) | collective-permute-done | bytes 4128 | tf_op jit(solution)/shard_map/ppermute | solution.py:365
  74.1 1.3 %final.1 = (f32[4,32768]{1,0:T(4,128)}, f32[4]{0:T(128)}) custom-call(f32[8,128]{1,0:T(8,128)S(1)} %pair.5.refs_0_, f32[8,128]{1,0:T(8,128)S(1)} %collective-permute-done.23.refs_1_, f32[8,128]{1,0:T(8,128)S(1)} %collective-permute-done.24.refs_2_, f32[8,128]{1,0:T(8,128)S(1)} %collective-permute-done.25.refs_3_, ...), custom_call_target="tpu_custom_call" | custom-call | tf_op jit(solution)/shard_map/final/pallas_call | solution.py:459
  (10 shorter events, 0.1 us)
Async XLA Ops:
  0.6 12.1 %copy-start = (bf16[32,2,256,256]{3,2,1,0:T(8,128)(2,1)S(1)}, bf16[32,2,256,256]{3,2,1,0:T(8,128)(2,1)}, u32[]{:S(2)}) copy-start(bf16[32,2,256,256]{3,2,1,0:T(8,128)(2,1)} %tiles_ref.7) | copy-start | bytes 25165828
  0.6 0.9 %copy-start.1 = (f32[4,1024]{1,0:T(4,128)S(1)}, f32[4,1024]{1,0:T(4,128)}, u32[]{:S(2)}) copy-start(f32[4,1024]{1,0:T(4,128)} %obs_ref.1) | copy-start | bytes 49156
  1.5 7.0 %copy-start.2 = (s32[32,2]{0,1:T(2,128)S(1)}, s32[32,2]{0,1:T(2,128)}, u32[]{:S(2)}) copy-start(s32[32,2]{0,1:T(2,128)} %param.5) | copy-start | bytes 772
  1.5 1.4 %collective-permute-start = (f32[5,8,128]{2,1,0:T(8,128)S(1)}, f32[5,8,128]{2,1,0:T(8,128)S(1)}, u32[]{:S(2)}, u32[]{:S(2)}) collective-permute-start(f32[5,8,128]{2,1,0:T(8,128)S(1)} %pack.1.unread_ref.own_ref), channel_id=1, source_target_pairs={{0,1},{1,0},{2,3},{3,2},{4,5},{5,4},{6,7},{7,6},{8,9},{9,8},{10,11... | collective-permute-start | bytes 61448 | tf_op jit(solution)/shard_map/ppermute | solution.py:365
  2.9 6.9 %collective-permute-start.3 = (f32[9,8,128]{2,1,0:T(8,128)S(1)}, f32[9,8,128]{2,1,0:T(8,128)S(1)}, u32[]{:S(2)}, u32[]{:S(2)}) collective-permute-start(f32[9,8,128]{2,1,0:T(8,128)S(1)} %join.1.refs_0_.refs_4_), channel_id=1, source_target_pairs={{0,6},{1,7},{2,4},{3,5},{4,2},{5,3},{6,0},{7,1},{8,14},{9,15},{10,... | collective-permute-start | bytes 110600 | tf_op jit(solution)/shard_map/ppermute | solution.py:365
  7.8 4.9 %collective-permute-start.2 = (f32[9,8,128]{2,1,0:T(8,128)S(1)}, f32[9,8,128]{2,1,0:T(8,128)S(1)}, u32[]{:S(2)}, u32[]{:S(2)}) collective-permute-start(f32[9,8,128]{2,1,0:T(8,128)S(1)} %join.1.refs_0_.refs_4_), channel_id=1, source_target_pairs={{0,4},{1,5},{2,6},{3,7},{4,0},{5,1},{6,2},{7,3},{8,12},{9,13},{10,... | collective-permute-start | bytes 110600 | tf_op jit(solution)/shard_map/ppermute | solution.py:365
  7.8 4.9 %collective-permute-start.1 = (f32[9,8,128]{2,1,0:T(8,128)S(1)}, f32[9,8,128]{2,1,0:T(8,128)S(1)}, u32[]{:S(2)}, u32[]{:S(2)}) collective-permute-start(f32[9,8,128]{2,1,0:T(8,128)S(1)} %join.1.refs_0_.refs_4_), channel_id=1, source_target_pairs={{0,2},{1,3},{2,0},{3,1},{4,6},{5,7},{6,4},{7,5},{8,10},{9,11},{10,... | collective-permute-start | bytes 110600 | tf_op jit(solution)/shard_map/ppermute | solution.py:365
  13.9 6.9 %collective-permute-start.6 = (bf16[272,256]{1,0:T(8,128)(2,1)S(1)}, bf16[272,256]{1,0:T(8,128)(2,1)S(1)}, u32[]{:S(2)}, u32[]{:S(2)}) collective-permute-start(bf16[272,256]{1,0:T(8,128)(2,1)S(1)} %get-tuple-element.23.refs_0_), channel_id=1, source_target_pairs={{0,24},{8,16},{16,8},{24,0},{1,25},{9,17},{17,9},{25,1},{2,26},{10... | collective-permute-start | bytes 417800 | tf_op jit(solution)/shard_map/ppermute | solution.py:365
  16.4 6.2 %collective-permute-start.5 = (bf16[272,256]{1,0:T(8,128)(2,1)S(1)}, bf16[272,256]{1,0:T(8,128)(2,1)S(1)}, u32[]{:S(2)}, u32[]{:S(2)}) collective-permute-start(bf16[272,256]{1,0:T(8,128)(2,1)S(1)} %get-tuple-element.23.refs_0_), channel_id=1, source_target_pairs={{0,16},{8,24},{16,0},{24,8},{1,17},{9,25},{17,1},{25,9},{2,18},{10... | collective-permute-start | bytes 417800 | tf_op jit(solution)/shard_map/ppermute | solution.py:365
  16.9 5.7 %collective-permute-start.4 = (bf16[272,256]{1,0:T(8,128)(2,1)S(1)}, bf16[272,256]{1,0:T(8,128)(2,1)S(1)}, u32[]{:S(2)}, u32[]{:S(2)}) collective-permute-start(bf16[272,256]{1,0:T(8,128)(2,1)S(1)} %get-tuple-element.23.refs_0_), channel_id=1, source_target_pairs={{0,8},{8,0},{16,24},{24,16},{1,9},{9,1},{17,25},{25,17},{2,10},{10... | collective-permute-start | bytes 417800 | tf_op jit(solution)/shard_map/ppermute | solution.py:365
  26.6 1.3 %collective-permute-start.7 = (f32[17,8,128]{2,1,0:T(8,128)S(1)}, f32[17,8,128]{2,1,0:T(8,128)S(1)}, u32[]{:S(2)}, u32[]{:S(2)}) collective-permute-start(f32[17,8,128]{2,1,0:T(8,128)S(1)} %get-tuple-element.25), channel_id=1, source_target_pairs={{0,1},{1,0},{2,3},{3,2},{4,5},{5,4},{6,7},{7,6},{8,9},{9,8},{10,11... | collective-permute-start | bytes 208904 | tf_op jit(solution)/shard_map/ppermute | solution.py:365
  28.0 7.0 %collective-permute-start.10 = (f32[17,8,128]{2,1,0:T(8,128)S(1)}, f32[17,8,128]{2,1,0:T(8,128)S(1)}, u32[]{:S(2)}, u32[]{:S(2)}) collective-permute-start(f32[17,8,128]{2,1,0:T(8,128)S(1)} %pair.3.refs_0_), channel_id=1, source_target_pairs={{0,6},{1,7},{2,4},{3,5},{4,2},{5,3},{6,0},{7,1},{8,14},{9,15},{10,... | collective-permute-start | bytes 208904 | tf_op jit(solution)/shard_map/ppermute | solution.py:365
  29.6 7.5 %collective-permute-start.9 = (f32[17,8,128]{2,1,0:T(8,128)S(1)}, f32[17,8,128]{2,1,0:T(8,128)S(1)}, u32[]{:S(2)}, u32[]{:S(2)}) collective-permute-start(f32[17,8,128]{2,1,0:T(8,128)S(1)} %pair.3.refs_0_), channel_id=1, source_target_pairs={{0,4},{1,5},{2,6},{3,7},{4,0},{5,1},{6,2},{7,3},{8,12},{9,13},{10,... | collective-permute-start | bytes 208904 | tf_op jit(solution)/shard_map/ppermute | solution.py:365
  30.0 7.1 %collective-permute-start.8 = (f32[17,8,128]{2,1,0:T(8,128)S(1)}, f32[17,8,128]{2,1,0:T(8,128)S(1)}, u32[]{:S(2)}, u32[]{:S(2)}) collective-permute-start(f32[17,8,128]{2,1,0:T(8,128)S(1)} %pair.3.refs_0_), channel_id=1, source_target_pairs={{0,2},{1,3},{2,0},{3,1},{4,6},{5,7},{6,4},{7,5},{8,10},{9,11},{10,... | collective-permute-start | bytes 208904 | tf_op jit(solution)/shard_map/ppermute | solution.py:365
  37.8 1.2 %collective-permute-start.11 = (bf16[80,256]{1,0:T(8,128)(2,1)S(1)}, bf16[80,256]{1,0:T(8,128)(2,1)S(1)}, u32[]{:S(2)}, u32[]{:S(2)}) collective-permute-start(bf16[80,256]{1,0:T(8,128)(2,1)S(1)} %get-tuple-element.27.refs_0_), channel_id=1, source_target_pairs={{0,1},{1,0},{2,3},{3,2},{4,5},{5,4},{6,7},{7,6},{8,9},{9,8},{10,11... | collective-permute-start | bytes 122888 | tf_op jit(solution)/shard_map/ppermute | solution.py:365
  40.2 7.5 %collective-permute-start.14 = (bf16[272,256]{1,0:T(8,128)(2,1)S(1)}, bf16[272,256]{1,0:T(8,128)(2,1)S(1)}, u32[]{:S(2)}, u32[]{:S(2)}) collective-permute-start(bf16[272,256]{1,0:T(8,128)(2,1)S(1)} %adjoint.3.refs_0_.unread_ref), channel_id=1, source_target_pairs={{0,24},{8,16},{16,8},{24,0},{1,25},{9,17},{17,9},{25,1},{2,26},{10... | collective-permute-start | bytes 417800 | tf_op jit(solution)/shard_map/ppermute | solution.py:365
  42.0 7.9 %collective-permute-start.13 = (bf16[272,256]{1,0:T(8,128)(2,1)S(1)}, bf16[272,256]{1,0:T(8,128)(2,1)S(1)}, u32[]{:S(2)}, u32[]{:S(2)}) collective-permute-start(bf16[272,256]{1,0:T(8,128)(2,1)S(1)} %adjoint.3.refs_0_.unread_ref), channel_id=1, source_target_pairs={{0,16},{8,24},{16,0},{24,8},{1,17},{9,25},{17,1},{25,9},{2,18},{10... | collective-permute-start | bytes 417800 | tf_op jit(solution)/shard_map/ppermute | solution.py:365
  43.3 6.7 %collective-permute-start.12 = (bf16[272,256]{1,0:T(8,128)(2,1)S(1)}, bf16[272,256]{1,0:T(8,128)(2,1)S(1)}, u32[]{:S(2)}, u32[]{:S(2)}) collective-permute-start(bf16[272,256]{1,0:T(8,128)(2,1)S(1)} %adjoint.3.refs_0_.unread_ref), channel_id=1, source_target_pairs={{0,8},{8,0},{16,24},{24,16},{1,9},{9,1},{17,25},{25,17},{2,10},{10... | collective-permute-start | bytes 417800 | tf_op jit(solution)/shard_map/ppermute | solution.py:365
  52.9 1.3 %collective-permute-start.15 = (f32[17,8,128]{2,1,0:T(8,128)S(1)}, f32[17,8,128]{2,1,0:T(8,128)S(1)}, u32[]{:S(2)}, u32[]{:S(2)}) collective-permute-start(f32[17,8,128]{2,1,0:T(8,128)S(1)} %get-tuple-element.33), channel_id=1, source_target_pairs={{0,1},{1,0},{2,3},{3,2},{4,5},{5,4},{6,7},{7,6},{8,9},{9,8},{10,11... | collective-permute-start | bytes 208904 | tf_op jit(solution)/shard_map/ppermute | solution.py:365
  54.3 6.2 %collective-permute-start.21 = (f32[17,8,128]{2,1,0:T(8,128)S(1)}, f32[17,8,128]{2,1,0:T(8,128)S(1)}, u32[]{:S(2)}, u32[]{:S(2)}) collective-permute-start(f32[17,8,128]{2,1,0:T(8,128)S(1)} %get-tuple-element.36.refs_4_), channel_id=1, source_target_pairs={{0,6},{1,7},{2,4},{3,5},{4,2},{5,3},{6,0},{7,1},{8,14},{9,15},{10,... | collective-permute-start | bytes 208904 | tf_op jit(solution)/shard_map/ppermute | solution.py:365
  56.6 9.0 %collective-permute-start.18 = (bf16[256,256]{1,0:T(8,128)(2,1)S(1)}, bf16[256,256]{1,0:T(8,128)(2,1)S(1)}, u32[]{:S(2)}, u32[]{:S(2)}) collective-permute-start(bf16[256,256]{1,0:T(8,128)(2,1)S(1)} %get-tuple-element.35.refs_0_.refs_2_), channel_id=1, source_target_pairs={{0,24},{8,16},{16,8},{24,0},{1,25},{9,17},{17,9},{25,1},{2,26},{10... | collective-permute-start | bytes 393224 | tf_op jit(solution)/shard_map/ppermute | solution.py:365
  58.3 7.3 %collective-permute-start.17 = (bf16[256,256]{1,0:T(8,128)(2,1)S(1)}, bf16[256,256]{1,0:T(8,128)(2,1)S(1)}, u32[]{:S(2)}, u32[]{:S(2)}) collective-permute-start(bf16[256,256]{1,0:T(8,128)(2,1)S(1)} %get-tuple-element.35.refs_0_.refs_2_), channel_id=1, source_target_pairs={{0,16},{8,24},{16,0},{24,8},{1,17},{9,25},{17,1},{25,9},{2,18},{10... | collective-permute-start | bytes 393224 | tf_op jit(solution)/shard_map/ppermute | solution.py:365
  59.6 6.0 %collective-permute-start.16 = (bf16[256,256]{1,0:T(8,128)(2,1)S(1)}, bf16[256,256]{1,0:T(8,128)(2,1)S(1)}, u32[]{:S(2)}, u32[]{:S(2)}) collective-permute-start(bf16[256,256]{1,0:T(8,128)(2,1)S(1)} %get-tuple-element.35.refs_0_.refs_2_), channel_id=1, source_target_pairs={{0,8},{8,0},{16,24},{24,16},{1,9},{9,1},{17,25},{25,17},{2,10},{10... | collective-permute-start | bytes 393224 | tf_op jit(solution)/shard_map/ppermute | solution.py:365
  60.1 5.3 %collective-permute-start.20 = (f32[17,8,128]{2,1,0:T(8,128)S(1)}, f32[17,8,128]{2,1,0:T(8,128)S(1)}, u32[]{:S(2)}, u32[]{:S(2)}) collective-permute-start(f32[17,8,128]{2,1,0:T(8,128)S(1)} %get-tuple-element.36.refs_4_), channel_id=1, source_target_pairs={{0,4},{1,5},{2,6},{3,7},{4,0},{5,1},{6,2},{7,3},{8,12},{9,13},{10,... | collective-permute-start | bytes 208904 | tf_op jit(solution)/shard_map/ppermute | solution.py:365
  60.5 5.1 %collective-permute-start.19 = (f32[17,8,128]{2,1,0:T(8,128)S(1)}, f32[17,8,128]{2,1,0:T(8,128)S(1)}, u32[]{:S(2)}, u32[]{:S(2)}) collective-permute-start(f32[17,8,128]{2,1,0:T(8,128)S(1)} %get-tuple-element.36.refs_4_), channel_id=1, source_target_pairs={{0,2},{1,3},{2,0},{3,1},{4,6},{5,7},{6,4},{7,5},{8,10},{9,11},{10,... | collective-permute-start | bytes 208904 | tf_op jit(solution)/shard_map/ppermute | solution.py:365
  66.4 1.2 %collective-permute-start.22 = (f32[8,128]{1,0:T(8,128)S(1)}, f32[8,128]{1,0:T(8,128)S(1)}, u32[]{:S(2)}, u32[]{:S(2)}) collective-permute-start(f32[8,128]{1,0:T(8,128)S(1)} %get-tuple-element.39.refs_0_), channel_id=1, source_target_pairs={{0,1},{1,0},{2,3},{3,2},{4,5},{5,4},{6,7},{7,6},{8,9},{9,8},{10,11... | collective-permute-start | bytes 12296 | tf_op jit(solution)/shard_map/ppermute | solution.py:365
  67.5 5.0 %collective-permute-start.25 = (f32[8,128]{1,0:T(8,128)S(1)}, f32[8,128]{1,0:T(8,128)S(1)}, u32[]{:S(2)}, u32[]{:S(2)}) collective-permute-start(f32[8,128]{1,0:T(8,128)S(1)} %pair.5.refs_0_), channel_id=1, source_target_pairs={{0,24},{8,16},{16,8},{24,0},{1,25},{9,17},{17,9},{25,1},{2,26},{10... | collective-permute-start | bytes 12296 | tf_op jit(solution)/shard_map/ppermute | solution.py:365
  69.2 3.6 %collective-permute-start.24 = (f32[8,128]{1,0:T(8,128)S(1)}, f32[8,128]{1,0:T(8,128)S(1)}, u32[]{:S(2)}, u32[]{:S(2)}) collective-permute-start(f32[8,128]{1,0:T(8,128)S(1)} %pair.5.refs_0_), channel_id=1, source_target_pairs={{0,16},{8,24},{16,0},{24,8},{1,17},{9,25},{17,1},{25,9},{2,18},{10... | collective-permute-start | bytes 12296 | tf_op jit(solution)/shard_map/ppermute | solution.py:365
  70.5 3.6 %collective-permute-start.23 = (f32[8,128]{1,0:T(8,128)S(1)}, f32[8,128]{1,0:T(8,128)S(1)}, u32[]{:S(2)}, u32[]{:S(2)}) collective-permute-start(f32[8,128]{1,0:T(8,128)S(1)} %pair.5.refs_0_), channel_id=1, source_target_pairs={{0,8},{8,0},{16,24},{24,16},{1,9},{9,1},{17,25},{25,17},{2,10},{10... | collective-permute-start | bytes 12296 | tf_op jit(solution)/shard_map/ppermute | solution.py:365

commit v10 on v9

--- a/solution.py
+++ b/solution.py
@@ -188,10 +188,10 @@
 def voxel_kernel(first, rows, tiles_ref, *refs):
     terms, refs = refs[:rows], list(refs[rows:])
     if first:
-        own_ref, other_ref, beta_ref, raw_ref, all_ref, equal_ref, weight_ref, keys_ref = refs
+        own_ref, other_ref, beta_ref, all_ref, raw_ref, equal_ref, weight_ref, keys_ref = refs
     else:
         equal_ref, weight_ref, right_ref, alpha_ref = refs[:4]
-        own_ref, other_ref, beta_ref, raw_ref, all_ref = refs[-5:]
+        own_ref, other_ref, beta_ref, all_ref, raw_ref = refs[-5:]
     my_row = lax.axis_index("row")
     row_tiles, per_block = tiles_ref.shape[:2]
     shares = lax.axis_size("col")
@@ -249,39 +249,66 @@
     other_ref[own_ref.shape[0] - 1] = acc
 
 
-def pair_kernel(*refs):
-    passed = (len(refs) - 3) // 2
-    refs[2 + passed][...] = refs[0][...] + refs[1][...]
+def pair_kernel(narrow, own_ref, other_ref, *refs):
+    passed = len(refs) // 2
+    out_ref = refs[passed]
     for i in range(passed):
-        refs[3 + passed + i][...] = refs[2 + i][...]
-
-
-def half_ray_kernel(peers, first, unread, *refs):
+        refs[1 + passed + i][...] = refs[i][...]
+    if not narrow:
+        out_ref[...] = own_ref[...] + other_ref[...]
+        return
+    count = own_ref.shape[0] - 1
+    for b in range(0, count, 2):
+        two = [own_ref[b + i] + other_ref[b + i] for i in range(2)]
+        out_ref[8 * b : 8 * b + 16, :] = jnp.concatenate(two, axis=0).astype(jnp.bfloat16)
+    out_ref[8 * count :, :] = packed_squares(own_ref[count] + other_ref[count])
+
+
+def half_ray_kernel(peers, first, narrow, update, unread, *refs):
     refs = refs[unread:]
     parts, refs = refs[:peers], refs[peers:]
-    lefts, (beta_ref, raw_ref, alpha_ref, half_ref, acc_ref) = refs[:-5], refs[-5:]
-    per_share = raw_ref.shape[0] // peers
-    rows = (half_ref.shape[0] - 16) // peers
-    alpha = norm_of(tree_sum([p[p.shape[0] - 1] for p in parts]))
+    if update:
+        lefts, (beta_ref, alpha_ref, raw_ref, half_ref) = refs[:-4], refs[-4:]
+        rows = (half_ref.shape[0] - 16) // peers
+    else:
+        lefts, (beta_ref, alpha_ref, acc_ref) = refs[:-3], refs[-3:]
+    if narrow:
+        count = (parts[0].shape[0] - 16) // 8
+        squares = [read_squares(p[8 * count :, :]) for p in parts]
+    else:
+        count = parts[0].shape[0] - 1
+        squares = [p[count] for p in parts]
+    per_share = count // peers
+    alpha = norm_of(tree_sum(squares))
     alpha_ref[...] = alpha
     alpha_inv = 1.0 / alpha
     left_scale = alpha / beta_ref[...]
     squares = []
     for e in range(peers):
         slot = jnp.bitwise_xor(lax.axis_index("col") // 2, e)
+        if narrow:
+            at = pl.ds(pl.multiple_of(slot * per_share * 8, 16), per_share * 8)
+            whole = tree_sum([p[at, :].astype(jnp.float32) for p in parts])
+            totals = [whole[8 * b : 8 * b + 8] for b in range(per_share)]
+        else:
+            totals = [tree_sum([p[slot * per_share + b] for p in parts]) for b in range(per_share)]
         blocks = []
         for b in range(per_share):
             at = slot * per_share + b
             left = lefts[e][b] if first else lefts[0][at]
-            blocks.append(tree_sum([p[at] for p in parts]) * alpha_inv - left * left_scale)
-            raw_ref[at] = blocks[-1]
-        half_ref[pl.ds(pl.multiple_of(slot * rows, 16), rows), :] = packed(blocks, rows)
+            blocks.append(totals[b] * alpha_inv - left * left_scale)
+            if update:
+                raw_ref[at] = blocks[-1]
+        if update:
+            half_ref[pl.ds(pl.multiple_of(slot * rows, 16), rows), :] = packed(blocks, rows)
         squares.append(tree_sum([b * b for b in blocks]))
     acc = tree_sum(squares)
-    acc_ref[...] = acc
-    pieces = packed_squares(acc)
-    half_ref[peers * rows :, :LANES] = pieces
-    half_ref[peers * rows :, LANES:] = jnp.zeros_like(pieces)
+    if update:
+        pieces = packed_squares(acc)
+        half_ref[peers * rows :, :LANES] = pieces
+        half_ref[peers * rows :, LANES:] = jnp.zeros_like(pieces)
+    else:
+        acc_ref[...] = acc
 
 
 def share_kernel(remainders, *refs):
@@ -395,10 +422,11 @@
         args = [keys, tile_values, *payloads]
         return call(functools.partial(adjoint_kernel, first), "adjoint", out_shape, args)
 
-    def voxel(term_list, previous):
+    def voxel(term_list, previous, keep):
         first = not previous
-        out_shape = [f32(half_blocks + 1, 8, LANES)] * 2
-        out_shape += [f32(8, LANES), f32(rows * per_row, tile_size), bf16(rows * per_row, tile_size)]
+        out_shape = [f32(half_blocks + 1, 8, LANES)] * 2 + [f32(8, LANES), bf16(rows * per_row, tile_size)]
+        raw_shape = (rows * per_row, tile_size)
+        out_shape += [f32(*raw_shape)] * keep
         if first:
             out_shape += [
                 bf16(rows * per_row, rows * per_row),
@@ -406,21 +434,23 @@
                 f32(rows, 8, per_row),
             ]
         args = [tile_values, *term_list, *previous]
-        return call(functools.partial(voxel_kernel, first, rows), "voxel", out_shape, args)
-
-    def pair(own, other, passed):
+        scratch = [pltpu.VMEM(raw_shape, jnp.float32)] * (not keep)
+        return call(functools.partial(voxel_kernel, first, rows), "voxel", out_shape, args, None, scratch)
+
+    def pair(own, other, passed, narrow):
         args = [own, from_peer(other, "col", 1), *passed]
         out_shape = [jax.ShapeDtypeStruct(x.shape, x.dtype) for x in [own, *passed]]
-        return call(pair_kernel, "pair", out_shape, args)
-
-    def half_ray(parts, lefts, beta, after):
-        out_shape = [
-            f32(half_blocks, 8, LANES),
-            f32(8, LANES),
-            bf16(half_shares * ray_rows + 16, 2 * LANES),
-            f32(8, LANES),
-        ]
-        kernel = functools.partial(half_ray_kernel, half_shares, len(lefts) > 1, len(after))
+        if narrow:
+            out_shape[0] = bf16(8 * half_blocks + 16, LANES)
+        return call(functools.partial(pair_kernel, narrow), "pair", out_shape, args)
+
+    def half_ray(parts, lefts, beta, after, narrow, update):
+        out_shape = [f32(8, LANES)]
+        if update:
+            out_shape += [f32(half_blocks, 8, LANES), bf16(half_shares * ray_rows + 16, 2 * LANES)]
+        else:
+            out_shape += [f32(8, LANES)]
+        kernel = functools.partial(half_ray_kernel, half_shares, len(lefts) > 1, narrow, update, len(after))
         args = [*after, *parts, *lefts, beta]
         specs = [ANY] * len(after) + [VMEM] * (len(args) - len(after))
         return call(kernel, "half_ray", out_shape, args, specs)
@@ -437,25 +467,38 @@
     both = call(join_kernel, "join", f32(2 * per_share + 1, 8, LANES), [blocks, from_peer(blocks, "col", 1)])
     lefts = exchange(both, "col", 2)
     terms, remainder = adjoint(lefts, True)
-    own, other, beta, right_raw, upper_terms, equal, weight, all_keys = voxel(exchange(terms, "row"), [])
+    terms = exchange(terms, "row")
+    own, other, beta, upper_terms, right_raw, equal, weight, all_keys = voxel(terms, [], True)
     betas, alphas, combined = [], [], []
+    remainders = [None] * rows
     for iteration in range(ITERS):
         last = iteration == ITERS - 1
         betas.append(beta)
         combined.append(upper_terms)
-        summed, *passed = pair(own, other, [remainder] * last)
-        remainders = exchange(passed[0], "row") if last else []
-        left_raw, alpha, half, squares = half_ray(exchange(summed, "col", 2), lefts, beta, remainders)
+        crossing = range(1, rows // 2 + 1) if iteration == 0 else range(rows // 2 + 1, rows) if last else []
+        summed, *passed = pair(own, other, [remainder] * (len(crossing) > 0), last)
+        for d in crossing:
+            remainders[d] = from_peer(passed[0], "row", d)
+        after = [remainders[d] for d in crossing]
+        gathered = exchange(summed, "col", 2)
+        if last:
+            alpha, squares = half_ray(gathered, lefts, beta, after, True, False)
+        alpha, left_raw, half = half_ray(gathered, lefts, beta, after, last, True) if not last else (
+            alpha,
+            *half_ray(gathered, lefts, beta, after, True, True)[1:],
+        )
         alphas.append(alpha)
         lefts = [left_raw]
-        (terms,) = adjoint([half, from_peer(half, "col", 1)], False)
+        (new_terms,) = adjoint([half, from_peer(half, "col", 1)], False)
         if iteration == 0:
-            selector = call(pick_kernel, "pick", bf16(share_rows, rows * per_row), [terms, all_keys], [ANY, VMEM])
-        own, other, beta, right_raw, upper_terms = voxel(
-            exchange(terms, "row"), [equal, weight, right_raw, alpha]
-        )
+            selector = call(pick_kernel, "pick", bf16(share_rows, rows * per_row), [new_terms, all_keys], [ANY, VMEM])
+        new_terms = exchange(new_terms, "row")
+        fixed = [equal, weight, right_raw, alpha]
+        own, other, beta, upper_terms = voxel(new_terms, fixed, False)
+        right_raw = voxel(new_terms, fixed, True)[4]
+    remainders[0] = remainder
     products = [share(selector, c, [] if i else remainders) for i, c in enumerate(combined)]
-    (squares,) = call(pair_kernel, "pair", [f32(8, LANES)], [squares, from_peer(squares, "col", 1)])
+    (squares,) = call(functools.partial(pair_kernel, False), "pair", [f32(8, LANES)], [squares, from_peer(squares, "col", 1)])
     result, ratio = pl.pallas_call(
         functools.partial(final_kernel, rows, ITERS),
         out_shape=[f32(RHS, col_tiles // rows * tile_size), f32(RHS)],

time: 75.7 us -> 73.4 us (0.970)
  waiting for transfers between devices: 30.6 us -> 29 us
  Pallas kernels: 14.3 us -> 13.1 us
    ppermute x26, waiting for transfers between devices: 30.6 us -> 29 us  [from_peer(): lax.ppermute(value, axis, [(i, i ^ d) for i in range(lax.axis_size(axis))])]
    pallas_call x15, Pallas kernels: 13 us -> 11.7 us  [call(): pl.pallas_call(kernel, out_shape=out_shape, in_specs=in_specs or [VMEM] *...]
  transfers between devices with their start and end apart: 26 -> 26, of which waited for: 19 -> 18; matrix products, arithmetic and copies ran while one was open for 0% -> 0% of each run, Pallas kernels for 3% -> 3%
where the time goes in v10:
time: 73.4 us; the launch traced here: 73.2 us
  starting transfers between devices  29.4 us (40%)
  waiting for transfers between devices  29 us (40%)
  Pallas kernels  13.1 us (18%)
  local copies, waits for them, and re-layouts  0.87 us (1%)
  between operations  0.77 us (1%)
    ppermute x26, starting transfers between devices, from_peer(): lax.ppermute(value, axis, [(i, i ^ d) for i in range(lax.axis_size(axis))])  29.4 us
    ppermute x26, waiting for transfers between devices, from_peer(): lax.ppermute(value, axis, [(i, i ^ d) for i in range(lax.axis_size(axis))])  29 us
    pallas_call x15, Pallas kernels, call(): pl.pallas_call(kernel, out_shape=out_shape, in_specs=in_specs or [VMEM] *...  11.7 us
  transfers between devices with their start and end apart: 26, of which 18 were waited for; matrix products, arithmetic and copies ran while one was open for 0% of the time, Pallas kernels for 3%

profile of v10, /device:TPU:0, one launch (start us, length us, event | category | flops | bytes accessed | tf_op | source)
XLA Modules:
  0.0 73.2 jit_solution(10542809281779200781)
XLA Ops:
  0.6 0.9 %copy-done.1 = f32[4,1024]{1,0:T(4,128)S(1)} copy-done((f32[4,1024]{1,0:T(4,128)S(1)}, f32[4,1024]{1,0:T(4,128)}, u32[]{:S(2)}) %copy-start.1) | copy-done | bytes 16408
  1.5 0.5 collective-permute-start
  2.0 0.8 %collective-permute-done.other_ref = f32[5,8,128]{2,1,0:T(8,128)S(1)} collective-permute-done((f32[5,8,128]{2,1,0:T(8,128)S(1)}, f32[5,8,128]{2,1,0:T(8,128)S(1)}, u32[]{:S(2)}, u32[]{:S(2)}) %collective-permute-start) | collective-permute-done | bytes 20512 | tf_op jit(solution)/shard_map/ppermute | solution.py:392
  2.9 4.9 %collective-permute-start.3 = (f32[9,8,128]{2,1,0:T(8,128)S(1)}, f32[9,8,128]{2,1,0:T(8,128)S(1)}, u32[]{:S(2)}, u32[]{:S(2)}) collective-permute-start(f32[9,8,128]{2,1,0:T(8,128)S(1)} %join.1.refs_0_.refs_6_), channel_id=1, source_target_pairs={{0,6},{1,7},{2,4},{3,5},{4,2},{5,3},{6,0},{7,1},{8,14},{9,15},{10,... | collective-permute-start | bytes 110600 | tf_op jit(solution)/shard_map/ppermute | solution.py:392
  7.8 0.0 collective-permute-start.2
  7.8 0.6 collective-permute-start.1
  8.5 0.6 keys.1.keys_ref
  9.1 0.7 %collective-permute-done.3.refs_3_.refs_9_ = f32[9,8,128]{2,1,0:T(8,128)S(1)} collective-permute-done((f32[9,8,128]{2,1,0:T(8,128)S(1)}, f32[9,8,128]{2,1,0:T(8,128)S(1)}, u32[]{:S(2)}, u32[]{:S(2)}) %collective-permute-start.3) | collective-permute-done | bytes 36896 | tf_op jit(solution)/shard_map/ppermute | solution.py:392
  9.8 2.9 %collective-permute-done.2.refs_2_.refs_8_ = f32[9,8,128]{2,1,0:T(8,128)S(1)} collective-permute-done((f32[9,8,128]{2,1,0:T(8,128)S(1)}, f32[9,8,128]{2,1,0:T(8,128)S(1)}, u32[]{:S(2)}, u32[]{:S(2)}) %collective-permute-start.2) | collective-permute-done | bytes 36896 | tf_op jit(solution)/shard_map/ppermute | solution.py:392
  12.7 0.0 collective-permute-done.1.refs_1_.refs_7_
  12.7 1.2 %adjoint.2 = (bf16[272,256]{1,0:T(8,128)(2,1)S(1)}, bf16[256,256]{1,0:T(8,128)(2,1)S(1)}) custom-call(f32[8,256]{1,0:T(8,128)S(1)} %keys.1.keys_ref, bf16[32,2,256,256]{3,2,1,0:T(8,128)(2,1)S(1)} %copy-done, f32[9,8,128]{2,1,0:T(8,128)S(1)} %join.1.refs_0_.refs_6_, f32[9,8,128]{2,1,0:T(8,128)S(1)} %collective-permute-done.1.refs_1_.refs_7_, ...), custom_call_target="tpu_custom_call" | custom-call | tf_op jit(solution)/shard_map/adjoint/pallas_call | solution.py:410
  13.9 2.5 %collective-permute-start.6 = (bf16[272,256]{1,0:T(8,128)(2,1)S(1)}, bf16[272,256]{1,0:T(8,128)(2,1)S(1)}, u32[]{:S(2)}, u32[]{:S(2)}) collective-permute-start(bf16[272,256]{1,0:T(8,128)(2,1)S(1)} %get-tuple-element.25.refs_0_), channel_id=1, source_target_pairs={{0,24},{8,16},{16,8},{24,0},{1,25},{9,17},{17,9},{25,1},{2,26},{10... | collective-permute-start | bytes 417800 | tf_op jit(solution)/shard_map/ppermute | solution.py:392
  16.4 0.5 collective-permute-start.5
  16.9 0.5 collective-permute-start.4
  17.4 3.4 %collective-permute-done.6.refs_3_ = bf16[272,256]{1,0:T(8,128)(2,1)S(1)} collective-permute-done((bf16[272,256]{1,0:T(8,128)(2,1)S(1)}, bf16[272,256]{1,0:T(8,128)(2,1)S(1)}, u32[]{:S(2)}, u32[]{:S(2)}) %collective-permute-start.6) | collective-permute-done | bytes 139296 | tf_op jit(solution)/shard_map/ppermute | solution.py:392
  20.8 1.7 %collective-permute-done.5.refs_2_ = bf16[272,256]{1,0:T(8,128)(2,1)S(1)} collective-permute-done((bf16[272,256]{1,0:T(8,128)(2,1)S(1)}, bf16[272,256]{1,0:T(8,128)(2,1)S(1)}, u32[]{:S(2)}, u32[]{:S(2)}) %collective-permute-start.5) | collective-permute-done | bytes 139296 | tf_op jit(solution)/shard_map/ppermute | solution.py:392
  22.6 0.1 collective-permute-done.4.refs_1_
  22.6 4.0 %voxel.2 = (f32[17,8,128]{2,1,0:T(8,128)S(1)}, f32[17,8,128]{2,1,0:T(8,128)S(1)}, f32[8,128]{1,0:T(8,128)S(1)}, bf16[1024,256]{1,0:T(8,128)(2,1)S(1)}, f32[1024,...) custom-call(bf16[32,2,256,256]{3,2,1,0:T(8,128)(2,1)S(1)} %copy-done, ...), custom_call_target="tpu_custom_call" | custom-call | tf_op jit(solution)/shard_map/voxel/pallas_call | solution.py:410
  26.6 0.1 collective-permute-start.7
  26.7 1.3 %collective-permute-done.7.other_ref = f32[17,8,128]{2,1,0:T(8,128)S(1)} collective-permute-done((f32[17,8,128]{2,1,0:T(8,128)S(1)}, f32[17,8,128]{2,1,0:T(8,128)S(1)}, u32[]{:S(2)}, u32[]{:S(2)}) %collective-permute-start.7) | collective-permute-done | bytes 69664 | tf_op jit(solution)/shard_map/ppermute | solution.py:392
  28.0 1.5 %collective-permute-start.9 = (bf16[256,256]{1,0:T(8,128)(2,1)S(1)}, bf16[256,256]{1,0:T(8,128)(2,1)S(1)}, u32[]{:S(2)}, u32[]{:S(2)}) collective-permute-start(bf16[256,256]{1,0:T(8,128)(2,1)S(1)} %get-tuple-element.29), channel_id=1, source_target_pairs={{0,16},{8,24},{16,0},{24,8},{1,17},{9,25},{17,1},{25,9},{2,18},{10... | collective-permute-start | bytes 393224 | tf_op jit(solution)/shard_map/ppermute | solution.py:392
  29.5 0.8 %collective-permute-start.8 = (bf16[256,256]{1,0:T(8,128)(2,1)S(1)}, bf16[256,256]{1,0:T(8,128)(2,1)S(1)}, u32[]{:S(2)}, u32[]{:S(2)}) collective-permute-start(bf16[256,256]{1,0:T(8,128)(2,1)S(1)} %get-tuple-element.29), channel_id=1, source_target_pairs={{0,8},{8,0},{16,24},{24,16},{1,9},{9,1},{17,25},{25,17},{2,10},{10... | collective-permute-start | bytes 393224 | tf_op jit(solution)/shard_map/ppermute | solution.py:392
  30.3 1.6 %collective-permute-start.12 = (f32[17,8,128]{2,1,0:T(8,128)S(1)}, f32[17,8,128]{2,1,0:T(8,128)S(1)}, u32[]{:S(2)}, u32[]{:S(2)}) collective-permute-start(f32[17,8,128]{2,1,0:T(8,128)S(1)} %get-tuple-element.30.refs_2_), channel_id=1, source_target_pairs={{0,6},{1,7},{2,4},{3,5},{4,2},{5,3},{6,0},{7,1},{8,14},{9,15},{10,... | collective-permute-start | bytes 208904 | tf_op jit(solution)/shard_map/ppermute | solution.py:392
  31.9 0.4 collective-permute-start.11
  32.2 2.5 %collective-permute-start.10 = (f32[17,8,128]{2,1,0:T(8,128)S(1)}, f32[17,8,128]{2,1,0:T(8,128)S(1)}, u32[]{:S(2)}, u32[]{:S(2)}) collective-permute-start(f32[17,8,128]{2,1,0:T(8,128)S(1)} %get-tuple-element.30.refs_2_), channel_id=1, source_target_pairs={{0,2},{1,3},{2,0},{3,1},{4,6},{5,7},{6,4},{7,5},{8,10},{9,11},{10,... | collective-permute-start | bytes 208904 | tf_op jit(solution)/shard_map/ppermute | solution.py:392
  34.7 2.6 %collective-permute-done.12.refs_5_ = f32[17,8,128]{2,1,0:T(8,128)S(1)} collective-permute-done((f32[17,8,128]{2,1,0:T(8,128)S(1)}, f32[17,8,128]{2,1,0:T(8,128)S(1)}, u32[]{:S(2)}, u32[]{:S(2)}) %collective-permute-start.12) | collective-permute-done | bytes 69664 | tf_op jit(solution)/shard_map/ppermute | solution.py:392
  37.3 1.7 %collective-permute-done.11.refs_4_ = f32[17,8,128]{2,1,0:T(8,128)S(1)} collective-permute-done((f32[17,8,128]{2,1,0:T(8,128)S(1)}, f32[17,8,128]{2,1,0:T(8,128)S(1)}, u32[]{:S(2)}, u32[]{:S(2)}) %collective-permute-start.11) | collective-permute-done | bytes 69664 | tf_op jit(solution)/shard_map/ppermute | solution.py:392
  39.0 0.0 collective-permute-done.10.refs_3_
  39.0 0.0 collective-permute-done.9.refs_1_.refs_4_
  39.0 0.0 collective-permute-done.8.refs_0_.refs_3_
  39.0 0.1 half_ray.2
  39.1 0.1 collective-permute-start.13
  39.2 1.2 %collective-permute-done.13.refs_1_ = bf16[80,256]{1,0:T(8,128)(2,1)S(1)} collective-permute-done((bf16[80,256]{1,0:T(8,128)(2,1)S(1)}, bf16[80,256]{1,0:T(8,128)(2,1)S(1)}, u32[]{:S(2)}, u32[]{:S(2)}) %collective-permute-start.13) | collective-permute-done | bytes 40992 | tf_op jit(solution)/shard_map/ppermute | solution.py:392
  40.4 1.2 %adjoint.3.refs_0_.unread_ref = bf16[272,256]{1,0:T(8,128)(2,1)S(1)} custom-call(f32[8,256]{1,0:T(8,128)S(1)} %keys.1.keys_ref, bf16[32,2,256,256]{3,2,1,0:T(8,128)(2,1)S(1)} %copy-done, bf16[80,256]{1,0:T(8,128)(2,1)S(1)} %get-tuple-element.32.refs_0_, bf16[80,256]{1,0:T(8,128)(2,1)S(1)} %collective-permute-done.13.refs_1_), custom_call_target="tpu_custom_call" | custom-call | tf_op jit(solution)/shard_map/adjoint/pallas_call | solution.py:410
  41.6 1.3 %collective-permute-start.16 = (bf16[272,256]{1,0:T(8,128)(2,1)S(1)}, bf16[272,256]{1,0:T(8,128)(2,1)S(1)}, u32[]{:S(2)}, u32[]{:S(2)}) collective-permute-start(bf16[272,256]{1,0:T(8,128)(2,1)S(1)} %adjoint.3.refs_0_.unread_ref), channel_id=1, source_target_pairs={{0,24},{8,16},{16,8},{24,0},{1,25},{9,17},{17,9},{25,1},{2,26},{10... | collective-permute-start | bytes 417800 | tf_op jit(solution)/shard_map/ppermute | solution.py:392
  42.9 1.5 %collective-permute-start.15 = (bf16[272,256]{1,0:T(8,128)(2,1)S(1)}, bf16[272,256]{1,0:T(8,128)(2,1)S(1)}, u32[]{:S(2)}, u32[]{:S(2)}) collective-permute-start(bf16[272,256]{1,0:T(8,128)(2,1)S(1)} %adjoint.3.refs_0_.unread_ref), channel_id=1, source_target_pairs={{0,16},{8,24},{16,0},{24,8},{1,17},{9,25},{17,1},{25,9},{2,18},{10... | collective-permute-start | bytes 417800 | tf_op jit(solution)/shard_map/ppermute | solution.py:392
  44.4 0.8 %collective-permute-start.14 = (bf16[272,256]{1,0:T(8,128)(2,1)S(1)}, bf16[272,256]{1,0:T(8,128)(2,1)S(1)}, u32[]{:S(2)}, u32[]{:S(2)}) collective-permute-start(bf16[272,256]{1,0:T(8,128)(2,1)S(1)} %adjoint.3.refs_0_.unread_ref), channel_id=1, source_target_pairs={{0,8},{8,0},{16,24},{24,16},{1,9},{9,1},{17,25},{25,17},{2,10},{10... | collective-permute-start | bytes 417800 | tf_op jit(solution)/shard_map/ppermute | solution.py:392
  45.2 4.0 %collective-permute-done.16.refs_3_ = bf16[272,256]{1,0:T(8,128)(2,1)S(1)} collective-permute-done((bf16[272,256]{1,0:T(8,128)(2,1)S(1)}, bf16[272,256]{1,0:T(8,128)(2,1)S(1)}, u32[]{:S(2)}, u32[]{:S(2)}) %collective-permute-start.16) | collective-permute-done | bytes 139296 | tf_op jit(solution)/shard_map/ppermute | solution.py:392
  49.1 2.2 %collective-permute-done.15.refs_2_ = bf16[272,256]{1,0:T(8,128)(2,1)S(1)} collective-permute-done((bf16[272,256]{1,0:T(8,128)(2,1)S(1)}, bf16[272,256]{1,0:T(8,128)(2,1)S(1)}, u32[]{:S(2)}, u32[]{:S(2)}) %collective-permute-start.15) | collective-permute-done | bytes 139296 | tf_op jit(solution)/shard_map/ppermute | solution.py:392
  51.3 0.0 collective-permute-done.14.refs_1_
  51.3 3.0 %voxel.3 = (f32[17,8,128]{2,1,0:T(8,128)S(1)}, f32[17,8,128]{2,1,0:T(8,128)S(1)}, f32[8,128]{1,0:T(8,128)S(1)}, bf16[1024,256]{1,0:T(8,128)(2,1)S(1)}) custom-call(bf16[32,2,256,256]{3,2,1,0:T(8,128)(2,1)S(1)} %copy-done, bf16[272,256]{1,0:T(8,128)(2,1)S(1)} %adjoint.3.refs_0_.unread_ref, bf16[272,256]{1,0:T(8,128)(2,1)S(1)} %collective-permute-done.14.refs_1_, ...), custom_call_target="tpu_custom_call" | custom-call | tf_op jit(solution)/shard_map/voxel/pallas_call | solution.py:410
  54.3 0.1 collective-permute-start.17
  54.4 1.2 %collective-permute-done.17.other_ref = f32[17,8,128]{2,1,0:T(8,128)S(1)} collective-permute-done((f32[17,8,128]{2,1,0:T(8,128)S(1)}, f32[17,8,128]{2,1,0:T(8,128)S(1)}, u32[]{:S(2)}, u32[]{:S(2)}) %collective-permute-start.17) | collective-permute-done | bytes 69664 | tf_op jit(solution)/shard_map/ppermute | solution.py:392
  55.7 1.3 %collective-permute-start.18 = (bf16[256,256]{1,0:T(8,128)(2,1)S(1)}, bf16[256,256]{1,0:T(8,128)(2,1)S(1)}, u32[]{:S(2)}, u32[]{:S(2)}) collective-permute-start(bf16[256,256]{1,0:T(8,128)(2,1)S(1)} %get-tuple-element.39), channel_id=1, source_target_pairs={{0,24},{8,16},{16,8},{24,0},{1,25},{9,17},{17,9},{25,1},{2,26},{10... | collective-permute-start | bytes 393224 | tf_op jit(solution)/shard_map/ppermute | solution.py:392
  57.0 2.1 %collective-permute-start.21 = (bf16[144,128]{1,0:T(8,128)(2,1)S(1)}, bf16[144,128]{1,0:T(8,128)(2,1)S(1)}, u32[]{:S(2)}, u32[]{:S(2)}) collective-permute-start(bf16[144,128]{1,0:T(8,128)(2,1)S(1)} %get-tuple-element.40.refs_1_), channel_id=1, source_target_pairs={{0,6},{1,7},{2,4},{3,5},{4,2},{5,3},{6,0},{7,1},{8,14},{9,15},{10,... | collective-permute-start | bytes 110600 | tf_op jit(solution)/shard_map/ppermute | solution.py:392
  59.0 0.0 collective-permute-start.20
  59.1 2.3 %collective-permute-start.19 = (bf16[144,128]{1,0:T(8,128)(2,1)S(1)}, bf16[144,128]{1,0:T(8,128)(2,1)S(1)}, u32[]{:S(2)}, u32[]{:S(2)}) collective-permute-start(bf16[144,128]{1,0:T(8,128)(2,1)S(1)} %get-tuple-element.40.refs_1_), channel_id=1, source_target_pairs={{0,2},{1,3},{2,0},{3,1},{4,6},{5,7},{6,4},{7,5},{8,10},{9,11},{10,... | collective-permute-start | bytes 110600 | tf_op jit(solution)/shard_map/ppermute | solution.py:392
  61.4 1.5 %collective-permute-done.21.refs_4_ = bf16[144,128]{1,0:T(8,128)(2,1)S(1)} collective-permute-done((bf16[144,128]{1,0:T(8,128)(2,1)S(1)}, bf16[144,128]{1,0:T(8,128)(2,1)S(1)}, u32[]{:S(2)}, u32[]{:S(2)}) %collective-permute-start.21) | collective-permute-done | bytes 36896 | tf_op jit(solution)/shard_map/ppermute | solution.py:392
  62.8 1.1 %collective-permute-done.20.refs_3_ = bf16[144,128]{1,0:T(8,128)(2,1)S(1)} collective-permute-done((bf16[144,128]{1,0:T(8,128)(2,1)S(1)}, bf16[144,128]{1,0:T(8,128)(2,1)S(1)}, u32[]{:S(2)}, u32[]{:S(2)}) %collective-permute-start.20) | collective-permute-done | bytes 36896 | tf_op jit(solution)/shard_map/ppermute | solution.py:392
  63.9 0.0 collective-permute-done.19.refs_2_
  63.9 0.0 collective-permute-done.18.refs_0_.refs_5_
  63.9 0.1 half_ray.3
  64.0 0.1 collective-permute-start.22
  64.1 1.2 %collective-permute-done.22.other_ref = f32[8,128]{1,0:T(8,128)S(1)} collective-permute-done((f32[8,128]{1,0:T(8,128)S(1)}, f32[8,128]{1,0:T(8,128)S(1)}, u32[]{:S(2)}, u32[]{:S(2)}) %collective-permute-start.22) | collective-permute-done | bytes 4128 | tf_op jit(solution)/shard_map/ppermute | solution.py:392
  65.3 1.7 %collective-permute-start.25 = (f32[8,128]{1,0:T(8,128)S(1)}, f32[8,128]{1,0:T(8,128)S(1)}, u32[]{:S(2)}, u32[]{:S(2)}) collective-permute-start(f32[8,128]{1,0:T(8,128)S(1)} %pair.5.refs_0_), channel_id=1, source_target_pairs={{0,24},{8,16},{16,8},{24,0},{1,25},{9,17},{17,9},{25,1},{2,26},{10... | collective-permute-start | bytes 12296 | tf_op jit(solution)/shard_map/ppermute | solution.py:392
  66.9 1.3 %collective-permute-start.24 = (f32[8,128]{1,0:T(8,128)S(1)}, f32[8,128]{1,0:T(8,128)S(1)}, u32[]{:S(2)}, u32[]{:S(2)}) collective-permute-start(f32[8,128]{1,0:T(8,128)S(1)} %pair.5.refs_0_), channel_id=1, source_target_pairs={{0,16},{8,24},{16,0},{24,8},{1,17},{9,25},{17,1},{25,9},{2,18},{10... | collective-permute-start | bytes 12296 | tf_op jit(solution)/shard_map/ppermute | solution.py:392
  68.2 0.5 collective-permute-start.23
  68.8 0.3 pick.1.refs_0_
  69.1 0.4 share.3.refs_9_
  69.5 0.8 %share.2.refs_8_ = f32[512,256]{1,0:T(8,128)S(1)} custom-call(bf16[512,1024]{1,0:T(8,128)(2,1)S(1)} %pick.1.refs_0_, bf16[1024,256]{1,0:T(8,128)(2,1)S(1)} %get-tuple-element.46.refs_1_, bf16[256,256]{1,0:T(8,128)(2,1)S(1)} %get-tuple-element.28.refs_0_.refs_2_, bf16[256,256]{1,0:T(8,128)(2,1)S(1)} %collective-permute-done.8.refs_0_.refs_3_, ...), custom_call_target="tpu_custom_call" | custom-call | tf_op jit(solution)/shard_map/share/pallas_call | solution.py:410
  70.3 0.0 collective-permute-done.25.refs_3_
  70.3 0.3 collective-permute-done.24.refs_2_
  70.6 1.3 %collective-permute-done.23.refs_1_ = f32[8,128]{1,0:T(8,128)S(1)} collective-permute-done((f32[8,128]{1,0:T(8,128)S(1)}, f32[8,128]{1,0:T(8,128)S(1)}, u32[]{:S(2)}, u32[]{:S(2)}) %collective-permute-start.23) | collective-permute-done | bytes 4128 | tf_op jit(solution)/shard_map/ppermute | solution.py:392
  71.8 1.3 %final.1 = (f32[4,32768]{1,0:T(4,128)}, f32[4]{0:T(128)}) custom-call(f32[8,128]{1,0:T(8,128)S(1)} %pair.5.refs_0_, f32[8,128]{1,0:T(8,128)S(1)} %collective-permute-done.23.refs_1_, f32[8,128]{1,0:T(8,128)S(1)} %collective-permute-done.24.refs_2_, f32[8,128]{1,0:T(8,128)S(1)} %collective-permute-done.25.refs_3_, ...), custom_call_target="tpu_custom_call" | custom-call | tf_op jit(solution)/shard_map/final/pallas_call | solution.py:502
  (10 shorter events, 0.1 us)
Async XLA Ops:
  0.6 12.1 %copy-start = (bf16[32,2,256,256]{3,2,1,0:T(8,128)(2,1)S(1)}, bf16[32,2,256,256]{3,2,1,0:T(8,128)(2,1)}, u32[]{:S(2)}) copy-start(bf16[32,2,256,256]{3,2,1,0:T(8,128)(2,1)} %tiles_ref.7) | copy-start | bytes 25165828
  0.6 0.9 %copy-start.1 = (f32[4,1024]{1,0:T(4,128)S(1)}, f32[4,1024]{1,0:T(4,128)}, u32[]{:S(2)}) copy-start(f32[4,1024]{1,0:T(4,128)} %obs_ref.1) | copy-start | bytes 49156
  1.5 7.0 %copy-start.2 = (s32[32,2]{0,1:T(2,128)S(1)}, s32[32,2]{0,1:T(2,128)}, u32[]{:S(2)}) copy-start(s32[32,2]{0,1:T(2,128)} %param.5) | copy-start | bytes 772
  1.5 1.4 %collective-permute-start = (f32[5,8,128]{2,1,0:T(8,128)S(1)}, f32[5,8,128]{2,1,0:T(8,128)S(1)}, u32[]{:S(2)}, u32[]{:S(2)}) collective-permute-start(f32[5,8,128]{2,1,0:T(8,128)S(1)} %pack.1.unread_ref.own_ref), channel_id=1, source_target_pairs={{0,1},{1,0},{2,3},{3,2},{4,5},{5,4},{6,7},{7,6},{8,9},{9,8},{10,11... | collective-permute-start | bytes 61448 | tf_op jit(solution)/shard_map/ppermute | solution.py:392
  2.9 6.9 %collective-permute-start.3 = (f32[9,8,128]{2,1,0:T(8,128)S(1)}, f32[9,8,128]{2,1,0:T(8,128)S(1)}, u32[]{:S(2)}, u32[]{:S(2)}) collective-permute-start(f32[9,8,128]{2,1,0:T(8,128)S(1)} %join.1.refs_0_.refs_6_), channel_id=1, source_target_pairs={{0,6},{1,7},{2,4},{3,5},{4,2},{5,3},{6,0},{7,1},{8,14},{9,15},{10,... | collective-permute-start | bytes 110600 | tf_op jit(solution)/shard_map/ppermute | solution.py:392
  7.8 4.9 %collective-permute-start.2 = (f32[9,8,128]{2,1,0:T(8,128)S(1)}, f32[9,8,128]{2,1,0:T(8,128)S(1)}, u32[]{:S(2)}, u32[]{:S(2)}) collective-permute-start(f32[9,8,128]{2,1,0:T(8,128)S(1)} %join.1.refs_0_.refs_6_), channel_id=1, source_target_pairs={{0,4},{1,5},{2,6},{3,7},{4,0},{5,1},{6,2},{7,3},{8,12},{9,13},{10,... | collective-permute-start | bytes 110600 | tf_op jit(solution)/shard_map/ppermute | solution.py:392
  7.8 4.9 %collective-permute-start.1 = (f32[9,8,128]{2,1,0:T(8,128)S(1)}, f32[9,8,128]{2,1,0:T(8,128)S(1)}, u32[]{:S(2)}, u32[]{:S(2)}) collective-permute-start(f32[9,8,128]{2,1,0:T(8,128)S(1)} %join.1.refs_0_.refs_6_), channel_id=1, source_target_pairs={{0,2},{1,3},{2,0},{3,1},{4,6},{5,7},{6,4},{7,5},{8,10},{9,11},{10,... | collective-permute-start | bytes 110600 | tf_op jit(solution)/shard_map/ppermute | solution.py:392
  13.9 6.9 %collective-permute-start.6 = (bf16[272,256]{1,0:T(8,128)(2,1)S(1)}, bf16[272,256]{1,0:T(8,128)(2,1)S(1)}, u32[]{:S(2)}, u32[]{:S(2)}) collective-permute-start(bf16[272,256]{1,0:T(8,128)(2,1)S(1)} %get-tuple-element.25.refs_0_), channel_id=1, source_target_pairs={{0,24},{8,16},{16,8},{24,0},{1,25},{9,17},{17,9},{25,1},{2,26},{10... | collective-permute-start | bytes 417800 | tf_op jit(solution)/shard_map/ppermute | solution.py:392
  16.4 6.2 %collective-permute-start.5 = (bf16[272,256]{1,0:T(8,128)(2,1)S(1)}, bf16[272,256]{1,0:T(8,128)(2,1)S(1)}, u32[]{:S(2)}, u32[]{:S(2)}) collective-permute-start(bf16[272,256]{1,0:T(8,128)(2,1)S(1)} %get-tuple-element.25.refs_0_), channel_id=1, source_target_pairs={{0,16},{8,24},{16,0},{24,8},{1,17},{9,25},{17,1},{25,9},{2,18},{10... | collective-permute-start | bytes 417800 | tf_op jit(solution)/shard_map/ppermute | solution.py:392
  16.9 5.7 %collective-permute-start.4 = (bf16[272,256]{1,0:T(8,128)(2,1)S(1)}, bf16[272,256]{1,0:T(8,128)(2,1)S(1)}, u32[]{:S(2)}, u32[]{:S(2)}) collective-permute-start(bf16[272,256]{1,0:T(8,128)(2,1)S(1)} %get-tuple-element.25.refs_0_), channel_id=1, source_target_pairs={{0,8},{8,0},{16,24},{24,16},{1,9},{9,1},{17,25},{25,17},{2,10},{10... | collective-permute-start | bytes 417800 | tf_op jit(solution)/shard_map/ppermute | solution.py:392
  26.6 1.3 %collective-permute-start.7 = (f32[17,8,128]{2,1,0:T(8,128)S(1)}, f32[17,8,128]{2,1,0:T(8,128)S(1)}, u32[]{:S(2)}, u32[]{:S(2)}) collective-permute-start(f32[17,8,128]{2,1,0:T(8,128)S(1)} %get-tuple-element.27), channel_id=1, source_target_pairs={{0,1},{1,0},{2,3},{3,2},{4,5},{5,4},{6,7},{7,6},{8,9},{9,8},{10,11... | collective-permute-start | bytes 208904 | tf_op jit(solution)/shard_map/ppermute | solution.py:392
  28.0 11.0 %collective-permute-start.9 = (bf16[256,256]{1,0:T(8,128)(2,1)S(1)}, bf16[256,256]{1,0:T(8,128)(2,1)S(1)}, u32[]{:S(2)}, u32[]{:S(2)}) collective-permute-start(bf16[256,256]{1,0:T(8,128)(2,1)S(1)} %get-tuple-element.29), channel_id=1, source_target_pairs={{0,16},{8,24},{16,0},{24,8},{1,17},{9,25},{17,1},{25,9},{2,18},{10... | collective-permute-start | bytes 393224 | tf_op jit(solution)/shard_map/ppermute | solution.py:392
  29.5 9.5 %collective-permute-start.8 = (bf16[256,256]{1,0:T(8,128)(2,1)S(1)}, bf16[256,256]{1,0:T(8,128)(2,1)S(1)}, u32[]{:S(2)}, u32[]{:S(2)}) collective-permute-start(bf16[256,256]{1,0:T(8,128)(2,1)S(1)} %get-tuple-element.29), channel_id=1, source_target_pairs={{0,8},{8,0},{16,24},{24,16},{1,9},{9,1},{17,25},{25,17},{2,10},{10... | collective-permute-start | bytes 393224 | tf_op jit(solution)/shard_map/ppermute | solution.py:392
  30.3 7.0 %collective-permute-start.12 = (f32[17,8,128]{2,1,0:T(8,128)S(1)}, f32[17,8,128]{2,1,0:T(8,128)S(1)}, u32[]{:S(2)}, u32[]{:S(2)}) collective-permute-start(f32[17,8,128]{2,1,0:T(8,128)S(1)} %get-tuple-element.30.refs_2_), channel_id=1, source_target_pairs={{0,6},{1,7},{2,4},{3,5},{4,2},{5,3},{6,0},{7,1},{8,14},{9,15},{10,... | collective-permute-start | bytes 208904 | tf_op jit(solution)/shard_map/ppermute | solution.py:392
  31.9 7.1 %collective-permute-start.11 = (f32[17,8,128]{2,1,0:T(8,128)S(1)}, f32[17,8,128]{2,1,0:T(8,128)S(1)}, u32[]{:S(2)}, u32[]{:S(2)}) collective-permute-start(f32[17,8,128]{2,1,0:T(8,128)S(1)} %get-tuple-element.30.refs_2_), channel_id=1, source_target_pairs={{0,4},{1,5},{2,6},{3,7},{4,0},{5,1},{6,2},{7,3},{8,12},{9,13},{10,... | collective-permute-start | bytes 208904 | tf_op jit(solution)/shard_map/ppermute | solution.py:392
  32.2 6.8 %collective-permute-start.10 = (f32[17,8,128]{2,1,0:T(8,128)S(1)}, f32[17,8,128]{2,1,0:T(8,128)S(1)}, u32[]{:S(2)}, u32[]{:S(2)}) collective-permute-start(f32[17,8,128]{2,1,0:T(8,128)S(1)} %get-tuple-element.30.refs_2_), channel_id=1, source_target_pairs={{0,2},{1,3},{2,0},{3,1},{4,6},{5,7},{6,4},{7,5},{8,10},{9,11},{10,... | collective-permute-start | bytes 208904 | tf_op jit(solution)/shard_map/ppermute | solution.py:392
  39.1 1.3 %collective-permute-start.13 = (bf16[80,256]{1,0:T(8,128)(2,1)S(1)}, bf16[80,256]{1,0:T(8,128)(2,1)S(1)}, u32[]{:S(2)}, u32[]{:S(2)}) collective-permute-start(bf16[80,256]{1,0:T(8,128)(2,1)S(1)} %get-tuple-element.32.refs_0_), channel_id=1, source_target_pairs={{0,1},{1,0},{2,3},{3,2},{4,5},{5,4},{6,7},{7,6},{8,9},{9,8},{10,11... | collective-permute-start | bytes 122888 | tf_op jit(solution)/shard_map/ppermute | solution.py:392
  41.6 7.5 %collective-permute-start.16 = (bf16[272,256]{1,0:T(8,128)(2,1)S(1)}, bf16[272,256]{1,0:T(8,128)(2,1)S(1)}, u32[]{:S(2)}, u32[]{:S(2)}) collective-permute-start(bf16[272,256]{1,0:T(8,128)(2,1)S(1)} %adjoint.3.refs_0_.unread_ref), channel_id=1, source_target_pairs={{0,24},{8,16},{16,8},{24,0},{1,25},{9,17},{17,9},{25,1},{2,26},{10... | collective-permute-start | bytes 417800 | tf_op jit(solution)/shard_map/ppermute | solution.py:392
  42.9 8.4 %collective-permute-start.15 = (bf16[272,256]{1,0:T(8,128)(2,1)S(1)}, bf16[272,256]{1,0:T(8,128)(2,1)S(1)}, u32[]{:S(2)}, u32[]{:S(2)}) collective-permute-start(bf16[272,256]{1,0:T(8,128)(2,1)S(1)} %adjoint.3.refs_0_.unread_ref), channel_id=1, source_target_pairs={{0,16},{8,24},{16,0},{24,8},{1,17},{9,25},{17,1},{25,9},{2,18},{10... | collective-permute-start | bytes 417800 | tf_op jit(solution)/shard_map/ppermute | solution.py:392
  44.4 6.9 %collective-permute-start.14 = (bf16[272,256]{1,0:T(8,128)(2,1)S(1)}, bf16[272,256]{1,0:T(8,128)(2,1)S(1)}, u32[]{:S(2)}, u32[]{:S(2)}) collective-permute-start(bf16[272,256]{1,0:T(8,128)(2,1)S(1)} %adjoint.3.refs_0_.unread_ref), channel_id=1, source_target_pairs={{0,8},{8,0},{16,24},{24,16},{1,9},{9,1},{17,25},{25,17},{2,10},{10... | collective-permute-start | bytes 417800 | tf_op jit(solution)/shard_map/ppermute | solution.py:392
  54.3 1.3 %collective-permute-start.17 = (f32[17,8,128]{2,1,0:T(8,128)S(1)}, f32[17,8,128]{2,1,0:T(8,128)S(1)}, u32[]{:S(2)}, u32[]{:S(2)}) collective-permute-start(f32[17,8,128]{2,1,0:T(8,128)S(1)} %get-tuple-element.38), channel_id=1, source_target_pairs={{0,1},{1,0},{2,3},{3,2},{4,5},{5,4},{6,7},{7,6},{8,9},{9,8},{10,11... | collective-permute-start | bytes 208904 | tf_op jit(solution)/shard_map/ppermute | solution.py:392
  55.7 8.3 %collective-permute-start.18 = (bf16[256,256]{1,0:T(8,128)(2,1)S(1)}, bf16[256,256]{1,0:T(8,128)(2,1)S(1)}, u32[]{:S(2)}, u32[]{:S(2)}) collective-permute-start(bf16[256,256]{1,0:T(8,128)(2,1)S(1)} %get-tuple-element.39), channel_id=1, source_target_pairs={{0,24},{8,16},{16,8},{24,0},{1,25},{9,17},{17,9},{25,1},{2,26},{10... | collective-permute-start | bytes 393224 | tf_op jit(solution)/shard_map/ppermute | solution.py:392
  57.0 5.9 %collective-permute-start.21 = (bf16[144,128]{1,0:T(8,128)(2,1)S(1)}, bf16[144,128]{1,0:T(8,128)(2,1)S(1)}, u32[]{:S(2)}, u32[]{:S(2)}) collective-permute-start(bf16[144,128]{1,0:T(8,128)(2,1)S(1)} %get-tuple-element.40.refs_1_), channel_id=1, source_target_pairs={{0,6},{1,7},{2,4},{3,5},{4,2},{5,3},{6,0},{7,1},{8,14},{9,15},{10,... | collective-permute-start | bytes 110600 | tf_op jit(solution)/shard_map/ppermute | solution.py:392
  59.0 4.9 %collective-permute-start.20 = (bf16[144,128]{1,0:T(8,128)(2,1)S(1)}, bf16[144,128]{1,0:T(8,128)(2,1)S(1)}, u32[]{:S(2)}, u32[]{:S(2)}) collective-permute-start(bf16[144,128]{1,0:T(8,128)(2,1)S(1)} %get-tuple-element.40.refs_1_), channel_id=1, source_target_pairs={{0,4},{1,5},{2,6},{3,7},{4,0},{5,1},{6,2},{7,3},{8,12},{9,13},{10,... | collective-permute-start | bytes 110600 | tf_op jit(solution)/shard_map/ppermute | solution.py:392
  59.1 4.9 %collective-permute-start.19 = (bf16[144,128]{1,0:T(8,128)(2,1)S(1)}, bf16[144,128]{1,0:T(8,128)(2,1)S(1)}, u32[]{:S(2)}, u32[]{:S(2)}) collective-permute-start(bf16[144,128]{1,0:T(8,128)(2,1)S(1)} %get-tuple-element.40.refs_1_), channel_id=1, source_target_pairs={{0,2},{1,3},{2,0},{3,1},{4,6},{5,7},{6,4},{7,5},{8,10},{9,11},{10,... | collective-permute-start | bytes 110600 | tf_op jit(solution)/shard_map/ppermute | solution.py:392
  64.0 1.2 %collective-permute-start.22 = (f32[8,128]{1,0:T(8,128)S(1)}, f32[8,128]{1,0:T(8,128)S(1)}, u32[]{:S(2)}, u32[]{:S(2)}) collective-permute-start(f32[8,128]{1,0:T(8,128)S(1)} %get-tuple-element.43.own_ref), channel_id=1, source_target_pairs={{0,1},{1,0},{2,3},{3,2},{4,5},{5,4},{6,7},{7,6},{8,9},{9,8},{10,11... | collective-permute-start | bytes 12296 | tf_op jit(solution)/shard_map/ppermute | solution.py:392
  65.3 5.0 %collective-permute-start.25 = (f32[8,128]{1,0:T(8,128)S(1)}, f32[8,128]{1,0:T(8,128)S(1)}, u32[]{:S(2)}, u32[]{:S(2)}) collective-permute-start(f32[8,128]{1,0:T(8,128)S(1)} %pair.5.refs_0_), channel_id=1, source_target_pairs={{0,24},{8,16},{16,8},{24,0},{1,25},{9,17},{17,9},{25,1},{2,26},{10... | collective-permute-start | bytes 12296 | tf_op jit(solution)/shard_map/ppermute | solution.py:392
  66.9 3.6 %collective-permute-start.24 = (f32[8,128]{1,0:T(8,128)S(1)}, f32[8,128]{1,0:T(8,128)S(1)}, u32[]{:S(2)}, u32[]{:S(2)}) collective-permute-start(f32[8,128]{1,0:T(8,128)S(1)} %pair.5.refs_0_), channel_id=1, source_target_pairs={{0,16},{8,24},{16,0},{24,8},{1,17},{9,25},{17,1},{25,9},{2,18},{10... | collective-permute-start | bytes 12296 | tf_op jit(solution)/shard_map/ppermute | solution.py:392
  68.2 3.6 %collective-permute-start.23 = (f32[8,128]{1,0:T(8,128)S(1)}, f32[8,128]{1,0:T(8,128)S(1)}, u32[]{:S(2)}, u32[]{:S(2)}) collective-permute-start(f32[8,128]{1,0:T(8,128)S(1)} %pair.5.refs_0_), channel_id=1, source_target_pairs={{0,8},{8,0},{16,24},{24,16},{1,9},{9,1},{17,25},{25,17},{2,10},{10... | collective-permute-start | bytes 12296 | tf_op jit(solution)/shard_map/ppermute | solution.py:392

commit v11 on v10

--- a/solution.py
+++ b/solution.py
@@ -130,7 +130,8 @@
                 pick_ref[at, lane : lane + LANES] = jnp.where(down == across, 1.0, 0.0).astype(jnp.bfloat16)
 
 
-def adjoint_kernel(first, keys_ref, tiles_ref, *refs):
+def adjoint_kernel(first, unread, keys_ref, tiles_ref, *refs):
+    refs = refs[unread:]
     row_tiles, per_block = tiles_ref.shape[:2]
     shares = lax.axis_size("col")
     me = lax.axis_index("col")
@@ -188,14 +189,12 @@
 def voxel_kernel(first, rows, tiles_ref, *refs):
     terms, refs = refs[:rows], list(refs[rows:])
     if first:
-        own_ref, other_ref, beta_ref, all_ref, raw_ref, equal_ref, weight_ref, keys_ref = refs
+        lhs_ref, acc_ref, other_ref, beta_ref, all_ref, raw_ref, equal_ref, weight_ref, keys_ref = refs
     else:
         equal_ref, weight_ref, right_ref, alpha_ref = refs[:4]
-        own_ref, other_ref, beta_ref, all_ref, raw_ref = refs[-5:]
+        lhs_ref, acc_ref, other_ref, beta_ref, all_ref, raw_ref = refs[-6:]
     my_row = lax.axis_index("row")
     row_tiles, per_block = tiles_ref.shape[:2]
-    shares = lax.axis_size("col")
-    per_share = row_tiles // shares
     per_row = row_tiles * per_block * RHS
     low = low_half(2 * LANES)
     squares = []
@@ -227,14 +226,22 @@
             raw_ref[at : at + 8] = raw
             square = raw * raw
             acc = acc + (square[:, :LANES] + square[:, LANES:]) * weight_ref[at : at + 8]
-    own = my_row * per_row
+    lhs_ref[...] = raw_ref[pl.ds(pl.multiple_of(my_row * per_row, 16), per_row), :].astype(jnp.bfloat16)
+    forward_half(1, tiles_ref, lhs_ref, other_ref)
+    other_ref[other_ref.shape[0] - 1] = acc
+    acc_ref[...] = acc
+
+
+def forward_half(half, tiles_ref, lhs_ref, out_ref):
+    shares = lax.axis_size("col")
+    per_share = tiles_ref.shape[0] // shares
+    low = low_half(2 * LANES)
     core = lax.axis_index("col") % 2
-    for half, slot in [(h, s) for h in range(2) for s in range(shares // 2)]:
+    for slot in range(shares // 2):
         c = 2 * slot + jnp.bitwise_xor(core, half)
-        ref, at = (own_ref, other_ref)[half], slot * per_share
         for g in range(per_share // 2):
             i = c * per_share + 2 * g
-            lhs = raw_ref[pl.ds(pl.multiple_of(own + 8 * i, 16), 16), :].astype(jnp.bfloat16)
+            lhs = lhs_ref[pl.ds(pl.multiple_of(8 * i, 16), 16), :]
             wide = [
                 lax.dot_general(
                     lhs, tiles_ref[i + e, k], (((1,), (1,)), ((), ())), preferred_element_type=jnp.float32
@@ -243,10 +250,14 @@
                 for k in range(2)
             ]
             value = jnp.where(low, wide[0], wide[3]) + pltpu.roll(jnp.where(low, wide[2], wide[1]), 4, 0)
-            ref[at + 2 * g] = value[:, :LANES]
-            ref[at + 2 * g + 1] = value[:, LANES:]
-    own_ref[own_ref.shape[0] - 1] = acc
-    other_ref[own_ref.shape[0] - 1] = acc
+            at = slot * per_share + 2 * g
+            out_ref[at] = value[:, :LANES]
+            out_ref[at + 1] = value[:, LANES:]
+
+
+def forward_kernel(tiles_ref, lhs_ref, acc_ref, own_ref):
+    forward_half(0, tiles_ref, lhs_ref, own_ref)
+    own_ref[own_ref.shape[0] - 1] = acc_ref[...]
 
 
 def pair_kernel(narrow, own_ref, other_ref, *refs):
@@ -262,6 +273,10 @@
         two = [own_ref[b + i] + other_ref[b + i] for i in range(2)]
         out_ref[8 * b : 8 * b + 16, :] = jnp.concatenate(two, axis=0).astype(jnp.bfloat16)
     out_ref[8 * count :, :] = packed_squares(own_ref[count] + other_ref[count])
+
+
+def sum_kernel(*refs):
+    refs[-1][...] = refs[-3][...] + refs[-2][...]
 
 
 def half_ray_kernel(peers, first, narrow, update, unread, *refs):
@@ -406,7 +421,7 @@
     ray_rows = max(16, RHS * per_share)
     half_shares = shares // 2
     half_blocks = half_shares * per_share
-    def call(kernel, name, out_shape, args, in_specs=None, scratch=()):
+    def call(kernel, name, out_shape, args, in_specs=None, scratch=(), flops=None):
         return pl.pallas_call(
             kernel,
             out_shape=out_shape,
@@ -414,17 +429,20 @@
             out_specs=jax.tree.map(lambda _: VMEM, out_shape),
             scratch_shapes=list(scratch),
             compiler_params=PARAMS,
+            cost_estimate=flops and pl.CostEstimate(flops=flops, bytes_accessed=0, transcendentals=0),
             name=name,
         )(*args)
 
-    def adjoint(payloads, first):
+    def adjoint(payloads, first, after):
         out_shape = [bf16(per_row + 16, tile_size)] + [bf16(per_row, tile_size)] * first
-        args = [keys, tile_values, *payloads]
-        return call(functools.partial(adjoint_kernel, first), "adjoint", out_shape, args)
+        args = [keys, tile_values, *after, *payloads]
+        specs = [VMEM] * 2 + [ANY] * len(after) + [VMEM] * len(payloads)
+        return call(functools.partial(adjoint_kernel, first, len(after)), "adjoint", out_shape, args, specs)
 
     def voxel(term_list, previous, keep):
         first = not previous
-        out_shape = [f32(half_blocks + 1, 8, LANES)] * 2 + [f32(8, LANES), bf16(rows * per_row, tile_size)]
+        out_shape = [bf16(per_row, tile_size), f32(8, LANES), f32(half_blocks + 1, 8, LANES)]
+        out_shape += [f32(8, LANES), bf16(rows * per_row, tile_size)]
         raw_shape = (rows * per_row, tile_size)
         out_shape += [f32(*raw_shape)] * keep
         if first:
@@ -435,7 +453,11 @@
             ]
         args = [tile_values, *term_list, *previous]
         scratch = [pltpu.VMEM(raw_shape, jnp.float32)] * (not keep)
-        return call(functools.partial(voxel_kernel, first, rows), "voxel", out_shape, args, None, scratch)
+        lhs, acc, other, *rest = call(
+            functools.partial(voxel_kernel, first, rows), "voxel", out_shape, args, None, scratch
+        )
+        own = call(forward_kernel, "forward", f32(half_blocks + 1, 8, LANES), [tile_values, lhs, acc])
+        return own, other, *rest
 
     def pair(own, other, passed, narrow):
         args = [own, from_peer(other, "col", 1), *passed]
@@ -453,7 +475,7 @@
         kernel = functools.partial(half_ray_kernel, half_shares, len(lefts) > 1, narrow, update, len(after))
         args = [*after, *parts, *lefts, beta]
         specs = [ANY] * len(after) + [VMEM] * (len(args) - len(after))
-        return call(kernel, "half_ray", out_shape, args, specs)
+        return call(kernel, "half_ray", out_shape, args, specs, (), 2 * 10**9)
 
     def share(selector, all_terms, lower_terms):
         scratch = [pltpu.VMEM((rows * per_row, tile_size), jnp.bfloat16)] * (len(lower_terms) > 0)
@@ -466,7 +488,7 @@
     keys = call(keys_kernel, "keys", f32(8, per_row), [blocks, tile_cols.T], [ANY, SMEM])
     both = call(join_kernel, "join", f32(2 * per_share + 1, 8, LANES), [blocks, from_peer(blocks, "col", 1)])
     lefts = exchange(both, "col", 2)
-    terms, remainder = adjoint(lefts, True)
+    terms, remainder = adjoint(lefts, True, [])
     terms = exchange(terms, "row")
     own, other, beta, upper_terms, right_raw, equal, weight, all_keys = voxel(terms, [], True)
     betas, alphas, combined = [], [], []
@@ -477,19 +499,18 @@
         combined.append(upper_terms)
         crossing = range(1, rows // 2 + 1) if iteration == 0 else range(rows // 2 + 1, rows) if last else []
         summed, *passed = pair(own, other, [remainder] * (len(crossing) > 0), last)
+        gathered = exchange(summed, "col", 2)
         for d in crossing:
             remainders[d] = from_peer(passed[0], "row", d)
         after = [remainders[d] for d in crossing]
-        gathered = exchange(summed, "col", 2)
         if last:
-            alpha, squares = half_ray(gathered, lefts, beta, after, True, False)
-        alpha, left_raw, half = half_ray(gathered, lefts, beta, after, last, True) if not last else (
-            alpha,
-            *half_ray(gathered, lefts, beta, after, True, True)[1:],
-        )
+            alpha, squares = half_ray(gathered, lefts, beta, [], True, False)
+            _, left_raw, half = half_ray(gathered, lefts, beta, [], True, True)
+        else:
+            alpha, left_raw, half = half_ray(gathered, lefts, beta, [], False, True)
         alphas.append(alpha)
         lefts = [left_raw]
-        (new_terms,) = adjoint([half, from_peer(half, "col", 1)], False)
+        (new_terms,) = adjoint([half, from_peer(half, "col", 1)], False, after)
         if iteration == 0:
             selector = call(pick_kernel, "pick", bf16(share_rows, rows * per_row), [new_terms, all_keys], [ANY, VMEM])
         new_terms = exchange(new_terms, "row")
@@ -498,7 +519,9 @@
         right_raw = voxel(new_terms, fixed, True)[4]
     remainders[0] = remainder
     products = [share(selector, c, [] if i else remainders) for i, c in enumerate(combined)]
-    (squares,) = call(functools.partial(pair_kernel, False), "pair", [f32(8, LANES)], [squares, from_peer(squares, "col", 1)])
+    squares = call(
+        sum_kernel, "sum", f32(8, LANES), [*after, squares, from_peer(squares, "col", 1)], [ANY] * len(after) + [VMEM] * 2
+    )
     result, ratio = pl.pallas_call(
         functools.partial(final_kernel, rows, ITERS),
         out_shape=[f32(RHS, col_tiles // rows * tile_size), f32(RHS)],

time: 73.4 us -> 70.6 us (0.962)
  waiting for transfers between devices: 29 us -> 25.6 us
    ppermute x26, waiting for transfers between devices: 29 us -> 25.6 us  [from_peer(): lax.ppermute(value, axis, [(i, i ^ d) for i in range(lax.axis_size(axis))])]
    pallas_call x15 -> x17, Pallas kernels: 11.7 us -> 12 us  [call(): pl.pallas_call(kernel, out_shape=out_shape, in_specs=in_specs or [VMEM] *...]
  transfers between devices with their start and end apart: 26 -> 26, of which waited for: 18 -> 19; matrix products, arithmetic and copies ran while one was open for 0% -> 0% of each run, Pallas kernels for 3% -> 7%
where the time goes in v11:
time: 70.6 us; the launch traced here: 70.4 us
  starting transfers between devices  29.8 us (42%)
  waiting for transfers between devices  25.6 us (36%)
  Pallas kernels  13.4 us (19%)
  local copies, waits for them, and re-layouts  0.87 us (1%)
  between operations  0.77 us (1%)
    ppermute x26, starting transfers between devices, from_peer(): lax.ppermute(value, axis, [(i, i ^ d) for i in range(lax.axis_size(axis))])  29.8 us
    ppermute x26, waiting for transfers between devices, from_peer(): lax.ppermute(value, axis, [(i, i ^ d) for i in range(lax.axis_size(axis))])  25.6 us
    pallas_call x17, Pallas kernels, call(): pl.pallas_call(kernel, out_shape=out_shape, in_specs=in_specs or [VMEM] *...  12 us
  transfers between devices with their start and end apart: 26, of which 19 were waited for; matrix products, arithmetic and copies ran while one was open for 0% of the time, Pallas kernels for 7%

profile of v11, /device:TPU:0, one launch (start us, length us, event | category | flops | bytes accessed | tf_op | source)
XLA Modules:
  0.0 70.4 jit_solution(12736481389931610483)
XLA Ops:
  0.6 0.9 %copy-done.1 = f32[4,1024]{1,0:T(4,128)S(1)} copy-done((f32[4,1024]{1,0:T(4,128)S(1)}, f32[4,1024]{1,0:T(4,128)}, u32[]{:S(2)}) %copy-start.1) | copy-done | bytes 16408
  1.5 0.5 collective-permute-start
  2.0 0.8 %collective-permute-done.other_ref = f32[5,8,128]{2,1,0:T(8,128)S(1)} collective-permute-done((f32[5,8,128]{2,1,0:T(8,128)S(1)}, f32[5,8,128]{2,1,0:T(8,128)S(1)}, u32[]{:S(2)}, u32[]{:S(2)}) %collective-permute-start) | collective-permute-done | bytes 20512 | tf_op jit(solution)/shard_map/ppermute | solution.py:407
  2.9 4.9 %collective-permute-start.3 = (f32[9,8,128]{2,1,0:T(8,128)S(1)}, f32[9,8,128]{2,1,0:T(8,128)S(1)}, u32[]{:S(2)}, u32[]{:S(2)}) collective-permute-start(f32[9,8,128]{2,1,0:T(8,128)S(1)} %join.1.refs_0_.refs_4_), channel_id=1, source_target_pairs={{0,6},{1,7},{2,4},{3,5},{4,2},{5,3},{6,0},{7,1},{8,14},{9,15},{10,... | collective-permute-start | bytes 110600 | tf_op jit(solution)/shard_map/ppermute | solution.py:407
  7.8 0.0 collective-permute-start.2
  7.8 0.6 collective-permute-start.1
  8.5 0.6 keys.1.keys_ref
  9.1 0.7 %collective-permute-done.3.refs_3_.refs_7_ = f32[9,8,128]{2,1,0:T(8,128)S(1)} collective-permute-done((f32[9,8,128]{2,1,0:T(8,128)S(1)}, f32[9,8,128]{2,1,0:T(8,128)S(1)}, u32[]{:S(2)}, u32[]{:S(2)}) %collective-permute-start.3) | collective-permute-done | bytes 36896 | tf_op jit(solution)/shard_map/ppermute | solution.py:407
  9.8 2.9 %collective-permute-done.2.refs_2_.refs_6_ = f32[9,8,128]{2,1,0:T(8,128)S(1)} collective-permute-done((f32[9,8,128]{2,1,0:T(8,128)S(1)}, f32[9,8,128]{2,1,0:T(8,128)S(1)}, u32[]{:S(2)}, u32[]{:S(2)}) %collective-permute-start.2) | collective-permute-done | bytes 36896 | tf_op jit(solution)/shard_map/ppermute | solution.py:407
  12.7 1.2 %adjoint.2 = (bf16[272,256]{1,0:T(8,128)(2,1)S(1)}, bf16[256,256]{1,0:T(8,128)(2,1)S(1)}) custom-call(f32[8,256]{1,0:T(8,128)S(1)} %keys.1.keys_ref, bf16[32,2,256,256]{3,2,1,0:T(8,128)(2,1)S(1)} %copy-done, f32[9,8,128]{2,1,0:T(8,128)S(1)} %join.1.refs_0_.refs_4_, f32[9,8,128]{2,1,0:T(8,128)S(1)} %collective-permute-done.1.refs_1_.refs_5_, ...), custom_call_target="tpu_custom_call" | custom-call | tf_op jit(solution)/shard_map/adjoint/pallas_call | solution.py:425
  13.9 2.5 %collective-permute-start.6 = (bf16[272,256]{1,0:T(8,128)(2,1)S(1)}, bf16[272,256]{1,0:T(8,128)(2,1)S(1)}, u32[]{:S(2)}, u32[]{:S(2)}) collective-permute-start(bf16[272,256]{1,0:T(8,128)(2,1)S(1)} %get-tuple-element.27.refs_0_), channel_id=1, source_target_pairs={{0,24},{8,16},{16,8},{24,0},{1,25},{9,17},{17,9},{25,1},{2,26},{10... | collective-permute-start | bytes 417800 | tf_op jit(solution)/shard_map/ppermute | solution.py:407
  16.4 0.5 collective-permute-start.5
  16.9 0.5 collective-permute-start.4
  17.4 3.4 %collective-permute-done.6.refs_3_ = bf16[272,256]{1,0:T(8,128)(2,1)S(1)} collective-permute-done((bf16[272,256]{1,0:T(8,128)(2,1)S(1)}, bf16[272,256]{1,0:T(8,128)(2,1)S(1)}, u32[]{:S(2)}, u32[]{:S(2)}) %collective-permute-start.6) | collective-permute-done | bytes 139296 | tf_op jit(solution)/shard_map/ppermute | solution.py:407
  20.8 1.7 %collective-permute-done.5.refs_2_ = bf16[272,256]{1,0:T(8,128)(2,1)S(1)} collective-permute-done((bf16[272,256]{1,0:T(8,128)(2,1)S(1)}, bf16[272,256]{1,0:T(8,128)(2,1)S(1)}, u32[]{:S(2)}, u32[]{:S(2)}) %collective-permute-start.5) | collective-permute-done | bytes 139296 | tf_op jit(solution)/shard_map/ppermute | solution.py:407
  22.6 0.1 collective-permute-done.4.refs_1_
  22.6 3.0 %voxel.2 = (bf16[256,256]{1,0:T(8,128)(2,1)S(1)}, f32[8,128]{1,0:T(8,128)S(1)}, f32[17,8,128]{2,1,0:T(8,128)S(1)}, f32[8,128]{1,0:T(8,128)S(1)}, bf16[1024,256]{...) custom-call(bf16[32,2,256,256]{3,2,1,0:T(8,128)(2,1)S(1)} %copy-done, ...), custom_call_target="tpu_custom_call" | custom-call | tf_op jit(solution)/shard_map/voxel/pallas_call | solution.py:425
  25.6 0.1 collective-permute-start.7
  25.7 1.1 %forward.2.own_ref = f32[17,8,128]{2,1,0:T(8,128)S(1)} custom-call(bf16[32,2,256,256]{3,2,1,0:T(8,128)(2,1)S(1)} %copy-done, bf16[256,256]{1,0:T(8,128)(2,1)S(1)} %get-tuple-element.28.lhs_ref, f32[8,128]{1,0:T(8,128)S(1)} %get-tuple-element.29.acc_ref), custom_call_target="tpu_custom_call" | custom-call | tf_op jit(solution)/shard_map/forward/pallas_call | solution.py:425
  26.8 0.1 collective-permute-done.7.other_ref
  27.0 1.6 %collective-permute-start.12 = (f32[17,8,128]{2,1,0:T(8,128)S(1)}, f32[17,8,128]{2,1,0:T(8,128)S(1)}, u32[]{:S(2)}, u32[]{:S(2)}) collective-permute-start(f32[17,8,128]{2,1,0:T(8,128)S(1)} %get-tuple-element.33.refs_0_), channel_id=1, source_target_pairs={{0,6},{1,7},{2,4},{3,5},{4,2},{5,3},{6,0},{7,1},{8,14},{9,15},{10,... | collective-permute-start | bytes 208904 | tf_op jit(solution)/shard_map/ppermute | solution.py:407
  28.6 0.4 collective-permute-start.11
  29.0 2.5 %collective-permute-start.10 = (f32[17,8,128]{2,1,0:T(8,128)S(1)}, f32[17,8,128]{2,1,0:T(8,128)S(1)}, u32[]{:S(2)}, u32[]{:S(2)}) collective-permute-start(f32[17,8,128]{2,1,0:T(8,128)S(1)} %get-tuple-element.33.refs_0_), channel_id=1, source_target_pairs={{0,2},{1,3},{2,0},{3,1},{4,6},{5,7},{6,4},{7,5},{8,10},{9,11},{10,... | collective-permute-start | bytes 208904 | tf_op jit(solution)/shard_map/ppermute | solution.py:407
  31.4 1.5 %collective-permute-start.9 = (bf16[256,256]{1,0:T(8,128)(2,1)S(1)}, bf16[256,256]{1,0:T(8,128)(2,1)S(1)}, u32[]{:S(2)}, u32[]{:S(2)}) collective-permute-start(bf16[256,256]{1,0:T(8,128)(2,1)S(1)} %get-tuple-element.32), channel_id=1, source_target_pairs={{0,16},{8,24},{16,0},{24,8},{1,17},{9,25},{17,1},{25,9},{2,18},{10... | collective-permute-start | bytes 393224 | tf_op jit(solution)/shard_map/ppermute | solution.py:407
  32.9 0.8 %collective-permute-start.8 = (bf16[256,256]{1,0:T(8,128)(2,1)S(1)}, bf16[256,256]{1,0:T(8,128)(2,1)S(1)}, u32[]{:S(2)}, u32[]{:S(2)}) collective-permute-start(bf16[256,256]{1,0:T(8,128)(2,1)S(1)} %get-tuple-element.32), channel_id=1, source_target_pairs={{0,8},{8,0},{16,24},{24,16},{1,9},{9,1},{17,25},{25,17},{2,10},{10... | collective-permute-start | bytes 393224 | tf_op jit(solution)/shard_map/ppermute | solution.py:407
  33.7 0.2 collective-permute-done.12.refs_3_
  33.9 2.5 %collective-permute-done.11.refs_2_ = f32[17,8,128]{2,1,0:T(8,128)S(1)} collective-permute-done((f32[17,8,128]{2,1,0:T(8,128)S(1)}, f32[17,8,128]{2,1,0:T(8,128)S(1)}, u32[]{:S(2)}, u32[]{:S(2)}) %collective-permute-start.11) | collective-permute-done | bytes 69664 | tf_op jit(solution)/shard_map/ppermute | solution.py:407
  36.4 0.0 collective-permute-done.10.refs_1_
  36.4 0.1 half_ray.2
  36.5 0.1 collective-permute-start.13
  36.6 1.2 %collective-permute-done.13.refs_3_ = bf16[80,256]{1,0:T(8,128)(2,1)S(1)} collective-permute-done((bf16[80,256]{1,0:T(8,128)(2,1)S(1)}, bf16[80,256]{1,0:T(8,128)(2,1)S(1)}, u32[]{:S(2)}, u32[]{:S(2)}) %collective-permute-start.13) | collective-permute-done | bytes 40992 | tf_op jit(solution)/shard_map/ppermute | solution.py:407
  37.8 0.0 collective-permute-done.9.refs_1_.refs_4_
  37.8 0.1 collective-permute-done.8.refs_0_.refs_3_
  37.9 1.2 %adjoint.3.refs_0_.unread_ref = bf16[272,256]{1,0:T(8,128)(2,1)S(1)} custom-call(f32[8,256]{1,0:T(8,128)S(1)} %keys.1.keys_ref, bf16[32,2,256,256]{3,2,1,0:T(8,128)(2,1)S(1)} %copy-done, bf16[256,256]{1,0:T(8,128)(2,1)S(1)} %collective-permute-done.8.refs_0_.refs_3_, bf16[256,256]{1,0:T(8,128)(2,1)S(1)} %collective-permute-done.9.refs_1_.refs_4_, ...), custom_call_target="tpu_custom_call" | custom-call | tf_op jit(solution)/shard_map/adjoint/pallas_call | solution.py:425
  39.0 1.7 %collective-permute-start.16 = (bf16[272,256]{1,0:T(8,128)(2,1)S(1)}, bf16[272,256]{1,0:T(8,128)(2,1)S(1)}, u32[]{:S(2)}, u32[]{:S(2)}) collective-permute-start(bf16[272,256]{1,0:T(8,128)(2,1)S(1)} %adjoint.3.refs_0_.unread_ref), channel_id=1, source_target_pairs={{0,24},{8,16},{16,8},{24,0},{1,25},{9,17},{17,9},{25,1},{2,26},{10... | collective-permute-start | bytes 417800 | tf_op jit(solution)/shard_map/ppermute | solution.py:407
  40.7 1.3 %collective-permute-start.15 = (bf16[272,256]{1,0:T(8,128)(2,1)S(1)}, bf16[272,256]{1,0:T(8,128)(2,1)S(1)}, u32[]{:S(2)}, u32[]{:S(2)}) collective-permute-start(bf16[272,256]{1,0:T(8,128)(2,1)S(1)} %adjoint.3.refs_0_.unread_ref), channel_id=1, source_target_pairs={{0,16},{8,24},{16,0},{24,8},{1,17},{9,25},{17,1},{25,9},{2,18},{10... | collective-permute-start | bytes 417800 | tf_op jit(solution)/shard_map/ppermute | solution.py:407
  42.0 0.6 collective-permute-start.14
  42.6 3.9 %collective-permute-done.16.refs_3_ = bf16[272,256]{1,0:T(8,128)(2,1)S(1)} collective-permute-done((bf16[272,256]{1,0:T(8,128)(2,1)S(1)}, bf16[272,256]{1,0:T(8,128)(2,1)S(1)}, u32[]{:S(2)}, u32[]{:S(2)}) %collective-permute-start.16) | collective-permute-done | bytes 139296 | tf_op jit(solution)/shard_map/ppermute | solution.py:407
  46.6 2.1 %collective-permute-done.15.refs_2_ = bf16[272,256]{1,0:T(8,128)(2,1)S(1)} collective-permute-done((bf16[272,256]{1,0:T(8,128)(2,1)S(1)}, bf16[272,256]{1,0:T(8,128)(2,1)S(1)}, u32[]{:S(2)}, u32[]{:S(2)}) %collective-permute-start.15) | collective-permute-done | bytes 139296 | tf_op jit(solution)/shard_map/ppermute | solution.py:407
  48.7 0.0 collective-permute-done.14.refs_1_
  48.7 2.0 %voxel.3 = (bf16[256,256]{1,0:T(8,128)(2,1)S(1)}, f32[8,128]{1,0:T(8,128)S(1)}, f32[17,8,128]{2,1,0:T(8,128)S(1)}, f32[8,128]{1,0:T(8,128)S(1)}, bf16[1024,256]{1,0:T(8,128)(2,1)S(1)}) custom-call(bf16[32,2,256,256]{3,2,1,0:T(8,128)(2,1)S(1)} %copy-done, bf16[272,256]{1,0:T(8,128)(2,1)S(1)} %adjoint.3.refs_0_.unread_ref, ...), custom_call_target="tpu_custom_call" | custom-call | tf_op jit(solution)/shard_map/voxel/pallas_call | solution.py:425
  50.7 0.1 collective-permute-start.17
  50.8 1.1 %forward.3.own_ref = f32[17,8,128]{2,1,0:T(8,128)S(1)} custom-call(bf16[32,2,256,256]{3,2,1,0:T(8,128)(2,1)S(1)} %copy-done, bf16[256,256]{1,0:T(8,128)(2,1)S(1)} %get-tuple-element.40.lhs_ref, f32[8,128]{1,0:T(8,128)S(1)} %get-tuple-element.41.acc_ref), custom_call_target="tpu_custom_call" | custom-call | tf_op jit(solution)/shard_map/forward/pallas_call | solution.py:425
  51.9 0.1 collective-permute-done.17.other_ref
  52.1 2.3 %collective-permute-start.21 = (bf16[144,128]{1,0:T(8,128)(2,1)S(1)}, bf16[144,128]{1,0:T(8,128)(2,1)S(1)}, u32[]{:S(2)}, u32[]{:S(2)}) collective-permute-start(bf16[144,128]{1,0:T(8,128)(2,1)S(1)} %get-tuple-element.44.refs_0_), channel_id=1, source_target_pairs={{0,6},{1,7},{2,4},{3,5},{4,2},{5,3},{6,0},{7,1},{8,14},{9,15},{10,... | collective-permute-start | bytes 110600 | tf_op jit(solution)/shard_map/ppermute | solution.py:407
  54.4 0.0 collective-permute-start.20
  54.4 2.2 %collective-permute-start.19 = (bf16[144,128]{1,0:T(8,128)(2,1)S(1)}, bf16[144,128]{1,0:T(8,128)(2,1)S(1)}, u32[]{:S(2)}, u32[]{:S(2)}) collective-permute-start(bf16[144,128]{1,0:T(8,128)(2,1)S(1)} %get-tuple-element.44.refs_0_), channel_id=1, source_target_pairs={{0,2},{1,3},{2,0},{3,1},{4,6},{5,7},{6,4},{7,5},{8,10},{9,11},{10,... | collective-permute-start | bytes 110600 | tf_op jit(solution)/shard_map/ppermute | solution.py:407
  56.5 1.7 %collective-permute-start.18 = (bf16[256,256]{1,0:T(8,128)(2,1)S(1)}, bf16[256,256]{1,0:T(8,128)(2,1)S(1)}, u32[]{:S(2)}, u32[]{:S(2)}) collective-permute-start(bf16[256,256]{1,0:T(8,128)(2,1)S(1)} %get-tuple-element.43), channel_id=1, source_target_pairs={{0,24},{8,16},{16,8},{24,0},{1,25},{9,17},{17,9},{25,1},{2,26},{10... | collective-permute-start | bytes 393224 | tf_op jit(solution)/shard_map/ppermute | solution.py:407
  58.2 0.0 collective-permute-done.21.refs_3_
  58.2 1.2 %collective-permute-done.20.refs_2_ = bf16[144,128]{1,0:T(8,128)(2,1)S(1)} collective-permute-done((bf16[144,128]{1,0:T(8,128)(2,1)S(1)}, bf16[144,128]{1,0:T(8,128)(2,1)S(1)}, u32[]{:S(2)}, u32[]{:S(2)}) %collective-permute-start.20) | collective-permute-done | bytes 36896 | tf_op jit(solution)/shard_map/ppermute | solution.py:407
  59.4 0.0 collective-permute-done.19.refs_1_
  59.4 0.1 half_ray.3
  59.5 0.1 collective-permute-start.22
  59.6 1.2 %collective-permute-done.22.refs_2_ = f32[8,128]{1,0:T(8,128)S(1)} collective-permute-done((f32[8,128]{1,0:T(8,128)S(1)}, f32[8,128]{1,0:T(8,128)S(1)}, u32[]{:S(2)}, u32[]{:S(2)}) %collective-permute-start.22) | collective-permute-done | bytes 4128 | tf_op jit(solution)/shard_map/ppermute | solution.py:407
  60.7 1.7 %collective-permute-done.18.refs_0_.refs_5_ = bf16[256,256]{1,0:T(8,128)(2,1)S(1)} collective-permute-done((bf16[256,256]{1,0:T(8,128)(2,1)S(1)}, bf16[256,256]{1,0:T(8,128)(2,1)S(1)}, u32[]{:S(2)}, u32[]{:S(2)}) %collective-permute-start.18) | collective-permute-done | bytes 131104 | tf_op jit(solution)/shard_map/ppermute | solution.py:407
  62.5 1.7 %collective-permute-start.25 = (f32[8,128]{1,0:T(8,128)S(1)}, f32[8,128]{1,0:T(8,128)S(1)}, u32[]{:S(2)}, u32[]{:S(2)}) collective-permute-start(f32[8,128]{1,0:T(8,128)S(1)} %sum.1.refs_0_), channel_id=1, source_target_pairs={{0,24},{8,16},{16,8},{24,0},{1,25},{9,17},{17,9},{25,1},{2,26},{10... | collective-permute-start | bytes 12296 | tf_op jit(solution)/shard_map/ppermute | solution.py:407
  64.1 1.3 %collective-permute-start.24 = (f32[8,128]{1,0:T(8,128)S(1)}, f32[8,128]{1,0:T(8,128)S(1)}, u32[]{:S(2)}, u32[]{:S(2)}) collective-permute-start(f32[8,128]{1,0:T(8,128)S(1)} %sum.1.refs_0_), channel_id=1, source_target_pairs={{0,16},{8,24},{16,0},{24,8},{1,17},{9,25},{17,1},{25,9},{2,18},{10... | collective-permute-start | bytes 12296 | tf_op jit(solution)/shard_map/ppermute | solution.py:407
  65.4 0.5 collective-permute-start.23
  66.0 0.3 pick.1.refs_0_
  66.3 0.4 share.3.refs_9_
  66.7 0.8 %share.2.refs_8_ = f32[512,256]{1,0:T(8,128)S(1)} custom-call(bf16[512,1024]{1,0:T(8,128)(2,1)S(1)} %pick.1.refs_0_, bf16[1024,256]{1,0:T(8,128)(2,1)S(1)} %get-tuple-element.50.refs_1_, bf16[256,256]{1,0:T(8,128)(2,1)S(1)} %get-tuple-element.31.refs_0_.refs_2_, bf16[256,256]{1,0:T(8,128)(2,1)S(1)} %collective-permute-done.8.refs_0_.refs_3_, ...), custom_call_target="tpu_custom_call" | custom-call | tf_op jit(solution)/shard_map/share/pallas_call | solution.py:425
  67.5 0.2 collective-permute-done.24.refs_2_
  67.7 1.3 %collective-permute-done.23.refs_1_ = f32[8,128]{1,0:T(8,128)S(1)} collective-permute-done((f32[8,128]{1,0:T(8,128)S(1)}, f32[8,128]{1,0:T(8,128)S(1)}, u32[]{:S(2)}, u32[]{:S(2)}) %collective-permute-start.23) | collective-permute-done | bytes 4128 | tf_op jit(solution)/shard_map/ppermute | solution.py:407
  69.0 1.3 %final.1 = (f32[4,32768]{1,0:T(4,128)}, f32[4]{0:T(128)}) custom-call(f32[8,128]{1,0:T(8,128)S(1)} %sum.1.refs_0_, f32[8,128]{1,0:T(8,128)S(1)} %collective-permute-done.23.refs_1_, f32[8,128]{1,0:T(8,128)S(1)} %collective-permute-done.24.refs_2_, f32[8,128]{1,0:T(8,128)S(1)} %collective-permute-done.25.refs_3_, ...), custom_call_target="tpu_custom_call" | custom-call | tf_op jit(solution)/shard_map/final/pallas_call | solution.py:525
  (12 shorter events, 0.1 us)
Async XLA Ops:
  0.6 12.1 %copy-start = (bf16[32,2,256,256]{3,2,1,0:T(8,128)(2,1)S(1)}, bf16[32,2,256,256]{3,2,1,0:T(8,128)(2,1)}, u32[]{:S(2)}) copy-start(bf16[32,2,256,256]{3,2,1,0:T(8,128)(2,1)} %tiles_ref.11) | copy-start | bytes 25165828
  0.6 0.9 %copy-start.1 = (f32[4,1024]{1,0:T(4,128)S(1)}, f32[4,1024]{1,0:T(4,128)}, u32[]{:S(2)}) copy-start(f32[4,1024]{1,0:T(4,128)} %obs_ref.1) | copy-start | bytes 49156
  1.5 7.0 %copy-start.2 = (s32[32,2]{0,1:T(2,128)S(1)}, s32[32,2]{0,1:T(2,128)}, u32[]{:S(2)}) copy-start(s32[32,2]{0,1:T(2,128)} %param.5) | copy-start | bytes 772
  1.5 1.4 %collective-permute-start = (f32[5,8,128]{2,1,0:T(8,128)S(1)}, f32[5,8,128]{2,1,0:T(8,128)S(1)}, u32[]{:S(2)}, u32[]{:S(2)}) collective-permute-start(f32[5,8,128]{2,1,0:T(8,128)S(1)} %pack.1.unread_ref.own_ref), channel_id=1, source_target_pairs={{0,1},{1,0},{2,3},{3,2},{4,5},{5,4},{6,7},{7,6},{8,9},{9,8},{10,11... | collective-permute-start | bytes 61448 | tf_op jit(solution)/shard_map/ppermute | solution.py:407
  2.9 6.9 %collective-permute-start.3 = (f32[9,8,128]{2,1,0:T(8,128)S(1)}, f32[9,8,128]{2,1,0:T(8,128)S(1)}, u32[]{:S(2)}, u32[]{:S(2)}) collective-permute-start(f32[9,8,128]{2,1,0:T(8,128)S(1)} %join.1.refs_0_.refs_4_), channel_id=1, source_target_pairs={{0,6},{1,7},{2,4},{3,5},{4,2},{5,3},{6,0},{7,1},{8,14},{9,15},{10,... | collective-permute-start | bytes 110600 | tf_op jit(solution)/shard_map/ppermute | solution.py:407
  7.8 4.9 %collective-permute-start.2 = (f32[9,8,128]{2,1,0:T(8,128)S(1)}, f32[9,8,128]{2,1,0:T(8,128)S(1)}, u32[]{:S(2)}, u32[]{:S(2)}) collective-permute-start(f32[9,8,128]{2,1,0:T(8,128)S(1)} %join.1.refs_0_.refs_4_), channel_id=1, source_target_pairs={{0,4},{1,5},{2,6},{3,7},{4,0},{5,1},{6,2},{7,3},{8,12},{9,13},{10,... | collective-permute-start | bytes 110600 | tf_op jit(solution)/shard_map/ppermute | solution.py:407
  7.8 4.9 %collective-permute-start.1 = (f32[9,8,128]{2,1,0:T(8,128)S(1)}, f32[9,8,128]{2,1,0:T(8,128)S(1)}, u32[]{:S(2)}, u32[]{:S(2)}) collective-permute-start(f32[9,8,128]{2,1,0:T(8,128)S(1)} %join.1.refs_0_.refs_4_), channel_id=1, source_target_pairs={{0,2},{1,3},{2,0},{3,1},{4,6},{5,7},{6,4},{7,5},{8,10},{9,11},{10,... | collective-permute-start | bytes 110600 | tf_op jit(solution)/shard_map/ppermute | solution.py:407
  13.9 6.9 %collective-permute-start.6 = (bf16[272,256]{1,0:T(8,128)(2,1)S(1)}, bf16[272,256]{1,0:T(8,128)(2,1)S(1)}, u32[]{:S(2)}, u32[]{:S(2)}) collective-permute-start(bf16[272,256]{1,0:T(8,128)(2,1)S(1)} %get-tuple-element.27.refs_0_), channel_id=1, source_target_pairs={{0,24},{8,16},{16,8},{24,0},{1,25},{9,17},{17,9},{25,1},{2,26},{10... | collective-permute-start | bytes 417800 | tf_op jit(solution)/shard_map/ppermute | solution.py:407
  16.4 6.2 %collective-permute-start.5 = (bf16[272,256]{1,0:T(8,128)(2,1)S(1)}, bf16[272,256]{1,0:T(8,128)(2,1)S(1)}, u32[]{:S(2)}, u32[]{:S(2)}) collective-permute-start(bf16[272,256]{1,0:T(8,128)(2,1)S(1)} %get-tuple-element.27.refs_0_), channel_id=1, source_target_pairs={{0,16},{8,24},{16,0},{24,8},{1,17},{9,25},{17,1},{25,9},{2,18},{10... | collective-permute-start | bytes 417800 | tf_op jit(solution)/shard_map/ppermute | solution.py:407
  16.9 5.7 %collective-permute-start.4 = (bf16[272,256]{1,0:T(8,128)(2,1)S(1)}, bf16[272,256]{1,0:T(8,128)(2,1)S(1)}, u32[]{:S(2)}, u32[]{:S(2)}) collective-permute-start(bf16[272,256]{1,0:T(8,128)(2,1)S(1)} %get-tuple-element.27.refs_0_), channel_id=1, source_target_pairs={{0,8},{8,0},{16,24},{24,16},{1,9},{9,1},{17,25},{25,17},{2,10},{10... | collective-permute-start | bytes 417800 | tf_op jit(solution)/shard_map/ppermute | solution.py:407
  25.6 1.3 %collective-permute-start.7 = (f32[17,8,128]{2,1,0:T(8,128)S(1)}, f32[17,8,128]{2,1,0:T(8,128)S(1)}, u32[]{:S(2)}, u32[]{:S(2)}) collective-permute-start(f32[17,8,128]{2,1,0:T(8,128)S(1)} %get-tuple-element.30), channel_id=1, source_target_pairs={{0,1},{1,0},{2,3},{3,2},{4,5},{5,4},{6,7},{7,6},{8,9},{9,8},{10,11... | collective-permute-start | bytes 208904 | tf_op jit(solution)/shard_map/ppermute | solution.py:407
  27.0 6.9 %collective-permute-start.12 = (f32[17,8,128]{2,1,0:T(8,128)S(1)}, f32[17,8,128]{2,1,0:T(8,128)S(1)}, u32[]{:S(2)}, u32[]{:S(2)}) collective-permute-start(f32[17,8,128]{2,1,0:T(8,128)S(1)} %get-tuple-element.33.refs_0_), channel_id=1, source_target_pairs={{0,6},{1,7},{2,4},{3,5},{4,2},{5,3},{6,0},{7,1},{8,14},{9,15},{10,... | collective-permute-start | bytes 208904 | tf_op jit(solution)/shard_map/ppermute | solution.py:407
  28.6 7.8 %collective-permute-start.11 = (f32[17,8,128]{2,1,0:T(8,128)S(1)}, f32[17,8,128]{2,1,0:T(8,128)S(1)}, u32[]{:S(2)}, u32[]{:S(2)}) collective-permute-start(f32[17,8,128]{2,1,0:T(8,128)S(1)} %get-tuple-element.33.refs_0_), channel_id=1, source_target_pairs={{0,4},{1,5},{2,6},{3,7},{4,0},{5,1},{6,2},{7,3},{8,12},{9,13},{10,... | collective-permute-start | bytes 208904 | tf_op jit(solution)/shard_map/ppermute | solution.py:407
  29.0 7.4 %collective-permute-start.10 = (f32[17,8,128]{2,1,0:T(8,128)S(1)}, f32[17,8,128]{2,1,0:T(8,128)S(1)}, u32[]{:S(2)}, u32[]{:S(2)}) collective-permute-start(f32[17,8,128]{2,1,0:T(8,128)S(1)} %get-tuple-element.33.refs_0_), channel_id=1, source_target_pairs={{0,2},{1,3},{2,0},{3,1},{4,6},{5,7},{6,4},{7,5},{8,10},{9,11},{10,... | collective-permute-start | bytes 208904 | tf_op jit(solution)/shard_map/ppermute | solution.py:407
  31.4 6.3 %collective-permute-start.9 = (bf16[256,256]{1,0:T(8,128)(2,1)S(1)}, bf16[256,256]{1,0:T(8,128)(2,1)S(1)}, u32[]{:S(2)}, u32[]{:S(2)}) collective-permute-start(bf16[256,256]{1,0:T(8,128)(2,1)S(1)} %get-tuple-element.32), channel_id=1, source_target_pairs={{0,16},{8,24},{16,0},{24,8},{1,17},{9,25},{17,1},{25,9},{2,18},{10... | collective-permute-start | bytes 393224 | tf_op jit(solution)/shard_map/ppermute | solution.py:407
  32.9 5.0 %collective-permute-start.8 = (bf16[256,256]{1,0:T(8,128)(2,1)S(1)}, bf16[256,256]{1,0:T(8,128)(2,1)S(1)}, u32[]{:S(2)}, u32[]{:S(2)}) collective-permute-start(bf16[256,256]{1,0:T(8,128)(2,1)S(1)} %get-tuple-element.32), channel_id=1, source_target_pairs={{0,8},{8,0},{16,24},{24,16},{1,9},{9,1},{17,25},{25,17},{2,10},{10... | collective-permute-start | bytes 393224 | tf_op jit(solution)/shard_map/ppermute | solution.py:407
  36.5 1.3 %collective-permute-start.13 = (bf16[80,256]{1,0:T(8,128)(2,1)S(1)}, bf16[80,256]{1,0:T(8,128)(2,1)S(1)}, u32[]{:S(2)}, u32[]{:S(2)}) collective-permute-start(bf16[80,256]{1,0:T(8,128)(2,1)S(1)} %get-tuple-element.35.refs_2_), channel_id=1, source_target_pairs={{0,1},{1,0},{2,3},{3,2},{4,5},{5,4},{6,7},{7,6},{8,9},{9,8},{10,11... | collective-permute-start | bytes 122888 | tf_op jit(solution)/shard_map/ppermute | solution.py:407
  39.0 7.5 %collective-permute-start.16 = (bf16[272,256]{1,0:T(8,128)(2,1)S(1)}, bf16[272,256]{1,0:T(8,128)(2,1)S(1)}, u32[]{:S(2)}, u32[]{:S(2)}) collective-permute-start(bf16[272,256]{1,0:T(8,128)(2,1)S(1)} %adjoint.3.refs_0_.unread_ref), channel_id=1, source_target_pairs={{0,24},{8,16},{16,8},{24,0},{1,25},{9,17},{17,9},{25,1},{2,26},{10... | collective-permute-start | bytes 417800 | tf_op jit(solution)/shard_map/ppermute | solution.py:407
  40.7 7.9 %collective-permute-start.15 = (bf16[272,256]{1,0:T(8,128)(2,1)S(1)}, bf16[272,256]{1,0:T(8,128)(2,1)S(1)}, u32[]{:S(2)}, u32[]{:S(2)}) collective-permute-start(bf16[272,256]{1,0:T(8,128)(2,1)S(1)} %adjoint.3.refs_0_.unread_ref), channel_id=1, source_target_pairs={{0,16},{8,24},{16,0},{24,8},{1,17},{9,25},{17,1},{25,9},{2,18},{10... | collective-permute-start | bytes 417800 | tf_op jit(solution)/shard_map/ppermute | solution.py:407
  42.0 6.7 %collective-permute-start.14 = (bf16[272,256]{1,0:T(8,128)(2,1)S(1)}, bf16[272,256]{1,0:T(8,128)(2,1)S(1)}, u32[]{:S(2)}, u32[]{:S(2)}) collective-permute-start(bf16[272,256]{1,0:T(8,128)(2,1)S(1)} %adjoint.3.refs_0_.unread_ref), channel_id=1, source_target_pairs={{0,8},{8,0},{16,24},{24,16},{1,9},{9,1},{17,25},{25,17},{2,10},{10... | collective-permute-start | bytes 417800 | tf_op jit(solution)/shard_map/ppermute | solution.py:407
  50.7 1.3 %collective-permute-start.17 = (f32[17,8,128]{2,1,0:T(8,128)S(1)}, f32[17,8,128]{2,1,0:T(8,128)S(1)}, u32[]{:S(2)}, u32[]{:S(2)}) collective-permute-start(f32[17,8,128]{2,1,0:T(8,128)S(1)} %get-tuple-element.42), channel_id=1, source_target_pairs={{0,1},{1,0},{2,3},{3,2},{4,5},{5,4},{6,7},{7,6},{8,9},{9,8},{10,11... | collective-permute-start | bytes 208904 | tf_op jit(solution)/shard_map/ppermute | solution.py:407
  52.1 6.1 %collective-permute-start.21 = (bf16[144,128]{1,0:T(8,128)(2,1)S(1)}, bf16[144,128]{1,0:T(8,128)(2,1)S(1)}, u32[]{:S(2)}, u32[]{:S(2)}) collective-permute-start(bf16[144,128]{1,0:T(8,128)(2,1)S(1)} %get-tuple-element.44.refs_0_), channel_id=1, source_target_pairs={{0,6},{1,7},{2,4},{3,5},{4,2},{5,3},{6,0},{7,1},{8,14},{9,15},{10,... | collective-permute-start | bytes 110600 | tf_op jit(solution)/shard_map/ppermute | solution.py:407
  54.4 5.0 %collective-permute-start.20 = (bf16[144,128]{1,0:T(8,128)(2,1)S(1)}, bf16[144,128]{1,0:T(8,128)(2,1)S(1)}, u32[]{:S(2)}, u32[]{:S(2)}) collective-permute-start(bf16[144,128]{1,0:T(8,128)(2,1)S(1)} %get-tuple-element.44.refs_0_), channel_id=1, source_target_pairs={{0,4},{1,5},{2,6},{3,7},{4,0},{5,1},{6,2},{7,3},{8,12},{9,13},{10,... | collective-permute-start | bytes 110600 | tf_op jit(solution)/shard_map/ppermute | solution.py:407
  54.4 5.0 %collective-permute-start.19 = (bf16[144,128]{1,0:T(8,128)(2,1)S(1)}, bf16[144,128]{1,0:T(8,128)(2,1)S(1)}, u32[]{:S(2)}, u32[]{:S(2)}) collective-permute-start(bf16[144,128]{1,0:T(8,128)(2,1)S(1)} %get-tuple-element.44.refs_0_), channel_id=1, source_target_pairs={{0,2},{1,3},{2,0},{3,1},{4,6},{5,7},{6,4},{7,5},{8,10},{9,11},{10,... | collective-permute-start | bytes 110600 | tf_op jit(solution)/shard_map/ppermute | solution.py:407
  56.5 5.9 %collective-permute-start.18 = (bf16[256,256]{1,0:T(8,128)(2,1)S(1)}, bf16[256,256]{1,0:T(8,128)(2,1)S(1)}, u32[]{:S(2)}, u32[]{:S(2)}) collective-permute-start(bf16[256,256]{1,0:T(8,128)(2,1)S(1)} %get-tuple-element.43), channel_id=1, source_target_pairs={{0,24},{8,16},{16,8},{24,0},{1,25},{9,17},{17,9},{25,1},{2,26},{10... | collective-permute-start | bytes 393224 | tf_op jit(solution)/shard_map/ppermute | solution.py:407
  59.5 1.2 %collective-permute-start.22 = (f32[8,128]{1,0:T(8,128)S(1)}, f32[8,128]{1,0:T(8,128)S(1)}, u32[]{:S(2)}, u32[]{:S(2)}) collective-permute-start(f32[8,128]{1,0:T(8,128)S(1)} %get-tuple-element.47.refs_1_), channel_id=1, source_target_pairs={{0,1},{1,0},{2,3},{3,2},{4,5},{5,4},{6,7},{7,6},{8,9},{9,8},{10,11... | collective-permute-start | bytes 12296 | tf_op jit(solution)/shard_map/ppermute | solution.py:407
  62.5 5.0 %collective-permute-start.25 = (f32[8,128]{1,0:T(8,128)S(1)}, f32[8,128]{1,0:T(8,128)S(1)}, u32[]{:S(2)}, u32[]{:S(2)}) collective-permute-start(f32[8,128]{1,0:T(8,128)S(1)} %sum.1.refs_0_), channel_id=1, source_target_pairs={{0,24},{8,16},{16,8},{24,0},{1,25},{9,17},{17,9},{25,1},{2,26},{10... | collective-permute-start | bytes 12296 | tf_op jit(solution)/shard_map/ppermute | solution.py:407
  64.1 3.6 %collective-permute-start.24 = (f32[8,128]{1,0:T(8,128)S(1)}, f32[8,128]{1,0:T(8,128)S(1)}, u32[]{:S(2)}, u32[]{:S(2)}) collective-permute-start(f32[8,128]{1,0:T(8,128)S(1)} %sum.1.refs_0_), channel_id=1, source_target_pairs={{0,16},{8,24},{16,0},{24,8},{1,17},{9,25},{17,1},{25,9},{2,18},{10... | collective-permute-start | bytes 12296 | tf_op jit(solution)/shard_map/ppermute | solution.py:407
  65.4 3.6 %collective-permute-start.23 = (f32[8,128]{1,0:T(8,128)S(1)}, f32[8,128]{1,0:T(8,128)S(1)}, u32[]{:S(2)}, u32[]{:S(2)}) collective-permute-start(f32[8,128]{1,0:T(8,128)S(1)} %sum.1.refs_0_), channel_id=1, source_target_pairs={{0,8},{8,0},{16,24},{24,16},{1,9},{9,1},{17,25},{25,17},{2,10},{10... | collective-permute-start | bytes 12296 | tf_op jit(solution)/shard_map/ppermute | solution.py:407

commit v12 on v11

--- a/solution.py
+++ b/solution.py
@@ -128,6 +128,41 @@
                 across = keys_ref[other, :1, h * LANES : (h + 1) * LANES]
                 lane = other * per_row + h * LANES
                 pick_ref[at, lane : lane + LANES] = jnp.where(down == across, 1.0, 0.0).astype(jnp.bfloat16)
+
+
+def adjoint_rows(rays, tiles_ref, owner, per_share, g):
+    low = low_half(2 * LANES)
+    i = owner * per_share + 2 * g
+    wide = [
+        jnp.dot(rays, tiles_ref[i + e, k], preferred_element_type=jnp.float32)[8 * g : 8 * g + 8]
+        for e in range(2)
+        for k in range(2)
+    ]
+    value = jnp.concatenate(
+        [
+            jnp.where(low, wide[0], pltpu.roll(wide[1], 4, 0)),
+            jnp.where(low, pltpu.roll(wide[2], 4, 0), wide[3]),
+        ],
+        axis=0,
+    )
+    return value, pl.multiple_of(8 * i, 16)
+
+
+def half_sources(half_ref, half):
+    peers = lax.axis_size("col") // 2
+    rows = (half_ref.shape[0] - 16) // peers
+    core = jnp.bitwise_xor(lax.axis_index("col") % 2, half)
+    return [(2 * slot + core, half_ref[slot * rows : (slot + 1) * rows]) for slot in range(peers)]
+
+
+def own_adjoint_kernel(tiles_ref, half_ref, out_ref):
+    per_share = tiles_ref.shape[0] // lax.axis_size("col")
+    at = 0
+    for owner, rays in half_sources(half_ref, 0):
+        for g in range(per_share // 2):
+            value, _ = adjoint_rows(rays, tiles_ref, owner, per_share, g)
+            out_ref[at : at + 16] = value.astype(jnp.bfloat16)
+            at += 16
 
 
 def adjoint_kernel(first, unread, keys_ref, tiles_ref, *refs):
@@ -147,39 +182,26 @@
                 owner = jnp.bitwise_xor(me, 2 * e + h)
                 sources.append((owner, packed(blocks, max(16, 4 * per_share))))
     else:
-        halves, (term_ref,) = refs[:2], refs[2:]
-        rows = (halves[0].shape[0] - 16) // (shares // 2)
-        squares = [read_squares(half[-16:, :LANES]) for half in halves]
-        sources = [
-            (2 * slot + jnp.bitwise_xor(me % 2, h), half[slot * rows : (slot + 1) * rows])
-            for h, half in enumerate(halves)
-            for slot in range(shares // 2)
-        ]
+        done_ref, own_ref, other_ref, term_ref = refs
+        squares = [read_squares(half[-16:, :LANES]) for half in (own_ref, other_ref)]
+        sources = half_sources(other_ref, 1)
+        at = 0
+        for slot in range(shares // 2):
+            for g in range(per_share // 2):
+                i = (2 * slot + me % 2) * per_share + 2 * g
+                term_ref[pl.ds(pl.multiple_of(8 * i, 16), 16), :] = done_ref[at : at + 16]
+                at += 16
     squares = tree_sum(squares)
-    low = low_half(2 * LANES)
     pieces = jnp.concatenate(in_two(squares), axis=1)
     extra = jnp.zeros_like(pieces)
     if first:
         keys = keys_ref[...]
         coarse = jnp.floor(keys * (1.0 / 64))
-        extra = jnp.where(low, coarse, keys - 64 * coarse)
+        extra = jnp.where(low_half(2 * LANES), coarse, keys - 64 * coarse)
     term_ref[terms:] = jnp.concatenate([pieces, extra], axis=0).astype(jnp.bfloat16)
     for owner, rays in sources:
         for g in range(per_share // 2):
-            i = owner * per_share + 2 * g
-            wide = [
-                jnp.dot(rays, tiles_ref[i + e, k], preferred_element_type=jnp.float32)[8 * g : 8 * g + 8]
-                for e in range(2)
-                for k in range(2)
-            ]
-            value = jnp.concatenate(
-                [
-                    jnp.where(low, wide[0], pltpu.roll(wide[1], 4, 0)),
-                    jnp.where(low, pltpu.roll(wide[2], 4, 0), wide[3]),
-                ],
-                axis=0,
-            )
-            at = pl.multiple_of(8 * i, 16)
+            value, at = adjoint_rows(rays, tiles_ref, owner, per_share, g)
             upper = value.astype(jnp.bfloat16)
             term_ref[pl.ds(at, 16), :] = upper
             if first:
@@ -497,7 +519,8 @@
         last = iteration == ITERS - 1
         betas.append(beta)
         combined.append(upper_terms)
-        crossing = range(1, rows // 2 + 1) if iteration == 0 else range(rows // 2 + 1, rows) if last else []
+        late = range(rows // 2, rows - 1)
+        crossing = [d for d in range(1, rows) if d not in late] if iteration == 0 else late if last else []
         summed, *passed = pair(own, other, [remainder] * (len(crossing) > 0), last)
         gathered = exchange(summed, "col", 2)
         for d in crossing:
@@ -510,7 +533,9 @@
             alpha, left_raw, half = half_ray(gathered, lefts, beta, [], False, True)
         alphas.append(alpha)
         lefts = [left_raw]
-        (new_terms,) = adjoint([half, from_peer(half, "col", 1)], False, after)
+        other_half = from_peer(half, "col", 1)
+        done = call(own_adjoint_kernel, "own_adjoint", bf16(per_row // 2, tile_size), [tile_values, half])
+        (new_terms,) = adjoint([done, half, other_half], False, after)
         if iteration == 0:
             selector = call(pick_kernel, "pick", bf16(share_rows, rows * per_row), [new_terms, all_keys], [ANY, VMEM])
         new_terms = exchange(new_terms, "row")

time: 70.6 us -> 69.4 us (0.983)
  waiting for transfers between devices: 25.6 us -> 24.6 us
    ppermute x26, waiting for transfers between devices: 25.6 us -> 24.6 us  [from_peer(): lax.ppermute(value, axis, [(i, i ^ d) for i in range(lax.axis_size(axis))])]
    pallas_call x17 -> x18, Pallas kernels: 12 us -> 12.1 us  [call(): pl.pallas_call(kernel, out_shape=out_shape, in_specs=in_specs or [VMEM] *...]
  transfers between devices with their start and end apart: 26 -> 26, of which waited for: 19 -> 20; matrix products, arithmetic and copies ran while one was open for 0% -> 0% of each run, Pallas kernels for 7% -> 8%
where the time goes in v12:
time: 69.4 us; the launch traced here: 69.1 us
  starting transfers between devices  29.5 us (43%)
  waiting for transfers between devices  24.6 us (35%)
  Pallas kernels  13.5 us (19%)
  local copies, waits for them, and re-layouts  0.87 us (1%)
  between operations  0.77 us (1%)
    ppermute x26, starting transfers between devices, from_peer(): lax.ppermute(value, axis, [(i, i ^ d) for i in range(lax.axis_size(axis))])  29.5 us
    ppermute x26, waiting for transfers between devices, from_peer(): lax.ppermute(value, axis, [(i, i ^ d) for i in range(lax.axis_size(axis))])  24.6 us
    pallas_call x18, Pallas kernels, call(): pl.pallas_call(kernel, out_shape=out_shape, in_specs=in_specs or [VMEM] *...  12.1 us
  transfers between devices with their start and end apart: 26, of which 20 were waited for; matrix products, arithmetic and copies ran while one was open for 0% of the time, Pallas kernels for 8%

profile of v12, /device:TPU:0, one launch (start us, length us, event | category | flops | bytes accessed | tf_op | source)
XLA Modules:
  0.0 69.1 jit_solution(12989006176401688395)
XLA Ops:
  0.6 0.9 %copy-done.1 = f32[4,1024]{1,0:T(4,128)S(1)} copy-done((f32[4,1024]{1,0:T(4,128)S(1)}, f32[4,1024]{1,0:T(4,128)}, u32[]{:S(2)}) %copy-start.1) | copy-done | bytes 16408
  1.5 0.5 collective-permute-start
  2.0 0.8 %collective-permute-done.other_ref = f32[5,8,128]{2,1,0:T(8,128)S(1)} collective-permute-done((f32[5,8,128]{2,1,0:T(8,128)S(1)}, f32[5,8,128]{2,1,0:T(8,128)S(1)}, u32[]{:S(2)}, u32[]{:S(2)}) %collective-permute-start) | collective-permute-done | bytes 20512 | tf_op jit(solution)/shard_map/ppermute | solution.py:429
  2.9 4.9 %collective-permute-start.3 = (f32[9,8,128]{2,1,0:T(8,128)S(1)}, f32[9,8,128]{2,1,0:T(8,128)S(1)}, u32[]{:S(2)}, u32[]{:S(2)}) collective-permute-start(f32[9,8,128]{2,1,0:T(8,128)S(1)} %join.1.refs_0_.refs_4_), channel_id=1, source_target_pairs={{0,6},{1,7},{2,4},{3,5},{4,2},{5,3},{6,0},{7,1},{8,14},{9,15},{10,... | collective-permute-start | bytes 110600 | tf_op jit(solution)/shard_map/ppermute | solution.py:429
  7.8 0.0 collective-permute-start.2
  7.8 0.6 collective-permute-start.1
  8.5 0.6 keys.1.keys_ref
  9.1 0.7 %collective-permute-done.3.refs_3_.refs_7_ = f32[9,8,128]{2,1,0:T(8,128)S(1)} collective-permute-done((f32[9,8,128]{2,1,0:T(8,128)S(1)}, f32[9,8,128]{2,1,0:T(8,128)S(1)}, u32[]{:S(2)}, u32[]{:S(2)}) %collective-permute-start.3) | collective-permute-done | bytes 36896 | tf_op jit(solution)/shard_map/ppermute | solution.py:429
  9.8 2.9 %collective-permute-done.2.refs_2_.refs_6_ = f32[9,8,128]{2,1,0:T(8,128)S(1)} collective-permute-done((f32[9,8,128]{2,1,0:T(8,128)S(1)}, f32[9,8,128]{2,1,0:T(8,128)S(1)}, u32[]{:S(2)}, u32[]{:S(2)}) %collective-permute-start.2) | collective-permute-done | bytes 36896 | tf_op jit(solution)/shard_map/ppermute | solution.py:429
  12.7 0.0 collective-permute-done.1.refs_1_.refs_5_
  12.7 1.2 %adjoint.2 = (bf16[272,256]{1,0:T(8,128)(2,1)S(1)}, bf16[256,256]{1,0:T(8,128)(2,1)S(1)}) custom-call(f32[8,256]{1,0:T(8,128)S(1)} %keys.1.keys_ref, bf16[32,2,256,256]{3,2,1,0:T(8,128)(2,1)S(1)} %copy-done, f32[9,8,128]{2,1,0:T(8,128)S(1)} %join.1.refs_0_.refs_4_, f32[9,8,128]{2,1,0:T(8,128)S(1)} %collective-permute-done.1.refs_1_.refs_5_, ...), custom_call_target="tpu_custom_call" | custom-call | tf_op jit(solution)/shard_map/adjoint/pallas_call | solution.py:447
  13.9 2.5 %collective-permute-start.6 = (bf16[272,256]{1,0:T(8,128)(2,1)S(1)}, bf16[272,256]{1,0:T(8,128)(2,1)S(1)}, u32[]{:S(2)}, u32[]{:S(2)}) collective-permute-start(bf16[272,256]{1,0:T(8,128)(2,1)S(1)} %get-tuple-element.27.refs_0_), channel_id=1, source_target_pairs={{0,24},{8,16},{16,8},{24,0},{1,25},{9,17},{17,9},{25,1},{2,26},{10... | collective-permute-start | bytes 417800 | tf_op jit(solution)/shard_map/ppermute | solution.py:429
  16.4 0.5 collective-permute-start.5
  16.9 0.5 collective-permute-start.4
  17.4 3.4 %collective-permute-done.6.refs_3_ = bf16[272,256]{1,0:T(8,128)(2,1)S(1)} collective-permute-done((bf16[272,256]{1,0:T(8,128)(2,1)S(1)}, bf16[272,256]{1,0:T(8,128)(2,1)S(1)}, u32[]{:S(2)}, u32[]{:S(2)}) %collective-permute-start.6) | collective-permute-done | bytes 139296 | tf_op jit(solution)/shard_map/ppermute | solution.py:429
  20.8 1.7 %collective-permute-done.5.refs_2_ = bf16[272,256]{1,0:T(8,128)(2,1)S(1)} collective-permute-done((bf16[272,256]{1,0:T(8,128)(2,1)S(1)}, bf16[272,256]{1,0:T(8,128)(2,1)S(1)}, u32[]{:S(2)}, u32[]{:S(2)}) %collective-permute-start.5) | collective-permute-done | bytes 139296 | tf_op jit(solution)/shard_map/ppermute | solution.py:429
  22.6 0.1 collective-permute-done.4.refs_1_
  22.6 3.0 %voxel.2 = (bf16[256,256]{1,0:T(8,128)(2,1)S(1)}, f32[8,128]{1,0:T(8,128)S(1)}, f32[17,8,128]{2,1,0:T(8,128)S(1)}, f32[8,128]{1,0:T(8,128)S(1)}, bf16[1024,256]{...) custom-call(bf16[32,2,256,256]{3,2,1,0:T(8,128)(2,1)S(1)} %copy-done, ...), custom_call_target="tpu_custom_call" | custom-call | tf_op jit(solution)/shard_map/voxel/pallas_call | solution.py:447
  25.6 0.1 collective-permute-start.7
  25.7 1.1 %forward.2.own_ref = f32[17,8,128]{2,1,0:T(8,128)S(1)} custom-call(bf16[32,2,256,256]{3,2,1,0:T(8,128)(2,1)S(1)} %copy-done, bf16[256,256]{1,0:T(8,128)(2,1)S(1)} %get-tuple-element.28.lhs_ref, f32[8,128]{1,0:T(8,128)S(1)} %get-tuple-element.29.acc_ref), custom_call_target="tpu_custom_call" | custom-call | tf_op jit(solution)/shard_map/forward/pallas_call | solution.py:447
  26.8 0.1 collective-permute-done.7.other_ref
  27.0 1.6 %collective-permute-start.12 = (f32[17,8,128]{2,1,0:T(8,128)S(1)}, f32[17,8,128]{2,1,0:T(8,128)S(1)}, u32[]{:S(2)}, u32[]{:S(2)}) collective-permute-start(f32[17,8,128]{2,1,0:T(8,128)S(1)} %get-tuple-element.33.refs_0_), channel_id=1, source_target_pairs={{0,6},{1,7},{2,4},{3,5},{4,2},{5,3},{6,0},{7,1},{8,14},{9,15},{10,... | collective-permute-start | bytes 208904 | tf_op jit(solution)/shard_map/ppermute | solution.py:429
  28.6 0.4 collective-permute-start.11
  29.0 2.5 %collective-permute-start.10 = (f32[17,8,128]{2,1,0:T(8,128)S(1)}, f32[17,8,128]{2,1,0:T(8,128)S(1)}, u32[]{:S(2)}, u32[]{:S(2)}) collective-permute-start(f32[17,8,128]{2,1,0:T(8,128)S(1)} %get-tuple-element.33.refs_0_), channel_id=1, source_target_pairs={{0,2},{1,3},{2,0},{3,1},{4,6},{5,7},{6,4},{7,5},{8,10},{9,11},{10,... | collective-permute-start | bytes 208904 | tf_op jit(solution)/shard_map/ppermute | solution.py:429
  31.4 1.7 %collective-permute-start.9 = (bf16[256,256]{1,0:T(8,128)(2,1)S(1)}, bf16[256,256]{1,0:T(8,128)(2,1)S(1)}, u32[]{:S(2)}, u32[]{:S(2)}) collective-permute-start(bf16[256,256]{1,0:T(8,128)(2,1)S(1)} %get-tuple-element.32), channel_id=1, source_target_pairs={{0,24},{8,16},{16,8},{24,0},{1,25},{9,17},{17,9},{25,1},{2,26},{10... | collective-permute-start | bytes 393224 | tf_op jit(solution)/shard_map/ppermute | solution.py:429
  33.1 1.2 %collective-permute-start.8 = (bf16[256,256]{1,0:T(8,128)(2,1)S(1)}, bf16[256,256]{1,0:T(8,128)(2,1)S(1)}, u32[]{:S(2)}, u32[]{:S(2)}) collective-permute-start(bf16[256,256]{1,0:T(8,128)(2,1)S(1)} %get-tuple-element.32), channel_id=1, source_target_pairs={{0,8},{8,0},{16,24},{24,16},{1,9},{9,1},{17,25},{25,17},{2,10},{10... | collective-permute-start | bytes 393224 | tf_op jit(solution)/shard_map/ppermute | solution.py:429
  34.4 0.0 collective-permute-done.12.refs_3_
  34.4 2.0 %collective-permute-done.11.refs_2_ = f32[17,8,128]{2,1,0:T(8,128)S(1)} collective-permute-done((f32[17,8,128]{2,1,0:T(8,128)S(1)}, f32[17,8,128]{2,1,0:T(8,128)S(1)}, u32[]{:S(2)}, u32[]{:S(2)}) %collective-permute-start.11) | collective-permute-done | bytes 69664 | tf_op jit(solution)/shard_map/ppermute | solution.py:429
  36.4 0.0 collective-permute-done.10.refs_1_
  36.4 0.1 half_ray.2
  36.5 0.1 collective-permute-start.13
  36.6 0.6 own_adjoint.1.refs_2_
  37.2 0.5 collective-permute-done.13.refs_4_
  37.8 1.0 %collective-permute-done.9.refs_1_.refs_5_ = bf16[256,256]{1,0:T(8,128)(2,1)S(1)} collective-permute-done((bf16[256,256]{1,0:T(8,128)(2,1)S(1)}, bf16[256,256]{1,0:T(8,128)(2,1)S(1)}, u32[]{:S(2)}, u32[]{:S(2)}) %collective-permute-start.9) | collective-permute-done | bytes 131104 | tf_op jit(solution)/shard_map/ppermute | solution.py:429
  38.7 1.4 %collective-permute-done.8.refs_0_.refs_3_ = bf16[256,256]{1,0:T(8,128)(2,1)S(1)} collective-permute-done((bf16[256,256]{1,0:T(8,128)(2,1)S(1)}, bf16[256,256]{1,0:T(8,128)(2,1)S(1)}, u32[]{:S(2)}, u32[]{:S(2)}) %collective-permute-start.8) | collective-permute-done | bytes 131104 | tf_op jit(solution)/shard_map/ppermute | solution.py:429
  40.2 0.6 adjoint.3.refs_0_.unread_ref
  40.8 1.6 %collective-permute-start.16 = (bf16[272,256]{1,0:T(8,128)(2,1)S(1)}, bf16[272,256]{1,0:T(8,128)(2,1)S(1)}, u32[]{:S(2)}, u32[]{:S(2)}) collective-permute-start(bf16[272,256]{1,0:T(8,128)(2,1)S(1)} %adjoint.3.refs_0_.unread_ref), channel_id=1, source_target_pairs={{0,24},{8,16},{16,8},{24,0},{1,25},{9,17},{17,9},{25,1},{2,26},{10... | collective-permute-start | bytes 417800 | tf_op jit(solution)/shard_map/ppermute | solution.py:429
  42.4 0.7 %collective-permute-start.15 = (bf16[272,256]{1,0:T(8,128)(2,1)S(1)}, bf16[272,256]{1,0:T(8,128)(2,1)S(1)}, u32[]{:S(2)}, u32[]{:S(2)}) collective-permute-start(bf16[272,256]{1,0:T(8,128)(2,1)S(1)} %adjoint.3.refs_0_.unread_ref), channel_id=1, source_target_pairs={{0,16},{8,24},{16,0},{24,8},{1,17},{9,25},{17,1},{25,9},{2,18},{10... | collective-permute-start | bytes 417800 | tf_op jit(solution)/shard_map/ppermute | solution.py:429
  43.1 1.2 %collective-permute-start.14 = (bf16[272,256]{1,0:T(8,128)(2,1)S(1)}, bf16[272,256]{1,0:T(8,128)(2,1)S(1)}, u32[]{:S(2)}, u32[]{:S(2)}) collective-permute-start(bf16[272,256]{1,0:T(8,128)(2,1)S(1)} %adjoint.3.refs_0_.unread_ref), channel_id=1, source_target_pairs={{0,8},{8,0},{16,24},{24,16},{1,9},{9,1},{17,25},{25,17},{2,10},{10... | collective-permute-start | bytes 417800 | tf_op jit(solution)/shard_map/ppermute | solution.py:429
  44.4 3.3 %collective-permute-done.16.refs_3_ = bf16[272,256]{1,0:T(8,128)(2,1)S(1)} collective-permute-done((bf16[272,256]{1,0:T(8,128)(2,1)S(1)}, bf16[272,256]{1,0:T(8,128)(2,1)S(1)}, u32[]{:S(2)}, u32[]{:S(2)}) %collective-permute-start.16) | collective-permute-done | bytes 139296 | tf_op jit(solution)/shard_map/ppermute | solution.py:429
  47.7 1.4 %collective-permute-done.15.refs_2_ = bf16[272,256]{1,0:T(8,128)(2,1)S(1)} collective-permute-done((bf16[272,256]{1,0:T(8,128)(2,1)S(1)}, bf16[272,256]{1,0:T(8,128)(2,1)S(1)}, u32[]{:S(2)}, u32[]{:S(2)}) %collective-permute-start.15) | collective-permute-done | bytes 139296 | tf_op jit(solution)/shard_map/ppermute | solution.py:429
  49.1 2.0 %voxel.3 = (bf16[256,256]{1,0:T(8,128)(2,1)S(1)}, f32[8,128]{1,0:T(8,128)S(1)}, f32[17,8,128]{2,1,0:T(8,128)S(1)}, f32[8,128]{1,0:T(8,128)S(1)}, bf16[1024,256]{1,0:T(8,128)(2,1)S(1)}) custom-call(bf16[32,2,256,256]{3,2,1,0:T(8,128)(2,1)S(1)} %copy-done, bf16[272,256]{1,0:T(8,128)(2,1)S(1)} %adjoint.3.refs_0_.unread_ref, ...), custom_call_target="tpu_custom_call" | custom-call | tf_op jit(solution)/shard_map/voxel/pallas_call | solution.py:447
  51.1 0.1 collective-permute-start.17
  51.1 1.1 %forward.3.own_ref = f32[17,8,128]{2,1,0:T(8,128)S(1)} custom-call(bf16[32,2,256,256]{3,2,1,0:T(8,128)(2,1)S(1)} %copy-done, bf16[256,256]{1,0:T(8,128)(2,1)S(1)} %get-tuple-element.40.lhs_ref, f32[8,128]{1,0:T(8,128)S(1)} %get-tuple-element.41.acc_ref), custom_call_target="tpu_custom_call" | custom-call | tf_op jit(solution)/shard_map/forward/pallas_call | solution.py:447
  52.3 0.1 collective-permute-done.17.other_ref
  52.5 1.6 %collective-permute-start.21 = (bf16[144,128]{1,0:T(8,128)(2,1)S(1)}, bf16[144,128]{1,0:T(8,128)(2,1)S(1)}, u32[]{:S(2)}, u32[]{:S(2)}) collective-permute-start(bf16[144,128]{1,0:T(8,128)(2,1)S(1)} %get-tuple-element.44.refs_0_), channel_id=1, source_target_pairs={{0,6},{1,7},{2,4},{3,5},{4,2},{5,3},{6,0},{7,1},{8,14},{9,15},{10,... | collective-permute-start | bytes 110600 | tf_op jit(solution)/shard_map/ppermute | solution.py:429
  54.0 0.5 collective-permute-start.20
  54.6 2.3 %collective-permute-start.19 = (bf16[144,128]{1,0:T(8,128)(2,1)S(1)}, bf16[144,128]{1,0:T(8,128)(2,1)S(1)}, u32[]{:S(2)}, u32[]{:S(2)}) collective-permute-start(bf16[144,128]{1,0:T(8,128)(2,1)S(1)} %get-tuple-element.44.refs_0_), channel_id=1, source_target_pairs={{0,2},{1,3},{2,0},{3,1},{4,6},{5,7},{6,4},{7,5},{8,10},{9,11},{10,... | collective-permute-start | bytes 110600 | tf_op jit(solution)/shard_map/ppermute | solution.py:429
  56.9 0.6 collective-permute-start.18
  57.5 1.1 %collective-permute-done.21.refs_3_ = bf16[144,128]{1,0:T(8,128)(2,1)S(1)} collective-permute-done((bf16[144,128]{1,0:T(8,128)(2,1)S(1)}, bf16[144,128]{1,0:T(8,128)(2,1)S(1)}, u32[]{:S(2)}, u32[]{:S(2)}) %collective-permute-start.21) | collective-permute-done | bytes 36896 | tf_op jit(solution)/shard_map/ppermute | solution.py:429
  58.6 1.1 %collective-permute-done.20.refs_2_ = bf16[144,128]{1,0:T(8,128)(2,1)S(1)} collective-permute-done((bf16[144,128]{1,0:T(8,128)(2,1)S(1)}, bf16[144,128]{1,0:T(8,128)(2,1)S(1)}, u32[]{:S(2)}, u32[]{:S(2)}) %collective-permute-start.20) | collective-permute-done | bytes 36896 | tf_op jit(solution)/shard_map/ppermute | solution.py:429
  59.7 0.1 half_ray.3
  59.9 0.1 collective-permute-start.22
  60.0 1.1 %collective-permute-done.22.refs_2_ = f32[8,128]{1,0:T(8,128)S(1)} collective-permute-done((f32[8,128]{1,0:T(8,128)S(1)}, f32[8,128]{1,0:T(8,128)S(1)}, u32[]{:S(2)}, u32[]{:S(2)}) %collective-permute-start.22) | collective-permute-done | bytes 4128 | tf_op jit(solution)/shard_map/ppermute | solution.py:429
  61.1 0.8 %collective-permute-done.18.refs_0_.refs_4_ = bf16[256,256]{1,0:T(8,128)(2,1)S(1)} collective-permute-done((bf16[256,256]{1,0:T(8,128)(2,1)S(1)}, bf16[256,256]{1,0:T(8,128)(2,1)S(1)}, u32[]{:S(2)}, u32[]{:S(2)}) %collective-permute-start.18) | collective-permute-done | bytes 131104 | tf_op jit(solution)/shard_map/ppermute | solution.py:429
  61.9 1.5 %collective-permute-start.25 = (f32[8,128]{1,0:T(8,128)S(1)}, f32[8,128]{1,0:T(8,128)S(1)}, u32[]{:S(2)}, u32[]{:S(2)}) collective-permute-start(f32[8,128]{1,0:T(8,128)S(1)} %sum.1.refs_0_), channel_id=1, source_target_pairs={{0,24},{8,16},{16,8},{24,0},{1,25},{9,17},{17,9},{25,1},{2,26},{10... | collective-permute-start | bytes 12296 | tf_op jit(solution)/shard_map/ppermute | solution.py:429
  63.5 0.7 %collective-permute-start.24 = (f32[8,128]{1,0:T(8,128)S(1)}, f32[8,128]{1,0:T(8,128)S(1)}, u32[]{:S(2)}, u32[]{:S(2)}) collective-permute-start(f32[8,128]{1,0:T(8,128)S(1)} %sum.1.refs_0_), channel_id=1, source_target_pairs={{0,16},{8,24},{16,0},{24,8},{1,17},{9,25},{17,1},{25,9},{2,18},{10... | collective-permute-start | bytes 12296 | tf_op jit(solution)/shard_map/ppermute | solution.py:429
  64.2 1.2 %collective-permute-start.23 = (f32[8,128]{1,0:T(8,128)S(1)}, f32[8,128]{1,0:T(8,128)S(1)}, u32[]{:S(2)}, u32[]{:S(2)}) collective-permute-start(f32[8,128]{1,0:T(8,128)S(1)} %sum.1.refs_0_), channel_id=1, source_target_pairs={{0,8},{8,0},{16,24},{24,16},{1,9},{9,1},{17,25},{25,17},{2,10},{10... | collective-permute-start | bytes 12296 | tf_op jit(solution)/shard_map/ppermute | solution.py:429
  65.4 0.3 pick.1.refs_0_
  65.7 0.4 share.3.refs_9_
  66.2 0.8 %share.2.refs_8_ = f32[512,256]{1,0:T(8,128)S(1)} custom-call(bf16[512,1024]{1,0:T(8,128)(2,1)S(1)} %pick.1.refs_0_, bf16[1024,256]{1,0:T(8,128)(2,1)S(1)} %get-tuple-element.50.refs_1_, bf16[256,256]{1,0:T(8,128)(2,1)S(1)} %get-tuple-element.31.refs_0_.refs_2_, bf16[256,256]{1,0:T(8,128)(2,1)S(1)} %collective-permute-done.8.refs_0_.refs_3_, ...), custom_call_target="tpu_custom_call" | custom-call | tf_op jit(solution)/shard_map/share/pallas_call | solution.py:447
  67.0 0.1 collective-permute-done.24.refs_2_
  67.1 0.7 %collective-permute-done.23.refs_1_ = f32[8,128]{1,0:T(8,128)S(1)} collective-permute-done((f32[8,128]{1,0:T(8,128)S(1)}, f32[8,128]{1,0:T(8,128)S(1)}, u32[]{:S(2)}, u32[]{:S(2)}) %collective-permute-start.23) | collective-permute-done | bytes 4128 | tf_op jit(solution)/shard_map/ppermute | solution.py:429
  67.8 1.3 %final.1 = (f32[4,32768]{1,0:T(4,128)}, f32[4]{0:T(128)}) custom-call(f32[8,128]{1,0:T(8,128)S(1)} %sum.1.refs_0_, f32[8,128]{1,0:T(8,128)S(1)} %collective-permute-done.23.refs_1_, f32[8,128]{1,0:T(8,128)S(1)} %collective-permute-done.24.refs_2_, f32[8,128]{1,0:T(8,128)S(1)} %collective-permute-done.25.refs_3_, ...), custom_call_target="tpu_custom_call" | custom-call | tf_op jit(solution)/shard_map/final/pallas_call | solution.py:550
  (13 shorter events, 0.1 us)
Async XLA Ops:
  0.6 12.1 %copy-start = (bf16[32,2,256,256]{3,2,1,0:T(8,128)(2,1)S(1)}, bf16[32,2,256,256]{3,2,1,0:T(8,128)(2,1)}, u32[]{:S(2)}) copy-start(bf16[32,2,256,256]{3,2,1,0:T(8,128)(2,1)} %tiles_ref.13) | copy-start | bytes 25165828
  0.6 0.9 %copy-start.1 = (f32[4,1024]{1,0:T(4,128)S(1)}, f32[4,1024]{1,0:T(4,128)}, u32[]{:S(2)}) copy-start(f32[4,1024]{1,0:T(4,128)} %obs_ref.1) | copy-start | bytes 49156
  1.5 7.0 %copy-start.2 = (s32[32,2]{0,1:T(2,128)S(1)}, s32[32,2]{0,1:T(2,128)}, u32[]{:S(2)}) copy-start(s32[32,2]{0,1:T(2,128)} %param.5) | copy-start | bytes 772
  1.5 1.4 %collective-permute-start = (f32[5,8,128]{2,1,0:T(8,128)S(1)}, f32[5,8,128]{2,1,0:T(8,128)S(1)}, u32[]{:S(2)}, u32[]{:S(2)}) collective-permute-start(f32[5,8,128]{2,1,0:T(8,128)S(1)} %pack.1.unread_ref.own_ref), channel_id=1, source_target_pairs={{0,1},{1,0},{2,3},{3,2},{4,5},{5,4},{6,7},{7,6},{8,9},{9,8},{10,11... | collective-permute-start | bytes 61448 | tf_op jit(solution)/shard_map/ppermute | solution.py:429
  2.9 6.9 %collective-permute-start.3 = (f32[9,8,128]{2,1,0:T(8,128)S(1)}, f32[9,8,128]{2,1,0:T(8,128)S(1)}, u32[]{:S(2)}, u32[]{:S(2)}) collective-permute-start(f32[9,8,128]{2,1,0:T(8,128)S(1)} %join.1.refs_0_.refs_4_), channel_id=1, source_target_pairs={{0,6},{1,7},{2,4},{3,5},{4,2},{5,3},{6,0},{7,1},{8,14},{9,15},{10,... | collective-permute-start | bytes 110600 | tf_op jit(solution)/shard_map/ppermute | solution.py:429
  7.8 4.9 %collective-permute-start.2 = (f32[9,8,128]{2,1,0:T(8,128)S(1)}, f32[9,8,128]{2,1,0:T(8,128)S(1)}, u32[]{:S(2)}, u32[]{:S(2)}) collective-permute-start(f32[9,8,128]{2,1,0:T(8,128)S(1)} %join.1.refs_0_.refs_4_), channel_id=1, source_target_pairs={{0,4},{1,5},{2,6},{3,7},{4,0},{5,1},{6,2},{7,3},{8,12},{9,13},{10,... | collective-permute-start | bytes 110600 | tf_op jit(solution)/shard_map/ppermute | solution.py:429
  7.8 4.9 %collective-permute-start.1 = (f32[9,8,128]{2,1,0:T(8,128)S(1)}, f32[9,8,128]{2,1,0:T(8,128)S(1)}, u32[]{:S(2)}, u32[]{:S(2)}) collective-permute-start(f32[9,8,128]{2,1,0:T(8,128)S(1)} %join.1.refs_0_.refs_4_), channel_id=1, source_target_pairs={{0,2},{1,3},{2,0},{3,1},{4,6},{5,7},{6,4},{7,5},{8,10},{9,11},{10,... | collective-permute-start | bytes 110600 | tf_op jit(solution)/shard_map/ppermute | solution.py:429
  13.9 6.9 %collective-permute-start.6 = (bf16[272,256]{1,0:T(8,128)(2,1)S(1)}, bf16[272,256]{1,0:T(8,128)(2,1)S(1)}, u32[]{:S(2)}, u32[]{:S(2)}) collective-permute-start(bf16[272,256]{1,0:T(8,128)(2,1)S(1)} %get-tuple-element.27.refs_0_), channel_id=1, source_target_pairs={{0,24},{8,16},{16,8},{24,0},{1,25},{9,17},{17,9},{25,1},{2,26},{10... | collective-permute-start | bytes 417800 | tf_op jit(solution)/shard_map/ppermute | solution.py:429
  16.4 6.2 %collective-permute-start.5 = (bf16[272,256]{1,0:T(8,128)(2,1)S(1)}, bf16[272,256]{1,0:T(8,128)(2,1)S(1)}, u32[]{:S(2)}, u32[]{:S(2)}) collective-permute-start(bf16[272,256]{1,0:T(8,128)(2,1)S(1)} %get-tuple-element.27.refs_0_), channel_id=1, source_target_pairs={{0,16},{8,24},{16,0},{24,8},{1,17},{9,25},{17,1},{25,9},{2,18},{10... | collective-permute-start | bytes 417800 | tf_op jit(solution)/shard_map/ppermute | solution.py:429
  16.9 5.7 %collective-permute-start.4 = (bf16[272,256]{1,0:T(8,128)(2,1)S(1)}, bf16[272,256]{1,0:T(8,128)(2,1)S(1)}, u32[]{:S(2)}, u32[]{:S(2)}) collective-permute-start(bf16[272,256]{1,0:T(8,128)(2,1)S(1)} %get-tuple-element.27.refs_0_), channel_id=1, source_target_pairs={{0,8},{8,0},{16,24},{24,16},{1,9},{9,1},{17,25},{25,17},{2,10},{10... | collective-permute-start | bytes 417800 | tf_op jit(solution)/shard_map/ppermute | solution.py:429
  25.6 1.3 %collective-permute-start.7 = (f32[17,8,128]{2,1,0:T(8,128)S(1)}, f32[17,8,128]{2,1,0:T(8,128)S(1)}, u32[]{:S(2)}, u32[]{:S(2)}) collective-permute-start(f32[17,8,128]{2,1,0:T(8,128)S(1)} %get-tuple-element.30), channel_id=1, source_target_pairs={{0,1},{1,0},{2,3},{3,2},{4,5},{5,4},{6,7},{7,6},{8,9},{9,8},{10,11... | collective-permute-start | bytes 208904 | tf_op jit(solution)/shard_map/ppermute | solution.py:429
  27.0 7.4 %collective-permute-start.12 = (f32[17,8,128]{2,1,0:T(8,128)S(1)}, f32[17,8,128]{2,1,0:T(8,128)S(1)}, u32[]{:S(2)}, u32[]{:S(2)}) collective-permute-start(f32[17,8,128]{2,1,0:T(8,128)S(1)} %get-tuple-element.33.refs_0_), channel_id=1, source_target_pairs={{0,6},{1,7},{2,4},{3,5},{4,2},{5,3},{6,0},{7,1},{8,14},{9,15},{10,... | collective-permute-start | bytes 208904 | tf_op jit(solution)/shard_map/ppermute | solution.py:429
  28.6 7.8 %collective-permute-start.11 = (f32[17,8,128]{2,1,0:T(8,128)S(1)}, f32[17,8,128]{2,1,0:T(8,128)S(1)}, u32[]{:S(2)}, u32[]{:S(2)}) collective-permute-start(f32[17,8,128]{2,1,0:T(8,128)S(1)} %get-tuple-element.33.refs_0_), channel_id=1, source_target_pairs={{0,4},{1,5},{2,6},{3,7},{4,0},{5,1},{6,2},{7,3},{8,12},{9,13},{10,... | collective-permute-start | bytes 208904 | tf_op jit(solution)/shard_map/ppermute | solution.py:429
  29.0 7.4 %collective-permute-start.10 = (f32[17,8,128]{2,1,0:T(8,128)S(1)}, f32[17,8,128]{2,1,0:T(8,128)S(1)}, u32[]{:S(2)}, u32[]{:S(2)}) collective-permute-start(f32[17,8,128]{2,1,0:T(8,128)S(1)} %get-tuple-element.33.refs_0_), channel_id=1, source_target_pairs={{0,2},{1,3},{2,0},{3,1},{4,6},{5,7},{6,4},{7,5},{8,10},{9,11},{10,... | collective-permute-start | bytes 208904 | tf_op jit(solution)/shard_map/ppermute | solution.py:429
  31.4 7.3 %collective-permute-start.9 = (bf16[256,256]{1,0:T(8,128)(2,1)S(1)}, bf16[256,256]{1,0:T(8,128)(2,1)S(1)}, u32[]{:S(2)}, u32[]{:S(2)}) collective-permute-start(bf16[256,256]{1,0:T(8,128)(2,1)S(1)} %get-tuple-element.32), channel_id=1, source_target_pairs={{0,24},{8,16},{16,8},{24,0},{1,25},{9,17},{17,9},{25,1},{2,26},{10... | collective-permute-start | bytes 393224 | tf_op jit(solution)/shard_map/ppermute | solution.py:429
  33.1 7.0 %collective-permute-start.8 = (bf16[256,256]{1,0:T(8,128)(2,1)S(1)}, bf16[256,256]{1,0:T(8,128)(2,1)S(1)}, u32[]{:S(2)}, u32[]{:S(2)}) collective-permute-start(bf16[256,256]{1,0:T(8,128)(2,1)S(1)} %get-tuple-element.32), channel_id=1, source_target_pairs={{0,8},{8,0},{16,24},{24,16},{1,9},{9,1},{17,25},{25,17},{2,10},{10... | collective-permute-start | bytes 393224 | tf_op jit(solution)/shard_map/ppermute | solution.py:429
  36.5 1.3 %collective-permute-start.13 = (bf16[80,256]{1,0:T(8,128)(2,1)S(1)}, bf16[80,256]{1,0:T(8,128)(2,1)S(1)}, u32[]{:S(2)}, u32[]{:S(2)}) collective-permute-start(bf16[80,256]{1,0:T(8,128)(2,1)S(1)} %get-tuple-element.35.half_ref.refs_3_), channel_id=1, source_target_pairs={{0,1},{1,0},{2,3},{3,2},{4,5},{5,4},{6,7},{7,6},{8,9},{9,8},{10,11... | collective-permute-start | bytes 122888 | tf_op jit(solution)/shard_map/ppermute | solution.py:429
  40.8 6.9 %collective-permute-start.16 = (bf16[272,256]{1,0:T(8,128)(2,1)S(1)}, bf16[272,256]{1,0:T(8,128)(2,1)S(1)}, u32[]{:S(2)}, u32[]{:S(2)}) collective-permute-start(bf16[272,256]{1,0:T(8,128)(2,1)S(1)} %adjoint.3.refs_0_.unread_ref), channel_id=1, source_target_pairs={{0,24},{8,16},{16,8},{24,0},{1,25},{9,17},{17,9},{25,1},{2,26},{10... | collective-permute-start | bytes 417800 | tf_op jit(solution)/shard_map/ppermute | solution.py:429
  42.4 6.7 %collective-permute-start.15 = (bf16[272,256]{1,0:T(8,128)(2,1)S(1)}, bf16[272,256]{1,0:T(8,128)(2,1)S(1)}, u32[]{:S(2)}, u32[]{:S(2)}) collective-permute-start(bf16[272,256]{1,0:T(8,128)(2,1)S(1)} %adjoint.3.refs_0_.unread_ref), channel_id=1, source_target_pairs={{0,16},{8,24},{16,0},{24,8},{1,17},{9,25},{17,1},{25,9},{2,18},{10... | collective-permute-start | bytes 417800 | tf_op jit(solution)/shard_map/ppermute | solution.py:429
  43.1 5.9 %collective-permute-start.14 = (bf16[272,256]{1,0:T(8,128)(2,1)S(1)}, bf16[272,256]{1,0:T(8,128)(2,1)S(1)}, u32[]{:S(2)}, u32[]{:S(2)}) collective-permute-start(bf16[272,256]{1,0:T(8,128)(2,1)S(1)} %adjoint.3.refs_0_.unread_ref), channel_id=1, source_target_pairs={{0,8},{8,0},{16,24},{24,16},{1,9},{9,1},{17,25},{25,17},{2,10},{10... | collective-permute-start | bytes 417800 | tf_op jit(solution)/shard_map/ppermute | solution.py:429
  51.1 1.3 %collective-permute-start.17 = (f32[17,8,128]{2,1,0:T(8,128)S(1)}, f32[17,8,128]{2,1,0:T(8,128)S(1)}, u32[]{:S(2)}, u32[]{:S(2)}) collective-permute-start(f32[17,8,128]{2,1,0:T(8,128)S(1)} %get-tuple-element.42), channel_id=1, source_target_pairs={{0,1},{1,0},{2,3},{3,2},{4,5},{5,4},{6,7},{7,6},{8,9},{9,8},{10,11... | collective-permute-start | bytes 208904 | tf_op jit(solution)/shard_map/ppermute | solution.py:429
  52.5 6.2 %collective-permute-start.21 = (bf16[144,128]{1,0:T(8,128)(2,1)S(1)}, bf16[144,128]{1,0:T(8,128)(2,1)S(1)}, u32[]{:S(2)}, u32[]{:S(2)}) collective-permute-start(bf16[144,128]{1,0:T(8,128)(2,1)S(1)} %get-tuple-element.44.refs_0_), channel_id=1, source_target_pairs={{0,6},{1,7},{2,4},{3,5},{4,2},{5,3},{6,0},{7,1},{8,14},{9,15},{10,... | collective-permute-start | bytes 110600 | tf_op jit(solution)/shard_map/ppermute | solution.py:429
  54.0 5.7 %collective-permute-start.20 = (bf16[144,128]{1,0:T(8,128)(2,1)S(1)}, bf16[144,128]{1,0:T(8,128)(2,1)S(1)}, u32[]{:S(2)}, u32[]{:S(2)}) collective-permute-start(bf16[144,128]{1,0:T(8,128)(2,1)S(1)} %get-tuple-element.44.refs_0_), channel_id=1, source_target_pairs={{0,4},{1,5},{2,6},{3,7},{4,0},{5,1},{6,2},{7,3},{8,12},{9,13},{10,... | collective-permute-start | bytes 110600 | tf_op jit(solution)/shard_map/ppermute | solution.py:429
  54.6 5.2 %collective-permute-start.19 = (bf16[144,128]{1,0:T(8,128)(2,1)S(1)}, bf16[144,128]{1,0:T(8,128)(2,1)S(1)}, u32[]{:S(2)}, u32[]{:S(2)}) collective-permute-start(bf16[144,128]{1,0:T(8,128)(2,1)S(1)} %get-tuple-element.44.refs_0_), channel_id=1, source_target_pairs={{0,2},{1,3},{2,0},{3,1},{4,6},{5,7},{6,4},{7,5},{8,10},{9,11},{10,... | collective-permute-start | bytes 110600 | tf_op jit(solution)/shard_map/ppermute | solution.py:429
  56.9 5.0 %collective-permute-start.18 = (bf16[256,256]{1,0:T(8,128)(2,1)S(1)}, bf16[256,256]{1,0:T(8,128)(2,1)S(1)}, u32[]{:S(2)}, u32[]{:S(2)}) collective-permute-start(bf16[256,256]{1,0:T(8,128)(2,1)S(1)} %get-tuple-element.43), channel_id=1, source_target_pairs={{0,16},{8,24},{16,0},{24,8},{1,17},{9,25},{17,1},{25,9},{2,18},{10... | collective-permute-start | bytes 393224 | tf_op jit(solution)/shard_map/ppermute | solution.py:429
  59.9 1.2 %collective-permute-start.22 = (f32[8,128]{1,0:T(8,128)S(1)}, f32[8,128]{1,0:T(8,128)S(1)}, u32[]{:S(2)}, u32[]{:S(2)}) collective-permute-start(f32[8,128]{1,0:T(8,128)S(1)} %get-tuple-element.47.refs_1_), channel_id=1, source_target_pairs={{0,1},{1,0},{2,3},{3,2},{4,5},{5,4},{6,7},{7,6},{8,9},{9,8},{10,11... | collective-permute-start | bytes 12296 | tf_op jit(solution)/shard_map/ppermute | solution.py:429
  61.9 5.0 %collective-permute-start.25 = (f32[8,128]{1,0:T(8,128)S(1)}, f32[8,128]{1,0:T(8,128)S(1)}, u32[]{:S(2)}, u32[]{:S(2)}) collective-permute-start(f32[8,128]{1,0:T(8,128)S(1)} %sum.1.refs_0_), channel_id=1, source_target_pairs={{0,24},{8,16},{16,8},{24,0},{1,25},{9,17},{17,9},{25,1},{2,26},{10... | collective-permute-start | bytes 12296 | tf_op jit(solution)/shard_map/ppermute | solution.py:429
  63.5 3.6 %collective-permute-start.24 = (f32[8,128]{1,0:T(8,128)S(1)}, f32[8,128]{1,0:T(8,128)S(1)}, u32[]{:S(2)}, u32[]{:S(2)}) collective-permute-start(f32[8,128]{1,0:T(8,128)S(1)} %sum.1.refs_0_), channel_id=1, source_target_pairs={{0,16},{8,24},{16,0},{24,8},{1,17},{9,25},{17,1},{25,9},{2,18},{10... | collective-permute-start | bytes 12296 | tf_op jit(solution)/shard_map/ppermute | solution.py:429
  64.2 3.6 %collective-permute-start.23 = (f32[8,128]{1,0:T(8,128)S(1)}, f32[8,128]{1,0:T(8,128)S(1)}, u32[]{:S(2)}, u32[]{:S(2)}) collective-permute-start(f32[8,128]{1,0:T(8,128)S(1)} %sum.1.refs_0_), channel_id=1, source_target_pairs={{0,8},{8,0},{16,24},{24,16},{1,9},{9,1},{17,25},{25,17},{2,10},{10... | collective-permute-start | bytes 12296 | tf_op jit(solution)/shard_map/ppermute | solution.py:429

commit v13 on v12

--- a/solution.py
+++ b/solution.py
@@ -297,8 +297,8 @@
     out_ref[8 * count :, :] = packed_squares(own_ref[count] + other_ref[count])
 
 
-def sum_kernel(*refs):
-    refs[-1][...] = refs[-3][...] + refs[-2][...]
+def sum_kernel(own_ref, other_ref, out_ref):
+    out_ref[...] = own_ref[...] + other_ref[...]
 
 
 def half_ray_kernel(peers, first, narrow, update, unread, *refs):
@@ -519,8 +519,7 @@
         last = iteration == ITERS - 1
         betas.append(beta)
         combined.append(upper_terms)
-        late = range(rows // 2, rows - 1)
-        crossing = [d for d in range(1, rows) if d not in late] if iteration == 0 else late if last else []
+        crossing = range(1, rows // 2 + 1) if iteration == 0 else range(rows // 2 + 1, rows) if last else []
         summed, *passed = pair(own, other, [remainder] * (len(crossing) > 0), last)
         gathered = exchange(summed, "col", 2)
         for d in crossing:
@@ -544,9 +543,7 @@
         right_raw = voxel(new_terms, fixed, True)[4]
     remainders[0] = remainder
     products = [share(selector, c, [] if i else remainders) for i, c in enumerate(combined)]
-    squares = call(
-        sum_kernel, "sum", f32(8, LANES), [*after, squares, from_peer(squares, "col", 1)], [ANY] * len(after) + [VMEM] * 2
-    )
+    squares = call(sum_kernel, "sum", f32(8, LANES), [squares, from_peer(squares, "col", 1)])
     result, ratio = pl.pallas_call(
         functools.partial(final_kernel, rows, ITERS),
         out_shape=[f32(RHS, col_tiles // rows * tile_size), f32(RHS)],

time: 69.4 us -> 68.3 us (0.984)
  waiting for transfers between devices: 24.6 us -> 23.2 us
    ppermute x26, waiting for transfers between devices: 24.6 us -> 23.2 us  [from_peer(): lax.ppermute(value, axis, [(i, i ^ d) for i in range(lax.axis_size(axis))])]
  transfers between devices with their start and end apart: 26 -> 26, of which waited for: 20 -> 18; matrix products, arithmetic and copies ran while one was open for 0% -> 0% of each run, Pallas kernels for 8% -> 8%
where the time goes in v13:
time: 68.3 us; the launch traced here: 68.1 us
  starting transfers between devices  29.8 us (44%)
  waiting for transfers between devices  23.2 us (34%)
  Pallas kernels  13.5 us (20%)
  local copies, waits for them, and re-layouts  0.87 us (1%)
  between operations  0.78 us (1%)
    ppermute x26, starting transfers between devices, from_peer(): lax.ppermute(value, axis, [(i, i ^ d) for i in range(lax.axis_size(axis))])  29.8 us
    ppermute x26, waiting for transfers between devices, from_peer(): lax.ppermute(value, axis, [(i, i ^ d) for i in range(lax.axis_size(axis))])  23.2 us
    pallas_call x18, Pallas kernels, call(): pl.pallas_call(kernel, out_shape=out_shape, in_specs=in_specs or [VMEM] *...  12.1 us
  transfers between devices with their start and end apart: 26, of which 18 were waited for; matrix products, arithmetic and copies ran while one was open for 0% of the time, Pallas kernels for 8%

profile of v13, /device:TPU:0, one launch (start us, length us, event | category | flops | bytes accessed | tf_op | source)
XLA Modules:
  0.0 68.1 jit_solution(16379291135390053068)
XLA Ops:
  0.6 0.9 %copy-done.1 = f32[4,1024]{1,0:T(4,128)S(1)} copy-done((f32[4,1024]{1,0:T(4,128)S(1)}, f32[4,1024]{1,0:T(4,128)}, u32[]{:S(2)}) %copy-start.1) | copy-done | bytes 16408
  1.5 0.5 collective-permute-start
  2.0 0.8 %collective-permute-done.other_ref = f32[5,8,128]{2,1,0:T(8,128)S(1)} collective-permute-done((f32[5,8,128]{2,1,0:T(8,128)S(1)}, f32[5,8,128]{2,1,0:T(8,128)S(1)}, u32[]{:S(2)}, u32[]{:S(2)}) %collective-permute-start) | collective-permute-done | bytes 20512 | tf_op jit(solution)/shard_map/ppermute | solution.py:429
  2.9 4.9 %collective-permute-start.3 = (f32[9,8,128]{2,1,0:T(8,128)S(1)}, f32[9,8,128]{2,1,0:T(8,128)S(1)}, u32[]{:S(2)}, u32[]{:S(2)}) collective-permute-start(f32[9,8,128]{2,1,0:T(8,128)S(1)} %join.1.refs_0_.refs_4_), channel_id=1, source_target_pairs={{0,6},{1,7},{2,4},{3,5},{4,2},{5,3},{6,0},{7,1},{8,14},{9,15},{10,... | collective-permute-start | bytes 110600 | tf_op jit(solution)/shard_map/ppermute | solution.py:429
  7.8 0.0 collective-permute-start.2
  7.8 0.6 collective-permute-start.1
  8.5 0.6 keys.1.keys_ref
  9.1 0.7 %collective-permute-done.3.refs_3_.refs_7_ = f32[9,8,128]{2,1,0:T(8,128)S(1)} collective-permute-done((f32[9,8,128]{2,1,0:T(8,128)S(1)}, f32[9,8,128]{2,1,0:T(8,128)S(1)}, u32[]{:S(2)}, u32[]{:S(2)}) %collective-permute-start.3) | collective-permute-done | bytes 36896 | tf_op jit(solution)/shard_map/ppermute | solution.py:429
  9.8 2.9 %collective-permute-done.2.refs_2_.refs_6_ = f32[9,8,128]{2,1,0:T(8,128)S(1)} collective-permute-done((f32[9,8,128]{2,1,0:T(8,128)S(1)}, f32[9,8,128]{2,1,0:T(8,128)S(1)}, u32[]{:S(2)}, u32[]{:S(2)}) %collective-permute-start.2) | collective-permute-done | bytes 36896 | tf_op jit(solution)/shard_map/ppermute | solution.py:429
  12.7 0.0 collective-permute-done.1.refs_1_.refs_5_
  12.7 1.2 %adjoint.2 = (bf16[272,256]{1,0:T(8,128)(2,1)S(1)}, bf16[256,256]{1,0:T(8,128)(2,1)S(1)}) custom-call(f32[8,256]{1,0:T(8,128)S(1)} %keys.1.keys_ref, bf16[32,2,256,256]{3,2,1,0:T(8,128)(2,1)S(1)} %copy-done, f32[9,8,128]{2,1,0:T(8,128)S(1)} %join.1.refs_0_.refs_4_, f32[9,8,128]{2,1,0:T(8,128)S(1)} %collective-permute-done.1.refs_1_.refs_5_, ...), custom_call_target="tpu_custom_call" | custom-call | tf_op jit(solution)/shard_map/adjoint/pallas_call | solution.py:447
  13.9 2.5 %collective-permute-start.6 = (bf16[272,256]{1,0:T(8,128)(2,1)S(1)}, bf16[272,256]{1,0:T(8,128)(2,1)S(1)}, u32[]{:S(2)}, u32[]{:S(2)}) collective-permute-start(bf16[272,256]{1,0:T(8,128)(2,1)S(1)} %get-tuple-element.27.refs_0_), channel_id=1, source_target_pairs={{0,24},{8,16},{16,8},{24,0},{1,25},{9,17},{17,9},{25,1},{2,26},{10... | collective-permute-start | bytes 417800 | tf_op jit(solution)/shard_map/ppermute | solution.py:429
  16.4 0.5 collective-permute-start.5
  16.9 0.5 collective-permute-start.4
  17.4 3.4 %collective-permute-done.6.refs_3_ = bf16[272,256]{1,0:T(8,128)(2,1)S(1)} collective-permute-done((bf16[272,256]{1,0:T(8,128)(2,1)S(1)}, bf16[272,256]{1,0:T(8,128)(2,1)S(1)}, u32[]{:S(2)}, u32[]{:S(2)}) %collective-permute-start.6) | collective-permute-done | bytes 139296 | tf_op jit(solution)/shard_map/ppermute | solution.py:429
  20.8 1.7 %collective-permute-done.5.refs_2_ = bf16[272,256]{1,0:T(8,128)(2,1)S(1)} collective-permute-done((bf16[272,256]{1,0:T(8,128)(2,1)S(1)}, bf16[272,256]{1,0:T(8,128)(2,1)S(1)}, u32[]{:S(2)}, u32[]{:S(2)}) %collective-permute-start.5) | collective-permute-done | bytes 139296 | tf_op jit(solution)/shard_map/ppermute | solution.py:429
  22.6 0.1 collective-permute-done.4.refs_1_
  22.6 3.0 %voxel.2 = (bf16[256,256]{1,0:T(8,128)(2,1)S(1)}, f32[8,128]{1,0:T(8,128)S(1)}, f32[17,8,128]{2,1,0:T(8,128)S(1)}, f32[8,128]{1,0:T(8,128)S(1)}, bf16[1024,256]{...) custom-call(bf16[32,2,256,256]{3,2,1,0:T(8,128)(2,1)S(1)} %copy-done, ...), custom_call_target="tpu_custom_call" | custom-call | tf_op jit(solution)/shard_map/voxel/pallas_call | solution.py:447
  25.6 0.1 collective-permute-start.7
  25.7 1.1 %forward.2.own_ref = f32[17,8,128]{2,1,0:T(8,128)S(1)} custom-call(bf16[32,2,256,256]{3,2,1,0:T(8,128)(2,1)S(1)} %copy-done, bf16[256,256]{1,0:T(8,128)(2,1)S(1)} %get-tuple-element.28.lhs_ref, f32[8,128]{1,0:T(8,128)S(1)} %get-tuple-element.29.acc_ref), custom_call_target="tpu_custom_call" | custom-call | tf_op jit(solution)/shard_map/forward/pallas_call | solution.py:447
  26.8 0.1 collective-permute-done.7.other_ref
  27.0 1.6 %collective-permute-start.12 = (f32[17,8,128]{2,1,0:T(8,128)S(1)}, f32[17,8,128]{2,1,0:T(8,128)S(1)}, u32[]{:S(2)}, u32[]{:S(2)}) collective-permute-start(f32[17,8,128]{2,1,0:T(8,128)S(1)} %get-tuple-element.33.refs_0_), channel_id=1, source_target_pairs={{0,6},{1,7},{2,4},{3,5},{4,2},{5,3},{6,0},{7,1},{8,14},{9,15},{10,... | collective-permute-start | bytes 208904 | tf_op jit(solution)/shard_map/ppermute | solution.py:429
  28.6 0.4 collective-permute-start.11
  29.0 2.5 %collective-permute-start.10 = (f32[17,8,128]{2,1,0:T(8,128)S(1)}, f32[17,8,128]{2,1,0:T(8,128)S(1)}, u32[]{:S(2)}, u32[]{:S(2)}) collective-permute-start(f32[17,8,128]{2,1,0:T(8,128)S(1)} %get-tuple-element.33.refs_0_), channel_id=1, source_target_pairs={{0,2},{1,3},{2,0},{3,1},{4,6},{5,7},{6,4},{7,5},{8,10},{9,11},{10,... | collective-permute-start | bytes 208904 | tf_op jit(solution)/shard_map/ppermute | solution.py:429
  31.4 1.5 %collective-permute-start.9 = (bf16[256,256]{1,0:T(8,128)(2,1)S(1)}, bf16[256,256]{1,0:T(8,128)(2,1)S(1)}, u32[]{:S(2)}, u32[]{:S(2)}) collective-permute-start(bf16[256,256]{1,0:T(8,128)(2,1)S(1)} %get-tuple-element.32), channel_id=1, source_target_pairs={{0,16},{8,24},{16,0},{24,8},{1,17},{9,25},{17,1},{25,9},{2,18},{10... | collective-permute-start | bytes 393224 | tf_op jit(solution)/shard_map/ppermute | solution.py:429
  32.9 0.8 %collective-permute-start.8 = (bf16[256,256]{1,0:T(8,128)(2,1)S(1)}, bf16[256,256]{1,0:T(8,128)(2,1)S(1)}, u32[]{:S(2)}, u32[]{:S(2)}) collective-permute-start(bf16[256,256]{1,0:T(8,128)(2,1)S(1)} %get-tuple-element.32), channel_id=1, source_target_pairs={{0,8},{8,0},{16,24},{24,16},{1,9},{9,1},{17,25},{25,17},{2,10},{10... | collective-permute-start | bytes 393224 | tf_op jit(solution)/shard_map/ppermute | solution.py:429
  33.7 0.2 collective-permute-done.12.refs_3_
  33.9 2.5 %collective-permute-done.11.refs_2_ = f32[17,8,128]{2,1,0:T(8,128)S(1)} collective-permute-done((f32[17,8,128]{2,1,0:T(8,128)S(1)}, f32[17,8,128]{2,1,0:T(8,128)S(1)}, u32[]{:S(2)}, u32[]{:S(2)}) %collective-permute-start.11) | collective-permute-done | bytes 69664 | tf_op jit(solution)/shard_map/ppermute | solution.py:429
  36.4 0.0 collective-permute-done.10.refs_1_
  36.4 0.1 half_ray.2
  36.5 0.1 collective-permute-start.13
  36.6 0.6 own_adjoint.1.refs_2_
  37.2 0.5 collective-permute-done.13.refs_4_
  37.8 0.0 collective-permute-done.9.refs_1_.refs_4_
  37.8 0.1 collective-permute-done.8.refs_0_.refs_3_
  37.9 0.6 adjoint.3.refs_0_.unread_ref
  38.5 1.7 %collective-permute-start.16 = (bf16[272,256]{1,0:T(8,128)(2,1)S(1)}, bf16[272,256]{1,0:T(8,128)(2,1)S(1)}, u32[]{:S(2)}, u32[]{:S(2)}) collective-permute-start(bf16[272,256]{1,0:T(8,128)(2,1)S(1)} %adjoint.3.refs_0_.unread_ref), channel_id=1, source_target_pairs={{0,24},{8,16},{16,8},{24,0},{1,25},{9,17},{17,9},{25,1},{2,26},{10... | collective-permute-start | bytes 417800 | tf_op jit(solution)/shard_map/ppermute | solution.py:429
  40.2 1.3 %collective-permute-start.15 = (bf16[272,256]{1,0:T(8,128)(2,1)S(1)}, bf16[272,256]{1,0:T(8,128)(2,1)S(1)}, u32[]{:S(2)}, u32[]{:S(2)}) collective-permute-start(bf16[272,256]{1,0:T(8,128)(2,1)S(1)} %adjoint.3.refs_0_.unread_ref), channel_id=1, source_target_pairs={{0,16},{8,24},{16,0},{24,8},{1,17},{9,25},{17,1},{25,9},{2,18},{10... | collective-permute-start | bytes 417800 | tf_op jit(solution)/shard_map/ppermute | solution.py:429
  41.5 0.6 collective-permute-start.14
  42.1 3.9 %collective-permute-done.16.refs_3_ = bf16[272,256]{1,0:T(8,128)(2,1)S(1)} collective-permute-done((bf16[272,256]{1,0:T(8,128)(2,1)S(1)}, bf16[272,256]{1,0:T(8,128)(2,1)S(1)}, u32[]{:S(2)}, u32[]{:S(2)}) %collective-permute-start.16) | collective-permute-done | bytes 139296 | tf_op jit(solution)/shard_map/ppermute | solution.py:429
  46.0 2.1 %collective-permute-done.15.refs_2_ = bf16[272,256]{1,0:T(8,128)(2,1)S(1)} collective-permute-done((bf16[272,256]{1,0:T(8,128)(2,1)S(1)}, bf16[272,256]{1,0:T(8,128)(2,1)S(1)}, u32[]{:S(2)}, u32[]{:S(2)}) %collective-permute-start.15) | collective-permute-done | bytes 139296 | tf_op jit(solution)/shard_map/ppermute | solution.py:429
  48.1 0.0 collective-permute-done.14.refs_1_
  48.2 2.0 %voxel.3 = (bf16[256,256]{1,0:T(8,128)(2,1)S(1)}, f32[8,128]{1,0:T(8,128)S(1)}, f32[17,8,128]{2,1,0:T(8,128)S(1)}, f32[8,128]{1,0:T(8,128)S(1)}, bf16[1024,256]{1,0:T(8,128)(2,1)S(1)}) custom-call(bf16[32,2,256,256]{3,2,1,0:T(8,128)(2,1)S(1)} %copy-done, bf16[272,256]{1,0:T(8,128)(2,1)S(1)} %adjoint.3.refs_0_.unread_ref, ...), custom_call_target="tpu_custom_call" | custom-call | tf_op jit(solution)/shard_map/voxel/pallas_call | solution.py:447
  50.2 0.1 collective-permute-start.17
  50.2 1.1 %forward.3.own_ref = f32[17,8,128]{2,1,0:T(8,128)S(1)} custom-call(bf16[32,2,256,256]{3,2,1,0:T(8,128)(2,1)S(1)} %copy-done, bf16[256,256]{1,0:T(8,128)(2,1)S(1)} %get-tuple-element.40.lhs_ref, f32[8,128]{1,0:T(8,128)S(1)} %get-tuple-element.41.acc_ref), custom_call_target="tpu_custom_call" | custom-call | tf_op jit(solution)/shard_map/forward/pallas_call | solution.py:447
  51.4 0.1 collective-permute-done.17.other_ref
  51.6 2.3 %collective-permute-start.20 = (bf16[144,128]{1,0:T(8,128)(2,1)S(1)}, bf16[144,128]{1,0:T(8,128)(2,1)S(1)}, u32[]{:S(2)}, u32[]{:S(2)}) collective-permute-start(bf16[144,128]{1,0:T(8,128)(2,1)S(1)} %get-tuple-element.43.refs_0_), channel_id=1, source_target_pairs={{0,6},{1,7},{2,4},{3,5},{4,2},{5,3},{6,0},{7,1},{8,14},{9,15},{10,... | collective-permute-start | bytes 110600 | tf_op jit(solution)/shard_map/ppermute | solution.py:429
  53.8 2.2 %collective-permute-start.18 = (bf16[144,128]{1,0:T(8,128)(2,1)S(1)}, bf16[144,128]{1,0:T(8,128)(2,1)S(1)}, u32[]{:S(2)}, u32[]{:S(2)}) collective-permute-start(bf16[144,128]{1,0:T(8,128)(2,1)S(1)} %get-tuple-element.43.refs_0_), channel_id=1, source_target_pairs={{0,2},{1,3},{2,0},{3,1},{4,6},{5,7},{6,4},{7,5},{8,10},{9,11},{10,... | collective-permute-start | bytes 110600 | tf_op jit(solution)/shard_map/ppermute | solution.py:429
  56.0 1.7 %collective-permute-start.25 = (bf16[256,256]{1,0:T(8,128)(2,1)S(1)}, bf16[256,256]{1,0:T(8,128)(2,1)S(1)}, u32[]{:S(2)}, u32[]{:S(2)}) collective-permute-start(bf16[256,256]{1,0:T(8,128)(2,1)S(1)} %get-tuple-element.50), channel_id=1, source_target_pairs={{0,24},{8,16},{16,8},{24,0},{1,25},{9,17},{17,9},{25,1},{2,26},{10... | collective-permute-start | bytes 393224 | tf_op jit(solution)/shard_map/ppermute | solution.py:429
  57.7 1.2 %collective-permute-done.19.refs_2_ = bf16[144,128]{1,0:T(8,128)(2,1)S(1)} collective-permute-done((bf16[144,128]{1,0:T(8,128)(2,1)S(1)}, bf16[144,128]{1,0:T(8,128)(2,1)S(1)}, u32[]{:S(2)}, u32[]{:S(2)}) %collective-permute-start.19) | collective-permute-done | bytes 36896 | tf_op jit(solution)/shard_map/ppermute | solution.py:429
  58.8 0.0 collective-permute-done.18.refs_1_
  58.8 0.1 half_ray.3
  59.0 0.1 collective-permute-start.21
  59.0 1.2 %collective-permute-done.21.other_ref = f32[8,128]{1,0:T(8,128)S(1)} collective-permute-done((f32[8,128]{1,0:T(8,128)S(1)}, f32[8,128]{1,0:T(8,128)S(1)}, u32[]{:S(2)}, u32[]{:S(2)}) %collective-permute-start.21) | collective-permute-done | bytes 4128 | tf_op jit(solution)/shard_map/ppermute | solution.py:429
  60.2 1.7 %collective-permute-start.24 = (f32[8,128]{1,0:T(8,128)S(1)}, f32[8,128]{1,0:T(8,128)S(1)}, u32[]{:S(2)}, u32[]{:S(2)}) collective-permute-start(f32[8,128]{1,0:T(8,128)S(1)} %sum.1.refs_0_), channel_id=1, source_target_pairs={{0,24},{8,16},{16,8},{24,0},{1,25},{9,17},{17,9},{25,1},{2,26},{10... | collective-permute-start | bytes 12296 | tf_op jit(solution)/shard_map/ppermute | solution.py:429
  61.9 1.3 %collective-permute-start.23 = (f32[8,128]{1,0:T(8,128)S(1)}, f32[8,128]{1,0:T(8,128)S(1)}, u32[]{:S(2)}, u32[]{:S(2)}) collective-permute-start(f32[8,128]{1,0:T(8,128)S(1)} %sum.1.refs_0_), channel_id=1, source_target_pairs={{0,16},{8,24},{16,0},{24,8},{1,17},{9,25},{17,1},{25,9},{2,18},{10... | collective-permute-start | bytes 12296 | tf_op jit(solution)/shard_map/ppermute | solution.py:429
  63.1 0.5 collective-permute-start.22
  63.7 0.3 pick.1.refs_0_
  64.0 0.4 share.3.refs_9_
  64.4 0.0 collective-permute-done.25.refs_5_
  64.4 0.8 %share.2.refs_8_ = f32[512,256]{1,0:T(8,128)S(1)} custom-call(bf16[512,1024]{1,0:T(8,128)(2,1)S(1)} %pick.1.refs_0_, bf16[1024,256]{1,0:T(8,128)(2,1)S(1)} %get-tuple-element.49.refs_1_, bf16[256,256]{1,0:T(8,128)(2,1)S(1)} %get-tuple-element.31.refs_0_.refs_2_, bf16[256,256]{1,0:T(8,128)(2,1)S(1)} %collective-permute-done.8.refs_0_.refs_3_, ...), custom_call_target="tpu_custom_call" | custom-call | tf_op jit(solution)/shard_map/share/pallas_call | solution.py:447
  65.2 0.2 collective-permute-done.23.refs_2_
  65.5 1.3 %collective-permute-done.22.refs_1_ = f32[8,128]{1,0:T(8,128)S(1)} collective-permute-done((f32[8,128]{1,0:T(8,128)S(1)}, f32[8,128]{1,0:T(8,128)S(1)}, u32[]{:S(2)}, u32[]{:S(2)}) %collective-permute-start.22) | collective-permute-done | bytes 4128 | tf_op jit(solution)/shard_map/ppermute | solution.py:429
  66.8 1.3 %final.1 = (f32[4,32768]{1,0:T(4,128)}, f32[4]{0:T(128)}) custom-call(f32[8,128]{1,0:T(8,128)S(1)} %sum.1.refs_0_, f32[8,128]{1,0:T(8,128)S(1)} %collective-permute-done.22.refs_1_, f32[8,128]{1,0:T(8,128)S(1)} %collective-permute-done.23.refs_2_, f32[8,128]{1,0:T(8,128)S(1)} %collective-permute-done.24.refs_3_, ...), custom_call_target="tpu_custom_call" | custom-call | tf_op jit(solution)/shard_map/final/pallas_call | solution.py:547
  (13 shorter events, 0.1 us)
Async XLA Ops:
  0.6 12.1 %copy-start = (bf16[32,2,256,256]{3,2,1,0:T(8,128)(2,1)S(1)}, bf16[32,2,256,256]{3,2,1,0:T(8,128)(2,1)}, u32[]{:S(2)}) copy-start(bf16[32,2,256,256]{3,2,1,0:T(8,128)(2,1)} %tiles_ref.13) | copy-start | bytes 25165828
  0.6 0.9 %copy-start.1 = (f32[4,1024]{1,0:T(4,128)S(1)}, f32[4,1024]{1,0:T(4,128)}, u32[]{:S(2)}) copy-start(f32[4,1024]{1,0:T(4,128)} %obs_ref.1) | copy-start | bytes 49156
  1.5 7.0 %copy-start.2 = (s32[32,2]{0,1:T(2,128)S(1)}, s32[32,2]{0,1:T(2,128)}, u32[]{:S(2)}) copy-start(s32[32,2]{0,1:T(2,128)} %param.5) | copy-start | bytes 772
  1.5 1.4 %collective-permute-start = (f32[5,8,128]{2,1,0:T(8,128)S(1)}, f32[5,8,128]{2,1,0:T(8,128)S(1)}, u32[]{:S(2)}, u32[]{:S(2)}) collective-permute-start(f32[5,8,128]{2,1,0:T(8,128)S(1)} %pack.1.unread_ref.own_ref), channel_id=1, source_target_pairs={{0,1},{1,0},{2,3},{3,2},{4,5},{5,4},{6,7},{7,6},{8,9},{9,8},{10,11... | collective-permute-start | bytes 61448 | tf_op jit(solution)/shard_map/ppermute | solution.py:429
  2.9 6.9 %collective-permute-start.3 = (f32[9,8,128]{2,1,0:T(8,128)S(1)}, f32[9,8,128]{2,1,0:T(8,128)S(1)}, u32[]{:S(2)}, u32[]{:S(2)}) collective-permute-start(f32[9,8,128]{2,1,0:T(8,128)S(1)} %join.1.refs_0_.refs_4_), channel_id=1, source_target_pairs={{0,6},{1,7},{2,4},{3,5},{4,2},{5,3},{6,0},{7,1},{8,14},{9,15},{10,... | collective-permute-start | bytes 110600 | tf_op jit(solution)/shard_map/ppermute | solution.py:429
  7.8 4.9 %collective-permute-start.2 = (f32[9,8,128]{2,1,0:T(8,128)S(1)}, f32[9,8,128]{2,1,0:T(8,128)S(1)}, u32[]{:S(2)}, u32[]{:S(2)}) collective-permute-start(f32[9,8,128]{2,1,0:T(8,128)S(1)} %join.1.refs_0_.refs_4_), channel_id=1, source_target_pairs={{0,4},{1,5},{2,6},{3,7},{4,0},{5,1},{6,2},{7,3},{8,12},{9,13},{10,... | collective-permute-start | bytes 110600 | tf_op jit(solution)/shard_map/ppermute | solution.py:429
  7.8 4.9 %collective-permute-start.1 = (f32[9,8,128]{2,1,0:T(8,128)S(1)}, f32[9,8,128]{2,1,0:T(8,128)S(1)}, u32[]{:S(2)}, u32[]{:S(2)}) collective-permute-start(f32[9,8,128]{2,1,0:T(8,128)S(1)} %join.1.refs_0_.refs_4_), channel_id=1, source_target_pairs={{0,2},{1,3},{2,0},{3,1},{4,6},{5,7},{6,4},{7,5},{8,10},{9,11},{10,... | collective-permute-start | bytes 110600 | tf_op jit(solution)/shard_map/ppermute | solution.py:429
  13.9 6.9 %collective-permute-start.6 = (bf16[272,256]{1,0:T(8,128)(2,1)S(1)}, bf16[272,256]{1,0:T(8,128)(2,1)S(1)}, u32[]{:S(2)}, u32[]{:S(2)}) collective-permute-start(bf16[272,256]{1,0:T(8,128)(2,1)S(1)} %get-tuple-element.27.refs_0_), channel_id=1, source_target_pairs={{0,24},{8,16},{16,8},{24,0},{1,25},{9,17},{17,9},{25,1},{2,26},{10... | collective-permute-start | bytes 417800 | tf_op jit(solution)/shard_map/ppermute | solution.py:429
  16.4 6.2 %collective-permute-start.5 = (bf16[272,256]{1,0:T(8,128)(2,1)S(1)}, bf16[272,256]{1,0:T(8,128)(2,1)S(1)}, u32[]{:S(2)}, u32[]{:S(2)}) collective-permute-start(bf16[272,256]{1,0:T(8,128)(2,1)S(1)} %get-tuple-element.27.refs_0_), channel_id=1, source_target_pairs={{0,16},{8,24},{16,0},{24,8},{1,17},{9,25},{17,1},{25,9},{2,18},{10... | collective-permute-start | bytes 417800 | tf_op jit(solution)/shard_map/ppermute | solution.py:429
  16.9 5.7 %collective-permute-start.4 = (bf16[272,256]{1,0:T(8,128)(2,1)S(1)}, bf16[272,256]{1,0:T(8,128)(2,1)S(1)}, u32[]{:S(2)}, u32[]{:S(2)}) collective-permute-start(bf16[272,256]{1,0:T(8,128)(2,1)S(1)} %get-tuple-element.27.refs_0_), channel_id=1, source_target_pairs={{0,8},{8,0},{16,24},{24,16},{1,9},{9,1},{17,25},{25,17},{2,10},{10... | collective-permute-start | bytes 417800 | tf_op jit(solution)/shard_map/ppermute | solution.py:429
  25.6 1.3 %collective-permute-start.7 = (f32[17,8,128]{2,1,0:T(8,128)S(1)}, f32[17,8,128]{2,1,0:T(8,128)S(1)}, u32[]{:S(2)}, u32[]{:S(2)}) collective-permute-start(f32[17,8,128]{2,1,0:T(8,128)S(1)} %get-tuple-element.30), channel_id=1, source_target_pairs={{0,1},{1,0},{2,3},{3,2},{4,5},{5,4},{6,7},{7,6},{8,9},{9,8},{10,11... | collective-permute-start | bytes 208904 | tf_op jit(solution)/shard_map/ppermute | solution.py:429
  27.0 6.9 %collective-permute-start.12 = (f32[17,8,128]{2,1,0:T(8,128)S(1)}, f32[17,8,128]{2,1,0:T(8,128)S(1)}, u32[]{:S(2)}, u32[]{:S(2)}) collective-permute-start(f32[17,8,128]{2,1,0:T(8,128)S(1)} %get-tuple-element.33.refs_0_), channel_id=1, source_target_pairs={{0,6},{1,7},{2,4},{3,5},{4,2},{5,3},{6,0},{7,1},{8,14},{9,15},{10,... | collective-permute-start | bytes 208904 | tf_op jit(solution)/shard_map/ppermute | solution.py:429
  28.6 7.8 %collective-permute-start.11 = (f32[17,8,128]{2,1,0:T(8,128)S(1)}, f32[17,8,128]{2,1,0:T(8,128)S(1)}, u32[]{:S(2)}, u32[]{:S(2)}) collective-permute-start(f32[17,8,128]{2,1,0:T(8,128)S(1)} %get-tuple-element.33.refs_0_), channel_id=1, source_target_pairs={{0,4},{1,5},{2,6},{3,7},{4,0},{5,1},{6,2},{7,3},{8,12},{9,13},{10,... | collective-permute-start | bytes 208904 | tf_op jit(solution)/shard_map/ppermute | solution.py:429
  29.0 7.4 %collective-permute-start.10 = (f32[17,8,128]{2,1,0:T(8,128)S(1)}, f32[17,8,128]{2,1,0:T(8,128)S(1)}, u32[]{:S(2)}, u32[]{:S(2)}) collective-permute-start(f32[17,8,128]{2,1,0:T(8,128)S(1)} %get-tuple-element.33.refs_0_), channel_id=1, source_target_pairs={{0,2},{1,3},{2,0},{3,1},{4,6},{5,7},{6,4},{7,5},{8,10},{9,11},{10,... | collective-permute-start | bytes 208904 | tf_op jit(solution)/shard_map/ppermute | solution.py:429
  31.4 6.3 %collective-permute-start.9 = (bf16[256,256]{1,0:T(8,128)(2,1)S(1)}, bf16[256,256]{1,0:T(8,128)(2,1)S(1)}, u32[]{:S(2)}, u32[]{:S(2)}) collective-permute-start(bf16[256,256]{1,0:T(8,128)(2,1)S(1)} %get-tuple-element.32), channel_id=1, source_target_pairs={{0,16},{8,24},{16,0},{24,8},{1,17},{9,25},{17,1},{25,9},{2,18},{10... | collective-permute-start | bytes 393224 | tf_op jit(solution)/shard_map/ppermute | solution.py:429
  32.9 5.0 %collective-permute-start.8 = (bf16[256,256]{1,0:T(8,128)(2,1)S(1)}, bf16[256,256]{1,0:T(8,128)(2,1)S(1)}, u32[]{:S(2)}, u32[]{:S(2)}) collective-permute-start(bf16[256,256]{1,0:T(8,128)(2,1)S(1)} %get-tuple-element.32), channel_id=1, source_target_pairs={{0,8},{8,0},{16,24},{24,16},{1,9},{9,1},{17,25},{25,17},{2,10},{10... | collective-permute-start | bytes 393224 | tf_op jit(solution)/shard_map/ppermute | solution.py:429
  36.5 1.3 %collective-permute-start.13 = (bf16[80,256]{1,0:T(8,128)(2,1)S(1)}, bf16[80,256]{1,0:T(8,128)(2,1)S(1)}, u32[]{:S(2)}, u32[]{:S(2)}) collective-permute-start(bf16[80,256]{1,0:T(8,128)(2,1)S(1)} %get-tuple-element.35.half_ref.refs_3_), channel_id=1, source_target_pairs={{0,1},{1,0},{2,3},{3,2},{4,5},{5,4},{6,7},{7,6},{8,9},{9,8},{10,11... | collective-permute-start | bytes 122888 | tf_op jit(solution)/shard_map/ppermute | solution.py:429
  38.5 7.5 %collective-permute-start.16 = (bf16[272,256]{1,0:T(8,128)(2,1)S(1)}, bf16[272,256]{1,0:T(8,128)(2,1)S(1)}, u32[]{:S(2)}, u32[]{:S(2)}) collective-permute-start(bf16[272,256]{1,0:T(8,128)(2,1)S(1)} %adjoint.3.refs_0_.unread_ref), channel_id=1, source_target_pairs={{0,24},{8,16},{16,8},{24,0},{1,25},{9,17},{17,9},{25,1},{2,26},{10... | collective-permute-start | bytes 417800 | tf_op jit(solution)/shard_map/ppermute | solution.py:429
  40.2 7.9 %collective-permute-start.15 = (bf16[272,256]{1,0:T(8,128)(2,1)S(1)}, bf16[272,256]{1,0:T(8,128)(2,1)S(1)}, u32[]{:S(2)}, u32[]{:S(2)}) collective-permute-start(bf16[272,256]{1,0:T(8,128)(2,1)S(1)} %adjoint.3.refs_0_.unread_ref), channel_id=1, source_target_pairs={{0,16},{8,24},{16,0},{24,8},{1,17},{9,25},{17,1},{25,9},{2,18},{10... | collective-permute-start | bytes 417800 | tf_op jit(solution)/shard_map/ppermute | solution.py:429
  41.5 6.7 %collective-permute-start.14 = (bf16[272,256]{1,0:T(8,128)(2,1)S(1)}, bf16[272,256]{1,0:T(8,128)(2,1)S(1)}, u32[]{:S(2)}, u32[]{:S(2)}) collective-permute-start(bf16[272,256]{1,0:T(8,128)(2,1)S(1)} %adjoint.3.refs_0_.unread_ref), channel_id=1, source_target_pairs={{0,8},{8,0},{16,24},{24,16},{1,9},{9,1},{17,25},{25,17},{2,10},{10... | collective-permute-start | bytes 417800 | tf_op jit(solution)/shard_map/ppermute | solution.py:429
  50.2 1.3 %collective-permute-start.17 = (f32[17,8,128]{2,1,0:T(8,128)S(1)}, f32[17,8,128]{2,1,0:T(8,128)S(1)}, u32[]{:S(2)}, u32[]{:S(2)}) collective-permute-start(f32[17,8,128]{2,1,0:T(8,128)S(1)} %get-tuple-element.42), channel_id=1, source_target_pairs={{0,1},{1,0},{2,3},{3,2},{4,5},{5,4},{6,7},{7,6},{8,9},{9,8},{10,11... | collective-permute-start | bytes 208904 | tf_op jit(solution)/shard_map/ppermute | solution.py:429
  51.6 6.1 %collective-permute-start.20 = (bf16[144,128]{1,0:T(8,128)(2,1)S(1)}, bf16[144,128]{1,0:T(8,128)(2,1)S(1)}, u32[]{:S(2)}, u32[]{:S(2)}) collective-permute-start(bf16[144,128]{1,0:T(8,128)(2,1)S(1)} %get-tuple-element.43.refs_0_), channel_id=1, source_target_pairs={{0,6},{1,7},{2,4},{3,5},{4,2},{5,3},{6,0},{7,1},{8,14},{9,15},{10,... | collective-permute-start | bytes 110600 | tf_op jit(solution)/shard_map/ppermute | solution.py:429
  53.8 5.0 %collective-permute-start.19 = (bf16[144,128]{1,0:T(8,128)(2,1)S(1)}, bf16[144,128]{1,0:T(8,128)(2,1)S(1)}, u32[]{:S(2)}, u32[]{:S(2)}) collective-permute-start(bf16[144,128]{1,0:T(8,128)(2,1)S(1)} %get-tuple-element.43.refs_0_), channel_id=1, source_target_pairs={{0,4},{1,5},{2,6},{3,7},{4,0},{5,1},{6,2},{7,3},{8,12},{9,13},{10,... | collective-permute-start | bytes 110600 | tf_op jit(solution)/shard_map/ppermute | solution.py:429
  53.8 5.0 %collective-permute-start.18 = (bf16[144,128]{1,0:T(8,128)(2,1)S(1)}, bf16[144,128]{1,0:T(8,128)(2,1)S(1)}, u32[]{:S(2)}, u32[]{:S(2)}) collective-permute-start(bf16[144,128]{1,0:T(8,128)(2,1)S(1)} %get-tuple-element.43.refs_0_), channel_id=1, source_target_pairs={{0,2},{1,3},{2,0},{3,1},{4,6},{5,7},{6,4},{7,5},{8,10},{9,11},{10,... | collective-permute-start | bytes 110600 | tf_op jit(solution)/shard_map/ppermute | solution.py:429
  56.0 8.4 %collective-permute-start.25 = (bf16[256,256]{1,0:T(8,128)(2,1)S(1)}, bf16[256,256]{1,0:T(8,128)(2,1)S(1)}, u32[]{:S(2)}, u32[]{:S(2)}) collective-permute-start(bf16[256,256]{1,0:T(8,128)(2,1)S(1)} %get-tuple-element.50), channel_id=1, source_target_pairs={{0,24},{8,16},{16,8},{24,0},{1,25},{9,17},{17,9},{25,1},{2,26},{10... | collective-permute-start | bytes 393224 | tf_op jit(solution)/shard_map/ppermute | solution.py:429
  59.0 1.2 %collective-permute-start.21 = (f32[8,128]{1,0:T(8,128)S(1)}, f32[8,128]{1,0:T(8,128)S(1)}, u32[]{:S(2)}, u32[]{:S(2)}) collective-permute-start(f32[8,128]{1,0:T(8,128)S(1)} %get-tuple-element.46.own_ref), channel_id=1, source_target_pairs={{0,1},{1,0},{2,3},{3,2},{4,5},{5,4},{6,7},{7,6},{8,9},{9,8},{10,11... | collective-permute-start | bytes 12296 | tf_op jit(solution)/shard_map/ppermute | solution.py:429
  60.2 5.0 %collective-permute-start.24 = (f32[8,128]{1,0:T(8,128)S(1)}, f32[8,128]{1,0:T(8,128)S(1)}, u32[]{:S(2)}, u32[]{:S(2)}) collective-permute-start(f32[8,128]{1,0:T(8,128)S(1)} %sum.1.refs_0_), channel_id=1, source_target_pairs={{0,24},{8,16},{16,8},{24,0},{1,25},{9,17},{17,9},{25,1},{2,26},{10... | collective-permute-start | bytes 12296 | tf_op jit(solution)/shard_map/ppermute | solution.py:429
  61.9 3.6 %collective-permute-start.23 = (f32[8,128]{1,0:T(8,128)S(1)}, f32[8,128]{1,0:T(8,128)S(1)}, u32[]{:S(2)}, u32[]{:S(2)}) collective-permute-start(f32[8,128]{1,0:T(8,128)S(1)} %sum.1.refs_0_), channel_id=1, source_target_pairs={{0,16},{8,24},{16,0},{24,8},{1,17},{9,25},{17,1},{25,9},{2,18},{10... | collective-permute-start | bytes 12296 | tf_op jit(solution)/shard_map/ppermute | solution.py:429
  63.1 3.6 %collective-permute-start.22 = (f32[8,128]{1,0:T(8,128)S(1)}, f32[8,128]{1,0:T(8,128)S(1)}, u32[]{:S(2)}, u32[]{:S(2)}) collective-permute-start(f32[8,128]{1,0:T(8,128)S(1)} %sum.1.refs_0_), channel_id=1, source_target_pairs={{0,8},{8,0},{16,24},{24,16},{1,9},{9,1},{17,25},{25,17},{2,10},{10... | collective-permute-start | bytes 12296 | tf_op jit(solution)/shard_map/ppermute | solution.py:429

commit v14 on v13

--- a/solution.py
+++ b/solution.py
@@ -64,7 +64,7 @@
     return blocks
 
 
-def pack_kernel(obs_ref, unread_ref, blocks_ref):
+def pack_kernel(obs_ref, blocks_ref):
     count = blocks_ref.shape[0] - 1
     blocks = ray_blocks(obs_ref, count)
     for b, block in enumerate(blocks):
@@ -72,7 +72,7 @@
     blocks_ref[count] = tree_sum([b * b for b in blocks])
 
 
-def join_kernel(own_ref, other_ref, both_ref):
+def join_kernel(own_ref, other_ref, unread_ref, both_ref):
     count = own_ref.shape[0] - 1
     both_ref[:count] = own_ref[:count]
     both_ref[count : 2 * count] = other_ref[:count]
@@ -165,6 +165,27 @@
             at += 16
 
 
+def pair_sources(pair, e, per_share):
+    me = lax.axis_index("col")
+    sources = []
+    for h in range(2):
+        blocks = [pair[h * per_share + b] for b in range(per_share)]
+        sources.append((jnp.bitwise_xor(me, 2 * e + h), packed(blocks, max(16, 4 * per_share))))
+    return sources
+
+
+def pair_adjoint_kernel(tiles_ref, pair_ref, upper_ref, lower_ref):
+    per_share = tiles_ref.shape[0] // lax.axis_size("col")
+    at = 0
+    for owner, rays in pair_sources(pair_ref, 0, per_share):
+        for g in range(per_share // 2):
+            value, _ = adjoint_rows(rays, tiles_ref, owner, per_share, g)
+            upper = value.astype(jnp.bfloat16)
+            upper_ref[at : at + 16] = upper
+            lower_ref[at : at + 16] = (value - upper.astype(jnp.float32)).astype(jnp.bfloat16)
+            at += 16
+
+
 def adjoint_kernel(first, unread, keys_ref, tiles_ref, *refs):
     refs = refs[unread:]
     row_tiles, per_block = tiles_ref.shape[:2]
@@ -173,14 +194,18 @@
     per_share = row_tiles // shares
     terms = row_tiles * per_block * RHS
     if first:
-        pairs, (term_ref, lower_ref) = refs[: shares // 2], refs[shares // 2 :]
-        squares, sources = [], []
-        for e, pair in enumerate(pairs):
-            squares.append(pair[2 * per_share])
-            for h in range(2):
-                blocks = [pair[h * per_share + b] for b in range(per_share)]
-                owner = jnp.bitwise_xor(me, 2 * e + h)
-                sources.append((owner, packed(blocks, max(16, 4 * per_share))))
+        done_ref, done_lower_ref = refs[:2]
+        pairs, (term_ref, lower_ref) = refs[2:-2], refs[-2:]
+        squares = [pair[2 * per_share] for pair in pairs]
+        sources = [x for e in range(1, shares // 2) for x in pair_sources(pairs[e], e, per_share)]
+        at = 0
+        for h in range(2):
+            for g in range(per_share // 2):
+                i = jnp.bitwise_xor(me, h) * per_share + 2 * g
+                to = pl.ds(pl.multiple_of(8 * i, 16), 16)
+                term_ref[to, :] = done_ref[at : at + 16]
+                lower_ref[to, :] = done_lower_ref[at : at + 16]
+                at += 16
     else:
         done_ref, own_ref, other_ref, term_ref = refs
         squares = [read_squares(half[-16:, :LANES]) for half in (own_ref, other_ref)]
@@ -506,11 +531,18 @@
         return call(kernel, "share", f32(share_rows, tile_size), args, None, scratch)
 
     far = pltpu.with_memory_space_constraint(tile_values, pltpu.HBM)
-    blocks = call(pack_kernel, "pack", f32(per_share + 1, 8, LANES), [observed, far], [VMEM, HBM])
+    blocks = call(pack_kernel, "pack", f32(per_share + 1, 8, LANES), [observed])
     keys = call(keys_kernel, "keys", f32(8, per_row), [blocks, tile_cols.T], [ANY, SMEM])
-    both = call(join_kernel, "join", f32(2 * per_share + 1, 8, LANES), [blocks, from_peer(blocks, "col", 1)])
+    both = call(
+        join_kernel,
+        "join",
+        f32(2 * per_share + 1, 8, LANES),
+        [blocks, from_peer(blocks, "col", 1), far],
+        [VMEM, VMEM, HBM],
+    )
     lefts = exchange(both, "col", 2)
-    terms, remainder = adjoint(lefts, True, [])
+    done = call(pair_adjoint_kernel, "pair_adjoint", [bf16(2 * per_share * 8, tile_size)] * 2, [tile_values, both])
+    terms, remainder = adjoint([*done, *lefts], True, [])
     terms = exchange(terms, "row")
     own, other, beta, upper_terms, right_raw, equal, weight, all_keys = voxel(terms, [], True)
     betas, alphas, combined = [], [], []

time: 68.3 us -> 68.1 us (level)
    pallas_call x18 -> x19, Pallas kernels: 12.1 us -> 12.2 us  [call(): pl.pallas_call(kernel, out_shape=out_shape, in_specs=in_specs or [VMEM] *...]
where the time goes in v14:
time: 68.1 us; the launch traced here: 67.8 us
  starting transfers between devices  29.8 us (44%)
  waiting for transfers between devices  22.8 us (33%)
  Pallas kernels  13.6 us (20%)
  local copies, waits for them, and re-layouts  0.87 us (1%)
  between operations  0.8 us (1%)
    ppermute x26, starting transfers between devices, from_peer(): lax.ppermute(value, axis, [(i, i ^ d) for i in range(lax.axis_size(axis))])  29.8 us
    ppermute x26, waiting for transfers between devices, from_peer(): lax.ppermute(value, axis, [(i, i ^ d) for i in range(lax.axis_size(axis))])  22.8 us
    pallas_call x19, Pallas kernels, call(): pl.pallas_call(kernel, out_shape=out_shape, in_specs=in_specs or [VMEM] *...  12.2 us
  transfers between devices with their start and end apart: 26, of which 18 were waited for; matrix products, arithmetic and copies ran while one was open for 0% of the time, Pallas kernels for 8%

profile of v14, /device:TPU:0, one launch (start us, length us, event | category | flops | bytes accessed | tf_op | source)
XLA Modules:
  0.0 67.8 jit_solution(18334502084764150946)
XLA Ops:
  0.6 0.0 copy-start
  0.7 0.9 %copy-done.1 = f32[4,1024]{1,0:T(4,128)S(1)} copy-done((f32[4,1024]{1,0:T(4,128)S(1)}, f32[4,1024]{1,0:T(4,128)}, u32[]{:S(2)}) %copy-start.1) | copy-done | bytes 16408
  1.5 0.5 collective-permute-start
  2.0 0.8 %collective-permute-done.other_ref = f32[5,8,128]{2,1,0:T(8,128)S(1)} collective-permute-done((f32[5,8,128]{2,1,0:T(8,128)S(1)}, f32[5,8,128]{2,1,0:T(8,128)S(1)}, u32[]{:S(2)}, u32[]{:S(2)}) %collective-permute-start) | collective-permute-done | bytes 20512 | tf_op jit(solution)/shard_map/ppermute | solution.py:454
  2.9 4.9 %collective-permute-start.3 = (f32[9,8,128]{2,1,0:T(8,128)S(1)}, f32[9,8,128]{2,1,0:T(8,128)S(1)}, u32[]{:S(2)}, u32[]{:S(2)}) collective-permute-start(f32[9,8,128]{2,1,0:T(8,128)S(1)} %join.1.pair_ref.refs_2_.refs_4_), channel_id=1, source_target_pairs={{0,6},{1,7},{2,4},{3,5},{4,2},{5,3},{6,0},{7,1},{8,14},{9,15},{10,... | collective-permute-start | bytes 110600 | tf_op jit(solution)/shard_map/ppermute | solution.py:454
  7.8 0.6 collective-permute-start.1
  8.5 0.6 keys.1.keys_ref
  9.1 0.4 pair_adjoint.1
  9.5 0.4 collective-permute-done.3.refs_5_.refs_7_
  9.8 2.9 %collective-permute-done.2.refs_4_.refs_6_ = f32[9,8,128]{2,1,0:T(8,128)S(1)} collective-permute-done((f32[9,8,128]{2,1,0:T(8,128)S(1)}, f32[9,8,128]{2,1,0:T(8,128)S(1)}, u32[]{:S(2)}, u32[]{:S(2)}) %collective-permute-start.2) | collective-permute-done | bytes 36896 | tf_op jit(solution)/shard_map/ppermute | solution.py:454
  12.7 0.0 collective-permute-done.1.refs_3_.refs_5_
  12.7 0.9 %adjoint.2 = (bf16[272,256]{1,0:T(8,128)(2,1)S(1)}, bf16[256,256]{1,0:T(8,128)(2,1)S(1)}) custom-call(f32[8,256]{1,0:T(8,128)S(1)} %keys.1.keys_ref, bf16[32,2,256,256]{3,2,1,0:T(8,128)(2,1)S(1)} %copy-done, bf16[64,256]{1,0:T(8,128)(2,1)S(1)} %get-tuple-element.29.refs_0_, bf16[64,256]{1,0:T(8,128)(2,1)S(1)} %get-tuple-element.30.refs_1_, ...), custom_call_target="tpu_custom_call" | custom-call | tf_op jit(solution)/shard_map/adjoint/pallas_call | solution.py:472
  13.6 2.5 %collective-permute-start.6 = (bf16[272,256]{1,0:T(8,128)(2,1)S(1)}, bf16[272,256]{1,0:T(8,128)(2,1)S(1)}, u32[]{:S(2)}, u32[]{:S(2)}) collective-permute-start(bf16[272,256]{1,0:T(8,128)(2,1)S(1)} %get-tuple-element.31.refs_0_), channel_id=1, source_target_pairs={{0,24},{8,16},{16,8},{24,0},{1,25},{9,17},{17,9},{25,1},{2,26},{10... | collective-permute-start | bytes 417800 | tf_op jit(solution)/shard_map/ppermute | solution.py:454
  16.1 0.5 collective-permute-start.5
  16.6 0.5 collective-permute-start.4
  17.2 3.4 %collective-permute-done.6.refs_3_ = bf16[272,256]{1,0:T(8,128)(2,1)S(1)} collective-permute-done((bf16[272,256]{1,0:T(8,128)(2,1)S(1)}, bf16[272,256]{1,0:T(8,128)(2,1)S(1)}, u32[]{:S(2)}, u32[]{:S(2)}) %collective-permute-start.6) | collective-permute-done | bytes 139296 | tf_op jit(solution)/shard_map/ppermute | solution.py:454
  20.6 1.7 %collective-permute-done.5.refs_2_ = bf16[272,256]{1,0:T(8,128)(2,1)S(1)} collective-permute-done((bf16[272,256]{1,0:T(8,128)(2,1)S(1)}, bf16[272,256]{1,0:T(8,128)(2,1)S(1)}, u32[]{:S(2)}, u32[]{:S(2)}) %collective-permute-start.5) | collective-permute-done | bytes 139296 | tf_op jit(solution)/shard_map/ppermute | solution.py:454
  22.3 0.1 collective-permute-done.4.refs_1_
  22.3 3.0 %voxel.2 = (bf16[256,256]{1,0:T(8,128)(2,1)S(1)}, f32[8,128]{1,0:T(8,128)S(1)}, f32[17,8,128]{2,1,0:T(8,128)S(1)}, f32[8,128]{1,0:T(8,128)S(1)}, bf16[1024,256]{...) custom-call(bf16[32,2,256,256]{3,2,1,0:T(8,128)(2,1)S(1)} %copy-done, ...), custom_call_target="tpu_custom_call" | custom-call | tf_op jit(solution)/shard_map/voxel/pallas_call | solution.py:472
  25.3 0.1 collective-permute-start.7
  25.4 1.1 %forward.2.own_ref = f32[17,8,128]{2,1,0:T(8,128)S(1)} custom-call(bf16[32,2,256,256]{3,2,1,0:T(8,128)(2,1)S(1)} %copy-done, bf16[256,256]{1,0:T(8,128)(2,1)S(1)} %get-tuple-element.32.lhs_ref, f32[8,128]{1,0:T(8,128)S(1)} %get-tuple-element.33.acc_ref), custom_call_target="tpu_custom_call" | custom-call | tf_op jit(solution)/shard_map/forward/pallas_call | solution.py:472
  26.5 0.1 collective-permute-done.7.other_ref
  26.7 1.6 %collective-permute-start.12 = (f32[17,8,128]{2,1,0:T(8,128)S(1)}, f32[17,8,128]{2,1,0:T(8,128)S(1)}, u32[]{:S(2)}, u32[]{:S(2)}) collective-permute-start(f32[17,8,128]{2,1,0:T(8,128)S(1)} %get-tuple-element.37.refs_0_), channel_id=1, source_target_pairs={{0,6},{1,7},{2,4},{3,5},{4,2},{5,3},{6,0},{7,1},{8,14},{9,15},{10,... | collective-permute-start | bytes 208904 | tf_op jit(solution)/shard_map/ppermute | solution.py:454
  28.3 0.4 collective-permute-start.11
  28.7 2.5 %collective-permute-start.10 = (f32[17,8,128]{2,1,0:T(8,128)S(1)}, f32[17,8,128]{2,1,0:T(8,128)S(1)}, u32[]{:S(2)}, u32[]{:S(2)}) collective-permute-start(f32[17,8,128]{2,1,0:T(8,128)S(1)} %get-tuple-element.37.refs_0_), channel_id=1, source_target_pairs={{0,2},{1,3},{2,0},{3,1},{4,6},{5,7},{6,4},{7,5},{8,10},{9,11},{10,... | collective-permute-start | bytes 208904 | tf_op jit(solution)/shard_map/ppermute | solution.py:454
  31.2 1.5 %collective-permute-start.9 = (bf16[256,256]{1,0:T(8,128)(2,1)S(1)}, bf16[256,256]{1,0:T(8,128)(2,1)S(1)}, u32[]{:S(2)}, u32[]{:S(2)}) collective-permute-start(bf16[256,256]{1,0:T(8,128)(2,1)S(1)} %get-tuple-element.36), channel_id=1, source_target_pairs={{0,16},{8,24},{16,0},{24,8},{1,17},{9,25},{17,1},{25,9},{2,18},{10... | collective-permute-start | bytes 393224 | tf_op jit(solution)/shard_map/ppermute | solution.py:454
  32.6 0.8 %collective-permute-start.8 = (bf16[256,256]{1,0:T(8,128)(2,1)S(1)}, bf16[256,256]{1,0:T(8,128)(2,1)S(1)}, u32[]{:S(2)}, u32[]{:S(2)}) collective-permute-start(bf16[256,256]{1,0:T(8,128)(2,1)S(1)} %get-tuple-element.36), channel_id=1, source_target_pairs={{0,8},{8,0},{16,24},{24,16},{1,9},{9,1},{17,25},{25,17},{2,10},{10... | collective-permute-start | bytes 393224 | tf_op jit(solution)/shard_map/ppermute | solution.py:454
  33.4 0.2 collective-permute-done.12.refs_3_
  33.6 2.5 %collective-permute-done.11.refs_2_ = f32[17,8,128]{2,1,0:T(8,128)S(1)} collective-permute-done((f32[17,8,128]{2,1,0:T(8,128)S(1)}, f32[17,8,128]{2,1,0:T(8,128)S(1)}, u32[]{:S(2)}, u32[]{:S(2)}) %collective-permute-start.11) | collective-permute-done | bytes 69664 | tf_op jit(solution)/shard_map/ppermute | solution.py:454
  36.1 0.0 collective-permute-done.10.refs_1_
  36.1 0.1 half_ray.2
  36.2 0.1 collective-permute-start.13
  36.3 0.6 own_adjoint.1.refs_2_
  37.0 0.5 collective-permute-done.13.refs_4_
  37.5 0.1 collective-permute-done.8.refs_0_.refs_3_
  37.6 0.6 adjoint.3.refs_0_.unread_ref
  38.2 1.7 %collective-permute-start.16 = (bf16[272,256]{1,0:T(8,128)(2,1)S(1)}, bf16[272,256]{1,0:T(8,128)(2,1)S(1)}, u32[]{:S(2)}, u32[]{:S(2)}) collective-permute-start(bf16[272,256]{1,0:T(8,128)(2,1)S(1)} %adjoint.3.refs_0_.unread_ref), channel_id=1, source_target_pairs={{0,24},{8,16},{16,8},{24,0},{1,25},{9,17},{17,9},{25,1},{2,26},{10... | collective-permute-start | bytes 417800 | tf_op jit(solution)/shard_map/ppermute | solution.py:454
  39.9 1.3 %collective-permute-start.15 = (bf16[272,256]{1,0:T(8,128)(2,1)S(1)}, bf16[272,256]{1,0:T(8,128)(2,1)S(1)}, u32[]{:S(2)}, u32[]{:S(2)}) collective-permute-start(bf16[272,256]{1,0:T(8,128)(2,1)S(1)} %adjoint.3.refs_0_.unread_ref), channel_id=1, source_target_pairs={{0,16},{8,24},{16,0},{24,8},{1,17},{9,25},{17,1},{25,9},{2,18},{10... | collective-permute-start | bytes 417800 | tf_op jit(solution)/shard_map/ppermute | solution.py:454
  41.2 0.6 collective-permute-start.14
  41.8 3.9 %collective-permute-done.16.refs_3_ = bf16[272,256]{1,0:T(8,128)(2,1)S(1)} collective-permute-done((bf16[272,256]{1,0:T(8,128)(2,1)S(1)}, bf16[272,256]{1,0:T(8,128)(2,1)S(1)}, u32[]{:S(2)}, u32[]{:S(2)}) %collective-permute-start.16) | collective-permute-done | bytes 139296 | tf_op jit(solution)/shard_map/ppermute | solution.py:454
  45.7 2.1 %collective-permute-done.15.refs_2_ = bf16[272,256]{1,0:T(8,128)(2,1)S(1)} collective-permute-done((bf16[272,256]{1,0:T(8,128)(2,1)S(1)}, bf16[272,256]{1,0:T(8,128)(2,1)S(1)}, u32[]{:S(2)}, u32[]{:S(2)}) %collective-permute-start.15) | collective-permute-done | bytes 139296 | tf_op jit(solution)/shard_map/ppermute | solution.py:454
  47.8 0.0 collective-permute-done.14.refs_1_
  47.9 2.0 %voxel.3 = (bf16[256,256]{1,0:T(8,128)(2,1)S(1)}, f32[8,128]{1,0:T(8,128)S(1)}, f32[17,8,128]{2,1,0:T(8,128)S(1)}, f32[8,128]{1,0:T(8,128)S(1)}, bf16[1024,256]{1,0:T(8,128)(2,1)S(1)}) custom-call(bf16[32,2,256,256]{3,2,1,0:T(8,128)(2,1)S(1)} %copy-done, bf16[272,256]{1,0:T(8,128)(2,1)S(1)} %adjoint.3.refs_0_.unread_ref, ...), custom_call_target="tpu_custom_call" | custom-call | tf_op jit(solution)/shard_map/voxel/pallas_call | solution.py:472
  49.9 0.1 collective-permute-start.17
  50.0 1.1 %forward.3.own_ref = f32[17,8,128]{2,1,0:T(8,128)S(1)} custom-call(bf16[32,2,256,256]{3,2,1,0:T(8,128)(2,1)S(1)} %copy-done, bf16[256,256]{1,0:T(8,128)(2,1)S(1)} %get-tuple-element.44.lhs_ref, f32[8,128]{1,0:T(8,128)S(1)} %get-tuple-element.45.acc_ref), custom_call_target="tpu_custom_call" | custom-call | tf_op jit(solution)/shard_map/forward/pallas_call | solution.py:472
  51.1 0.1 collective-permute-done.17.other_ref
  51.3 2.3 %collective-permute-start.20 = (bf16[144,128]{1,0:T(8,128)(2,1)S(1)}, bf16[144,128]{1,0:T(8,128)(2,1)S(1)}, u32[]{:S(2)}, u32[]{:S(2)}) collective-permute-start(bf16[144,128]{1,0:T(8,128)(2,1)S(1)} %get-tuple-element.47.refs_0_), channel_id=1, source_target_pairs={{0,6},{1,7},{2,4},{3,5},{4,2},{5,3},{6,0},{7,1},{8,14},{9,15},{10,... | collective-permute-start | bytes 110600 | tf_op jit(solution)/shard_map/ppermute | solution.py:454
  53.6 2.2 %collective-permute-start.18 = (bf16[144,128]{1,0:T(8,128)(2,1)S(1)}, bf16[144,128]{1,0:T(8,128)(2,1)S(1)}, u32[]{:S(2)}, u32[]{:S(2)}) collective-permute-start(bf16[144,128]{1,0:T(8,128)(2,1)S(1)} %get-tuple-element.47.refs_0_), channel_id=1, source_target_pairs={{0,2},{1,3},{2,0},{3,1},{4,6},{5,7},{6,4},{7,5},{8,10},{9,11},{10,... | collective-permute-start | bytes 110600 | tf_op jit(solution)/shard_map/ppermute | solution.py:454
  55.7 1.7 %collective-permute-start.25 = (bf16[256,256]{1,0:T(8,128)(2,1)S(1)}, bf16[256,256]{1,0:T(8,128)(2,1)S(1)}, u32[]{:S(2)}, u32[]{:S(2)}) collective-permute-start(bf16[256,256]{1,0:T(8,128)(2,1)S(1)} %get-tuple-element.54), channel_id=1, source_target_pairs={{0,24},{8,16},{16,8},{24,0},{1,25},{9,17},{17,9},{25,1},{2,26},{10... | collective-permute-start | bytes 393224 | tf_op jit(solution)/shard_map/ppermute | solution.py:454
  57.4 0.0 collective-permute-done.20.refs_3_
  57.4 1.2 %collective-permute-done.19.refs_2_ = bf16[144,128]{1,0:T(8,128)(2,1)S(1)} collective-permute-done((bf16[144,128]{1,0:T(8,128)(2,1)S(1)}, bf16[144,128]{1,0:T(8,128)(2,1)S(1)}, u32[]{:S(2)}, u32[]{:S(2)}) %collective-permute-start.19) | collective-permute-done | bytes 36896 | tf_op jit(solution)/shard_map/ppermute | solution.py:454
  58.6 0.0 collective-permute-done.18.refs_1_
  58.6 0.1 half_ray.3
  58.7 0.1 collective-permute-start.21
  58.8 1.2 %collective-permute-done.21.other_ref = f32[8,128]{1,0:T(8,128)S(1)} collective-permute-done((f32[8,128]{1,0:T(8,128)S(1)}, f32[8,128]{1,0:T(8,128)S(1)}, u32[]{:S(2)}, u32[]{:S(2)}) %collective-permute-start.21) | collective-permute-done | bytes 4128 | tf_op jit(solution)/shard_map/ppermute | solution.py:454
  59.9 1.7 %collective-permute-start.24 = (f32[8,128]{1,0:T(8,128)S(1)}, f32[8,128]{1,0:T(8,128)S(1)}, u32[]{:S(2)}, u32[]{:S(2)}) collective-permute-start(f32[8,128]{1,0:T(8,128)S(1)} %sum.1.refs_0_), channel_id=1, source_target_pairs={{0,24},{8,16},{16,8},{24,0},{1,25},{9,17},{17,9},{25,1},{2,26},{10... | collective-permute-start | bytes 12296 | tf_op jit(solution)/shard_map/ppermute | solution.py:454
  61.6 1.3 %collective-permute-start.23 = (f32[8,128]{1,0:T(8,128)S(1)}, f32[8,128]{1,0:T(8,128)S(1)}, u32[]{:S(2)}, u32[]{:S(2)}) collective-permute-start(f32[8,128]{1,0:T(8,128)S(1)} %sum.1.refs_0_), channel_id=1, source_target_pairs={{0,16},{8,24},{16,0},{24,8},{1,17},{9,25},{17,1},{25,9},{2,18},{10... | collective-permute-start | bytes 12296 | tf_op jit(solution)/shard_map/ppermute | solution.py:454
  62.9 0.5 collective-permute-start.22
  63.4 0.3 pick.1.refs_0_
  63.7 0.4 share.3.refs_9_
  64.2 0.8 %share.2.refs_8_ = f32[512,256]{1,0:T(8,128)S(1)} custom-call(bf16[512,1024]{1,0:T(8,128)(2,1)S(1)} %pick.1.refs_0_, bf16[1024,256]{1,0:T(8,128)(2,1)S(1)} %get-tuple-element.53.refs_1_, bf16[256,256]{1,0:T(8,128)(2,1)S(1)} %get-tuple-element.35.refs_0_.refs_2_, bf16[256,256]{1,0:T(8,128)(2,1)S(1)} %collective-permute-done.8.refs_0_.refs_3_, ...), custom_call_target="tpu_custom_call" | custom-call | tf_op jit(solution)/shard_map/share/pallas_call | solution.py:472
  65.0 0.2 collective-permute-done.23.refs_2_
  65.2 1.3 %collective-permute-done.22.refs_1_ = f32[8,128]{1,0:T(8,128)S(1)} collective-permute-done((f32[8,128]{1,0:T(8,128)S(1)}, f32[8,128]{1,0:T(8,128)S(1)}, u32[]{:S(2)}, u32[]{:S(2)}) %collective-permute-start.22) | collective-permute-done | bytes 4128 | tf_op jit(solution)/shard_map/ppermute | solution.py:454
  66.5 1.3 %final.1 = (f32[4,32768]{1,0:T(4,128)}, f32[4]{0:T(128)}) custom-call(f32[8,128]{1,0:T(8,128)S(1)} %sum.1.refs_0_, f32[8,128]{1,0:T(8,128)S(1)} %collective-permute-done.22.refs_1_, f32[8,128]{1,0:T(8,128)S(1)} %collective-permute-done.23.refs_2_, f32[8,128]{1,0:T(8,128)S(1)} %collective-permute-done.24.refs_3_, ...), custom_call_target="tpu_custom_call" | custom-call | tf_op jit(solution)/shard_map/final/pallas_call | solution.py:579
  (14 shorter events, 0.1 us)
Async XLA Ops:
  0.6 8.4 %copy-start = (bf16[32,2,256,256]{3,2,1,0:T(8,128)(2,1)S(1)}, bf16[32,2,256,256]{3,2,1,0:T(8,128)(2,1)}, u32[]{:S(2)}) copy-start(bf16[32,2,256,256]{3,2,1,0:T(8,128)(2,1)} %tiles_ref.15) | copy-start | bytes 25165828
  0.6 0.9 %copy-start.1 = (f32[4,1024]{1,0:T(4,128)S(1)}, f32[4,1024]{1,0:T(4,128)}, u32[]{:S(2)}) copy-start(f32[4,1024]{1,0:T(4,128)} %obs_ref.1) | copy-start | bytes 49156
  1.5 7.0 %copy-start.2 = (s32[32,2]{0,1:T(2,128)S(1)}, s32[32,2]{0,1:T(2,128)}, u32[]{:S(2)}) copy-start(s32[32,2]{0,1:T(2,128)} %param.5) | copy-start | bytes 772
  1.5 1.4 %collective-permute-start = (f32[5,8,128]{2,1,0:T(8,128)S(1)}, f32[5,8,128]{2,1,0:T(8,128)S(1)}, u32[]{:S(2)}, u32[]{:S(2)}) collective-permute-start(f32[5,8,128]{2,1,0:T(8,128)S(1)} %pack.1.unread_ref.own_ref), channel_id=1, source_target_pairs={{0,1},{1,0},{2,3},{3,2},{4,5},{5,4},{6,7},{7,6},{8,9},{9,8},{10,11... | collective-permute-start | bytes 61448 | tf_op jit(solution)/shard_map/ppermute | solution.py:454
  2.9 6.9 %collective-permute-start.3 = (f32[9,8,128]{2,1,0:T(8,128)S(1)}, f32[9,8,128]{2,1,0:T(8,128)S(1)}, u32[]{:S(2)}, u32[]{:S(2)}) collective-permute-start(f32[9,8,128]{2,1,0:T(8,128)S(1)} %join.1.pair_ref.refs_2_.refs_4_), channel_id=1, source_target_pairs={{0,6},{1,7},{2,4},{3,5},{4,2},{5,3},{6,0},{7,1},{8,14},{9,15},{10,... | collective-permute-start | bytes 110600 | tf_op jit(solution)/shard_map/ppermute | solution.py:454
  7.8 4.9 %collective-permute-start.2 = (f32[9,8,128]{2,1,0:T(8,128)S(1)}, f32[9,8,128]{2,1,0:T(8,128)S(1)}, u32[]{:S(2)}, u32[]{:S(2)}) collective-permute-start(f32[9,8,128]{2,1,0:T(8,128)S(1)} %join.1.pair_ref.refs_2_.refs_4_), channel_id=1, source_target_pairs={{0,4},{1,5},{2,6},{3,7},{4,0},{5,1},{6,2},{7,3},{8,12},{9,13},{10,... | collective-permute-start | bytes 110600 | tf_op jit(solution)/shard_map/ppermute | solution.py:454
  7.8 4.9 %collective-permute-start.1 = (f32[9,8,128]{2,1,0:T(8,128)S(1)}, f32[9,8,128]{2,1,0:T(8,128)S(1)}, u32[]{:S(2)}, u32[]{:S(2)}) collective-permute-start(f32[9,8,128]{2,1,0:T(8,128)S(1)} %join.1.pair_ref.refs_2_.refs_4_), channel_id=1, source_target_pairs={{0,2},{1,3},{2,0},{3,1},{4,6},{5,7},{6,4},{7,5},{8,10},{9,11},{10,... | collective-permute-start | bytes 110600 | tf_op jit(solution)/shard_map/ppermute | solution.py:454
  13.6 6.9 %collective-permute-start.6 = (bf16[272,256]{1,0:T(8,128)(2,1)S(1)}, bf16[272,256]{1,0:T(8,128)(2,1)S(1)}, u32[]{:S(2)}, u32[]{:S(2)}) collective-permute-start(bf16[272,256]{1,0:T(8,128)(2,1)S(1)} %get-tuple-element.31.refs_0_), channel_id=1, source_target_pairs={{0,24},{8,16},{16,8},{24,0},{1,25},{9,17},{17,9},{25,1},{2,26},{10... | collective-permute-start | bytes 417800 | tf_op jit(solution)/shard_map/ppermute | solution.py:454
  16.1 6.2 %collective-permute-start.5 = (bf16[272,256]{1,0:T(8,128)(2,1)S(1)}, bf16[272,256]{1,0:T(8,128)(2,1)S(1)}, u32[]{:S(2)}, u32[]{:S(2)}) collective-permute-start(bf16[272,256]{1,0:T(8,128)(2,1)S(1)} %get-tuple-element.31.refs_0_), channel_id=1, source_target_pairs={{0,16},{8,24},{16,0},{24,8},{1,17},{9,25},{17,1},{25,9},{2,18},{10... | collective-permute-start | bytes 417800 | tf_op jit(solution)/shard_map/ppermute | solution.py:454
  16.6 5.7 %collective-permute-start.4 = (bf16[272,256]{1,0:T(8,128)(2,1)S(1)}, bf16[272,256]{1,0:T(8,128)(2,1)S(1)}, u32[]{:S(2)}, u32[]{:S(2)}) collective-permute-start(bf16[272,256]{1,0:T(8,128)(2,1)S(1)} %get-tuple-element.31.refs_0_), channel_id=1, source_target_pairs={{0,8},{8,0},{16,24},{24,16},{1,9},{9,1},{17,25},{25,17},{2,10},{10... | collective-permute-start | bytes 417800 | tf_op jit(solution)/shard_map/ppermute | solution.py:454
  25.3 1.3 %collective-permute-start.7 = (f32[17,8,128]{2,1,0:T(8,128)S(1)}, f32[17,8,128]{2,1,0:T(8,128)S(1)}, u32[]{:S(2)}, u32[]{:S(2)}) collective-permute-start(f32[17,8,128]{2,1,0:T(8,128)S(1)} %get-tuple-element.34), channel_id=1, source_target_pairs={{0,1},{1,0},{2,3},{3,2},{4,5},{5,4},{6,7},{7,6},{8,9},{9,8},{10,11... | collective-permute-start | bytes 208904 | tf_op jit(solution)/shard_map/ppermute | solution.py:454
  26.7 6.9 %collective-permute-start.12 = (f32[17,8,128]{2,1,0:T(8,128)S(1)}, f32[17,8,128]{2,1,0:T(8,128)S(1)}, u32[]{:S(2)}, u32[]{:S(2)}) collective-permute-start(f32[17,8,128]{2,1,0:T(8,128)S(1)} %get-tuple-element.37.refs_0_), channel_id=1, source_target_pairs={{0,6},{1,7},{2,4},{3,5},{4,2},{5,3},{6,0},{7,1},{8,14},{9,15},{10,... | collective-permute-start | bytes 208904 | tf_op jit(solution)/shard_map/ppermute | solution.py:454
  28.3 7.8 %collective-permute-start.11 = (f32[17,8,128]{2,1,0:T(8,128)S(1)}, f32[17,8,128]{2,1,0:T(8,128)S(1)}, u32[]{:S(2)}, u32[]{:S(2)}) collective-permute-start(f32[17,8,128]{2,1,0:T(8,128)S(1)} %get-tuple-element.37.refs_0_), channel_id=1, source_target_pairs={{0,4},{1,5},{2,6},{3,7},{4,0},{5,1},{6,2},{7,3},{8,12},{9,13},{10,... | collective-permute-start | bytes 208904 | tf_op jit(solution)/shard_map/ppermute | solution.py:454
  28.7 7.4 %collective-permute-start.10 = (f32[17,8,128]{2,1,0:T(8,128)S(1)}, f32[17,8,128]{2,1,0:T(8,128)S(1)}, u32[]{:S(2)}, u32[]{:S(2)}) collective-permute-start(f32[17,8,128]{2,1,0:T(8,128)S(1)} %get-tuple-element.37.refs_0_), channel_id=1, source_target_pairs={{0,2},{1,3},{2,0},{3,1},{4,6},{5,7},{6,4},{7,5},{8,10},{9,11},{10,... | collective-permute-start | bytes 208904 | tf_op jit(solution)/shard_map/ppermute | solution.py:454
  31.2 6.3 %collective-permute-start.9 = (bf16[256,256]{1,0:T(8,128)(2,1)S(1)}, bf16[256,256]{1,0:T(8,128)(2,1)S(1)}, u32[]{:S(2)}, u32[]{:S(2)}) collective-permute-start(bf16[256,256]{1,0:T(8,128)(2,1)S(1)} %get-tuple-element.36), channel_id=1, source_target_pairs={{0,16},{8,24},{16,0},{24,8},{1,17},{9,25},{17,1},{25,9},{2,18},{10... | collective-permute-start | bytes 393224 | tf_op jit(solution)/shard_map/ppermute | solution.py:454
  32.6 5.0 %collective-permute-start.8 = (bf16[256,256]{1,0:T(8,128)(2,1)S(1)}, bf16[256,256]{1,0:T(8,128)(2,1)S(1)}, u32[]{:S(2)}, u32[]{:S(2)}) collective-permute-start(bf16[256,256]{1,0:T(8,128)(2,1)S(1)} %get-tuple-element.36), channel_id=1, source_target_pairs={{0,8},{8,0},{16,24},{24,16},{1,9},{9,1},{17,25},{25,17},{2,10},{10... | collective-permute-start | bytes 393224 | tf_op jit(solution)/shard_map/ppermute | solution.py:454
  36.2 1.3 %collective-permute-start.13 = (bf16[80,256]{1,0:T(8,128)(2,1)S(1)}, bf16[80,256]{1,0:T(8,128)(2,1)S(1)}, u32[]{:S(2)}, u32[]{:S(2)}) collective-permute-start(bf16[80,256]{1,0:T(8,128)(2,1)S(1)} %get-tuple-element.39.half_ref.refs_3_), channel_id=1, source_target_pairs={{0,1},{1,0},{2,3},{3,2},{4,5},{5,4},{6,7},{7,6},{8,9},{9,8},{10,11... | collective-permute-start | bytes 122888 | tf_op jit(solution)/shard_map/ppermute | solution.py:454
  38.2 7.5 %collective-permute-start.16 = (bf16[272,256]{1,0:T(8,128)(2,1)S(1)}, bf16[272,256]{1,0:T(8,128)(2,1)S(1)}, u32[]{:S(2)}, u32[]{:S(2)}) collective-permute-start(bf16[272,256]{1,0:T(8,128)(2,1)S(1)} %adjoint.3.refs_0_.unread_ref), channel_id=1, source_target_pairs={{0,24},{8,16},{16,8},{24,0},{1,25},{9,17},{17,9},{25,1},{2,26},{10... | collective-permute-start | bytes 417800 | tf_op jit(solution)/shard_map/ppermute | solution.py:454
  39.9 7.9 %collective-permute-start.15 = (bf16[272,256]{1,0:T(8,128)(2,1)S(1)}, bf16[272,256]{1,0:T(8,128)(2,1)S(1)}, u32[]{:S(2)}, u32[]{:S(2)}) collective-permute-start(bf16[272,256]{1,0:T(8,128)(2,1)S(1)} %adjoint.3.refs_0_.unread_ref), channel_id=1, source_target_pairs={{0,16},{8,24},{16,0},{24,8},{1,17},{9,25},{17,1},{25,9},{2,18},{10... | collective-permute-start | bytes 417800 | tf_op jit(solution)/shard_map/ppermute | solution.py:454
  41.2 6.7 %collective-permute-start.14 = (bf16[272,256]{1,0:T(8,128)(2,1)S(1)}, bf16[272,256]{1,0:T(8,128)(2,1)S(1)}, u32[]{:S(2)}, u32[]{:S(2)}) collective-permute-start(bf16[272,256]{1,0:T(8,128)(2,1)S(1)} %adjoint.3.refs_0_.unread_ref), channel_id=1, source_target_pairs={{0,8},{8,0},{16,24},{24,16},{1,9},{9,1},{17,25},{25,17},{2,10},{10... | collective-permute-start | bytes 417800 | tf_op jit(solution)/shard_map/ppermute | solution.py:454
  49.9 1.3 %collective-permute-start.17 = (f32[17,8,128]{2,1,0:T(8,128)S(1)}, f32[17,8,128]{2,1,0:T(8,128)S(1)}, u32[]{:S(2)}, u32[]{:S(2)}) collective-permute-start(f32[17,8,128]{2,1,0:T(8,128)S(1)} %get-tuple-element.46), channel_id=1, source_target_pairs={{0,1},{1,0},{2,3},{3,2},{4,5},{5,4},{6,7},{7,6},{8,9},{9,8},{10,11... | collective-permute-start | bytes 208904 | tf_op jit(solution)/shard_map/ppermute | solution.py:454
  51.3 6.1 %collective-permute-start.20 = (bf16[144,128]{1,0:T(8,128)(2,1)S(1)}, bf16[144,128]{1,0:T(8,128)(2,1)S(1)}, u32[]{:S(2)}, u32[]{:S(2)}) collective-permute-start(bf16[144,128]{1,0:T(8,128)(2,1)S(1)} %get-tuple-element.47.refs_0_), channel_id=1, source_target_pairs={{0,6},{1,7},{2,4},{3,5},{4,2},{5,3},{6,0},{7,1},{8,14},{9,15},{10,... | collective-permute-start | bytes 110600 | tf_op jit(solution)/shard_map/ppermute | solution.py:454
  53.6 5.0 %collective-permute-start.19 = (bf16[144,128]{1,0:T(8,128)(2,1)S(1)}, bf16[144,128]{1,0:T(8,128)(2,1)S(1)}, u32[]{:S(2)}, u32[]{:S(2)}) collective-permute-start(bf16[144,128]{1,0:T(8,128)(2,1)S(1)} %get-tuple-element.47.refs_0_), channel_id=1, source_target_pairs={{0,4},{1,5},{2,6},{3,7},{4,0},{5,1},{6,2},{7,3},{8,12},{9,13},{10,... | collective-permute-start | bytes 110600 | tf_op jit(solution)/shard_map/ppermute | solution.py:454
  53.6 5.0 %collective-permute-start.18 = (bf16[144,128]{1,0:T(8,128)(2,1)S(1)}, bf16[144,128]{1,0:T(8,128)(2,1)S(1)}, u32[]{:S(2)}, u32[]{:S(2)}) collective-permute-start(bf16[144,128]{1,0:T(8,128)(2,1)S(1)} %get-tuple-element.47.refs_0_), channel_id=1, source_target_pairs={{0,2},{1,3},{2,0},{3,1},{4,6},{5,7},{6,4},{7,5},{8,10},{9,11},{10,... | collective-permute-start | bytes 110600 | tf_op jit(solution)/shard_map/ppermute | solution.py:454
  55.7 8.4 %collective-permute-start.25 = (bf16[256,256]{1,0:T(8,128)(2,1)S(1)}, bf16[256,256]{1,0:T(8,128)(2,1)S(1)}, u32[]{:S(2)}, u32[]{:S(2)}) collective-permute-start(bf16[256,256]{1,0:T(8,128)(2,1)S(1)} %get-tuple-element.54), channel_id=1, source_target_pairs={{0,24},{8,16},{16,8},{24,0},{1,25},{9,17},{17,9},{25,1},{2,26},{10... | collective-permute-start | bytes 393224 | tf_op jit(solution)/shard_map/ppermute | solution.py:454
  58.7 1.2 %collective-permute-start.21 = (f32[8,128]{1,0:T(8,128)S(1)}, f32[8,128]{1,0:T(8,128)S(1)}, u32[]{:S(2)}, u32[]{:S(2)}) collective-permute-start(f32[8,128]{1,0:T(8,128)S(1)} %get-tuple-element.50.own_ref), channel_id=1, source_target_pairs={{0,1},{1,0},{2,3},{3,2},{4,5},{5,4},{6,7},{7,6},{8,9},{9,8},{10,11... | collective-permute-start | bytes 12296 | tf_op jit(solution)/shard_map/ppermute | solution.py:454
  59.9 5.0 %collective-permute-start.24 = (f32[8,128]{1,0:T(8,128)S(1)}, f32[8,128]{1,0:T(8,128)S(1)}, u32[]{:S(2)}, u32[]{:S(2)}) collective-permute-start(f32[8,128]{1,0:T(8,128)S(1)} %sum.1.refs_0_), channel_id=1, source_target_pairs={{0,24},{8,16},{16,8},{24,0},{1,25},{9,17},{17,9},{25,1},{2,26},{10... | collective-permute-start | bytes 12296 | tf_op jit(solution)/shard_map/ppermute | solution.py:454
  61.6 3.6 %collective-permute-start.23 = (f32[8,128]{1,0:T(8,128)S(1)}, f32[8,128]{1,0:T(8,128)S(1)}, u32[]{:S(2)}, u32[]{:S(2)}) collective-permute-start(f32[8,128]{1,0:T(8,128)S(1)} %sum.1.refs_0_), channel_id=1, source_target_pairs={{0,16},{8,24},{16,0},{24,8},{1,17},{9,25},{17,1},{25,9},{2,18},{10... | collective-permute-start | bytes 12296 | tf_op jit(solution)/shard_map/ppermute | solution.py:454
  62.9 3.6 %collective-permute-start.22 = (f32[8,128]{1,0:T(8,128)S(1)}, f32[8,128]{1,0:T(8,128)S(1)}, u32[]{:S(2)}, u32[]{:S(2)}) collective-permute-start(f32[8,128]{1,0:T(8,128)S(1)} %sum.1.refs_0_), channel_id=1, source_target_pairs={{0,8},{8,0},{16,24},{24,16},{1,9},{9,1},{17,25},{25,17},{2,10},{10... | collective-permute-start | bytes 12296 | tf_op jit(solution)/shard_map/ppermute | solution.py:454
